TPU v7x, 32 devices: a whole 2x2x4 slice. The times are simulated.
32 devices in a mesh: inst: 16 (over z, y, core), tp: 2 (over x).
Axes of the slice: x: 2, y: 2, z: 4, core: 2. Of those that a mesh axis runs over, the one named last changes fastest.
Arguments:
- tokens_in: bfloat16 [4096, 8192], P('inst', 'tp'), may hold values from -32 to 32
- w_query: bfloat16 [8192, 4096], P('inst', 'tp'), may hold values from -1 to 1
- w_key: bfloat16 [8192, 1024], P('inst', 'tp'), may hold values from -1 to 1
- w_value: bfloat16 [8192, 1024], P('inst', 'tp'), may hold values from -0.0625 to 0.0625
- stored_key_cache: bfloat16 [28672, 1024], P('inst', 'tp'), may hold values from -6 to 6
- stored_value_cache: bfloat16 [28672, 1024], P('inst', 'tp'), may hold values from -6 to 6
- prompt_len: int32 [16], P('inst'), may hold values from 64 to 256
Outputs:
- attended: bfloat16 [4096, 4096], P('inst', 'tp')
- handoff: bfloat16 [16, 4096], P(None, 'tp')
All inputs are finite; a program needn't handle non-finite values.
Results may differ from a plain program's by a relative error of at most 0.011.
Values may be sent and summed in bfloat16 or wider, within the bound.
No kernel may reach another device: no remote copies, remote signals or barrier semaphores. Data moves between devices by JAX's collectives and lax.ppermute only.
A program may use at most 128 MiB of HBM per device.

v0:
```python
import jax
import jax.numpy as jnp
from jax import lax
from jax.sharding import PartitionSpec as P

HEAD_SIZE = 128
QUERY_PER_GROUP = 4


def add_rows(whole, piece):
    return jnp.dot(whole, piece, preferred_element_type=jnp.float32)


def shards(tokens_in, w_query, w_key, w_value, stored_key_cache, stored_value_cache, prompt_len):
    whole = lax.all_gather(tokens_in, "tp", axis=1, tiled=True)
    block_rows = whole.shape[0]
    qsum = add_rows(whole, lax.all_gather(w_query, "inst", axis=0, tiled=True))
    ksum = add_rows(whole, lax.all_gather(w_key, "inst", axis=0, tiled=True))
    vsum = add_rows(whole, lax.all_gather(w_value, "inst", axis=0, tiled=True))
    heads = w_key.shape[1] // HEAD_SIZE
    prefix_rows = stored_key_cache.shape[0]
    query_matrix = qsum.astype(jnp.bfloat16).reshape(block_rows, heads, QUERY_PER_GROUP, HEAD_SIZE)
    key_matrix = ksum.astype(jnp.bfloat16).reshape(block_rows, heads, HEAD_SIZE)
    value_matrix = vsum.astype(jnp.bfloat16).reshape(block_rows, heads, HEAD_SIZE)
    key_all = jnp.concatenate(
        [stored_key_cache.reshape(prefix_rows, heads, HEAD_SIZE), key_matrix], axis=0
    )
    value_all = jnp.concatenate(
        [stored_value_cache.reshape(prefix_rows, heads, HEAD_SIZE), value_matrix], axis=0
    )
    positions = jnp.arange(block_rows, dtype=jnp.int32)
    key_pos = jnp.arange(prefix_rows + block_rows, dtype=jnp.int32) - prefix_rows
    length = prompt_len[0]
    allowed = (key_pos[None, :] <= positions[:, None]) & (key_pos[None, :] < length)
    scale = jnp.sqrt(jnp.float32(HEAD_SIZE))
    outputs = []
    for member in range(QUERY_PER_GROUP):
        scores = (
            jnp.einsum(
                "tgd,sgd->gts",
                query_matrix[:, :, member, :],
                key_all,
                preferred_element_type=jnp.float32,
            )
            / scale
        )
        scores = jnp.where(allowed[None], scores, -jnp.inf)
        probs = jax.nn.softmax(scores, axis=-1).astype(jnp.bfloat16)
        outputs.append(
            jnp.einsum("gts,sgd->tgd", probs, value_all, preferred_element_type=jnp.float32)
        )
    mixed = jnp.stack(outputs, axis=2)
    attended = mixed.astype(jnp.bfloat16).reshape(block_rows, heads * QUERY_PER_GROUP * HEAD_SIZE)
    last_row = lax.dynamic_slice_in_dim(attended, length - 1, 1, 0)
    handoff = lax.all_gather(last_row, "inst", axis=0, tiled=True)
    return (attended, handoff)


def solution(mesh):
    return jax.shard_map(
        shards,
        mesh=mesh,
        in_specs=(
            P("inst", "tp"),
            P("inst", "tp"),
            P("inst", "tp"),
            P("inst", "tp"),
            P("inst", "tp"),
            P("inst", "tp"),
            P("inst"),
        ),
        out_specs=(P("inst", "tp"), P(None, "tp")),
        check_vma=False,
    )
```

profile of v0, /device:TPU:0, one launch (start us, length us, event | category | flops | bytes accessed | tf_op | source)
XLA Modules:
  0.0 486.8 jit_solution(14030106890563586491)
XLA Ops:
  7.2 0.7 all-gather.6.cloned.1.call-update
  7.9 0.7 all-gather.12.cloned.1.call-update
  8.7 0.7 all-gather.8.cloned.1.call-update
  9.4 0.5 all-gather.10.cloned.1.call-update
  10.6 2.8 copy.52
  13.4 2.3 copy.53
  15.7 2.8 copy.49
  18.6 0.4 fusion.24
  18.9 50.1 %all-gather.6.cloned.1.call-done = bf16[256,8192]{1,0:T(8,128)(2,1)} async-done(((bf16[256,4096]{1,0:T(8,128)(2,1)}), bf16[256,8192]{1,0:T(8,128)(2,1)}) %all-gather.6.cloned.1.call-update) | async-done | bytes 4194320 | tf_op jit(solution)/shard_map/all_gather | solution.py:15
  69.0 77.1 %all-gather.12.cloned.1.call-done = bf16[8192,512]{1,0:T(8,128)(2,1)} async-done(((bf16[512,512]{1,0:T(8,128)(2,1)}), bf16[8192,512]{1,0:T(8,128)(2,1)}) %all-gather.12.cloned.1.call-update) | async-done | bytes 8388624 | tf_op jit(solution)/shard_map/all_gather | solution.py:18
  146.1 7.0 %fusion.29 = bf16[32,4,8,128]{3,2,1,0:T(8,128)(2,1)S(1)} fusion(bf16[256,8192]{1,0:T(8,128)(2,1)} %all-gather.6.cloned.1.call-done, bf16[8192,512]{1,0:T(8,128)(2,1)} %all-gather.12.cloned.1.call-done), kind=kOutput, calls=%fused_computation.47 | convolution fusion | flops 2147614720 | bytes 12845056 | tf_op jit(solution)/shard_map/dot_general | solution.py:11
  153.1 0.8 copy.113
  153.9 67.6 %all-gather.8.cloned.1.call-done = bf16[8192,512]{1,0:T(8,128)(2,1)} async-done(((bf16[512,512]{1,0:T(8,128)(2,1)}), bf16[8192,512]{1,0:T(8,128)(2,1)}) %all-gather.8.cloned.1.call-update) | async-done | bytes 8388624 | tf_op jit(solution)/shard_map/all_gather | solution.py:19
  221.5 7.0 %convolution_convert_fusion.2 = bf16[256,512]{1,0:T(8,128)(2,1)S(1)} fusion(bf16[256,8192]{1,0:T(8,128)(2,1)} %all-gather.6.cloned.1.call-done, bf16[8192,512]{1,0:T(8,128)(2,1)} %all-gather.8.cloned.1.call-done), kind=kOutput, calls=%fused_computation.46 | convolution fusion | flops 2147614720 | bytes 12845056 | tf_op jit(solution)/shard_map/dot_general | solution.py:11
  228.4 0.9 copy.60
  229.3 160.0 %all-gather.10.cloned.1.call-done = bf16[8192,2048]{1,0:T(8,128)(2,1)} async-done(((bf16[512,2048]{1,0:T(8,128)(2,1)}), bf16[8192,2048]{1,0:T(8,128)(2,1)}) %all-gather.10.cloned.1.call-update) | async-done | bytes 33554448 | tf_op jit(solution)/shard_map/all_gather | solution.py:17
  389.3 17.0 %convolution_convert_fusion = bf16[256,2048]{1,0:T(8,128)(2,1)} fusion(bf16[256,8192]{1,0:T(8,128)(2,1)} %all-gather.6.cloned.1.call-done, bf16[8192,2048]{1,0:T(8,128)(2,1)} %all-gather.10.cloned.1.call-done), kind=kOutput, calls=%fused_computation.36 | convolution fusion | flops 8590458880 | bytes 38797312 | tf_op jit(solution)/shard_map/dot_general | solution.py:11
  406.3 1.8 reshape.75
  408.1 2.6 fusion.54
  410.6 7.9 %fusion.58 = (f32[4,256]{1,0:T(4,128)S(1)}, f32[4,256,2048]{2,1,0:T(8,128)}) fusion(pred[256,2048]{1,0:T(8,128)(4,1)S(1)} %fusion.24, bf16[256,4,1,128]{3,2,1,0:T(2,128)(2,1)} %get-tuple-element.10, bf16[256,4,128]{2,0,1:T(8,128)(2,1)} %bitcast.97, bf16[1792,4,128]{2,0,1:T(8,128)(2,1)} %copy.53), kind=kOutput, calls=%fused_computation.82 | convolution fusion | flops 549455872 | bytes 11276288 | tf_op jit(solution)/shard_map/sub | solution.py:48
  418.6 7.8 %fusion.57 = (f32[4,256]{1,0:T(4,128)S(1)}, f32[4,256,2048]{2,1,0:T(8,128)}) fusion(pred[256,2048]{1,0:T(8,128)(4,1)S(1)} %fusion.24, bf16[256,4,1,128]{3,2,1,0:T(2,128)(2,1)S(1)} %copy-done.2, bf16[256,4,128]{2,0,1:T(8,128)(2,1)} %bitcast.98, bf16[1792,4,128]{2,0,1:T(8,128)(2,1)} %copy.53), kind=kOutput, calls=%fused_computation.81 | convolution fusion | flops 549455872 | bytes 11276288 | tf_op jit(solution)/shard_map/sub | solution.py:48
  426.4 7.8 %fusion.56 = (f32[4,256]{1,0:T(4,128)S(1)}, f32[4,256,2048]{2,1,0:T(8,128)}) fusion(pred[256,2048]{1,0:T(8,128)(4,1)S(1)} %fusion.24, bf16[256,4,1,128]{3,2,1,0:T(2,128)(2,1)S(1)} %copy-done.1, bf16[256,4,128]{2,0,1:T(8,128)(2,1)} %bitcast.99, bf16[1792,4,128]{2,0,1:T(8,128)(2,1)} %copy.53), kind=kOutput, calls=%fused_computation.80 | convolution fusion | flops 549455872 | bytes 11276288 | tf_op jit(solution)/shard_map/sub | solution.py:48
  434.1 7.8 %fusion.55 = (f32[4,256]{1,0:T(4,128)S(1)}, f32[4,256,2048]{2,1,0:T(8,128)}) fusion(pred[256,2048]{1,0:T(8,128)(4,1)S(1)} %fusion.24, bf16[256,4,1,128]{3,2,1,0:T(2,128)(2,1)S(1)} %copy-done, bf16[256,4,128]{2,0,1:T(8,128)(2,1)} %bitcast.100, bf16[1792,4,128]{2,0,1:T(8,128)(2,1)} %copy.53), kind=kOutput, calls=%fused_computation.79 | convolution fusion | flops 549455872 | bytes 11276288 | tf_op jit(solution)/shard_map/sub | solution.py:48
  441.9 5.3 %fusion.30 = bf16[256,4,1,128]{0,3,1,2:T(8,128)(2,1)S(1)} fusion(f32[4,256,2048]{2,1,0:T(8,128)} %get-tuple-element.21, f32[4,256]{1,0:T(4,128)S(1)} %get-tuple-element.20, bf16[256,4,128]{0,2,1:T(8,128)(2,1)S(1)} %bitcast.93, bf16[1792,4,128]{0,2,1:T(8,128)(2,1)S(1)} %bitcast.89), kind=kOutput, calls=%fused_computation.48 | convolution fusion | flops 545390592 | bytes 10752000 | tf_op jit(solution)/shard_map/gts,sgd->tgd/dot_general | solution.py:50
  447.3 5.1 %fusion.31 = bf16[256,4,1,128]{0,3,1,2:T(8,128)(2,1)S(1)} fusion(f32[4,256,2048]{2,1,0:T(8,128)} %get-tuple-element.19, f32[4,256]{1,0:T(4,128)S(1)} %get-tuple-element.18, bf16[256,4,128]{0,2,1:T(8,128)(2,1)S(1)} %bitcast.94, bf16[1792,4,128]{0,2,1:T(8,128)(2,1)S(1)} %bitcast.90), kind=kOutput, calls=%fused_computation.49 | convolution fusion | flops 545390592 | bytes 10752000 | tf_op jit(solution)/shard_map/gts,sgd->tgd/dot_general | solution.py:50
  452.5 1.9 fusion.32
  454.4 0.4 slice-done.1
  454.8 1.9 fusion.33
  457.0 1.4 copy.59
  458.4 0.4 dynamic-slice_reduce_fusion
  458.8 20.8 %all-gather = bf16[16,1,2048]{2,1,0:T(2,128)(2,1)S(1)} all-gather(bf16[1,1,2048]{2,1,0:T(2,128)(2,1)S(1)} %reshape.78), channel_id=1, replica_groups=mesh['inst'=16,'tp'=2] {'inst'}, dimensions={0}, use_global_device_ids=true | all-gather | bytes 69632 | tf_op jit(solution)/shard_map/all_gather | solution.py:55
  479.6 0.7 copy.114
  (26 shorter events, 0.4 us)
Async XLA Ops:
  7.2 61.9 %all-gather.6.cloned.1.call-start = ((), (), s32[]{:S(2)}) async-start(), calls=%async_computation | async-start | bytes 6291456 | tf_op jit(solution)/shard_map/all_gather | solution.py:15
  7.9 138.2 %all-gather.12.cloned.1.call-start = ((), (), s32[]{:S(2)}) async-start(), calls=%async_computation.3 | async-start | bytes 8912896 | tf_op jit(solution)/shard_map/all_gather | solution.py:18
  8.6 212.8 %all-gather.8.cloned.1.call-start = ((), (), s32[]{:S(2)}) async-start(), calls=%async_computation.1 | async-start | bytes 8912896 | tf_op jit(solution)/shard_map/all_gather | solution.py:19
  9.4 379.9 %all-gather.10.cloned.1.call-start = ((), (), s32[]{:S(2)}) async-start(), calls=%async_computation.2 | async-start | bytes 35651584 | tf_op jit(solution)/shard_map/all_gather | solution.py:17
  410.6 7.9 %copy-start.2 = (bf16[256,4,1,128]{3,2,1,0:T(2,128)(2,1)S(1)}, bf16[256,4,1,128]{3,2,1,0:T(2,128)(2,1)}, u32[]{:S(2)}) copy-start(bf16[256,4,1,128]{3,2,1,0:T(2,128)(2,1)} %get-tuple-element.12) | copy-start | bytes 786436
  418.6 7.8 %copy-start.1 = (bf16[256,4,1,128]{3,2,1,0:T(2,128)(2,1)S(1)}, bf16[256,4,1,128]{3,2,1,0:T(2,128)(2,1)}, u32[]{:S(2)}) copy-start(bf16[256,4,1,128]{3,2,1,0:T(2,128)(2,1)} %get-tuple-element.11) | copy-start | bytes 786436
  426.4 7.8 %copy-start = (bf16[256,4,1,128]{3,2,1,0:T(2,128)(2,1)S(1)}, bf16[256,4,1,128]{3,2,1,0:T(2,128)(2,1)}, u32[]{:S(2)}) copy-start(bf16[256,4,1,128]{3,2,1,0:T(2,128)(2,1)} %get-tuple-element.13) | copy-start | bytes 786436
  434.1 7.8 %copy-start.3 = (bf16[256,512]{0,1:T(8,128)(2,1)S(1)}, bf16[256,512]{0,1:T(8,128)(2,1)}, u32[]{:S(2)}) copy-start(bf16[256,512]{0,1:T(8,128)(2,1)} %copy.60) | copy-start | bytes 786436
  441.9 10.5 %slice-start.2 = ((s8[8388608]{0:T(1024)(128)(4,1)}), s8[4194304]{0:T(1024)(128)(4,1)S(1)}, s32[]{:S(2)}) async-start(s8[8388608]{0:T(1024)(128)(4,1)} %bitcast.104), calls=%async_computation.6 | async-start | bytes 8388608
  447.2 5.2 %slice-start.3 = ((s8[8388608]{0:T(1024)(128)(4,1)}), s8[4194304]{0:T(1024)(128)(4,1)S(1)}, s32[]{:S(2)}) async-start(s8[8388608]{0:T(1024)(128)(4,1)} %bitcast.104), calls=%async_computation.7 | async-start | bytes 8388608
  447.3 7.1 %slice-start = ((s8[8388608]{0:T(1024)(128)(4,1)}), s8[4194304]{0:T(1024)(128)(4,1)S(1)}, s32[]{:S(2)}) async-start(s8[8388608]{0:T(1024)(128)(4,1)} %bitcast.102), calls=%async_computation.4 | async-start | bytes 8388608
  452.4 2.4 slice-start.1
Sparse Core Ops, SparseCore 0:
  9.5 59.4 all-gather.5
  71.2 74.8 all-gather.11
  148.3 73.1 all-gather.7
  222.9 166.2 all-gather.9
where the time goes:
time: 487 us
  waiting for transfers between devices  357 us (73%)
  matrix products  76.5 us (16%)
  blocking collectives  20.8 us (4%)
  local copies, waits for them, and re-layouts  16.9 us (3%)
  between operations  14.6 us (3%)
    all_gather x1, waiting for transfers between devices, shards(): qsum = add_rows(whole, lax.all_gather(w_query, 'inst', axis=0, tiled=True))  160 us
    all_gather x1, waiting for transfers between devices, shards(): ksum = add_rows(whole, lax.all_gather(w_key, 'inst', axis=0, tiled=True))  77.1 us
    all_gather x1, waiting for transfers between devices, shards(): vsum = add_rows(whole, lax.all_gather(w_value, 'inst', axis=0, tiled=True))  67.6 us
    all_gather x1, waiting for transfers between devices, shards(): whole = lax.all_gather(tokens_in, 'tp', axis=1, tiled=True)  50.1 us
    sub x4, matrix products, shards(): probs = jax.nn.softmax(scores, axis=-1).astype(jnp.bfloat16)  31.2 us
    dot_general x3, matrix products, add_rows(): return jnp.dot(whole, piece, preferred_element_type=jnp.float32)  31 us
    all_gather x1, blocking collectives, shards(): handoff = lax.all_gather(last_row, 'inst', axis=0, tiled=True)  20.8 us
    dot_general x4, matrix products, shards(): jnp.einsum('gts,sgd->tgd', probs, value_all, preferred_element_type=jnp.f...  14.3 us
  transfers between devices with their start and end apart: 4, of which 4 were waited for; matrix products, arithmetic and copies ran while one was open for 5% of the time, Pallas kernels for 0%

commit v1 on v0

v1 whole, which is shorter than its diff:
```python
import functools

import jax
import jax.numpy as jnp
from jax import lax
from jax.experimental import pallas as pl
from jax.experimental.pallas import tpu as pltpu
from jax.sharding import PartitionSpec as P

HEAD_SIZE = 128
QUERY_PER_GROUP = 4
INNER = 4


def dot(a, b):
    return jnp.dot(a, b, preferred_element_type=jnp.float32)


def attention_kernel(len_ref, q_ref, kc_ref, vc_ref, kb_ref, vb_ref, prev_ref, o_ref):
    del prev_ref
    length = len_ref[0]
    rows = q_ref.shape[0]
    block = kb_ref.shape[0]
    factor = 1.4426950408889634 / HEAD_SIZE**0.5
    row = lax.broadcasted_iota(jnp.int32, (rows, block), 0)
    col = lax.broadcasted_iota(jnp.int32, (rows, block), 1)
    allowed = (col <= row) & (col < length)
    contract = (((1,), (1,)), ((), ()))
    for member in range(QUERY_PER_GROUP):
        cols = slice(member * HEAD_SIZE, (member + 1) * HEAD_SIZE)
        q = q_ref[:, cols]
        s1 = lax.dot_general(q, kc_ref[...], contract, preferred_element_type=jnp.float32)
        s2 = lax.dot_general(q, kb_ref[...], contract, preferred_element_type=jnp.float32)
        s2 = jnp.where(allowed, s2, -jnp.inf)
        top = jnp.maximum(
            jnp.max(s1, axis=1, keepdims=True), jnp.max(s2, axis=1, keepdims=True)
        )
        p1 = jnp.exp2((s1 - top) * factor)
        p2 = jnp.exp2((s2 - top) * factor)
        total = jnp.sum(p1, axis=1, keepdims=True) + jnp.sum(p2, axis=1, keepdims=True)
        out = dot(p1.astype(jnp.bfloat16), vc_ref[...]) + dot(p2.astype(jnp.bfloat16), vb_ref[...])
        o_ref[:, cols] = (out / total).astype(o_ref.dtype)


def attend(length, q, k_cache, v_cache, k_block, v_block, group, buffer):
    rows = q.shape[0]
    wide = QUERY_PER_GROUP * HEAD_SIZE
    cached = k_cache.shape[0]
    column = lambda i: (0, group)
    return pl.pallas_call(
        attention_kernel,
        grid=(1,),
        out_shape=jax.ShapeDtypeStruct(buffer.shape, buffer.dtype),
        in_specs=[
            pl.BlockSpec(memory_space=pltpu.SMEM),
            pl.BlockSpec((rows, wide), lambda i: (0, 0)),
            pl.BlockSpec((cached, HEAD_SIZE), column),
            pl.BlockSpec((cached, HEAD_SIZE), column),
            pl.BlockSpec((rows, HEAD_SIZE), column),
            pl.BlockSpec((rows, HEAD_SIZE), column),
            pl.BlockSpec(memory_space=pl.ANY),
        ],
        out_specs=pl.BlockSpec((rows, wide), column),
        input_output_aliases={6: 0},
        compiler_params=pltpu.CompilerParams(vmem_limit_bytes=40 * 1024 * 1024),
        cost_estimate=pl.CostEstimate(
            flops=4 * rows * wide * (cached + rows),
            bytes_accessed=4 * (cached + rows) * HEAD_SIZE + 4 * rows * wide,
            transcendentals=rows * QUERY_PER_GROUP * (cached + rows),
        ),
        name="attention",
    )(length, q, k_cache, v_cache, k_block, v_block, buffer)


def shards(tokens_in, w_query, w_key, w_value, stored_key_cache, stored_value_cache, prompt_len):
    n_inst, n_tp = lax.axis_size("inst"), lax.axis_size("tp")
    outer = n_inst // INNER
    me = lax.axis_index("inst")
    z, w = me // INNER, me % INNER
    x = lax.axis_index("tp")
    rows, local = tokens_in.shape
    part = local // outer
    groups = [list(range(o * INNER, (o + 1) * INNER)) for o in range(outer)]

    def over_outer(value, bits):
        return lax.ppermute(value, "inst", [(i, i ^ (bits * INNER)) for i in range(n_inst)])

    w_kv = jnp.concatenate([w_key, w_value], axis=1)
    kv_all = lax.all_gather(w_kv, "inst", axis=0, tiled=True, axis_index_groups=groups)
    q_all = lax.all_gather(w_query, "inst", axis=0, tiled=True, axis_index_groups=groups)

    own = tokens_in.reshape(rows, outer // n_tp, n_tp, part)
    if n_tp == 2:
        mine = lax.dynamic_index_in_dim(own, x, 2, keepdims=False)
        swap = lax.ppermute(
            lax.dynamic_index_in_dim(own, 1 - x, 2, keepdims=False), "tp", [(0, 1), (1, 0)]
        )
        parts = jnp.where(
            x == 0,
            jnp.concatenate([mine, swap], axis=1),
            jnp.concatenate([swap, mine], axis=1),
        )
    else:
        parts = lax.all_to_all(own, "tp", 2, 1, tiled=True).reshape(rows, outer, part)
    got = {}
    order = [b for b in range(outer) if b % 2] + [b for b in range(outer) if b % 2 == 0]
    for bits in order:
        mine = lax.dynamic_index_in_dim(parts, z ^ bits, 1, keepdims=False)
        got[bits] = over_outer(mine, bits) if bits else mine
    odd = [b for b in range(outer) if b % 2]
    even = [b for b in range(outer) if b % 2 == 0]

    def whole(list_of_bits):
        stack = jnp.concatenate([got[b] for b in list_of_bits], axis=0)
        if n_tp == 2:
            other = lax.ppermute(stack, "tp", [(0, 1), (1, 0)])
            first = jnp.where(x == 0, stack, other)
            second = jnp.where(x == 0, other, stack)
            return jnp.concatenate([first, second], axis=1)
        return lax.all_gather(stack, "tp", axis=1, tiled=True)

    t_odd = whole(odd)
    t_even = whole(even)

    def reduced(weight):
        cols = weight.shape[1]
        send = dot(t_odd, weight).astype(jnp.bfloat16)
        keep = dot(t_even, weight)
        keep = keep + over_outer(send, 1).astype(jnp.float32)
        bits, count = 2, outer // 2
        while count > 1:
            pairs = keep.reshape(count // 2, 2, rows, cols)
            send = pairs[:, 1].astype(jnp.bfloat16)
            keep = pairs[:, 0] + over_outer(send, bits).astype(jnp.float32)
            bits, count = bits * 2, count // 2
        return keep.reshape(rows, cols).astype(jnp.bfloat16)

    kv = reduced(kv_all)
    half = w_key.shape[1]
    k_block, v_block = kv[:, :half], kv[:, half:]
    heads = half // HEAD_SIZE
    wide = QUERY_PER_GROUP * HEAD_SIZE
    attended = jnp.zeros((rows, heads * wide), jnp.bfloat16)
    for group in range(heads):
        q = reduced(q_all[:, group * wide : (group + 1) * wide])
        attended = attend(
            prompt_len, q, stored_key_cache, stored_value_cache, k_block, v_block, group, attended
        )
    last_row = lax.dynamic_slice_in_dim(attended, prompt_len[0] - 1, 1, 0)
    handoff = lax.all_gather(last_row, "inst", axis=0, tiled=True)
    return (attended, handoff)


def solution(mesh):
    return jax.shard_map(
        shards,
        mesh=mesh,
        in_specs=(
            P("inst", "tp"),
            P("inst", "tp"),
            P("inst", "tp"),
            P("inst", "tp"),
            P("inst", "tp"),
            P("inst", "tp"),
            P("inst"),
        ),
        out_specs=(P("inst", "tp"), P(None, "tp")),
        check_vma=False,
    )
```

time: 487 us -> 283 us (0.58)
  waiting for transfers between devices: 357 us -> 171 us
  matrix products: 76.5 us -> 21.9 us
  starting transfers between devices: 0.15 us -> 19.7 us
  Pallas kernels: 0 us -> 16.4 us
  other arithmetic: 0.5 us -> 7 us
  local copies, waits for them, and re-layouts: 16.9 us -> 11.2 us
    all_gather x4 -> x2, waiting for transfers between devices: 355 us -> 0.04 us  [the longest x1 0.02 us: shards(): lax.all_gather(w_query, 'inst', axis=0, tiled=True, axis_index_groups=gro...]
    ppermute x0 -> x16, waiting for transfers between devices: none -> 170 us  [the longest x13 128 us: over_outer(): lax.ppermute(value, 'inst', [(i, i ^ bits * INNER) for i in range(n_inst)])]
    sub x4 -> x0, matrix products: 31.2 us -> none  [shards(): probs = jax.nn.softmax(scores, axis=-1).astype(jnp.bfloat16)]
    dot_general x7 -> x10, matrix products: 45.3 us -> 21.9 us  [dot(): return jnp.dot(a, b, preferred_element_type=jnp.float32)]
    ppermute x0 -> x16, starting transfers between devices: none -> 19.6 us  [the longest x13 14.5 us: over_outer(): lax.ppermute(value, 'inst', [(i, i ^ bits * INNER) for i in range(n_inst)])]
    pallas_call x0 -> x4, Pallas kernels: none -> 16.4 us  [attend(): pl.pallas_call(attention_kernel, grid=(1,), out_shape=jax.ShapeDtypeStruc...]
    reshape x4 -> x0, local copies, waits for them, and re-layouts: 5.71 us -> none  [the longest x1 2.32 us: shards(): stored_key_cache.reshape(prefix_rows, heads, HEAD_SIZE)]
  transfers between devices with their start and end apart: 4 -> 18, of which waited for: 4 -> 12; matrix products, arithmetic and copies ran while one was open for 5% -> 12% of each run, Pallas kernels for 0% -> 4%
where the time goes in v1:
time: 283 us; the launch traced here: 282 us
  waiting for transfers between devices  171 us (60%)
  matrix products  21.9 us (8%)
  starting transfers between devices  19.7 us (7%)
  blocking collectives  19.7 us (7%)
  Pallas kernels  16.4 us (6%)
  between operations  15.3 us (5%)
  local copies, waits for them, and re-layouts  11.2 us (4%)
  other arithmetic  7 us (2%)
    ppermute x13, waiting for transfers between devices, over_outer(): lax.ppermute(value, 'inst', [(i, i ^ bits * INNER) for i in range(n_inst)])  128 us
    ppermute x1, waiting for transfers between devices, shards(): lax.ppermute(lax.dynamic_index_in_dim(own, 1 - x, 2, keepdims=False), 'tp...  22.8 us
    dot_general x10, matrix products, dot(): return jnp.dot(a, b, preferred_element_type=jnp.float32)  21.9 us
    all_gather x1, blocking collectives, shards(): handoff = lax.all_gather(last_row, 'inst', axis=0, tiled=True)  19.7 us
    ppermute x2, waiting for transfers between devices, whole(): other = lax.ppermute(stack, 'tp', [(0, 1), (1, 0)])  19.3 us
    pallas_call x4, Pallas kernels, attend(): pl.pallas_call(attention_kernel, grid=(1,), out_shape=jax.ShapeDtypeStruc...  16.4 us
    ppermute x13, starting transfers between devices, over_outer(): lax.ppermute(value, 'inst', [(i, i ^ bits * INNER) for i in range(n_inst)])  14.5 us
  transfers between devices with their start and end apart: 18, of which 12 were waited for; matrix products, arithmetic and copies ran while one was open for 12% of the time, Pallas kernels for 4%

profile of v1, /device:TPU:0, one launch (start us, length us, event | category | flops | bytes accessed | tf_op | source)
XLA Modules:
  0.0 282.2 jit_solution(12176388638360652357)
XLA Ops:
  7.2 2.3 pad_maximum_fusion.3
  10.3 3.3 %copy.19 = bf16[256,4096]{0,1:T(8,128)(2,1)S(1)} copy(bf16[256,4096]{1,0:T(8,128)(2,1)} %param.7) | data formatting | bytes 4194304 | tf_op args[0]
  14.7 2.3 copy.21
  17.0 2.9 %collective-permute-start = (bf16[256,2,1024]{2,0,1:T(8,128)(2,1)}, bf16[256,2,1024]{2,0,1:T(8,128)(2,1)S(1)}, u32[]{:S(2)}, u32[]{:S(2)}) collective-permute-start(bf16[256,2,1024]{2,0,1:T(8,128)(2,1)} %bitcast.2), channel_id=1, source_target_pairs={{0,1},{1,0},{2,3},{3,2},{4,5},{5,4},{6,7},{7,6},{8,9},{9,8},{10,11... | collective-permute-start | bytes 3145736 | tf_op jit(solution)/shard_map/ppermute | solution.py:95
  20.5 22.8 %collective-permute-done = bf16[256,2,1024]{2,0,1:T(8,128)(2,1)S(1)} collective-permute-done((bf16[256,2,1024]{2,0,1:T(8,128)(2,1)}, bf16[256,2,1024]{2,0,1:T(8,128)(2,1)S(1)}, u32[]{:S(2)}, u32[]{:S(2)}) %collective-permute-start) | collective-permute-done | bytes 1048608 | tf_op jit(solution)/shard_map/ppermute | solution.py:95
  43.9 1.9 collective-permute-start.3
  45.7 2.5 collective-permute-start.4
  48.2 9.9 %collective-permute-done.3 = bf16[256,1024]{1,0:T(8,128)(2,1)S(1)} collective-permute-done((bf16[256,1024]{1,0:T(8,128)(2,1)S(1)}, bf16[256,1024]{1,0:T(8,128)(2,1)S(1)}, u32[]{:S(2)}, u32[]{:S(2)}) %collective-permute-start.3) | collective-permute-done | bytes 524320 | tf_op jit(solution)/shard_map/ppermute | solution.py:86
  58.2 12.3 %collective-permute-done.4 = bf16[256,1024]{1,0:T(8,128)(2,1)S(1)} collective-permute-done((bf16[256,1024]{1,0:T(8,128)(2,1)S(1)}, bf16[256,1024]{1,0:T(8,128)(2,1)S(1)}, u32[]{:S(2)}, u32[]{:S(2)}) %collective-permute-start.4) | collective-permute-done | bytes 524320 | tf_op jit(solution)/shard_map/ppermute | solution.py:86
  70.5 1.6 collective-permute-start.5
  72.0 1.8 collective-permute-start.1
  73.8 20.7 %collective-permute-done.1 = bf16[256,1024]{1,0:T(8,128)(2,1)S(1)} collective-permute-done((bf16[256,1024]{1,0:T(8,128)(2,1)S(1)}, bf16[256,1024]{1,0:T(8,128)(2,1)S(1)}, u32[]{:S(2)}, u32[]{:S(2)}) %collective-permute-start.1) | collective-permute-done | bytes 524320 | tf_op jit(solution)/shard_map/ppermute | solution.py:86
  96.3 5.2 %convolution_convert_fusion = bf16[512,1024]{1,0:T(8,128)(2,1)S(1)} fusion(bf16[2048,1024]{1,0:T(8,128)(2,1)} %all-gather.6.cloned.1.call-done, bf16[512,1024]{1,0:T(8,128)(2,1)S(1)} %get-tuple-element.9, bf16[512,1024]{1,0:T(8,128)(2,1)S(1)} %get-tuple-element.8), kind=kOutput, calls=%fused_computation.20 | convolution fusion | flops 2152202240 | bytes 7340032 | tf_op jit(solution)/shard_map/dot_general | solution.py:16
  101.6 19.3 %collective-permute-done.2 = bf16[512,1024]{1,0:T(8,128)(2,1)} collective-permute-done((bf16[512,1024]{1,0:T(8,128)(2,1)}, bf16[512,1024]{1,0:T(8,128)(2,1)}, u32[]{:S(2)}, u32[]{:S(2)}) %collective-permute-start.2) | collective-permute-done | bytes 1048608 | tf_op jit(solution)/shard_map/ppermute | solution.py:116
  121.0 1.7 broadcast_select_fusion.3
  122.7 3.8 %collective-permute-done.8 = bf16[512,1024]{1,0:T(8,128)(2,1)S(1)} collective-permute-done((bf16[512,1024]{1,0:T(8,128)(2,1)S(1)}, bf16[512,1024]{1,0:T(8,128)(2,1)S(1)}, u32[]{:S(2)}, u32[]{:S(2)}) %collective-permute-start.8) | collective-permute-done | bytes 1048608 | tf_op jit(solution)/shard_map/ppermute | solution.py:86
  126.4 2.4 convert_add_fusion
  131.7 23.2 %collective-permute-done.9 = bf16[1,256,1024]{2,1,0:T(8,128)(2,1)} collective-permute-done((bf16[1,256,1024]{2,1,0:T(8,128)(2,1)}, bf16[1,256,1024]{2,1,0:T(8,128)(2,1)}, u32[]{:S(2)}, u32[]{:S(2)}) %collective-permute-start.9) | collective-permute-done | bytes 524320 | tf_op jit(solution)/shard_map/ppermute | solution.py:86
  156.2 3.6 %fusion.37 = bf16[512,512]{1,0:T(8,128)(2,1)S(1)} fusion(bf16[2048,2048]{1,0:T(8,128)(2,1)} %all-gather.4.cloned.1.call-done, bf16[512,1024]{1,0:T(8,128)(2,1)} %copy-done.7, bf16[512,1024]{1,0:T(8,128)(2,1)} %copy-done.4), kind=kOutput, calls=%fused_computation.28 | convolution fusion | flops 1078198272 | bytes 4718592 | tf_op jit(solution)/shard_map/dot_general | solution.py:16
  159.9 3.0 %fusion.34 = bf16[512,512]{1,0:T(8,128)(2,1)S(1)} fusion(bf16[2048,2048]{1,0:T(8,128)(2,1)} %all-gather.4.cloned.1.call-done, bf16[512,1024]{1,0:T(8,128)(2,1)S(1)} %copy-done.8, bf16[512,1024]{1,0:T(8,128)(2,1)S(1)} %copy-done.5), kind=kOutput, calls=%fused_computation.27 | convolution fusion | flops 1078198272 | bytes 4718592 | tf_op jit(solution)/shard_map/dot_general | solution.py:16
  162.9 1.9 collective-permute-start.12
  167.6 1.9 collective-permute-start.6
  169.6 5.1 %collective-permute-done.14 = bf16[512,512]{1,0:T(8,128)(2,1)S(1)} collective-permute-done((bf16[512,512]{1,0:T(8,128)(2,1)S(1)}, bf16[512,512]{1,0:T(8,128)(2,1)S(1)}, u32[]{:S(2)}, u32[]{:S(2)}) %collective-permute-start.14) | collective-permute-done | bytes 524320 | tf_op jit(solution)/shard_map/ppermute | solution.py:86
  177.0 14.5 %collective-permute-done.12 = bf16[512,512]{1,0:T(8,128)(2,1)S(1)} collective-permute-done((bf16[512,512]{1,0:T(8,128)(2,1)S(1)}, bf16[512,512]{1,0:T(8,128)(2,1)S(1)}, u32[]{:S(2)}, u32[]{:S(2)}) %collective-permute-start.12) | collective-permute-done | bytes 524320 | tf_op jit(solution)/shard_map/ppermute | solution.py:86
  193.4 14.9 %collective-permute-done.10 = bf16[512,512]{1,0:T(8,128)(2,1)S(1)} collective-permute-done((bf16[512,512]{1,0:T(8,128)(2,1)S(1)}, bf16[512,512]{1,0:T(8,128)(2,1)S(1)}, u32[]{:S(2)}, u32[]{:S(2)}) %collective-permute-start.10) | collective-permute-done | bytes 524320 | tf_op jit(solution)/shard_map/ppermute | solution.py:86
  210.5 8.2 %collective-permute-done.6 = bf16[512,512]{1,0:T(8,128)(2,1)S(1)} collective-permute-done((bf16[512,512]{1,0:T(8,128)(2,1)S(1)}, bf16[512,512]{1,0:T(8,128)(2,1)S(1)}, u32[]{:S(2)}, u32[]{:S(2)}) %collective-permute-start.6) | collective-permute-done | bytes 524320 | tf_op jit(solution)/shard_map/ppermute | solution.py:86
  220.8 15.5 %collective-permute-done.11 = bf16[1,256,512]{2,1,0:T(8,128)(2,1)S(1)} collective-permute-done((bf16[1,256,512]{2,1,0:T(8,128)(2,1)S(1)}, bf16[1,256,512]{2,1,0:T(8,128)(2,1)S(1)}, u32[]{:S(2)}, u32[]{:S(2)}) %collective-permute-start.11) | collective-permute-done | bytes 262176 | tf_op jit(solution)/shard_map/ppermute | solution.py:86
  237.5 4.1 %attention.4.prev_ref = bf16[256,2048]{1,0:T(8,128)(2,1)} custom-call(s32[1]{0:T(128)S(6)} %copy.30.len_ref, bf16[256,512]{1,0:T(8,128)(2,1)S(1)} %fusion.58.q_ref, bf16[1792,512]{1,0:T(8,128)(2,1)S(1)} %copy-done, bf16[1792,512]{1,0:T(8,128)(2,1)S(1)} %copy-done.1, bf16[256,512]{1,0:T(8,128)(2,1)S(1)} %get-tuple-element.13.kb_ref, ...), custom_call_target="tpu_custom_call", output_to_operand_aliasing={{}: (6, {})} | custom-call | flops 1073741824 | bytes 1572864 | tf_op jit(solution)/shard_map/attention/pallas_call | solution.py:50
  241.6 4.1 %attention.5.prev_ref = bf16[256,2048]{1,0:T(8,128)(2,1)} custom-call(s32[1]{0:T(128)S(6)} %copy.30.len_ref, bf16[256,512]{1,0:T(8,128)(2,1)S(1)} %fusion.56.q_ref, bf16[1792,512]{1,0:T(8,128)(2,1)S(1)} %copy-done, bf16[1792,512]{1,0:T(8,128)(2,1)S(1)} %copy-done.1, bf16[256,512]{1,0:T(8,128)(2,1)S(1)} %get-tuple-element.13.kb_ref, ...), custom_call_target="tpu_custom_call", output_to_operand_aliasing={{}: (6, {})} | custom-call | flops 1073741824 | bytes 1572864 | tf_op jit(solution)/shard_map/attention/pallas_call | solution.py:50
  245.6 4.1 %attention.6.prev_ref = bf16[256,2048]{1,0:T(8,128)(2,1)} custom-call(s32[1]{0:T(128)S(6)} %copy.30.len_ref, bf16[256,512]{1,0:T(8,128)(2,1)S(1)} %fusion.54.q_ref, bf16[1792,512]{1,0:T(8,128)(2,1)S(1)} %copy-done, bf16[1792,512]{1,0:T(8,128)(2,1)S(1)} %copy-done.1, bf16[256,512]{1,0:T(8,128)(2,1)S(1)} %get-tuple-element.13.kb_ref, ...), custom_call_target="tpu_custom_call", output_to_operand_aliasing={{}: (6, {})} | custom-call | flops 1073741824 | bytes 1572864 | tf_op jit(solution)/shard_map/attention/pallas_call | solution.py:50
  250.0 4.1 %attention.7 = bf16[256,2048]{1,0:T(8,128)(2,1)} custom-call(s32[1]{0:T(128)S(6)} %copy.30.len_ref, bf16[256,512]{1,0:T(8,128)(2,1)S(1)} %fusion.52.q_ref, bf16[1792,512]{1,0:T(8,128)(2,1)S(1)} %copy-done, bf16[1792,512]{1,0:T(8,128)(2,1)S(1)} %copy-done.1, bf16[256,512]{1,0:T(8,128)(2,1)S(1)} %get-tuple-element.13.kb_ref, ...), custom_call_target="tpu_custom_call", output_to_operand_aliasing={{}: (6, {})} | custom-call | flops 1073741824 | bytes 1572864 | tf_op jit(solution)/shard_map/attention/pallas_call | solution.py:50
  254.9 19.7 %all-gather = bf16[16,1,2048]{2,1,0:T(2,128)(2,1)S(1)} all-gather(bf16[1,1,2048]{2,1,0:T(2,128)(2,1)S(1)} %dynamic-slice_bitcast_fusion.4), channel_id=1, replica_groups=mesh['inst'=16,'tp'=2] {'inst'}, dimensions={0}, use_global_device_ids=true | all-gather | bytes 69632 | tf_op jit(solution)/shard_map/all_gather | solution.py:150
  (72 shorter events, 22.3 us)
Async XLA Ops:
  7.2 89.1 %all-gather.6.cloned.1.call-start = ((), (), s32[]{:S(2)}) async-start(), calls=%async_computation.1 | async-start | bytes 5242880 | tf_op jit(solution)/shard_map/all_gather | solution.py:89
  9.6 146.6 %all-gather.4.cloned.1.call-start = ((), (), s32[]{:S(2)}) async-start(), calls=%async_computation | async-start | bytes 10485760 | tf_op jit(solution)/shard_map/all_gather | solution.py:90
  17.0 26.3 %collective-permute-start = (bf16[256,2,1024]{2,0,1:T(8,128)(2,1)}, bf16[256,2,1024]{2,0,1:T(8,128)(2,1)S(1)}, u32[]{:S(2)}, u32[]{:S(2)}) collective-permute-start(bf16[256,2,1024]{2,0,1:T(8,128)(2,1)} %bitcast.2), channel_id=1, source_target_pairs={{0,1},{1,0},{2,3},{3,2},{4,5},{5,4},{6,7},{7,6},{8,9},{9,8},{10,11... | collective-permute-start | bytes 3145736 | tf_op jit(solution)/shard_map/ppermute | solution.py:95
  43.9 14.3 %collective-permute-start.3 = (bf16[256,1024]{1,0:T(8,128)(2,1)S(1)}, bf16[256,1024]{1,0:T(8,128)(2,1)S(1)}, u32[]{:S(2)}, u32[]{:S(2)}) collective-permute-start(bf16[256,1024]{1,0:T(8,128)(2,1)S(1)} %get-tuple-element.6), channel_id=1, source_target_pairs={{0,8},{2,10},{4,12},{6,14},{8,0},{10,2},{12,4},{14,6},{16,24},{18,... | collective-permute-start | bytes 1572872 | tf_op jit(solution)/shard_map/ppermute | solution.py:86
  45.7 24.7 %collective-permute-start.4 = (bf16[256,1024]{1,0:T(8,128)(2,1)S(1)}, bf16[256,1024]{1,0:T(8,128)(2,1)S(1)}, u32[]{:S(2)}, u32[]{:S(2)}) collective-permute-start(bf16[256,1024]{1,0:T(8,128)(2,1)S(1)} %get-tuple-element.5), channel_id=1, source_target_pairs={{0,24},{2,26},{4,28},{6,30},{8,16},{10,18},{12,20},{14,22},{16,8},... | collective-permute-start | bytes 1572872 | tf_op jit(solution)/shard_map/ppermute | solution.py:86
  70.5 25.6 %collective-permute-start.5 = (bf16[512,1024]{1,0:T(8,128)(2,1)S(1)}, bf16[512,1024]{1,0:T(8,128)(2,1)S(1)}, u32[]{:S(2)}, u32[]{:S(2)}) collective-permute-start(bf16[512,1024]{1,0:T(8,128)(2,1)S(1)} %constant_dynamic-update-slice_fusion), channel_id=1, source_target_pairs={{0,1},{1,0},{2,3},{3,2},{4,5},{5,4},{6,7},{7,6},{8,9},{9,8},{10,11... | collective-permute-start | bytes 3145736 | tf_op jit(solution)/shard_map/ppermute | solution.py:116
  72.0 22.5 %collective-permute-start.1 = (bf16[256,1024]{1,0:T(8,128)(2,1)S(1)}, bf16[256,1024]{1,0:T(8,128)(2,1)S(1)}, u32[]{:S(2)}, u32[]{:S(2)}) collective-permute-start(bf16[256,1024]{1,0:T(8,128)(2,1)S(1)} %get-tuple-element.7), channel_id=1, source_target_pairs={{0,16},{2,18},{4,20},{6,22},{8,24},{10,26},{12,28},{14,30},{16,0},... | collective-permute-start | bytes 1572872 | tf_op jit(solution)/shard_map/ppermute | solution.py:86
  95.6 25.4 %collective-permute-start.2 = (bf16[512,1024]{1,0:T(8,128)(2,1)}, bf16[512,1024]{1,0:T(8,128)(2,1)}, u32[]{:S(2)}, u32[]{:S(2)}) collective-permute-start(bf16[512,1024]{1,0:T(8,128)(2,1)} %pad_maximum_fusion.2), channel_id=1, source_target_pairs={{0,1},{1,0},{2,3},{3,2},{4,5},{5,4},{6,7},{7,6},{8,9},{9,8},{10,11... | collective-permute-start | bytes 3145736 | tf_op jit(solution)/shard_map/ppermute | solution.py:116
  96.2 5.3 %copy-start.4 = (bf16[512,1024]{1,0:T(8,128)(2,1)}, bf16[512,1024]{1,0:T(8,128)(2,1)S(1)}, u32[]{:S(2)}) copy-start(bf16[512,1024]{1,0:T(8,128)(2,1)S(1)} %get-tuple-element.8) | copy-start | bytes 3145732
  96.2 5.3 %copy-start.7 = (bf16[512,1024]{1,0:T(8,128)(2,1)}, bf16[512,1024]{1,0:T(8,128)(2,1)S(1)}, u32[]{:S(2)}) copy-start(bf16[512,1024]{1,0:T(8,128)(2,1)S(1)} %get-tuple-element.9) | copy-start | bytes 3145732
  101.6 24.9 %copy-start.9 = (bf16[2048,1024]{1,0:T(8,128)(2,1)S(1)}, bf16[2048,1024]{1,0:T(8,128)(2,1)}, u32[]{:S(2)}) copy-start(bf16[2048,1024]{1,0:T(8,128)(2,1)} %all-gather.6.cloned.1.call-done) | copy-start | bytes 12582916
  101.6 24.9 %collective-permute-start.8 = (bf16[512,1024]{1,0:T(8,128)(2,1)S(1)}, bf16[512,1024]{1,0:T(8,128)(2,1)S(1)}, u32[]{:S(2)}, u32[]{:S(2)}) collective-permute-start(bf16[512,1024]{1,0:T(8,128)(2,1)S(1)} %convolution_convert_fusion), channel_id=1, source_target_pairs={{0,8},{2,10},{4,12},{6,14},{8,0},{10,2},{12,4},{14,6},{16,24},{18,... | collective-permute-start | bytes 3145736 | tf_op jit(solution)/shard_map/ppermute | solution.py:86
  122.7 6.1 %copy-start.2 = (bf16[512,1024]{1,0:T(8,128)(2,1)}, bf16[512,1024]{1,0:T(8,128)(2,1)S(1)}, u32[]{:S(2)}) copy-start(bf16[512,1024]{1,0:T(8,128)(2,1)S(1)} %get-tuple-element.3) | copy-start | bytes 3145732
  129.7 25.1 %collective-permute-start.9 = (bf16[1,256,1024]{2,1,0:T(8,128)(2,1)}, bf16[1,256,1024]{2,1,0:T(8,128)(2,1)}, u32[]{:S(2)}, u32[]{:S(2)}) collective-permute-start(bf16[1,256,1024]{2,1,0:T(8,128)(2,1)} %fusion.43), channel_id=1, source_target_pairs={{0,16},{2,18},{4,20},{6,22},{8,24},{10,26},{12,28},{14,30},{16,0},... | collective-permute-start | bytes 1572872 | tf_op jit(solution)/shard_map/ppermute | solution.py:86
  156.1 3.8 %copy-start.5 = (bf16[512,1024]{1,0:T(8,128)(2,1)S(1)}, bf16[512,1024]{1,0:T(8,128)(2,1)}, u32[]{:S(2)}) copy-start(bf16[512,1024]{1,0:T(8,128)(2,1)} %copy-done.4) | copy-start | bytes 3145732
  156.1 3.7 %copy-start.8 = (bf16[512,1024]{1,0:T(8,128)(2,1)S(1)}, bf16[512,1024]{1,0:T(8,128)(2,1)}, u32[]{:S(2)}) copy-start(bf16[512,1024]{1,0:T(8,128)(2,1)} %copy-done.7) | copy-start | bytes 3145732
  156.2 8.7 %slice-start = ((s8[8388608]{0:T(1024)(128)(4,1)}), s8[4194304]{0:T(1024)(128)(4,1)S(1)}, s32[]{:S(2)}) async-start(s8[8388608]{0:T(1024)(128)(4,1)} %bitcast.98), calls=%async_computation.2 | async-start | bytes 8388608
  159.8 5.0 %slice-start.1 = ((s8[8388608]{0:T(1024)(128)(4,1)}), s8[4194304]{0:T(1024)(128)(4,1)S(1)}, s32[]{:S(2)}) async-start(s8[8388608]{0:T(1024)(128)(4,1)} %bitcast.98), calls=%async_computation.3 | async-start | bytes 8388608
  159.8 14.9 %collective-permute-start.14 = (bf16[512,512]{1,0:T(8,128)(2,1)S(1)}, bf16[512,512]{1,0:T(8,128)(2,1)S(1)}, u32[]{:S(2)}, u32[]{:S(2)}) collective-permute-start(bf16[512,512]{1,0:T(8,128)(2,1)S(1)} %fusion.37), channel_id=1, source_target_pairs={{0,8},{2,10},{4,12},{6,14},{8,0},{10,2},{12,4},{14,6},{16,24},{18,... | collective-permute-start | bytes 1572872 | tf_op jit(solution)/shard_map/ppermute | solution.py:86
  162.9 3.4 %copy-start.6 = (bf16[512,1024]{1,0:T(8,128)(2,1)S(1)}, bf16[512,1024]{1,0:T(8,128)(2,1)}, u32[]{:S(2)}) copy-start(bf16[512,1024]{1,0:T(8,128)(2,1)} %copy-done.4) | copy-start | bytes 3145732
  162.9 28.6 %collective-permute-start.12 = (bf16[512,512]{1,0:T(8,128)(2,1)S(1)}, bf16[512,512]{1,0:T(8,128)(2,1)S(1)}, u32[]{:S(2)}, u32[]{:S(2)}) collective-permute-start(bf16[512,512]{1,0:T(8,128)(2,1)S(1)} %fusion.34), channel_id=1, source_target_pairs={{0,8},{2,10},{4,12},{6,14},{8,0},{10,2},{12,4},{14,6},{16,24},{18,... | collective-permute-start | bytes 1572872 | tf_op jit(solution)/shard_map/ppermute | solution.py:86
  166.1 8.6 %copy-start.3 = (bf16[512,1024]{1,0:T(8,128)(2,1)S(1)}, bf16[512,1024]{1,0:T(8,128)(2,1)}, u32[]{:S(2)}) copy-start(bf16[512,1024]{1,0:T(8,128)(2,1)} %copy-done.2) | copy-start | bytes 3145732
  166.1 42.3 %collective-permute-start.10 = (bf16[512,512]{1,0:T(8,128)(2,1)S(1)}, bf16[512,512]{1,0:T(8,128)(2,1)S(1)}, u32[]{:S(2)}, u32[]{:S(2)}) collective-permute-start(bf16[512,512]{1,0:T(8,128)(2,1)S(1)} %fusion.31), channel_id=1, source_target_pairs={{0,8},{2,10},{4,12},{6,14},{8,0},{10,2},{12,4},{14,6},{16,24},{18,... | collective-permute-start | bytes 1572872 | tf_op jit(solution)/shard_map/ppermute | solution.py:86
  167.6 51.1 %collective-permute-start.6 = (bf16[512,512]{1,0:T(8,128)(2,1)S(1)}, bf16[512,512]{1,0:T(8,128)(2,1)S(1)}, u32[]{:S(2)}, u32[]{:S(2)}) collective-permute-start(bf16[512,512]{1,0:T(8,128)(2,1)S(1)} %fusion.28), channel_id=1, source_target_pairs={{0,8},{2,10},{4,12},{6,14},{8,0},{10,2},{12,4},{14,6},{16,24},{18,... | collective-permute-start | bytes 1572872 | tf_op jit(solution)/shard_map/ppermute | solution.py:86
  176.0 44.7 %collective-permute-start.15 = (bf16[1,256,512]{2,1,0:T(8,128)(2,1)S(1)}, bf16[1,256,512]{2,1,0:T(8,128)(2,1)S(1)}, u32[]{:S(2)}, u32[]{:S(2)}) collective-permute-start(bf16[1,256,512]{2,1,0:T(8,128)(2,1)S(1)} %fusion.59), channel_id=1, source_target_pairs={{0,16},{2,18},{4,20},{6,22},{8,24},{10,26},{12,28},{14,30},{16,0},... | collective-permute-start | bytes 786440 | tf_op jit(solution)/shard_map/ppermute | solution.py:86
  192.8 27.9 %collective-permute-start.13 = (bf16[1,256,512]{2,1,0:T(8,128)(2,1)S(1)}, bf16[1,256,512]{2,1,0:T(8,128)(2,1)S(1)}, u32[]{:S(2)}, u32[]{:S(2)}) collective-permute-start(bf16[1,256,512]{2,1,0:T(8,128)(2,1)S(1)} %fusion.57), channel_id=1, source_target_pairs={{0,16},{2,18},{4,20},{6,22},{8,24},{10,26},{12,28},{14,30},{16,0},... | collective-permute-start | bytes 786440 | tf_op jit(solution)/shard_map/ppermute | solution.py:86
  209.9 26.4 %collective-permute-start.11 = (bf16[1,256,512]{2,1,0:T(8,128)(2,1)S(1)}, bf16[1,256,512]{2,1,0:T(8,128)(2,1)S(1)}, u32[]{:S(2)}, u32[]{:S(2)}) collective-permute-start(bf16[1,256,512]{2,1,0:T(8,128)(2,1)S(1)} %fusion.55), channel_id=1, source_target_pairs={{0,16},{2,18},{4,20},{6,22},{8,24},{10,26},{12,28},{14,30},{16,0},... | collective-permute-start | bytes 786440 | tf_op jit(solution)/shard_map/ppermute | solution.py:86
  220.0 17.5 %copy-start = (bf16[1792,512]{1,0:T(8,128)(2,1)S(1)}, bf16[1792,512]{1,0:T(8,128)(2,1)}, u32[]{:S(2)}) copy-start(bf16[1792,512]{1,0:T(8,128)(2,1)} %kc_ref.7) | copy-start | bytes 5505028
  220.0 17.4 %copy-start.1 = (bf16[1792,512]{1,0:T(8,128)(2,1)S(1)}, bf16[1792,512]{1,0:T(8,128)(2,1)}, u32[]{:S(2)}) copy-start(bf16[1792,512]{1,0:T(8,128)(2,1)} %vc_ref.7) | copy-start | bytes 5505028
  220.0 29.7 %collective-permute-start.7 = (bf16[1,256,512]{2,1,0:T(8,128)(2,1)S(1)}, bf16[1,256,512]{2,1,0:T(8,128)(2,1)S(1)}, u32[]{:S(2)}, u32[]{:S(2)}) collective-permute-start(bf16[1,256,512]{2,1,0:T(8,128)(2,1)S(1)} %fusion.53), channel_id=1, source_target_pairs={{0,16},{2,18},{4,20},{6,22},{8,24},{10,26},{12,28},{14,30},{16,0},... | collective-permute-start | bytes 786440 | tf_op jit(solution)/shard_map/ppermute | solution.py:86
Sparse Core Ops, SparseCore 0:
  9.7 37.1 all-gather.5
  48.4 58.3 all-gather.3

commit v2 on v0

v2 whole, which is shorter than its diff:
```python
import functools

import jax
import jax.numpy as jnp
from jax import lax
from jax.experimental import pallas as pl
from jax.experimental.pallas import tpu as pltpu
from jax.sharding import PartitionSpec as P

HEAD_SIZE = 128
QUERY_PER_GROUP = 4
COST = 1 << 20
INNER = 4


def dot(a, b):
    return jnp.dot(a, b, preferred_element_type=jnp.float32)


def product(place_ref, t_refs, w_ref, t_whole):
    if len(t_refs) == 1:
        return dot(t_refs[0][...], w_ref[...])
    x = place_ref[0]
    part = t_refs[0].shape[1]
    n = len(t_refs) // 2

    @pl.when(pl.program_id(0) == 0)
    def _():
        for refs, where in ((t_refs[:n], x), (t_refs[n:], 1 - x)):
            cols = pl.ds(pl.multiple_of(where * part, part), part)
            row = 0
            for ref in refs:
                t_whole[row : row + ref.shape[0], cols] = ref[...]
                row += ref.shape[0]

    return dot(t_whole[...], w_ref[...])


def first_kernel(n_t, place_ref, *refs):
    out = product(place_ref, refs[:n_t], refs[n_t], refs[-1])
    row = 0
    for ref in refs[n_t + 1 : -1]:
        ref[...] = out[row : row + ref.shape[0]].astype(ref.dtype)
        row += ref.shape[0]


def later_kernel(n_t, place_ref, *refs):
    send_ref, keep_ref, t_whole = refs[-3:]
    out = product(place_ref, refs[:n_t], refs[n_t], t_whole)
    came = jnp.concatenate([ref[...] for ref in refs[n_t + 1 : -3]], axis=0)
    out = out + came.astype(jnp.float32)
    n = keep_ref.shape[0]
    keep_ref[...] = out[:n]
    send_ref[...] = out[n:].astype(send_ref.dtype)


def multiply(kernel, place, tokens, weight, came, outs, tile=512):
    columns = weight.shape[1]
    tile = min(tile, columns)
    column = lambda i, place: (0, i)
    some = lambda which: lambda i, place: (which, 0)
    held = len(tokens) // 2
    t_rows = sum(n for _, n, _ in tokens[: max(held, 1)])
    t_cols = tokens[0][0].shape[1] * (2 if held else 1)
    return pl.pallas_call(
        functools.partial(kernel, len(tokens)),
        grid_spec=pltpu.PrefetchScalarGridSpec(
            num_scalar_prefetch=1,
            grid=(columns // tile,),
            in_specs=[pl.BlockSpec((n, t.shape[1]), some(which)) for t, n, which in tokens]
            + [pl.BlockSpec((v.shape[0], tile), column) for v in (weight, *came)],
            out_specs=[pl.BlockSpec((n, tile), column) for n, _ in outs],
            scratch_shapes=[pltpu.VMEM((t_rows, t_cols), jnp.bfloat16)],
        ),
        out_shape=[jax.ShapeDtypeStruct((n, columns), dtype) for n, dtype in outs],
        compiler_params=pltpu.CompilerParams(vmem_limit_bytes=40 * 1024 * 1024),
        cost_estimate=pl.CostEstimate(flops=0, bytes_accessed=COST, transcendentals=0),
        name="product",
    )(place, *[t for t, _, _ in tokens], weight, *came)


def attention_kernel(
    place_ref, qm_ref, qc_ref, kc_ref, vc_ref, km_ref, kt_ref, vm_ref, vt_ref, *rest
):
    o_ref, last_ref = rest[-2:]
    length, here, first = place_ref[0], place_ref[1], place_ref[2]
    rows, block = qm_ref.shape[0], km_ref.shape[0]
    half = block // 2
    total = lambda mine, came: (mine + came.astype(jnp.float32)).astype(jnp.bfloat16)
    factor = 1.4426950408889634 / HEAD_SIZE**0.5
    row = lax.broadcasted_iota(jnp.int32, (rows, 1), 0)
    row = jnp.where(row < half, row + here * half, row - here * half)
    col = lax.broadcasted_iota(jnp.int32, (rows, block), 1)
    col = jnp.where(col < half, col + first * half, col - first * half)
    allowed = (col <= row) & (col < length)
    contract = (((1,), (1,)), ((), ()))
    at = row == length - 1
    keys = total(km_ref[...], kt_ref[...])
    values = total(vm_ref[...], vt_ref[...])
    for member in range(QUERY_PER_GROUP):
        cols = slice(member * HEAD_SIZE, (member + 1) * HEAD_SIZE)
        q = total(qm_ref[:, cols], qc_ref[:, cols])
        s1 = lax.dot_general(q, kc_ref[...], contract, preferred_element_type=jnp.float32)
        s2 = lax.dot_general(q, keys, contract, preferred_element_type=jnp.float32)
        s2 = jnp.where(allowed, s2, -jnp.inf)
        top = jnp.maximum(jnp.max(s1, axis=1, keepdims=True), jnp.max(s2, axis=1, keepdims=True))
        p1 = jnp.exp2((s1 - top) * factor)
        p2 = jnp.exp2((s2 - top) * factor)
        norm = jnp.sum(p1, axis=1, keepdims=True) + jnp.sum(p2, axis=1, keepdims=True)
        out = dot(p1.astype(jnp.bfloat16), vc_ref[...]) + dot(p2.astype(jnp.bfloat16), values)
        out = out / norm
        if rows == half:
            o_ref[:, cols] = out.astype(o_ref.dtype)
        else:
            for h, where in ((0, first), (1, 1 - first)):
                to = pl.ds(pl.multiple_of(where * half, half), half)
                o_ref[to, cols] = out[h * half : (h + 1) * half].astype(o_ref.dtype)
        last_ref[:, cols] = jnp.sum(jnp.where(at, out, 0.0), axis=0, keepdims=True).astype(
            last_ref.dtype
        )


def attend(place, q, k_cache, v_cache, kv, start, shape, buffer):
    rows, cols = q[0].shape
    wide = QUERY_PER_GROUP * HEAD_SIZE
    cached, block = k_cache.shape[0], kv[0].shape[0]
    heads = k_cache.shape[1] // HEAD_SIZE
    groups = cols // wide
    begin = start // wide
    column = lambda i, place: (0, begin + i)
    after = lambda i, place: (0, heads + begin + i)
    mine = lambda i, place: (0, i)
    out = column if rows == shape[0] else lambda i, place: (place[1], begin + i)
    buffers = [] if buffer is None else [buffer]
    return pl.pallas_call(
        attention_kernel,
        grid_spec=pltpu.PrefetchScalarGridSpec(
            num_scalar_prefetch=1,
            grid=(groups,),
            in_specs=[
                pl.BlockSpec((rows, wide), mine),
                pl.BlockSpec((rows, wide), mine),
                pl.BlockSpec((cached, HEAD_SIZE), column),
                pl.BlockSpec((cached, HEAD_SIZE), column),
                pl.BlockSpec((block, HEAD_SIZE), column),
                pl.BlockSpec((block, HEAD_SIZE), column),
                pl.BlockSpec((block, HEAD_SIZE), after),
                pl.BlockSpec((block, HEAD_SIZE), after),
            ]
            + [pl.BlockSpec(memory_space=pl.ANY)] * len(buffers),
            out_specs=[
                pl.BlockSpec((rows, wide), out),
                pl.BlockSpec((1, wide), mine),
            ],
        ),
        out_shape=[
            jax.ShapeDtypeStruct(shape, jnp.bfloat16),
            jax.ShapeDtypeStruct((1, cols), jnp.bfloat16),
        ],
        input_output_aliases={9: 0} if buffers else {},
        compiler_params=pltpu.CompilerParams(vmem_limit_bytes=40 * 1024 * 1024),
        cost_estimate=pl.CostEstimate(flops=0, bytes_accessed=COST, transcendentals=0),
        name="attention",
    )(place, *q, k_cache, v_cache, *kv, *kv, *buffers)


def shards(tokens_in, w_query, w_key, w_value, stored_key_cache, stored_value_cache, prompt_len):
    n_inst, n_tp = lax.axis_size("inst"), lax.axis_size("tp")
    outer = n_inst // INNER
    me = lax.axis_index("inst")
    z, w = me // INNER, me % INNER
    x = lax.axis_index("tp")
    rows, local = tokens_in.shape
    half = rows // 2
    part = local // outer
    groups = [list(range(o * INNER, (o + 1) * INNER)) for o in range(outer)]
    halves = (0, 1)
    count = outer // 2

    first = (prompt_len[0] - 1) // half

    def over_inst(value, bits):
        return lax.ppermute(value, "inst", [(i, i ^ bits) for i in range(n_inst)])

    def over_outer(value, bits):
        return over_inst(value, bits * INNER)

    def over_tp(value):
        return lax.ppermute(value, "tp", [(0, 1), (1, 0)])

    def swapped_if(flag, a, b, axis):
        return jnp.where(
            flag, jnp.concatenate([b, a], axis=axis), jnp.concatenate([a, b], axis=axis)
        )

    last_step = [None]

    def step(*values):
        if last_step[0] is not None:
            *values, _ = lax.optimization_barrier((*values, last_step[0]))
        last_step[0] = values[0]
        return values[0] if len(values) == 1 else values

    heads = w_key.shape[1] // HEAD_SIZE
    wide = QUERY_PER_GROUP * HEAD_SIZE
    pieces = 2 if heads % 2 == 0 else 1
    chunk = heads * wide // pieces
    fast = outer == 4 and n_tp == 2

    def group_gather(value):
        return lax.all_gather(value, "inst", axis=0, tiled=True, axis_index_groups=groups)

    weights = {}

    def gather_weights():
        w_kv = jnp.concatenate([w_key, w_value], axis=1)
        cut = [w_query[:, piece * chunk : (piece + 1) * chunk] for piece in range(pieces)]
        for name, value in ((0, cut[0]), ("kv", w_kv), (1, cut[-1])):
            if name != 1 or pieces == 2:
                weights[name] = group_gather(step(value))

    tokens = [{}, {}]
    spot = jnp.stack([x, w]).astype(jnp.int32)
    every = (None, 0, 1)
    if fast:

        def cut(j, p):
            column = (((z % 2) ^ j) * n_tp + p) * part
            return jnp.concatenate(
                [
                    lax.dynamic_slice(tokens_in, (h * half, column), (half, part))
                    for h in (first, 1 - first)
                ],
                axis=0,
            )

        swap = {j: over_tp(step(cut(j, 1 - x))) for j in (1, 0)}
        gather_weights()
        mine = z // 2 == x
        held, came = {}, {}
        own = {j: cut(j, x) for j in (1, 0)}
        swap[1] = step(swap[1])
        send = {b: jnp.where(mine == (b < 2), own[1], swap[1]) for b in (1, 3)}
        send[1], send[3] = step(send[1], send[3])
        got = {b: over_outer(send[b], b) for b in (1, 3)}
        swap[0] = step(swap[0])
        send = {b: jnp.where(mine == (b < 2), own[0], swap[0]) for b in (2, 0)}
        send[2] = step(send[2])
        got[2], got[0] = over_outer(send[2], 2), send[0]
        for b in (1, 3, 0, 2):
            held[b] = step(got[b])
            came[b] = over_tp(held[b])

        def arrived(j):
            bits = (j, j + 2)
            came[j], came[j + 2] = step(came[j], came[j + 2])
            arrays = [which[b] for which in (held, came) for b in bits]
            for h in every:
                tokens[j][h] = [(a, rows, 0) if h is None else (a, half, h) for a in arrays]

    else:
        gather_weights()
        swapped = jnp.where(first == 1, jnp.roll(tokens_in, half, axis=0), tokens_in)
        own = swapped.reshape(rows, outer // n_tp, n_tp, part)
        parts = lax.all_to_all(own, "tp", 2, 1, tiled=True).reshape(rows, outer, part)
        for j in (1, 0):
            come = jnp.stack(
                [
                    over_outer(lax.dynamic_index_in_dim(parts, z ^ b, 1, keepdims=False), b)
                    for b in range(j, outer, 2)
                ]
            )
            both = lax.all_gather(come.reshape(-1, part), "tp", axis=1, tiled=True)
            both = both.reshape(count, 2, half, -1)
            for h in every:
                array = (both if h is None else both[:, h]).reshape(-1, both.shape[-1])
                tokens[j][h] = [(array, array.shape[0], 0)]

        def arrived(j):
            pass

    def first_send(h, name):
        weight = step(weights[name])
        n = rows if h is None else half
        outs = [(n, jnp.bfloat16)] * count if h is None else [(count * n, jnp.bfloat16)]
        sends = multiply(first_kernel, spot, tokens[1][h], weight, (), outs)
        sends = step(*sends) if len(sends) > 1 else [step(*sends)]
        return [over_outer(send, 1) for send in sends]

    def later_sends(h, name, came):
        weight = weights[name]
        n, cols = rows if h is None else half, weight.shape[1]
        came = step(*came) if len(came) > 1 else [step(*came)]
        if count == 2:
            outs = [(n, jnp.bfloat16), (n, jnp.float32)]
            send, keep = multiply(later_kernel, spot, tokens[0][h], weight, came, outs)
            return keep, over_outer(step(send), 2)
        keep = dot(tokens[0][h][0][0], weight) + jnp.concatenate(came, axis=0).astype(jnp.float32)
        bits, left = 2, count
        while True:
            pairs = keep.reshape(left // 2, 2, n, cols)
            came = over_outer(step(pairs[:, 1].astype(jnp.bfloat16)), bits)
            bits, left = bits * 2, left // 2
            if left == 1:
                return pairs[:, 0].reshape(n, cols), came.reshape(n, cols)
            keep = pairs[:, 0] + came.astype(jnp.float32)

    if pieces == 2:
        jobs = [(None, 0), (None, "kv"), (0, 1), (1, 1)]
    else:
        jobs = [(None, "kv"), (0, 0), (1, 0)]
    opened, parts_of, lasts = {}, {}, []
    kv_job = jobs.index((None, "kv"))
    attended = [None]

    def start(n):
        opened[n] = first_send(*jobs[n])

    def advance(n):
        parts_of[n] = later_sends(*jobs[n], opened[n])

    def arrive(n):
        parts_of[n] = (parts_of[n][0], step(parts_of[n][1]))

    def attention(n):
        h, piece = jobs[n]
        here = first if h is None else h ^ first
        place = jnp.stack([prompt_len[0], here, first]).astype(jnp.int32)
        kv = parts_of[kv_job]
        shape = (rows, heads * wide)
        attended[0], last = attend(
            place, parts_of[n], stored_key_cache, stored_value_cache, kv, piece * chunk, shape, attended[0]
        )
        lasts.append(step(last))

    def from_xor_order(values, index):
        out = jnp.stack(values)
        shape = out.shape
        bits = len(values).bit_length() - 1
        for bit in range(bits):
            out = out.reshape(len(values) >> (bit + 1), 2, 1 << bit, *shape[1:])
            out = jnp.where((index >> bit) % 2 == 1, out[:, ::-1], out)
        return out.reshape(shape)

    last_a, last_b = len(jobs) - 2, len(jobs) - 1
    arrived(1)
    start(0)
    start(1)
    arrived(0)
    advance(0)
    if pieces == 2:
        advance(1)
        start(2)
        start(3)
        arrive(0)
        arrive(1)
        advance(2)
        attention(0)
        advance(3)
    else:
        start(2)
        advance(1)
        arrive(0)
        advance(2)
    arrive(last_a)
    attention(last_a)
    in_group = [jnp.concatenate(lasts, axis=1)]
    in_group += [over_inst(in_group[0], m) for m in range(1, INNER)]
    arrive(last_b)
    in_group[1] = step(in_group[1])
    in_group = from_xor_order(in_group, w)
    over_all = [in_group] + [over_outer(in_group, b) for b in range(1, outer)]
    attention(last_b)
    over_all[1] = step(over_all[1])
    handoff = from_xor_order(over_all, z).reshape(n_inst, heads * wide)
    return (attended[0], handoff)


def solution(mesh):
    return jax.shard_map(
        shards,
        mesh=mesh,
        in_specs=(
            P("inst", "tp"),
            P("inst", "tp"),
            P("inst", "tp"),
            P("inst", "tp"),
            P("inst", "tp"),
            P("inst", "tp"),
            P("inst"),
        ),
        out_specs=(P("inst", "tp"), P(None, "tp")),
        check_vma=False,
    )
```

time: 487 us -> 248 us (0.51)
  waiting for transfers between devices: 357 us -> 114 us
  matrix products: 76.5 us -> 0 us
  Pallas kernels: 0 us -> 52.6 us
  starting transfers between devices: 0.15 us -> 44.9 us
  blocking collectives: 20.8 us -> 0 us
    all_gather x4 -> x3, waiting for transfers between devices: 355 us -> 0.02 us  [group_gather(): lax.all_gather(value, 'inst', axis=0, tiled=True, axis_index_groups=groups)]
    ppermute x0 -> x25, waiting for transfers between devices: none -> 113 us  [the longest x19 92.7 us: over_inst(): return lax.ppermute(value, 'inst', [(i, i ^ bits) for i in range(n_inst)])]
    pallas_call x0 -> x11, Pallas kernels: none -> 52.6 us  [the longest x8 30.7 us: multiply(): pl.pallas_call(functools.partial(kernel, len(tokens)), grid_spec=pltpu.Pr...]
    dot_general x7 -> x0, matrix products: 45.3 us -> none  [the longest x3 31 us: add_rows(): return jnp.dot(whole, piece, preferred_element_type=jnp.float32)]
    ppermute x0 -> x25, starting transfers between devices: none -> 44.8 us  [the longest x19 37.6 us: over_inst(): return lax.ppermute(value, 'inst', [(i, i ^ bits) for i in range(n_inst)])]
    sub x4 -> x0, matrix products: 31.2 us -> none  [shards(): probs = jax.nn.softmax(scores, axis=-1).astype(jnp.bfloat16)]
    all_gather x1 -> x0, blocking collectives: 20.8 us -> none  [shards(): handoff = lax.all_gather(last_row, 'inst', axis=0, tiled=True)]
    unnamed x21 -> x47, local copies, waits for them, and re-layouts: 8.14 us -> 13.9 us
  transfers between devices with their start and end apart: 4 -> 28, of which waited for: 4 -> 12; matrix products, arithmetic and copies ran while one was open for 5% -> 1% of each run, Pallas kernels for 0% -> 21%
where the time goes in v2:
time: 248 us; the launch traced here: 247 us
  waiting for transfers between devices  114 us (46%)
  Pallas kernels  52.6 us (21%)
  starting transfers between devices  44.9 us (18%)
  local copies, waits for them, and re-layouts  18.4 us (7%)
  between operations  14.8 us (6%)
    ppermute x19, waiting for transfers between devices, over_inst(): return lax.ppermute(value, 'inst', [(i, i ^ bits) for i in range(n_inst)])  92.7 us
    ppermute x19, starting transfers between devices, over_inst(): return lax.ppermute(value, 'inst', [(i, i ^ bits) for i in range(n_inst)])  37.6 us
    pallas_call x8, Pallas kernels, multiply(): pl.pallas_call(functools.partial(kernel, len(tokens)), grid_spec=pltpu.Pr...  30.7 us
    pallas_call x3, Pallas kernels, attend(): pl.pallas_call(attention_kernel, grid_spec=pltpu.PrefetchScalarGridSpec(n...  21.9 us
    ppermute x6, waiting for transfers between devices, over_tp(): return lax.ppermute(value, 'tp', [(0, 1), (1, 0)])  20.6 us
    unnamed x47, local copies, waits for them, and re-layouts  13.9 us
    ppermute x6, starting transfers between devices, over_tp(): return lax.ppermute(value, 'tp', [(0, 1), (1, 0)])  7.13 us
  transfers between devices with their start and end apart: 28, of which 12 were waited for; matrix products, arithmetic and copies ran while one was open for 1% of the time, Pallas kernels for 21%

profile of v2, /device:TPU:0, one launch (start us, length us, event | category | flops | bytes accessed | tf_op | source)
XLA Modules:
  0.0 246.9 jit_solution(16769953031634016763)
XLA Ops:
  14.8 3.0 %collective-permute-start.1 = (bf16[256,1024]{1,0:T(8,128)(2,1)S(1)}, bf16[256,1024]{1,0:T(8,128)(2,1)S(1)}, u32[]{:S(2)}, u32[]{:S(2)}) collective-permute-start(bf16[256,1024]{1,0:T(8,128)(2,1)S(1)} %pad_maximum_fusion.3), channel_id=1, source_target_pairs={{0,1},{1,0},{2,3},{3,2},{4,5},{5,4},{6,7},{7,6},{8,9},{9,8},{10,11... | collective-permute-start | bytes 1572872 | tf_op jit(solution)/shard_map/ppermute | solution.py:189
  17.9 12.7 %collective-permute-done.1 = bf16[256,1024]{1,0:T(8,128)(2,1)S(1)} collective-permute-done((bf16[256,1024]{1,0:T(8,128)(2,1)S(1)}, bf16[256,1024]{1,0:T(8,128)(2,1)S(1)}, u32[]{:S(2)}, u32[]{:S(2)}) %collective-permute-start.1) | collective-permute-done | bytes 524320 | tf_op jit(solution)/shard_map/ppermute | solution.py:189
  30.8 2.2 collective-permute-start.3
  33.1 7.9 %collective-permute-done = bf16[256,1024]{1,0:T(8,128)(2,1)S(1)} collective-permute-done((bf16[256,1024]{1,0:T(8,128)(2,1)S(1)}, bf16[256,1024]{1,0:T(8,128)(2,1)S(1)}, u32[]{:S(2)}, u32[]{:S(2)}) %collective-permute-start) | collective-permute-done | bytes 524320 | tf_op jit(solution)/shard_map/ppermute | solution.py:189
  41.0 3.9 %collective-permute-start.2 = (bf16[256,1024]{1,0:T(8,128)(2,1)S(1)}, bf16[256,1024]{1,0:T(8,128)(2,1)S(1)}, u32[]{:S(2)}, u32[]{:S(2)}) collective-permute-start(bf16[256,1024]{1,0:T(8,128)(2,1)S(1)} %get-tuple-element.70), channel_id=1, source_target_pairs={{0,24},{2,26},{4,28},{6,30},{8,16},{10,18},{12,20},{14,22},{16,8},... | collective-permute-start | bytes 1572872 | tf_op jit(solution)/shard_map/ppermute | solution.py:183
  45.2 12.6 %collective-permute-done.2.refs_1_ = bf16[256,1024]{1,0:T(8,128)(2,1)S(1)} collective-permute-done((bf16[256,1024]{1,0:T(8,128)(2,1)S(1)}, bf16[256,1024]{1,0:T(8,128)(2,1)S(1)}, u32[]{:S(2)}, u32[]{:S(2)}) %collective-permute-start.2) | collective-permute-done | bytes 524320 | tf_op jit(solution)/shard_map/ppermute | solution.py:183
  59.8 29.1 %collective-permute-done.4.refs_1_ = bf16[256,1024]{1,0:T(8,128)(2,1)S(1)} collective-permute-done((bf16[256,1024]{1,0:T(8,128)(2,1)S(1)}, bf16[256,1024]{1,0:T(8,128)(2,1)S(1)}, u32[]{:S(2)}, u32[]{:S(2)}) %collective-permute-start.4) | collective-permute-done | bytes 524320 | tf_op jit(solution)/shard_map/ppermute | solution.py:183
  91.0 2.4 copy-done.4
  93.4 4.2 %product.8 = (bf16[256,1024]{1,0:T(8,128)(2,1)}, bf16[256,1024]{1,0:T(8,128)(2,1)}) custom-call(s32[2]{0:T(128)S(1)} %pad_add_fusion.place_ref, bf16[256,1024]{1,0:T(8,128)(2,1)S(1)} %collective-permute-done.3.refs_0_, bf16[256,1024]{1,0:T(8,128)(2,1)S(1)} %collective-permute-done.2.refs_1_, bf16[256,1024]{1,0:T(8,128)(2,1)S(1)} %collective-permute-done.7.refs_2_, ...), custom_call_target="tpu_custom_call" | custom-call | bytes 1048576 | tf_op jit(solution)/shard_map/product/pallas_call | solution.py:65
  97.6 14.8 %collective-permute-start.11 = (bf16[256,1024]{1,0:T(8,128)(2,1)}, bf16[256,1024]{1,0:T(8,128)(2,1)}, u32[]{:S(2)}, u32[]{:S(2)}) collective-permute-start(bf16[256,1024]{1,0:T(8,128)(2,1)} %get-tuple-element.81), channel_id=1, source_target_pairs={{0,8},{2,10},{4,12},{6,14},{8,0},{10,2},{12,4},{14,6},{16,24},{18,... | collective-permute-start | bytes 1572872 | tf_op jit(solution)/shard_map/ppermute | solution.py:183
  112.5 2.2 copy-done.2
  114.7 3.6 %product.9 = (bf16[256,1024]{1,0:T(8,128)(2,1)S(1)}, bf16[256,1024]{1,0:T(8,128)(2,1)S(1)}) custom-call(s32[2]{0:T(128)S(1)} %pad_add_fusion.place_ref, bf16[256,1024]{1,0:T(8,128)(2,1)S(1)} %collective-permute-done.3.refs_0_, bf16[256,1024]{1,0:T(8,128)(2,1)S(1)} %collective-permute-done.2.refs_1_, bf16[256,1024]{1,0:T(8,128)(2,1)S(1)} %collective-permute-done.7.refs_2_, ...), custom_call_target="tpu_custom_call" | custom-call | bytes 1048576 | tf_op jit(solution)/shard_map/product/pallas_call | solution.py:65
  118.3 2.0 collective-permute-start.10
  120.4 5.2 %collective-permute-done.11.refs_5_ = bf16[256,1024]{1,0:T(8,128)(2,1)} collective-permute-done((bf16[256,1024]{1,0:T(8,128)(2,1)}, bf16[256,1024]{1,0:T(8,128)(2,1)}, u32[]{:S(2)}, u32[]{:S(2)}) %collective-permute-start.11) | collective-permute-done | bytes 524320 | tf_op jit(solution)/shard_map/ppermute | solution.py:183
  125.6 16.9 %collective-permute-done.12.refs_6_ = bf16[256,1024]{1,0:T(8,128)(2,1)} collective-permute-done((bf16[256,1024]{1,0:T(8,128)(2,1)}, bf16[256,1024]{1,0:T(8,128)(2,1)}, u32[]{:S(2)}, u32[]{:S(2)}) %collective-permute-start.12) | collective-permute-done | bytes 524320 | tf_op jit(solution)/shard_map/ppermute | solution.py:183
  142.4 5.5 %product.10 = (bf16[256,1024]{1,0:T(8,128)(2,1)}, f32[256,1024]{1,0:T(8,128)S(1)}) custom-call(s32[2]{0:T(128)S(1)} %pad_add_fusion.place_ref, bf16[256,1024]{1,0:T(8,128)(2,1)S(1)} %get-tuple-element.74.refs_0_, bf16[256,1024]{1,0:T(8,128)(2,1)S(1)} %collective-permute-done.4.refs_1_, bf16[256,1024]{1,0:T(8,128)(2,1)} %collective-permute-done.5.refs_2_, ...), custom_call_target="tpu_custom_call" | custom-call | bytes 1048576 | tf_op jit(solution)/shard_map/product/pallas_call | solution.py:65
  151.2 9.9 %collective-permute-done.9.refs_5_ = bf16[256,1024]{1,0:T(8,128)(2,1)S(1)} collective-permute-done((bf16[256,1024]{1,0:T(8,128)(2,1)S(1)}, bf16[256,1024]{1,0:T(8,128)(2,1)S(1)}, u32[]{:S(2)}, u32[]{:S(2)}) %collective-permute-start.9) | collective-permute-done | bytes 524320 | tf_op jit(solution)/shard_map/ppermute | solution.py:183
  162.2 5.4 %product.11 = (bf16[256,1024]{1,0:T(8,128)(2,1)}, f32[256,1024]{1,0:T(8,128)S(1)}) custom-call(s32[2]{0:T(128)S(1)} %pad_add_fusion.place_ref, bf16[256,1024]{1,0:T(8,128)(2,1)S(1)} %get-tuple-element.74.refs_0_, bf16[256,1024]{1,0:T(8,128)(2,1)S(1)} %copy-done.14, bf16[256,1024]{1,0:T(8,128)(2,1)} %collective-permute-done.5.refs_2_, ...), custom_call_target="tpu_custom_call" | custom-call | bytes 1048576 | tf_op jit(solution)/shard_map/product/pallas_call | solution.py:65
  167.5 2.2 copy-done
  170.8 2.4 product.12
  174.2 2.4 product.13
  177.8 9.8 %collective-permute-done.15.kt_ref.vt_ref = bf16[256,1024]{1,0:T(8,128)(2,1)S(1)} collective-permute-done((bf16[256,1024]{1,0:T(8,128)(2,1)}, bf16[256,1024]{1,0:T(8,128)(2,1)S(1)}, u32[]{:S(2)}, u32[]{:S(2)}) %collective-permute-start.15) | collective-permute-done | bytes 524320 | tf_op jit(solution)/shard_map/ppermute | solution.py:183
  187.6 5.5 %collective-permute-done.16.refs_5_ = bf16[256,1024]{1,0:T(8,128)(2,1)S(1)} collective-permute-done((bf16[256,1024]{1,0:T(8,128)(2,1)S(1)}, bf16[256,1024]{1,0:T(8,128)(2,1)S(1)}, u32[]{:S(2)}, u32[]{:S(2)}) %collective-permute-start.16) | collective-permute-done | bytes 524320 | tf_op jit(solution)/shard_map/ppermute | solution.py:183
  193.1 3.3 %product.14 = (bf16[128,1024]{1,0:T(8,128)(2,1)S(1)}, f32[128,1024]{1,0:T(8,128)S(1)}) custom-call(s32[2]{0:T(128)S(1)} %pad_add_fusion.place_ref, bf16[256,1024]{1,0:T(8,128)(2,1)S(1)} %copy-done.10, bf16[256,1024]{1,0:T(8,128)(2,1)S(1)} %copy-done.15, bf16[256,1024]{1,0:T(8,128)(2,1)} %collective-permute-done.5.refs_2_, ...), custom_call_target="tpu_custom_call" | custom-call | bytes 1048576 | tf_op jit(solution)/shard_map/product/pallas_call | solution.py:65
  196.4 3.8 %collective-permute-start.18 = (bf16[128,1024]{1,0:T(8,128)(2,1)S(1)}, bf16[128,1024]{1,0:T(8,128)(2,1)S(1)}, u32[]{:S(2)}, u32[]{:S(2)}) collective-permute-start(bf16[128,1024]{1,0:T(8,128)(2,1)S(1)} %get-tuple-element.109), channel_id=1, source_target_pairs={{0,16},{2,18},{4,20},{6,22},{8,24},{10,26},{12,28},{14,30},{16,0},... | collective-permute-start | bytes 786440 | tf_op jit(solution)/shard_map/ppermute | solution.py:183
  200.3 8.9 %attention.3 = (bf16[256,2048]{1,0:T(8,128)(2,1)}, bf16[1,1024]{1,0:T(2,128)(2,1)S(1)}) custom-call(s32[3]{0:T(128)S(1)} %add_add_fusion.1.place_ref, f32[256,1024]{1,0:T(8,128)S(1)} %copy-done.17, bf16[256,1024]{1,0:T(8,128)(2,1)} %collective-permute-done.14.qc_ref, bf16[1792,512]{1,0:T(8,128)(2,1)S(1)} %copy-done.6, bf16[1792,512]{1,0:T(8,128)(2,1)S(1)} %copy-done.7, ...), custom_call_target="tpu_custom_call" | custom-call | bytes 1048576 | tf_op jit(solution)/shard_map/attention/pallas_call | solution.py:135
  209.2 4.0 %product.15 = (bf16[128,1024]{1,0:T(8,128)(2,1)}, f32[128,1024]{1,0:T(8,128)S(1)}) custom-call(s32[2]{0:T(128)S(1)} %pad_add_fusion.place_ref, bf16[256,1024]{1,0:T(8,128)(2,1)S(1)} %copy-done.10, bf16[256,1024]{1,0:T(8,128)(2,1)S(1)} %copy-done.15, bf16[256,1024]{1,0:T(8,128)(2,1)} %collective-permute-done.5.refs_2_, ...), custom_call_target="tpu_custom_call" | custom-call | bytes 1048576 | tf_op jit(solution)/shard_map/product/pallas_call | solution.py:65
  213.2 6.3 %attention.4 = (bf16[256,2048]{1,0:T(8,128)(2,1)}, bf16[1,1024]{1,0:T(2,128)(2,1)S(1)}) custom-call(s32[3]{0:T(128)S(1)} %add_add_fusion.1.place_ref, f32[128,1024]{1,0:T(8,128)S(1)} %get-tuple-element.115.qm_ref, bf16[128,1024]{1,0:T(8,128)(2,1)S(1)} %collective-permute-done.18.qc_ref, ...), custom_call_target="tpu_custom_call", output_to_operand_aliasing={{0}: (9, {})} | custom-call | bytes 1048576 | tf_op jit(solution)/shard_map/attention/pallas_call | solution.py:135
  221.5 2.1 collective-permute-done.17.qc_ref
  224.7 2.7 %collective-permute-start.22 = (bf16[4,1,2048]{2,0,1:T(4,128)(2,1)S(1)}, bf16[4,1,2048]{2,0,1:T(4,128)(2,1)S(1)}, u32[]{:S(2)}, u32[]{:S(2)}) collective-permute-start(bf16[4,1,2048]{2,0,1:T(4,128)(2,1)S(1)} %reshape.23), channel_id=1, source_target_pairs={{0,8},{2,10},{4,12},{6,14},{8,0},{10,2},{12,4},{14,6},{16,24},{18,... | collective-permute-start | bytes 49160 | tf_op jit(solution)/shard_map/ppermute | solution.py:183
  227.4 2.9 %collective-permute-start.23 = (bf16[4,1,2048]{2,0,1:T(4,128)(2,1)S(1)}, bf16[4,1,2048]{2,0,1:T(4,128)(2,1)S(1)}, u32[]{:S(2)}, u32[]{:S(2)}) collective-permute-start(bf16[4,1,2048]{2,0,1:T(4,128)(2,1)S(1)} %reshape.23), channel_id=1, source_target_pairs={{0,16},{2,18},{4,20},{6,22},{8,24},{10,26},{12,28},{14,30},{16,0},... | collective-permute-start | bytes 49160 | tf_op jit(solution)/shard_map/ppermute | solution.py:183
  233.0 6.6 %attention.5 = (bf16[256,2048]{1,0:T(8,128)(2,1)}, bf16[1,1024]{1,0:T(2,128)(2,1)}) custom-call(s32[3]{0:T(128)S(1)} %add_add_fusion.place_ref, f32[128,1024]{1,0:T(8,128)S(1)} %copy-done.19, bf16[128,1024]{1,0:T(8,128)(2,1)} %collective-permute-done.17.qc_ref, bf16[1792,512]{1,0:T(8,128)(2,1)S(1)} %copy-done.6, ...), custom_call_target="tpu_custom_call", output_to_operand_aliasing={{0}: (9, {})} | custom-call | bytes 1048576 | tf_op jit(solution)/shard_map/attention/pallas_call | solution.py:135
  (107 shorter events, 25.9 us)
Async XLA Ops:
  7.2 83.8 %all-gather.6.cloned.1.call-start = ((), (), s32[]{:S(2)}) async-start(), calls=%async_computation.1 | async-start | bytes 5242880 | tf_op jit(solution)/shard_map/all_gather | solution.py:211
  12.8 99.6 %all-gather.4.cloned.1.call-start = ((), (), s32[]{:S(2)}) async-start(), calls=%async_computation | async-start | bytes 5242880 | tf_op jit(solution)/shard_map/all_gather | solution.py:211
  14.1 153.5 %all-gather.8.cloned.1.call-start = ((), (), s32[]{:S(2)}) async-start(), calls=%async_computation.2 | async-start | bytes 5242880 | tf_op jit(solution)/shard_map/all_gather | solution.py:211
  14.8 15.8 %collective-permute-start.1 = (bf16[256,1024]{1,0:T(8,128)(2,1)S(1)}, bf16[256,1024]{1,0:T(8,128)(2,1)S(1)}, u32[]{:S(2)}, u32[]{:S(2)}) collective-permute-start(bf16[256,1024]{1,0:T(8,128)(2,1)S(1)} %pad_maximum_fusion.3), channel_id=1, source_target_pairs={{0,1},{1,0},{2,3},{3,2},{4,5},{5,4},{6,7},{7,6},{8,9},{9,8},{10,11... | collective-permute-start | bytes 1572872 | tf_op jit(solution)/shard_map/ppermute | solution.py:189
  17.8 23.2 %collective-permute-start = (bf16[256,1024]{1,0:T(8,128)(2,1)S(1)}, bf16[256,1024]{1,0:T(8,128)(2,1)S(1)}, u32[]{:S(2)}, u32[]{:S(2)}) collective-permute-start(bf16[256,1024]{1,0:T(8,128)(2,1)S(1)} %pad_maximum_fusion.2), channel_id=1, source_target_pairs={{0,1},{1,0},{2,3},{3,2},{4,5},{5,4},{6,7},{7,6},{8,9},{9,8},{10,11... | collective-permute-start | bytes 1572872 | tf_op jit(solution)/shard_map/ppermute | solution.py:189
  30.8 14.3 %collective-permute-start.3 = (bf16[256,1024]{1,0:T(8,128)(2,1)S(1)}, bf16[256,1024]{1,0:T(8,128)(2,1)S(1)}, u32[]{:S(2)}, u32[]{:S(2)}) collective-permute-start(bf16[256,1024]{1,0:T(8,128)(2,1)S(1)} %get-tuple-element.68), channel_id=1, source_target_pairs={{0,8},{2,10},{4,12},{6,14},{8,0},{10,2},{12,4},{14,6},{16,24},{18,... | collective-permute-start | bytes 1572872 | tf_op jit(solution)/shard_map/ppermute | solution.py:183
  41.0 16.8 %collective-permute-start.2 = (bf16[256,1024]{1,0:T(8,128)(2,1)S(1)}, bf16[256,1024]{1,0:T(8,128)(2,1)S(1)}, u32[]{:S(2)}, u32[]{:S(2)}) collective-permute-start(bf16[256,1024]{1,0:T(8,128)(2,1)S(1)} %get-tuple-element.70), channel_id=1, source_target_pairs={{0,24},{2,26},{4,28},{6,30},{8,16},{10,18},{12,20},{14,22},{16,8},... | collective-permute-start | bytes 1572872 | tf_op jit(solution)/shard_map/ppermute | solution.py:183
  45.1 116.0 %copy-start.9 = (bf16[256,1024]{1,0:T(8,128)(2,1)}, bf16[256,1024]{1,0:T(8,128)(2,1)S(1)}, u32[]{:S(2)}) copy-start(bf16[256,1024]{1,0:T(8,128)(2,1)S(1)} %get-tuple-element.74.refs_0_) | copy-start | bytes 1572868
  45.1 43.7 %collective-permute-start.4 = (bf16[256,1024]{1,0:T(8,128)(2,1)S(1)}, bf16[256,1024]{1,0:T(8,128)(2,1)S(1)}, u32[]{:S(2)}, u32[]{:S(2)}) collective-permute-start(bf16[256,1024]{1,0:T(8,128)(2,1)S(1)} %get-tuple-element.71), channel_id=1, source_target_pairs={{0,16},{2,18},{4,20},{6,22},{8,24},{10,26},{12,28},{14,30},{16,0},... | collective-permute-start | bytes 1572872 | tf_op jit(solution)/shard_map/ppermute | solution.py:183
  57.8 33.2 %collective-permute-start.8 = (bf16[256,1024]{1,0:T(8,128)(2,1)S(1)}, bf16[256,1024]{1,0:T(8,128)(2,1)S(1)}, u32[]{:S(2)}, u32[]{:S(2)}) collective-permute-start(bf16[256,1024]{1,0:T(8,128)(2,1)S(1)} %collective-permute-done.2.refs_1_), channel_id=1, source_target_pairs={{0,1},{1,0},{2,3},{3,2},{4,5},{5,4},{6,7},{7,6},{8,9},{9,8},{10,11... | collective-permute-start | bytes 1572872 | tf_op jit(solution)/shard_map/ppermute | solution.py:189
  59.5 31.5 %collective-permute-start.7 = (bf16[256,1024]{1,0:T(8,128)(2,1)S(1)}, bf16[256,1024]{1,0:T(8,128)(2,1)S(1)}, u32[]{:S(2)}, u32[]{:S(2)}) collective-permute-start(bf16[256,1024]{1,0:T(8,128)(2,1)S(1)} %collective-permute-done.3.refs_0_), channel_id=1, source_target_pairs={{0,1},{1,0},{2,3},{3,2},{4,5},{5,4},{6,7},{7,6},{8,9},{9,8},{10,11... | collective-permute-start | bytes 1572872 | tf_op jit(solution)/shard_map/ppermute | solution.py:189
  88.8 53.6 %copy-start.13 = (bf16[256,1024]{1,0:T(8,128)(2,1)}, bf16[256,1024]{1,0:T(8,128)(2,1)S(1)}, u32[]{:S(2)}) copy-start(bf16[256,1024]{1,0:T(8,128)(2,1)S(1)} %collective-permute-done.4.refs_1_) | copy-start | bytes 1572868
  88.9 31.5 %collective-permute-start.6 = (bf16[256,1024]{1,0:T(8,128)(2,1)S(1)}, bf16[256,1024]{1,0:T(8,128)(2,1)}, u32[]{:S(2)}, u32[]{:S(2)}) collective-permute-start(bf16[256,1024]{1,0:T(8,128)(2,1)S(1)} %collective-permute-done.4.refs_1_), channel_id=1, source_target_pairs={{0,1},{1,0},{2,3},{3,2},{4,5},{5,4},{6,7},{7,6},{8,9},{9,8},{10,11... | collective-permute-start | bytes 1572872 | tf_op jit(solution)/shard_map/ppermute | solution.py:189
  90.4 30.0 %collective-permute-start.5 = (bf16[256,1024]{1,0:T(8,128)(2,1)S(1)}, bf16[256,1024]{1,0:T(8,128)(2,1)}, u32[]{:S(2)}, u32[]{:S(2)}) collective-permute-start(bf16[256,1024]{1,0:T(8,128)(2,1)S(1)} %get-tuple-element.74.refs_0_), channel_id=1, source_target_pairs={{0,1},{1,0},{2,3},{3,2},{4,5},{5,4},{6,7},{7,6},{8,9},{9,8},{10,11... | collective-permute-start | bytes 1572872 | tf_op jit(solution)/shard_map/ppermute | solution.py:189
  97.6 28.0 %collective-permute-start.11 = (bf16[256,1024]{1,0:T(8,128)(2,1)}, bf16[256,1024]{1,0:T(8,128)(2,1)}, u32[]{:S(2)}, u32[]{:S(2)}) collective-permute-start(bf16[256,1024]{1,0:T(8,128)(2,1)} %get-tuple-element.81), channel_id=1, source_target_pairs={{0,8},{2,10},{4,12},{6,14},{8,0},{10,2},{12,4},{14,6},{16,24},{18,... | collective-permute-start | bytes 1572872 | tf_op jit(solution)/shard_map/ppermute | solution.py:183
  112.4 30.0 %collective-permute-start.12 = (bf16[256,1024]{1,0:T(8,128)(2,1)}, bf16[256,1024]{1,0:T(8,128)(2,1)}, u32[]{:S(2)}, u32[]{:S(2)}) collective-permute-start(bf16[256,1024]{1,0:T(8,128)(2,1)} %get-tuple-element.89), channel_id=1, source_target_pairs={{0,8},{2,10},{4,12},{6,14},{8,0},{10,2},{12,4},{14,6},{16,24},{18,... | collective-permute-start | bytes 1572872 | tf_op jit(solution)/shard_map/ppermute | solution.py:183
  114.7 27.7 %copy-start.5 = (bf16[2048,1024]{1,0:T(8,128)(2,1)S(1)}, bf16[2048,1024]{1,0:T(8,128)(2,1)}, u32[]{:S(2)}) copy-start(bf16[2048,1024]{1,0:T(8,128)(2,1)} %all-gather.6.cloned.1.call-done.refs_4_) | copy-start | bytes 12582916
  118.3 42.8 %copy-start.3 = (bf16[2048,1024]{1,0:T(8,128)(2,1)S(1)}, bf16[2048,1024]{1,0:T(8,128)(2,1)}, u32[]{:S(2)}) copy-start(bf16[2048,1024]{1,0:T(8,128)(2,1)} %all-gather.4.cloned.1.call-done.refs_4_) | copy-start | bytes 12582916
  118.3 32.9 %collective-permute-start.10 = (bf16[256,1024]{1,0:T(8,128)(2,1)S(1)}, bf16[256,1024]{1,0:T(8,128)(2,1)S(1)}, u32[]{:S(2)}, u32[]{:S(2)}) collective-permute-start(bf16[256,1024]{1,0:T(8,128)(2,1)S(1)} %get-tuple-element.88), channel_id=1, source_target_pairs={{0,8},{2,10},{4,12},{6,14},{8,0},{10,2},{12,4},{14,6},{16,24},{18,... | collective-permute-start | bytes 1572872 | tf_op jit(solution)/shard_map/ppermute | solution.py:183
  120.3 40.8 %collective-permute-start.9 = (bf16[256,1024]{1,0:T(8,128)(2,1)S(1)}, bf16[256,1024]{1,0:T(8,128)(2,1)S(1)}, u32[]{:S(2)}, u32[]{:S(2)}) collective-permute-start(bf16[256,1024]{1,0:T(8,128)(2,1)S(1)} %get-tuple-element.85), channel_id=1, source_target_pairs={{0,8},{2,10},{4,12},{6,14},{8,0},{10,2},{12,4},{14,6},{16,24},{18,... | collective-permute-start | bytes 1572872 | tf_op jit(solution)/shard_map/ppermute | solution.py:183
  148.9 28.8 %collective-permute-start.14 = (bf16[256,1024]{1,0:T(8,128)(2,1)}, bf16[256,1024]{1,0:T(8,128)(2,1)}, u32[]{:S(2)}, u32[]{:S(2)}) collective-permute-start(bf16[256,1024]{1,0:T(8,128)(2,1)} %get-tuple-element.93), channel_id=1, source_target_pairs={{0,16},{2,18},{4,20},{6,22},{8,24},{10,26},{12,28},{14,30},{16,0},... | collective-permute-start | bytes 1572872 | tf_op jit(solution)/shard_map/ppermute | solution.py:183
  167.5 20.0 %collective-permute-start.15 = (bf16[256,1024]{1,0:T(8,128)(2,1)}, bf16[256,1024]{1,0:T(8,128)(2,1)S(1)}, u32[]{:S(2)}, u32[]{:S(2)}) collective-permute-start(bf16[256,1024]{1,0:T(8,128)(2,1)} %get-tuple-element.97), channel_id=1, source_target_pairs={{0,16},{2,18},{4,20},{6,22},{8,24},{10,26},{12,28},{14,30},{16,0},... | collective-permute-start | bytes 1572872 | tf_op jit(solution)/shard_map/ppermute | solution.py:183
  173.2 19.9 %collective-permute-start.16 = (bf16[256,1024]{1,0:T(8,128)(2,1)S(1)}, bf16[256,1024]{1,0:T(8,128)(2,1)S(1)}, u32[]{:S(2)}, u32[]{:S(2)}) collective-permute-start(bf16[256,1024]{1,0:T(8,128)(2,1)S(1)} %product.12), channel_id=1, source_target_pairs={{0,8},{2,10},{4,12},{6,14},{8,0},{10,2},{12,4},{14,6},{16,24},{18,... | collective-permute-start | bytes 1572872 | tf_op jit(solution)/shard_map/ppermute | solution.py:183
  176.7 32.6 %collective-permute-start.13 = (bf16[256,1024]{1,0:T(8,128)(2,1)S(1)}, bf16[256,1024]{1,0:T(8,128)(2,1)S(1)}, u32[]{:S(2)}, u32[]{:S(2)}) collective-permute-start(bf16[256,1024]{1,0:T(8,128)(2,1)S(1)} %product.13), channel_id=1, source_target_pairs={{0,8},{2,10},{4,12},{6,14},{8,0},{10,2},{12,4},{14,6},{16,24},{18,... | collective-permute-start | bytes 1572872 | tf_op jit(solution)/shard_map/ppermute | solution.py:183
  196.4 16.8 %collective-permute-start.18 = (bf16[128,1024]{1,0:T(8,128)(2,1)S(1)}, bf16[128,1024]{1,0:T(8,128)(2,1)S(1)}, u32[]{:S(2)}, u32[]{:S(2)}) collective-permute-start(bf16[128,1024]{1,0:T(8,128)(2,1)S(1)} %get-tuple-element.109), channel_id=1, source_target_pairs={{0,16},{2,18},{4,20},{6,22},{8,24},{10,26},{12,28},{14,30},{16,0},... | collective-permute-start | bytes 786440 | tf_op jit(solution)/shard_map/ppermute | solution.py:183
  213.2 10.4 %collective-permute-start.17 = (bf16[128,1024]{1,0:T(8,128)(2,1)}, bf16[128,1024]{1,0:T(8,128)(2,1)}, u32[]{:S(2)}, u32[]{:S(2)}) collective-permute-start(bf16[128,1024]{1,0:T(8,128)(2,1)} %get-tuple-element.114), channel_id=1, source_target_pairs={{0,16},{2,18},{4,20},{6,22},{8,24},{10,26},{12,28},{14,30},{16,0},... | collective-permute-start | bytes 786440 | tf_op jit(solution)/shard_map/ppermute | solution.py:183
  219.6 4.0 %collective-permute-start.19 = (bf16[1,2048]{1,0:T(2,128)(2,1)S(1)}, bf16[1,2048]{1,0:T(2,128)(2,1)S(1)}, u32[]{:S(2)}, u32[]{:S(2)}) collective-permute-start(bf16[1,2048]{1,0:T(2,128)(2,1)S(1)} %constant_dynamic-update-slice_fusion), channel_id=1, source_target_pairs={{0,2},{2,0},{4,6},{6,4},{8,10},{10,8},{12,14},{14,12},{16,18},{18,... | collective-permute-start | bytes 12296 | tf_op jit(solution)/shard_map/ppermute | solution.py:183
  219.7 3.9 %collective-permute-start.20 = (bf16[1,2048]{1,0:T(2,128)(2,1)S(1)}, bf16[1,2048]{1,0:T(2,128)(2,1)S(1)}, u32[]{:S(2)}, u32[]{:S(2)}) collective-permute-start(bf16[1,2048]{1,0:T(2,128)(2,1)S(1)} %constant_dynamic-update-slice_fusion), channel_id=1, source_target_pairs={{0,4},{2,6},{4,0},{6,2},{8,12},{10,14},{12,8},{14,10},{16,20},{18,... | collective-permute-start | bytes 12296 | tf_op jit(solution)/shard_map/ppermute | solution.py:183
  221.0 3.1 %collective-permute-start.21 = (bf16[1,2048]{1,0:T(2,128)(2,1)S(1)}, bf16[1,2048]{1,0:T(2,128)(2,1)S(1)}, u32[]{:S(2)}, u32[]{:S(2)}) collective-permute-start(bf16[1,2048]{1,0:T(2,128)(2,1)S(1)} %constant_dynamic-update-slice_fusion), channel_id=1, source_target_pairs={{0,6},{2,4},{4,2},{6,0},{8,14},{10,12},{12,10},{14,8},{16,22},{18,... | collective-permute-start | bytes 12296 | tf_op jit(solution)/shard_map/ppermute | solution.py:183
  224.7 14.8 %collective-permute-start.22 = (bf16[4,1,2048]{2,0,1:T(4,128)(2,1)S(1)}, bf16[4,1,2048]{2,0,1:T(4,128)(2,1)S(1)}, u32[]{:S(2)}, u32[]{:S(2)}) collective-permute-start(bf16[4,1,2048]{2,0,1:T(4,128)(2,1)S(1)} %reshape.23), channel_id=1, source_target_pairs={{0,8},{2,10},{4,12},{6,14},{8,0},{10,2},{12,4},{14,6},{16,24},{18,... | collective-permute-start | bytes 49160 | tf_op jit(solution)/shard_map/ppermute | solution.py:183
  227.4 12.1 %collective-permute-start.23 = (bf16[4,1,2048]{2,0,1:T(4,128)(2,1)S(1)}, bf16[4,1,2048]{2,0,1:T(4,128)(2,1)S(1)}, u32[]{:S(2)}, u32[]{:S(2)}) collective-permute-start(bf16[4,1,2048]{2,0,1:T(4,128)(2,1)S(1)} %reshape.23), channel_id=1, source_target_pairs={{0,16},{2,18},{4,20},{6,22},{8,24},{10,26},{12,28},{14,30},{16,0},... | collective-permute-start | bytes 49160 | tf_op jit(solution)/shard_map/ppermute | solution.py:183
  230.4 9.2 %collective-permute-start.24 = (bf16[4,1,2048]{2,0,1:T(4,128)(2,1)S(1)}, bf16[4,1,2048]{2,0,1:T(4,128)(2,1)S(1)}, u32[]{:S(2)}, u32[]{:S(2)}) collective-permute-start(bf16[4,1,2048]{2,0,1:T(4,128)(2,1)S(1)} %reshape.23), channel_id=1, source_target_pairs={{0,24},{2,26},{4,28},{6,30},{8,16},{10,18},{12,20},{14,22},{16,8},... | collective-permute-start | bytes 49160 | tf_op jit(solution)/shard_map/ppermute | solution.py:183
  (19 other events, 175.6 us)
Sparse Core Ops, SparseCore 0:
  12.9 37.1 all-gather.5
  51.7 34.4 all-gather.3
  87.8 34.4 all-gather.7

commit v3 on v2

v3 whole, which is shorter than its diff:
```python
import jax
import jax.numpy as jnp
from jax import lax
from jax.experimental import pallas as pl
from jax.experimental.pallas import tpu as pltpu
from jax.sharding import PartitionSpec as P

HEAD_SIZE = 128
QUERY_PER_GROUP = 4
VMEM_LIMIT = 32 * 1024 * 1024
COST = 1 << 20
INNER = 4


def dot(a, b):
    return jnp.dot(a, b, preferred_element_type=jnp.float32)


def attention_kernel(
    place_ref, qm_ref, qc_ref, kc_ref, vc_ref, km_ref, kt_ref, vm_ref, vt_ref, *rest
):
    o_ref, last_ref = rest[-2:]
    length, here, first = place_ref[0], place_ref[1], place_ref[2]
    rows, block = qm_ref.shape[0], km_ref.shape[0]
    half = block // 2
    total = lambda mine, came: (mine + came.astype(jnp.float32)).astype(jnp.bfloat16)
    factor = 1.4426950408889634 / HEAD_SIZE**0.5
    row = lax.broadcasted_iota(jnp.int32, (rows, 1), 0) + here * half
    col = lax.broadcasted_iota(jnp.int32, (rows, block), 1)
    col = jnp.where(col < half, col + first * half, col - first * half)
    allowed = (col <= row) & (col < length)
    contract = (((1,), (1,)), ((), ()))
    at = row == length - 1
    keys = total(km_ref[...], kt_ref[...])
    values = total(vm_ref[...], vt_ref[...])
    stack = 2
    allowed = jnp.concatenate([allowed] * stack, axis=0)
    for member in range(0, QUERY_PER_GROUP, stack):
        each = [
            slice((member + i) * HEAD_SIZE, (member + i + 1) * HEAD_SIZE) for i in range(stack)
        ]
        q = jnp.concatenate([total(qm_ref[:, cols], qc_ref[:, cols]) for cols in each], axis=0)
        s1 = lax.dot_general(q, kc_ref[...], contract, preferred_element_type=jnp.float32)
        s2 = lax.dot_general(q, keys, contract, preferred_element_type=jnp.float32)
        s2 = jnp.where(allowed, s2, -jnp.inf)
        top = jnp.maximum(jnp.max(s1, axis=1, keepdims=True), jnp.max(s2, axis=1, keepdims=True))
        p1 = jnp.exp2((s1 - top) * factor)
        p2 = jnp.exp2((s2 - top) * factor)
        norm = jnp.sum(p1, axis=1, keepdims=True) + jnp.sum(p2, axis=1, keepdims=True)
        both = dot(p1.astype(jnp.bfloat16), vc_ref[...]) + dot(p2.astype(jnp.bfloat16), values)
        both = both / norm
        for i, cols in enumerate(each):
            out = both[i * rows : (i + 1) * rows]
            o_ref[:, cols] = out.astype(o_ref.dtype)
            last_ref[:, cols] = jnp.sum(jnp.where(at, out, 0.0), axis=0, keepdims=True).astype(
                last_ref.dtype
            )


def attend(place, q, which, k_cache, v_cache, kv, start, shape, buffer):
    cols = q[0].shape[1]
    wide = QUERY_PER_GROUP * HEAD_SIZE
    cached, block = k_cache.shape[0], kv[0].shape[0]
    rows = block // 2
    heads = k_cache.shape[1] // HEAD_SIZE
    groups = cols // wide
    begin = start // wide
    column = lambda i, place: (0, begin + i)
    after = lambda i, place: (0, heads + begin + i)
    mine = lambda i, place: (which, i)
    buffers = [] if buffer is None else [buffer]
    return pl.pallas_call(
        attention_kernel,
        grid_spec=pltpu.PrefetchScalarGridSpec(
            num_scalar_prefetch=1,
            grid=(groups,),
            in_specs=[
                pl.BlockSpec((rows, wide), mine),
                pl.BlockSpec((rows, wide), mine),
                pl.BlockSpec((cached, HEAD_SIZE), column),
                pl.BlockSpec((cached, HEAD_SIZE), column),
                pl.BlockSpec((block, HEAD_SIZE), column),
                pl.BlockSpec((block, HEAD_SIZE), column),
                pl.BlockSpec((block, HEAD_SIZE), after),
                pl.BlockSpec((block, HEAD_SIZE), after),
            ]
            + [pl.BlockSpec(memory_space=pl.ANY)] * len(buffers),
            out_specs=[
                pl.BlockSpec((rows, wide), lambda i, place: (place[1], begin + i)),
                pl.BlockSpec((1, wide), lambda i, place: (0, i)),
            ],
        ),
        out_shape=[
            jax.ShapeDtypeStruct(shape, jnp.bfloat16),
            jax.ShapeDtypeStruct((1, cols), jnp.bfloat16),
        ],
        input_output_aliases={9: 0} if buffers else {},
        compiler_params=pltpu.CompilerParams(vmem_limit_bytes=VMEM_LIMIT),
        cost_estimate=pl.CostEstimate(flops=0, bytes_accessed=COST, transcendentals=0),
        name="attention",
    )(place, *q, k_cache, v_cache, *kv, *kv, *buffers)


def shards(tokens_in, w_query, w_key, w_value, stored_key_cache, stored_value_cache, prompt_len):
    n_inst, n_tp = lax.axis_size("inst"), lax.axis_size("tp")
    outer = n_inst // INNER
    me = lax.axis_index("inst")
    z, w = me // INNER, me % INNER
    x = lax.axis_index("tp")
    rows, local = tokens_in.shape
    half = rows // 2
    part = local // outer
    groups = [list(range(o * INNER, (o + 1) * INNER)) for o in range(outer)]

    first = (prompt_len[0] - 1) // half

    def over_inst(value, bits):
        return lax.ppermute(value, "inst", [(i, i ^ bits) for i in range(n_inst)])

    def over_outer(value, bits):
        return over_inst(value, bits * INNER)

    def over_tp(value):
        return lax.ppermute(value, "tp", [(0, 1), (1, 0)])

    def swapped_if(flag, a, b, axis):
        return jnp.where(
            flag, jnp.concatenate([b, a], axis=axis), jnp.concatenate([a, b], axis=axis)
        )

    last_step = [None]

    def step(*values):
        if last_step[0] is not None:
            *values, _ = lax.optimization_barrier((*values, last_step[0]))
        last_step[0] = values[0]
        return values[0] if len(values) == 1 else values

    heads = w_key.shape[1] // HEAD_SIZE
    wide = QUERY_PER_GROUP * HEAD_SIZE
    pieces = 2 if heads % 2 == 0 else 1
    chunk = heads * wide // pieces
    fast = outer == 4 and n_tp == 2

    def group_gather(value):
        return lax.all_gather(value, "inst", axis=0, tiled=True, axis_index_groups=groups)

    weights = {}

    def gather_queries(piece):
        weights[piece] = group_gather(step(w_query[:, piece * chunk : (piece + 1) * chunk]))

    def gather_others():
        weights["kv"] = group_gather(step(jnp.concatenate([w_key, w_value], axis=1)))
        if pieces == 2:
            gather_queries(1)

    tokens = {}
    if fast:

        def cut(j, p):
            column = (((z % 2) ^ j) * n_tp + p) * part
            return jnp.concatenate(
                [
                    lax.dynamic_slice(tokens_in, (h * half, column), (half, part))
                    for h in (first, 1 - first)
                ],
                axis=0,
            )

        swap = {1: over_tp(step(cut(1, 1 - x)))}
        gather_queries(0)
        swap[0] = over_tp(step(cut(0, 1 - x)))
        gather_others()
        mine = z // 2 == x
        held, came = {}, {}
        own = {j: cut(j, x) for j in (1, 0)}
        swap[1] = step(swap[1])
        send = {b: jnp.where(mine == (b < 2), own[1], swap[1]) for b in (1, 3)}
        send[1], send[3] = step(send[1], send[3])
        got = {b: over_outer(send[b], b) for b in (1, 3)}

        def tp_exchange(b):
            held[b] = step(got[b])
            came[b] = over_tp(held[b])

        tp_exchange(1)
        tp_exchange(3)
        swap[0] = step(swap[0])
        send = {b: jnp.where(mine == (b < 2), own[0], swap[0]) for b in (2, 0)}
        send[2] = step(send[2])
        got[2], got[0] = over_outer(send[2], 2), send[0]
        tp_exchange(0)

        def arrived(b):
            if b not in tokens:
                tokens[b] = swapped_if(x == 1, held[b], step(came[b]), 1)

    else:
        gather_queries(0)
        gather_others()
        swapped = jnp.where(first == 1, jnp.roll(tokens_in, half, axis=0), tokens_in)
        own = swapped.reshape(rows, outer // n_tp, n_tp, part)
        parts = lax.all_to_all(own, "tp", 2, 1, tiled=True).reshape(rows, outer, part)
        come = jnp.stack(
            [
                over_outer(lax.dynamic_index_in_dim(parts, z ^ b, 1, keepdims=False), b)
                for b in range(outer)
            ]
        )
        both = lax.all_gather(come.reshape(-1, part), "tp", axis=1, tiled=True)
        both = both.reshape(outer, rows, -1)
        tokens.update({b: both[b] for b in range(outer)})

        def arrived(b):
            pass

    def rows_of(value, h):
        return value if h is None else value[h * half : (h + 1) * half]

    def first_send(h, name):
        weight = step(weights[name])
        bits = range(1, outer, 2)
        if h is None:
            come = {}
            for b in bits:
                arrived(b)
                come[b] = over_outer(step(dot(tokens[b], weight).astype(jnp.bfloat16)), 1)
            return come
        joined = jnp.concatenate([rows_of(tokens[b], h) for b in bits], axis=0)
        come = over_outer(step(dot(joined, weight).astype(jnp.bfloat16)), 1)
        return {b: (come, i) for i, b in enumerate(bits)}

    def later_sends(h, name, come):
        weight = weights[name]
        sums = {}
        if h is not None:
            whole = step(next(iter(come.values()))[0])
            come = {b: whole[i * half : (i + 1) * half] for b, (_, i) in come.items()}
        for b in reversed(range(0, outer, 2)):
            if h is None:
                come[b + 1] = step(come[b + 1])
            arrived(b)
            sums[b] = dot(rows_of(tokens[b], h), weight) + come[b + 1].astype(jnp.float32)
        bit = 2
        while True:
            for b in sorted(sums):
                if b & bit:
                    moved = over_outer(step(sums.pop(b).astype(jnp.bfloat16)), bit)
                    if 2 * bit == outer:
                        return sums[0], moved
                    sums[b ^ bit] = sums[b ^ bit] + moved.astype(jnp.float32)
            bit *= 2

    if pieces == 2:
        jobs = [(None, 0), (None, "kv"), (0, 1), (1, 1)]
    else:
        jobs = [(None, "kv"), (0, 0), (1, 0)]
    opened, parts_of, lasts = {}, {}, []
    attended = [None]

    def start(n):
        opened[n] = first_send(*jobs[n])

    def advance(n):
        parts_of[n] = later_sends(*jobs[n], opened[n])

    def arrive(n):
        parts_of[n] = (parts_of[n][0], step(parts_of[n][1]))

    def attention(n, h):
        own_half, piece = jobs[n]
        place = jnp.stack([prompt_len[0], h ^ first, first]).astype(jnp.int32)
        which = h if own_half is None else 0
        kv = parts_of[jobs.index((None, "kv"))]
        caches = (stored_key_cache, stored_value_cache)
        shape = (rows, heads * wide)
        attended[0], last = attend(
            place, parts_of[n], which, *caches, kv, piece * chunk, shape, attended[0]
        )
        lasts.append(step(last))

    def from_xor_order(values, index):
        out = jnp.stack(values)
        shape = out.shape
        bits = len(values).bit_length() - 1
        for bit in range(bits):
            out = out.reshape(len(values) >> (bit + 1), 2, 1 << bit, *shape[1:])
            out = jnp.where((index >> bit) % 2 == 1, out[:, ::-1], out)
        return out.reshape(shape)

    start(0)
    if fast:
        tp_exchange(2)
    start(1)
    advance(0)
    if pieces == 2:
        advance(1)
        start(2)
        arrive(0)
        start(3)
        advance(2)
        arrive(1)
        advance(3)
        attention(0, 0)
        arrive(2)
        attention(2, 0)
    else:
        start(2)
        advance(1)
        arrive(0)
        advance(2)
        arrive(1)
        attention(1, 0)
    arrive(len(jobs) - 1)
    row = jnp.concatenate(lasts, axis=1)
    in_group = [row] + [over_inst(row, m) for m in range(1, INNER)]
    if pieces == 2:
        attention(0, 1)
    in_group[1] = step(in_group[1])
    in_group = from_xor_order(in_group, w)
    over_all = [in_group] + [over_outer(in_group, b) for b in range(1, outer)]
    attention(len(jobs) - 1, 1)
    over_all[1] = step(over_all[1])
    handoff = from_xor_order(over_all, z).reshape(n_inst, heads * wide)
    return (attended[0], handoff)


def solution(mesh):
    return jax.shard_map(
        shards,
        mesh=mesh,
        in_specs=(
            P("inst", "tp"),
            P("inst", "tp"),
            P("inst", "tp"),
            P("inst", "tp"),
            P("inst", "tp"),
            P("inst", "tp"),
            P("inst"),
        ),
        out_specs=(P("inst", "tp"), P(None, "tp")),
        check_vma=False,
    )
```

time: 248 us -> 232 us (0.935)
  matrix products: 0 us -> 31.6 us
  Pallas kernels: 52.6 us -> 22.2 us
  starting transfers between devices: 44.9 us -> 30.7 us
  other arithmetic: 2.18 us -> 13.5 us
  waiting for transfers between devices: 114 us -> 106 us
  local copies, waits for them, and re-layouts: 18.4 us -> 12.6 us
    dot_general x0 -> x14, matrix products: none -> 31.6 us  [dot(): return jnp.dot(a, b, preferred_element_type=jnp.float32)]
    pallas_call x8 -> x0, Pallas kernels: 30.7 us -> none  [multiply(): pl.pallas_call(functools.partial(kernel, len(tokens)), grid_spec=pltpu.Pr...]
    ppermute x19, starting transfers between devices: 37.6 us -> 22 us  [over_inst(): return lax.ppermute(value, 'inst', [(i, i ^ bits) for i in range(n_inst)])]
    unnamed x47 -> x71, local copies, waits for them, and re-layouts: 13.9 us -> 5.3 us
    select_n x0 -> x4, other arithmetic: none -> 7.5 us  [swapped_if(): jnp.where(flag, jnp.concatenate([b, a], axis=axis), jnp.concatenate([a, b...]
    ppermute x6, waiting for transfers between devices: 20.6 us -> 15.8 us  [over_tp(): return lax.ppermute(value, 'tp', [(0, 1), (1, 0)])]
    slice x1 -> x3, local copies, waits for them, and re-layouts: 1.5 us -> 5.15 us  [the longest x1 3.03 us: gather_queries(): w_query[:, piece * chunk:(piece + 1) * chunk]]
    ppermute x19, waiting for transfers between devices: 92.7 us -> 89.1 us  [over_inst(): return lax.ppermute(value, 'inst', [(i, i ^ bits) for i in range(n_inst)])]
  transfers between devices with their start and end apart: 28 -> 28, of which waited for: 12 -> 14; matrix products, arithmetic and copies ran while one was open for 1% -> 21% of each run, Pallas kernels for 21% -> 5%
where the time goes in v3:
time: 232 us; the launch traced here: 231 us
  waiting for transfers between devices  106 us (46%)
  matrix products  31.6 us (14%)
  starting transfers between devices  30.7 us (13%)
  Pallas kernels  22.2 us (10%)
  between operations  15.2 us (7%)
  other arithmetic  13.5 us (6%)
  local copies, waits for them, and re-layouts  12.6 us (5%)
    ppermute x19, waiting for transfers between devices, over_inst(): return lax.ppermute(value, 'inst', [(i, i ^ bits) for i in range(n_inst)])  89.1 us
    dot_general x14, matrix products, dot(): return jnp.dot(a, b, preferred_element_type=jnp.float32)  31.6 us
    pallas_call x4, Pallas kernels, attend(): pl.pallas_call(attention_kernel, grid_spec=pltpu.PrefetchScalarGridSpec(n...  22.2 us
    ppermute x19, starting transfers between devices, over_inst(): return lax.ppermute(value, 'inst', [(i, i ^ bits) for i in range(n_inst)])  22 us
    ppermute x6, waiting for transfers between devices, over_tp(): return lax.ppermute(value, 'tp', [(0, 1), (1, 0)])  15.8 us
    ppermute x6, starting transfers between devices, over_tp(): return lax.ppermute(value, 'tp', [(0, 1), (1, 0)])  8.57 us
    select_n x4, other arithmetic, swapped_if(): jnp.where(flag, jnp.concatenate([b, a], axis=axis), jnp.concatenate([a, b...  7.5 us
    unnamed x71, local copies, waits for them, and re-layouts  5.3 us
  transfers between devices with their start and end apart: 28, of which 14 were waited for; matrix products, arithmetic and copies ran while one was open for 21% of the time, Pallas kernels for 5%

profile of v3, /device:TPU:0, one launch (start us, length us, event | category | flops | bytes accessed | tf_op | source)
XLA Modules:
  0.0 231.3 jit_solution(16143501045553388780)
XLA Ops:
  8.1 3.0 %fusion.37 = (bf16[512,1024]{1,0:T(8,128)(2,1)}, bf16[512,1024]{1,0:T(8,128)(2,1)}) fusion(bf16[512,2048]{1,0:T(8,128)(2,1)} %param.8), kind=kLoop, calls=%fused_computation.58 | loop fusion | bytes 4194304 | tf_op jit(solution)/shard_map/slice | solution.py:151
  12.2 2.3 pad_maximum_fusion
  14.6 3.0 %collective-permute-start.1 = (bf16[256,1024]{1,0:T(8,128)(2,1)S(1)}, bf16[256,1024]{1,0:T(8,128)(2,1)S(1)}, u32[]{:S(2)}, u32[]{:S(2)}) collective-permute-start(bf16[256,1024]{1,0:T(8,128)(2,1)S(1)} %pad_maximum_fusion.3), channel_id=1, source_target_pairs={{0,1},{1,0},{2,3},{3,2},{4,5},{5,4},{6,7},{7,6},{8,9},{9,8},{10,11... | collective-permute-start | bytes 1572872 | tf_op jit(solution)/shard_map/ppermute | solution.py:124
  17.6 11.9 %collective-permute-done.1 = bf16[256,1024]{1,0:T(8,128)(2,1)S(1)} collective-permute-done((bf16[256,1024]{1,0:T(8,128)(2,1)S(1)}, bf16[256,1024]{1,0:T(8,128)(2,1)S(1)}, u32[]{:S(2)}, u32[]{:S(2)}) %collective-permute-start.1) | collective-permute-done | bytes 524320 | tf_op jit(solution)/shard_map/ppermute | solution.py:124
  32.4 2.5 %collective-permute-start.2 = (bf16[256,1024]{1,0:T(8,128)(2,1)}, bf16[256,1024]{1,0:T(8,128)(2,1)S(1)}, u32[]{:S(2)}, u32[]{:S(2)}) collective-permute-start(bf16[256,1024]{1,0:T(8,128)(2,1)} %get-tuple-element.56), channel_id=1, source_target_pairs={{0,24},{2,26},{4,28},{6,30},{8,16},{10,18},{12,20},{14,22},{16,8},... | collective-permute-start | bytes 1572872 | tf_op jit(solution)/shard_map/ppermute | solution.py:118
  36.4 8.4 %collective-permute-done.3 = bf16[256,1024]{1,0:T(8,128)(2,1)S(1)} collective-permute-done((bf16[256,1024]{1,0:T(8,128)(2,1)S(1)}, bf16[256,1024]{1,0:T(8,128)(2,1)S(1)}, u32[]{:S(2)}, u32[]{:S(2)}) %collective-permute-start.3) | collective-permute-done | bytes 524320 | tf_op jit(solution)/shard_map/ppermute | solution.py:118
  46.3 10.7 %collective-permute-done.2 = bf16[256,1024]{1,0:T(8,128)(2,1)S(1)} collective-permute-done((bf16[256,1024]{1,0:T(8,128)(2,1)}, bf16[256,1024]{1,0:T(8,128)(2,1)S(1)}, u32[]{:S(2)}, u32[]{:S(2)}) %collective-permute-start.2) | collective-permute-done | bytes 524320 | tf_op jit(solution)/shard_map/ppermute | solution.py:118
  59.4 2.3 broadcast_select_fusion
  61.6 1.8 collective-permute-start.7
  64.0 1.9 maximum_select_fusion
  66.0 4.4 %convolution_convert_fusion.5 = bf16[256,1024]{1,0:T(8,128)(2,1)} fusion(bf16[256,2048]{1,0:T(8,128)(2,1)S(1)} %maximum_select_fusion, bf16[2048,1024]{1,0:T(8,128)(2,1)} %all-gather.4.cloned.1.call-done), kind=kOutput, calls=%fused_computation.5 | convolution fusion | flops 1074003968 | bytes 5767168 | tf_op jit(solution)/shard_map/dot_general | solution.py:16
  72.1 2.0 maximum_select_fusion.1
  74.1 2.1 convolution_convert_fusion.4
  77.6 6.8 %collective-permute-done.7 = bf16[256,1024]{1,0:T(8,128)(2,1)} collective-permute-done((bf16[256,1024]{1,0:T(8,128)(2,1)}, bf16[256,1024]{1,0:T(8,128)(2,1)}, u32[]{:S(2)}, u32[]{:S(2)}) %collective-permute-start.7) | collective-permute-done | bytes 524320 | tf_op jit(solution)/shard_map/ppermute | solution.py:118
  85.5 3.6 %convolution_convert_fusion.2 = bf16[256,1024]{1,0:T(8,128)(2,1)S(1)} fusion(bf16[256,2048]{1,0:T(8,128)(2,1)S(1)} %maximum_select_fusion, bf16[2048,1024]{1,0:T(8,128)(2,1)} %all-gather.6.cloned.1.call-done), kind=kOutput, calls=%fused_computation.2 | convolution fusion | flops 1074003968 | bytes 5767168 | tf_op jit(solution)/shard_map/dot_general | solution.py:16
  96.2 2.3 collective-permute-done.9
  98.5 2.0 maximum_select_fusion.3
  100.5 6.2 %collective-permute-done.6 = bf16[256,1024]{1,0:T(8,128)(2,1)S(1)} collective-permute-done((bf16[256,1024]{1,0:T(8,128)(2,1)S(1)}, bf16[256,1024]{1,0:T(8,128)(2,1)S(1)}, u32[]{:S(2)}, u32[]{:S(2)}) %collective-permute-start.6) | collective-permute-done | bytes 524320 | tf_op jit(solution)/shard_map/ppermute | solution.py:118
  107.5 3.2 %add_convert_fusion.1 = bf16[256,1024]{1,0:T(8,128)(2,1)} fusion(bf16[256,1024]{1,0:T(8,128)(2,1)} %collective-permute-done.10, bf16[256,2048]{1,0:T(8,128)(2,1)S(1)} %maximum_select_fusion.3, bf16[2048,1024]{1,0:T(8,128)(2,1)S(1)} %copy-done.26), kind=kOutput, calls=%fused_computation.20 | convolution fusion | flops 1074528256 | bytes 6291456 | tf_op jit(solution)/shard_map/dot_general | solution.py:16
  110.7 2.0 collective-permute-start.11
  112.7 27.6 %collective-permute-done.12 = bf16[256,1024]{1,0:T(8,128)(2,1)S(1)} collective-permute-done((bf16[256,1024]{1,0:T(8,128)(2,1)S(1)}, bf16[256,1024]{1,0:T(8,128)(2,1)S(1)}, u32[]{:S(2)}, u32[]{:S(2)}) %collective-permute-start.12) | collective-permute-done | bytes 524320 | tf_op jit(solution)/shard_map/ppermute | solution.py:118
  140.4 2.1 add_convert_fusion
  144.7 4.1 %convolution_convert_fusion.1 = bf16[256,1024]{1,0:T(8,128)(2,1)S(1)} fusion(bf16[2048,1024]{1,0:T(8,128)(2,1)} %all-gather.8.cloned.1.call-done, bf16[128,2048]{1,0:T(8,128)(2,1)} %get-tuple-element.113, bf16[128,2048]{1,0:T(8,128)(2,1)} %get-tuple-element.111), kind=kOutput, calls=%fused_computation.1 | convolution fusion | flops 1076101120 | bytes 5767168 | tf_op jit(solution)/shard_map/dot_general | solution.py:16
  148.9 2.5 %collective-permute-start.16 = (bf16[256,1024]{1,0:T(8,128)(2,1)S(1)}, bf16[256,1024]{1,0:T(8,128)(2,1)S(1)}, u32[]{:S(2)}, u32[]{:S(2)}) collective-permute-start(bf16[256,1024]{1,0:T(8,128)(2,1)S(1)} %convolution_convert_fusion.1), channel_id=1, source_target_pairs={{0,8},{2,10},{4,12},{6,14},{8,0},{10,2},{12,4},{14,6},{16,24},{18,... | collective-permute-start | bytes 1572872 | tf_op jit(solution)/shard_map/ppermute | solution.py:118
  157.7 17.7 %collective-permute-done.16 = bf16[256,1024]{1,0:T(8,128)(2,1)S(1)} collective-permute-done((bf16[256,1024]{1,0:T(8,128)(2,1)S(1)}, bf16[256,1024]{1,0:T(8,128)(2,1)S(1)}, u32[]{:S(2)}, u32[]{:S(2)}) %collective-permute-start.16) | collective-permute-done | bytes 524320 | tf_op jit(solution)/shard_map/ppermute | solution.py:118
  176.3 5.4 %attention.4 = (bf16[256,2048]{1,0:T(8,128)(2,1)}, bf16[1,1024]{1,0:T(2,128)(2,1)S(1)}) custom-call(s32[3]{0:T(128)S(1)} %get-tuple-element.119.place_ref, f32[256,1024]{1,0:T(8,128)S(1)} %convert_add_fusion.1.qm_ref, bf16[256,1024]{1,0:T(8,128)(2,1)S(1)} %copy-done.7, bf16[1792,512]{1,0:T(8,128)(2,1)S(1)} %copy-done, bf16[1792,512]{1,0:T(8,128)(2,1)S(1)} %copy-done.1, ...), custom_call_target="tpu_custom_call" | custom-call | bytes 1048576 | tf_op jit(solution)/shard_map/attention/pallas_call | solution.py:72
  182.5 8.4 %collective-permute-done.14 = bf16[256,1024]{1,0:T(8,128)(2,1)S(1)} collective-permute-done((bf16[256,1024]{1,0:T(8,128)(2,1)S(1)}, bf16[256,1024]{1,0:T(8,128)(2,1)S(1)}, u32[]{:S(2)}, u32[]{:S(2)}) %collective-permute-start.14) | collective-permute-done | bytes 524320 | tf_op jit(solution)/shard_map/ppermute | solution.py:118
  192.3 5.4 %attention.5 = (bf16[256,2048]{1,0:T(8,128)(2,1)}, bf16[1,1024]{1,0:T(2,128)(2,1)S(1)}) custom-call(s32[3]{0:T(128)S(1)} %get-tuple-element.119.place_ref, f32[128,1024]{1,0:T(8,128)S(1)} %fusion.8.qm_ref, bf16[128,1024]{1,0:T(8,128)(2,1)S(1)} %collective-permute-done.18.qc_ref, bf16[1792,512]{1,0:T(8,128)(2,1)S(1)} %copy-done, ...), custom_call_target="tpu_custom_call", output_to_operand_aliasing={{0}: (9, {})} | custom-call | bytes 1048576 | tf_op jit(solution)/shard_map/attention/pallas_call | solution.py:72
  199.7 1.8 collective-permute-done.20
  206.2 3.9 %fusion.29.qm_ref = f32[128,1024]{1,0:T(8,128)} fusion(bf16[2048,1024]{1,0:T(8,128)(2,1)} %all-gather.8.cloned.1.call-done, bf16[256,2048]{1,0:T(8,128)(2,1)} %copy-done.13, bf16[256,1024]{1,0:T(8,128)(2,1)} %copy-done.24), kind=kOutput, calls=%fused_computation.34 | convolution fusion | flops 537133056 | bytes 5505024 | tf_op jit(solution)/shard_map/dot_general | solution.py:16
  210.0 5.5 %attention.6 = (bf16[256,2048]{1,0:T(8,128)(2,1)}, bf16[1,1024]{1,0:T(2,128)(2,1)}) custom-call(s32[3]{0:T(128)S(1)} %get-tuple-element.118.place_ref, f32[256,1024]{1,0:T(8,128)S(1)} %copy-done.5, bf16[256,1024]{1,0:T(8,128)(2,1)S(1)} %copy-done.8, bf16[1792,512]{1,0:T(8,128)(2,1)S(1)} %copy-done, ...), custom_call_target="tpu_custom_call", output_to_operand_aliasing={{0}: (9, {})} | custom-call | bytes 1048576 | tf_op jit(solution)/shard_map/attention/pallas_call | solution.py:72
  218.9 5.8 %attention.7 = (bf16[256,2048]{1,0:T(8,128)(2,1)}, bf16[1,1024]{1,0:T(2,128)(2,1)}) custom-call(s32[3]{0:T(128)S(1)} %get-tuple-element.118.place_ref, f32[128,1024]{1,0:T(8,128)S(1)} %copy-done.9, bf16[128,1024]{1,0:T(8,128)(2,1)} %collective-permute-done.17.qc_ref, bf16[1792,512]{1,0:T(8,128)(2,1)S(1)} %copy-done, ...), custom_call_target="tpu_custom_call", output_to_operand_aliasing={{0}: (9, {})} | custom-call | bytes 1048576 | tf_op jit(solution)/shard_map/attention/pallas_call | solution.py:72
  (142 shorter events, 43.2 us)
Async XLA Ops:
  7.2 56.9 %all-gather.4.cloned.1.call-start = ((), (), s32[]{:S(2)}) async-start(), calls=%async_computation | async-start | bytes 5242880 | tf_op jit(solution)/shard_map/all_gather | solution.py:146
  12.1 73.4 %all-gather.6.cloned.1.call-start = ((), (), s32[]{:S(2)}) async-start(), calls=%async_computation.1 | async-start | bytes 5242880 | tf_op jit(solution)/shard_map/all_gather | solution.py:146
  14.5 130.2 %all-gather.8.cloned.1.call-start = ((), (), s32[]{:S(2)}) async-start(), calls=%async_computation.2 | async-start | bytes 5242880 | tf_op jit(solution)/shard_map/all_gather | solution.py:146
  14.6 14.9 %collective-permute-start.1 = (bf16[256,1024]{1,0:T(8,128)(2,1)S(1)}, bf16[256,1024]{1,0:T(8,128)(2,1)S(1)}, u32[]{:S(2)}, u32[]{:S(2)}) collective-permute-start(bf16[256,1024]{1,0:T(8,128)(2,1)S(1)} %pad_maximum_fusion.3), channel_id=1, source_target_pairs={{0,1},{1,0},{2,3},{3,2},{4,5},{5,4},{6,7},{7,6},{8,9},{9,8},{10,11... | collective-permute-start | bytes 1572872 | tf_op jit(solution)/shard_map/ppermute | solution.py:124
  30.6 14.2 %collective-permute-start.3 = (bf16[256,1024]{1,0:T(8,128)(2,1)S(1)}, bf16[256,1024]{1,0:T(8,128)(2,1)S(1)}, u32[]{:S(2)}, u32[]{:S(2)}) collective-permute-start(bf16[256,1024]{1,0:T(8,128)(2,1)S(1)} %get-tuple-element.57), channel_id=1, source_target_pairs={{0,8},{2,10},{4,12},{6,14},{8,0},{10,2},{12,4},{14,6},{16,24},{18,... | collective-permute-start | bytes 1572872 | tf_op jit(solution)/shard_map/ppermute | solution.py:118
  32.4 24.7 %collective-permute-start.2 = (bf16[256,1024]{1,0:T(8,128)(2,1)}, bf16[256,1024]{1,0:T(8,128)(2,1)S(1)}, u32[]{:S(2)}, u32[]{:S(2)}) collective-permute-start(bf16[256,1024]{1,0:T(8,128)(2,1)} %get-tuple-element.56), channel_id=1, source_target_pairs={{0,24},{2,26},{4,28},{6,30},{8,16},{10,18},{12,20},{14,22},{16,8},... | collective-permute-start | bytes 1572872 | tf_op jit(solution)/shard_map/ppermute | solution.py:118
  34.9 23.7 %collective-permute-start = (bf16[256,1024]{1,0:T(8,128)(2,1)S(1)}, bf16[256,1024]{1,0:T(8,128)(2,1)S(1)}, u32[]{:S(2)}, u32[]{:S(2)}) collective-permute-start(bf16[256,1024]{1,0:T(8,128)(2,1)S(1)} %pad_maximum_fusion.2), channel_id=1, source_target_pairs={{0,1},{1,0},{2,3},{3,2},{4,5},{5,4},{6,7},{7,6},{8,9},{9,8},{10,11... | collective-permute-start | bytes 1572872 | tf_op jit(solution)/shard_map/ppermute | solution.py:124
  44.8 19.3 %collective-permute-start.5 = (bf16[256,1024]{1,0:T(8,128)(2,1)S(1)}, bf16[256,1024]{1,0:T(8,128)(2,1)}, u32[]{:S(2)}, u32[]{:S(2)}) collective-permute-start(bf16[256,1024]{1,0:T(8,128)(2,1)S(1)} %collective-permute-done.3), channel_id=1, source_target_pairs={{0,1},{1,0},{2,3},{3,2},{4,5},{5,4},{6,7},{7,6},{8,9},{9,8},{10,11... | collective-permute-start | bytes 1572872 | tf_op jit(solution)/shard_map/ppermute | solution.py:124
  57.1 15.0 %collective-permute-start.8 = (bf16[256,1024]{1,0:T(8,128)(2,1)S(1)}, bf16[256,1024]{1,0:T(8,128)(2,1)}, u32[]{:S(2)}, u32[]{:S(2)}) collective-permute-start(bf16[256,1024]{1,0:T(8,128)(2,1)S(1)} %collective-permute-done.2), channel_id=1, source_target_pairs={{0,1},{1,0},{2,3},{3,2},{4,5},{5,4},{6,7},{7,6},{8,9},{9,8},{10,11... | collective-permute-start | bytes 1572872 | tf_op jit(solution)/shard_map/ppermute | solution.py:124
  61.6 22.7 %collective-permute-start.7 = (bf16[256,1024]{1,0:T(8,128)(2,1)}, bf16[256,1024]{1,0:T(8,128)(2,1)}, u32[]{:S(2)}, u32[]{:S(2)}) collective-permute-start(bf16[256,1024]{1,0:T(8,128)(2,1)} %get-tuple-element.61), channel_id=1, source_target_pairs={{0,16},{2,18},{4,20},{6,22},{8,24},{10,26},{12,28},{14,30},{16,0},... | collective-permute-start | bytes 1572872 | tf_op jit(solution)/shard_map/ppermute | solution.py:118
  63.5 43.3 %collective-permute-start.4 = (bf16[256,1024]{1,0:T(8,128)(2,1)S(1)}, bf16[256,1024]{1,0:T(8,128)(2,1)}, u32[]{:S(2)}, u32[]{:S(2)}) collective-permute-start(bf16[256,1024]{1,0:T(8,128)(2,1)S(1)} %get-tuple-element.62), channel_id=1, source_target_pairs={{0,1},{1,0},{2,3},{3,2},{4,5},{5,4},{6,7},{7,6},{8,9},{9,8},{10,11... | collective-permute-start | bytes 1572872 | tf_op jit(solution)/shard_map/ppermute | solution.py:124
  76.2 19.4 %collective-permute-start.10 = (bf16[256,1024]{1,0:T(8,128)(2,1)}, bf16[256,1024]{1,0:T(8,128)(2,1)}, u32[]{:S(2)}, u32[]{:S(2)}) collective-permute-start(bf16[256,1024]{1,0:T(8,128)(2,1)} %convolution_convert_fusion.4), channel_id=1, source_target_pairs={{0,8},{2,10},{4,12},{6,14},{8,0},{10,2},{12,4},{14,6},{16,24},{18,... | collective-permute-start | bytes 1572872 | tf_op jit(solution)/shard_map/ppermute | solution.py:118
  84.4 14.1 %collective-permute-start.9 = (bf16[256,1024]{1,0:T(8,128)(2,1)}, bf16[256,1024]{1,0:T(8,128)(2,1)}, u32[]{:S(2)}, u32[]{:S(2)}) collective-permute-start(bf16[256,1024]{1,0:T(8,128)(2,1)} %collective-permute-done.7), channel_id=1, source_target_pairs={{0,1},{1,0},{2,3},{3,2},{4,5},{5,4},{6,7},{7,6},{8,9},{9,8},{10,11... | collective-permute-start | bytes 1572872 | tf_op jit(solution)/shard_map/ppermute | solution.py:124
  91.5 15.2 %collective-permute-start.6 = (bf16[256,1024]{1,0:T(8,128)(2,1)S(1)}, bf16[256,1024]{1,0:T(8,128)(2,1)S(1)}, u32[]{:S(2)}, u32[]{:S(2)}) collective-permute-start(bf16[256,1024]{1,0:T(8,128)(2,1)S(1)} %copy-done.34), channel_id=1, source_target_pairs={{0,8},{2,10},{4,12},{6,14},{8,0},{10,2},{12,4},{14,6},{16,24},{18,... | collective-permute-start | bytes 1572872 | tf_op jit(solution)/shard_map/ppermute | solution.py:118
  93.1 47.3 %collective-permute-start.13 = (bf16[256,1024]{1,0:T(8,128)(2,1)S(1)}, bf16[256,1024]{1,0:T(8,128)(2,1)S(1)}, u32[]{:S(2)}, u32[]{:S(2)}) collective-permute-start(bf16[256,1024]{1,0:T(8,128)(2,1)S(1)} %convolution_convert_fusion.2), channel_id=1, source_target_pairs={{0,8},{2,10},{4,12},{6,14},{8,0},{10,2},{12,4},{14,6},{16,24},{18,... | collective-permute-start | bytes 1572872 | tf_op jit(solution)/shard_map/ppermute | solution.py:118
  95.6 44.7 %collective-permute-start.12 = (bf16[256,1024]{1,0:T(8,128)(2,1)S(1)}, bf16[256,1024]{1,0:T(8,128)(2,1)S(1)}, u32[]{:S(2)}, u32[]{:S(2)}) collective-permute-start(bf16[256,1024]{1,0:T(8,128)(2,1)S(1)} %convolution_convert_fusion.3), channel_id=1, source_target_pairs={{0,8},{2,10},{4,12},{6,14},{8,0},{10,2},{12,4},{14,6},{16,24},{18,... | collective-permute-start | bytes 1572872 | tf_op jit(solution)/shard_map/ppermute | solution.py:118
  100.5 42.0 %copy-start.11 = (bf16[256,2048]{1,0:T(8,128)(2,1)}, bf16[256,2048]{1,0:T(8,128)(2,1)S(1)}, u32[]{:S(2)}) copy-start(bf16[256,2048]{1,0:T(8,128)(2,1)S(1)} %maximum_select_fusion.3) | copy-start | bytes 3145732
  110.7 32.4 %copy-start.17 = (bf16[256,1024]{1,0:T(8,128)(2,1)S(1)}, bf16[256,1024]{1,0:T(8,128)(2,1)}, u32[]{:S(2)}) copy-start(bf16[256,1024]{1,0:T(8,128)(2,1)} %copy-done.16) | copy-start | bytes 1572868
  110.7 43.6 %collective-permute-start.11 = (bf16[256,1024]{1,0:T(8,128)(2,1)}, bf16[256,1024]{1,0:T(8,128)(2,1)S(1)}, u32[]{:S(2)}, u32[]{:S(2)}) collective-permute-start(bf16[256,1024]{1,0:T(8,128)(2,1)} %add_convert_fusion.1), channel_id=1, source_target_pairs={{0,16},{2,18},{4,20},{6,22},{8,24},{10,26},{12,28},{14,30},{16,0},... | collective-permute-start | bytes 1572872 | tf_op jit(solution)/shard_map/ppermute | solution.py:118
  142.5 33.8 %collective-permute-start.15 = (bf16[256,1024]{1,0:T(8,128)(2,1)}, bf16[256,1024]{1,0:T(8,128)(2,1)S(1)}, u32[]{:S(2)}, u32[]{:S(2)}) collective-permute-start(bf16[256,1024]{1,0:T(8,128)(2,1)} %add_convert_fusion), channel_id=1, source_target_pairs={{0,16},{2,18},{4,20},{6,22},{8,24},{10,26},{12,28},{14,30},{16,0},... | collective-permute-start | bytes 1572872 | tf_op jit(solution)/shard_map/ppermute | solution.py:118
  148.9 26.5 %collective-permute-start.16 = (bf16[256,1024]{1,0:T(8,128)(2,1)S(1)}, bf16[256,1024]{1,0:T(8,128)(2,1)S(1)}, u32[]{:S(2)}, u32[]{:S(2)}) collective-permute-start(bf16[256,1024]{1,0:T(8,128)(2,1)S(1)} %convolution_convert_fusion.1), channel_id=1, source_target_pairs={{0,8},{2,10},{4,12},{6,14},{8,0},{10,2},{12,4},{14,6},{16,24},{18,... | collective-permute-start | bytes 1572872 | tf_op jit(solution)/shard_map/ppermute | solution.py:118
  154.3 22.0 %copy-start.4 = (f32[256,1024]{1,0:T(8,128)}, f32[256,1024]{1,0:T(8,128)S(1)}, u32[]{:S(2)}) copy-start(f32[256,1024]{1,0:T(8,128)S(1)} %convert_add_fusion.1.qm_ref) | copy-start | bytes 3145732
  154.3 21.1 %copy-start.12 = (bf16[256,2048]{1,0:T(8,128)(2,1)S(1)}, bf16[256,2048]{1,0:T(8,128)(2,1)}, u32[]{:S(2)}) copy-start(bf16[256,2048]{1,0:T(8,128)(2,1)} %copy-done.11) | copy-start | bytes 3145732
  156.6 34.2 %collective-permute-start.14 = (bf16[256,1024]{1,0:T(8,128)(2,1)S(1)}, bf16[256,1024]{1,0:T(8,128)(2,1)S(1)}, u32[]{:S(2)}, u32[]{:S(2)}) collective-permute-start(bf16[256,1024]{1,0:T(8,128)(2,1)S(1)} %convolution_convert_fusion), channel_id=1, source_target_pairs={{0,8},{2,10},{4,12},{6,14},{8,0},{10,2},{12,4},{14,6},{16,24},{18,... | collective-permute-start | bytes 1572872 | tf_op jit(solution)/shard_map/ppermute | solution.py:118
  176.1 16.2 %collective-permute-start.18 = (bf16[128,1024]{1,0:T(8,128)(2,1)S(1)}, bf16[128,1024]{1,0:T(8,128)(2,1)S(1)}, u32[]{:S(2)}, u32[]{:S(2)}) collective-permute-start(bf16[128,1024]{1,0:T(8,128)(2,1)S(1)} %fusion.24), channel_id=1, source_target_pairs={{0,16},{2,18},{4,20},{6,22},{8,24},{10,26},{12,28},{14,30},{16,0},... | collective-permute-start | bytes 786440 | tf_op jit(solution)/shard_map/ppermute | solution.py:118
  197.8 1.9 collective-permute-start.19
  197.9 3.7 %collective-permute-start.20 = (bf16[1,2048]{1,0:T(2,128)(2,1)S(1)}, bf16[1,2048]{1,0:T(2,128)(2,1)S(1)}, u32[]{:S(2)}, u32[]{:S(2)}) collective-permute-start(bf16[1,2048]{1,0:T(2,128)(2,1)S(1)} %constant_dynamic-update-slice_fusion), channel_id=1, source_target_pairs={{0,4},{2,6},{4,0},{6,2},{8,12},{10,14},{12,8},{14,10},{16,20},{18,... | collective-permute-start | bytes 12296 | tf_op jit(solution)/shard_map/ppermute | solution.py:118
  198.8 3.1 %collective-permute-start.21 = (bf16[1,2048]{1,0:T(2,128)(2,1)S(1)}, bf16[1,2048]{1,0:T(2,128)(2,1)S(1)}, u32[]{:S(2)}, u32[]{:S(2)}) collective-permute-start(bf16[1,2048]{1,0:T(2,128)(2,1)S(1)} %constant_dynamic-update-slice_fusion), channel_id=1, source_target_pairs={{0,6},{2,4},{4,2},{6,0},{8,14},{10,12},{12,10},{14,8},{16,22},{18,... | collective-permute-start | bytes 12296 | tf_op jit(solution)/shard_map/ppermute | solution.py:118
  199.7 16.6 %collective-permute-start.17 = (bf16[128,1024]{1,0:T(8,128)(2,1)}, bf16[128,1024]{1,0:T(8,128)(2,1)}, u32[]{:S(2)}, u32[]{:S(2)}) collective-permute-start(bf16[128,1024]{1,0:T(8,128)(2,1)} %fusion.16), channel_id=1, source_target_pairs={{0,16},{2,18},{4,20},{6,22},{8,24},{10,26},{12,28},{14,30},{16,0},... | collective-permute-start | bytes 786440 | tf_op jit(solution)/shard_map/ppermute | solution.py:118
  202.6 13.0 %collective-permute-start.23 = (bf16[4,1,2048]{2,0,1:T(4,128)(2,1)S(1)}, bf16[4,1,2048]{2,0,1:T(4,128)(2,1)S(1)}, u32[]{:S(2)}, u32[]{:S(2)}) collective-permute-start(bf16[4,1,2048]{2,0,1:T(4,128)(2,1)S(1)} %reshape.23), channel_id=1, source_target_pairs={{0,16},{2,18},{4,20},{6,22},{8,24},{10,26},{12,28},{14,30},{16,0},... | collective-permute-start | bytes 49160 | tf_op jit(solution)/shard_map/ppermute | solution.py:118
  203.4 12.2 %collective-permute-start.24 = (bf16[4,1,2048]{2,0,1:T(4,128)(2,1)S(1)}, bf16[4,1,2048]{2,0,1:T(4,128)(2,1)S(1)}, u32[]{:S(2)}, u32[]{:S(2)}) collective-permute-start(bf16[4,1,2048]{2,0,1:T(4,128)(2,1)S(1)} %reshape.23), channel_id=1, source_target_pairs={{0,24},{2,26},{4,28},{6,30},{8,16},{10,18},{12,20},{14,22},{16,8},... | collective-permute-start | bytes 49160 | tf_op jit(solution)/shard_map/ppermute | solution.py:118
  205.1 10.4 %collective-permute-start.22 = (bf16[4,1,2048]{2,0,1:T(4,128)(2,1)S(1)}, bf16[4,1,2048]{2,0,1:T(4,128)(2,1)S(1)}, u32[]{:S(2)}, u32[]{:S(2)}) collective-permute-start(bf16[4,1,2048]{2,0,1:T(4,128)(2,1)S(1)} %reshape.23), channel_id=1, source_target_pairs={{0,8},{2,10},{4,12},{6,14},{8,0},{10,2},{12,4},{14,6},{16,24},{18,... | collective-permute-start | bytes 49160 | tf_op jit(solution)/shard_map/ppermute | solution.py:118
  (31 other events, 231.9 us)
Sparse Core Ops, SparseCore 0:
  12.2 37.1 all-gather.3
  51.0 34.4 all-gather.5
  87.1 34.4 all-gather.7

commit v4 on v3

--- a/solution.py
+++ b/solution.py
@@ -110,7 +110,6 @@
     rows, local = tokens_in.shape
     half = rows // 2
     part = local // outer
-    groups = [list(range(o * INNER, (o + 1) * INNER)) for o in range(outer)]
 
     first = (prompt_len[0] - 1) // half
 
@@ -142,43 +141,47 @@
     chunk = heads * wide // pieces
     fast = outer == 4 and n_tp == 2
 
+    groups = [list(range(o * INNER, (o + 1) * INNER)) for o in range(outer)]
+
     def group_gather(value):
         return lax.all_gather(value, "inst", axis=0, tiled=True, axis_index_groups=groups)
 
     weights = {}
 
-    def gather_queries(piece):
-        weights[piece] = group_gather(step(w_query[:, piece * chunk : (piece + 1) * chunk]))
+    def gather_queries(piece, source):
+        weights[piece] = group_gather(source[:, piece * chunk : (piece + 1) * chunk])
 
     def gather_others():
-        weights["kv"] = group_gather(step(jnp.concatenate([w_key, w_value], axis=1)))
+        key, value, query = step(w_key, w_value, w_query)
+        weights["kv"] = group_gather(jnp.concatenate([key, value], axis=1))
         if pieces == 2:
-            gather_queries(1)
+            gather_queries(1, query)
 
     tokens = {}
     if fast:
 
-        def cut(j, p):
+        def cut(source, j, p):
             column = (((z % 2) ^ j) * n_tp + p) * part
             return jnp.concatenate(
                 [
-                    lax.dynamic_slice(tokens_in, (h * half, column), (half, part))
+                    lax.dynamic_slice(source, (h * half, column), (half, part))
                     for h in (first, 1 - first)
                 ],
                 axis=0,
             )
 
-        swap = {1: over_tp(step(cut(1, 1 - x)))}
-        gather_queries(0)
-        swap[0] = over_tp(step(cut(0, 1 - x)))
-        gather_others()
+        gather_queries(0, w_query)
+        swap = {1: over_tp(step(cut(tokens_in, 1, 1 - x)))}
+        source = step(tokens_in)
+        swap[0] = over_tp(step(cut(source, 0, 1 - x)))
         mine = z // 2 == x
         held, came = {}, {}
-        own = {j: cut(j, x) for j in (1, 0)}
         swap[1] = step(swap[1])
-        send = {b: jnp.where(mine == (b < 2), own[1], swap[1]) for b in (1, 3)}
+        own = cut(source, 1, x)
+        send = {b: jnp.where(mine == (b < 2), own, swap[1]) for b in (1, 3)}
         send[1], send[3] = step(send[1], send[3])
         got = {b: over_outer(send[b], b) for b in (1, 3)}
+        gather_others()
 
         def tp_exchange(b):
             held[b] = step(got[b])
@@ -187,17 +190,18 @@
         tp_exchange(1)
         tp_exchange(3)
         swap[0] = step(swap[0])
-        send = {b: jnp.where(mine == (b < 2), own[0], swap[0]) for b in (2, 0)}
+        own = cut(source, 0, x)
+        send = {b: jnp.where(mine == (b < 2), own, swap[0]) for b in (2, 0)}
         send[2] = step(send[2])
         got[2], got[0] = over_outer(send[2], 2), send[0]
         tp_exchange(0)
 
         def arrived(b):
             if b not in tokens:
-                tokens[b] = swapped_if(x == 1, held[b], step(came[b]), 1)
+                tokens[b] = (swapped_if(x == 1, held[b], step(came[b]), 1),)
 
     else:
-        gather_queries(0)
+        gather_queries(0, w_query)
         gather_others()
         swapped = jnp.where(first == 1, jnp.roll(tokens_in, half, axis=0), tokens_in)
         own = swapped.reshape(rows, outer // n_tp, n_tp, part)
@@ -210,25 +214,35 @@
         )
         both = lax.all_gather(come.reshape(-1, part), "tp", axis=1, tiled=True)
         both = both.reshape(outer, rows, -1)
-        tokens.update({b: both[b] for b in range(outer)})
+        tokens.update({b: (both[b],) for b in range(outer)})
 
         def arrived(b):
             pass
 
-    def rows_of(value, h):
-        return value if h is None else value[h * half : (h + 1) * half]
+    def rows_of(values, h):
+        if h is None:
+            return values
+        return tuple(value[h * half : (h + 1) * half] for value in values)
+
+    def times(values, weight):
+        total, row = None, 0
+        for value in values:
+            one = dot(value, weight[row : row + value.shape[1]])
+            total = one if total is None else total + one
+            row += value.shape[1]
+        return total
 
     def first_send(h, name):
-        weight = step(weights[name])
+        weight = weights[name] = step(weights[name])
         bits = range(1, outer, 2)
         if h is None:
             come = {}
             for b in bits:
                 arrived(b)
-                come[b] = over_outer(step(dot(tokens[b], weight).astype(jnp.bfloat16)), 1)
+                come[b] = over_outer(step(times(tokens[b], weight).astype(jnp.bfloat16)), 1)
             return come
-        joined = jnp.concatenate([rows_of(tokens[b], h) for b in bits], axis=0)
-        come = over_outer(step(dot(joined, weight).astype(jnp.bfloat16)), 1)
+        joined = [jnp.concatenate(same) for same in zip(*[rows_of(tokens[b], h) for b in bits])]
+        come = over_outer(step(times(joined, weight).astype(jnp.bfloat16)), 1)
         return {b: (come, i) for i, b in enumerate(bits)}
 
     def later_sends(h, name, come):
@@ -237,11 +251,12 @@
         if h is not None:
             whole = step(next(iter(come.values()))[0])
             come = {b: whole[i * half : (i + 1) * half] for b, (_, i) in come.items()}
-        for b in reversed(range(0, outer, 2)):
+        for b in range(0, outer, 2):
             if h is None:
                 come[b + 1] = step(come[b + 1])
             arrived(b)
-            sums[b] = dot(rows_of(tokens[b], h), weight) + come[b + 1].astype(jnp.float32)
+        for b in range(0, outer, 2):
+            sums[b] = times(rows_of(tokens[b], h), weight) + come[b + 1].astype(jnp.float32)
         bit = 2
         while True:
             for b in sorted(sums):
@@ -266,7 +281,8 @@
         parts_of[n] = later_sends(*jobs[n], opened[n])
 
     def arrive(n):
-        parts_of[n] = (parts_of[n][0], step(parts_of[n][1]))
+        came_in, mine = step(parts_of[n][1], parts_of[n][0])
+        parts_of[n] = (mine, came_in)
 
     def attention(n, h):
         own_half, piece = jobs[n]
@@ -295,8 +311,8 @@
     start(1)
     advance(0)
     if pieces == 2:
+        start(2)
         advance(1)
-        start(2)
         arrive(0)
         start(3)
         advance(2)
@@ -313,7 +329,7 @@
         arrive(1)
         attention(1, 0)
     arrive(len(jobs) - 1)
-    row = jnp.concatenate(lasts, axis=1)
+    row = step(jnp.concatenate(lasts, axis=1))
     in_group = [row] + [over_inst(row, m) for m in range(1, INNER)]
     if pieces == 2:
         attention(0, 1)

time: 232 us -> 227 us (0.978)
  waiting for transfers between devices: 106 us -> 93.3 us
  matrix products: 31.6 us -> 34.6 us
  starting transfers between devices: 30.7 us -> 33.5 us
    ppermute x19, waiting for transfers between devices: 89.1 us -> 79.5 us  [over_inst(): return lax.ppermute(value, 'inst', [(i, i ^ bits) for i in range(n_inst)])]
    dot_general x14, matrix products: 31.6 us -> 34.6 us  [dot(): return jnp.dot(a, b, preferred_element_type=jnp.float32)]
    ppermute x19, starting transfers between devices: 22 us -> 24.9 us  [over_inst(): return lax.ppermute(value, 'inst', [(i, i ^ bits) for i in range(n_inst)])]
    ppermute x6, waiting for transfers between devices: 15.8 us -> 13 us  [over_tp(): return lax.ppermute(value, 'tp', [(0, 1), (1, 0)])]
    unnamed x71 -> x58, local copies, waits for them, and re-layouts: 5.3 us -> 4.57 us
    slice x3 -> x4, local copies, waits for them, and re-layouts: 5.15 us -> 5.62 us  [the longest x2 3.49 us: gather_queries(): weights[piece] = group_gather(source[:, piece * chunk:(piece + 1) * chunk])]
  transfers between devices with their start and end apart: 28 -> 28, of which waited for: 14 -> 13; matrix products, arithmetic and copies ran while one was open for 21% -> 24% of each run, Pallas kernels for 5% -> 10%
where the time goes in v4:
time: 227 us; the launch traced here: 226 us
  waiting for transfers between devices  93.3 us (41%)
  matrix products  34.6 us (15%)
  starting transfers between devices  33.5 us (15%)
  Pallas kernels  21.8 us (10%)
  other arithmetic  15.2 us (7%)
  between operations  14.9 us (7%)
  local copies, waits for them, and re-layouts  12.6 us (6%)
    ppermute x19, waiting for transfers between devices, over_inst(): return lax.ppermute(value, 'inst', [(i, i ^ bits) for i in range(n_inst)])  79.5 us
    dot_general x14, matrix products, dot(): return jnp.dot(a, b, preferred_element_type=jnp.float32)  34.6 us
    ppermute x19, starting transfers between devices, over_inst(): return lax.ppermute(value, 'inst', [(i, i ^ bits) for i in range(n_inst)])  24.9 us
    pallas_call x4, Pallas kernels, attend(): pl.pallas_call(attention_kernel, grid_spec=pltpu.PrefetchScalarGridSpec(n...  21.8 us
    ppermute x6, waiting for transfers between devices, over_tp(): return lax.ppermute(value, 'tp', [(0, 1), (1, 0)])  13 us
    ppermute x6, starting transfers between devices, over_tp(): return lax.ppermute(value, 'tp', [(0, 1), (1, 0)])  8.48 us
    select_n x4, other arithmetic, swapped_if(): jnp.where(flag, jnp.concatenate([b, a], axis=axis), jnp.concatenate([a, b...  7.52 us
    unnamed x58, local copies, waits for them, and re-layouts  4.57 us
  transfers between devices with their start and end apart: 28, of which 13 were waited for; matrix products, arithmetic and copies ran while one was open for 24% of the time, Pallas kernels for 10%

profile of v4, /device:TPU:0, one launch (start us, length us, event | category | flops | bytes accessed | tf_op | source)
XLA Modules:
  0.0 226.0 jit_solution(10524253959138628413)
XLA Ops:
  7.2 2.4 %slice.42 = bf16[512,1024]{1,0:T(8,128)(2,1)} slice(bf16[512,2048]{1,0:T(8,128)(2,1)} %param.8), slice={[0:512], [0:1024]} | slice | bytes 2097152 | tf_op jit(solution)/shard_map/slice | solution.py:152
  12.4 2.9 %collective-permute-start.1 = (bf16[256,1024]{1,0:T(8,128)(2,1)}, bf16[256,1024]{1,0:T(8,128)(2,1)}, u32[]{:S(2)}, u32[]{:S(2)}) collective-permute-start(bf16[256,1024]{1,0:T(8,128)(2,1)} %pad_maximum_fusion.1), channel_id=1, source_target_pairs={{0,1},{1,0},{2,3},{3,2},{4,5},{5,4},{6,7},{7,6},{8,9},{9,8},{10,11... | collective-permute-start | bytes 1572872 | tf_op jit(solution)/shard_map/ppermute | solution.py:123
  16.3 11.2 %collective-permute-done.1 = bf16[256,1024]{1,0:T(8,128)(2,1)} collective-permute-done((bf16[256,1024]{1,0:T(8,128)(2,1)}, bf16[256,1024]{1,0:T(8,128)(2,1)}, u32[]{:S(2)}, u32[]{:S(2)}) %collective-permute-start.1) | collective-permute-done | bytes 524320 | tf_op jit(solution)/shard_map/ppermute | solution.py:123
  27.5 2.3 %broadcast_select_fusion.3 = (bf16[256,1024]{1,0:T(8,128)(2,1)}, bf16[256,1024]{1,0:T(8,128)(2,1)}) fusion(bf16[256,1024]{1,0:T(8,128)(2,1)} %collective-permute-done.1, pred[]{:T(512)S(6)} %eq.37, bf16[128,1024]{1,0:T(8,128)(2,1)S(1)} %get-tuple-element.113, bf16[128,1024]{1,0:T(8,128)(2,1)S(1)} %get-tuple-element.114, pred[]{:T(512)S(6)} %eq.36), kind=kLoop, calls=%fused_computation.42 | loop fusion | flops 1572864 | bytes 2097154 | tf_op jit(solution)/shard_map/jit(_where)/select_n | solution.py:181
  29.8 2.4 %pad_maximum_fusion = bf16[512,1024]{1,0:T(8,128)(2,1)} fusion(bf16[512,512]{1,0:T(8,128)(2,1)} %param.10, bf16[512,512]{1,0:T(8,128)(2,1)} %param.9), kind=kLoop, calls=%fused_computation.8 | loop fusion | flops 2097152 | bytes 2097152 | tf_op jit(solution)/shard_map/concatenate | solution.py:156
  35.3 2.5 %collective-permute-start.2 = (bf16[256,1024]{1,0:T(8,128)(2,1)}, bf16[256,1024]{1,0:T(8,128)(2,1)S(1)}, u32[]{:S(2)}, u32[]{:S(2)}) collective-permute-start(bf16[256,1024]{1,0:T(8,128)(2,1)} %get-tuple-element.60), channel_id=1, source_target_pairs={{0,24},{2,26},{4,28},{6,30},{8,16},{10,18},{12,20},{14,22},{16,8},... | collective-permute-start | bytes 1572872 | tf_op jit(solution)/shard_map/ppermute | solution.py:117
  39.2 8.7 %collective-permute-done.3 = bf16[256,1024]{1,0:T(8,128)(2,1)S(1)} collective-permute-done((bf16[256,1024]{1,0:T(8,128)(2,1)}, bf16[256,1024]{1,0:T(8,128)(2,1)S(1)}, u32[]{:S(2)}, u32[]{:S(2)}) %collective-permute-start.3) | collective-permute-done | bytes 524320 | tf_op jit(solution)/shard_map/ppermute | solution.py:117
  49.5 10.5 %collective-permute-done.2 = bf16[256,1024]{1,0:T(8,128)(2,1)S(1)} collective-permute-done((bf16[256,1024]{1,0:T(8,128)(2,1)}, bf16[256,1024]{1,0:T(8,128)(2,1)S(1)}, u32[]{:S(2)}, u32[]{:S(2)}) %collective-permute-start.2) | collective-permute-done | bytes 524320 | tf_op jit(solution)/shard_map/ppermute | solution.py:117
  64.9 2.0 maximum_select_fusion
  66.9 4.5 %convolution_convert_fusion.5 = bf16[256,1024]{1,0:T(8,128)(2,1)} fusion(bf16[256,2048]{1,0:T(8,128)(2,1)S(1)} %maximum_select_fusion, bf16[2048,1024]{1,0:T(8,128)(2,1)} %all-gather.4.cloned.1.call-done), kind=kOutput, calls=%fused_computation.5 | convolution fusion | flops 1074003968 | bytes 5767168 | tf_op jit(solution)/shard_map/dot_general | solution.py:16
  75.0 1.9 maximum_select_fusion.1
  76.9 2.1 convolution_convert_fusion.4
  80.6 4.7 %collective-permute-done.4 = bf16[256,1024]{1,0:T(8,128)(2,1)S(1)} collective-permute-done((bf16[256,1024]{1,0:T(8,128)(2,1)}, bf16[256,1024]{1,0:T(8,128)(2,1)S(1)}, u32[]{:S(2)}, u32[]{:S(2)}) %collective-permute-start.4) | collective-permute-done | bytes 524320 | tf_op jit(solution)/shard_map/ppermute | solution.py:117
  87.9 4.4 %convolution_convert_fusion.2 = bf16[256,1024]{1,0:T(8,128)(2,1)} fusion(bf16[256,2048]{1,0:T(8,128)(2,1)S(1)} %maximum_select_fusion, bf16[2048,1024]{1,0:T(8,128)(2,1)} %all-gather.6.cloned.1.call-done), kind=kOutput, calls=%fused_computation.2 | convolution fusion | flops 1074003968 | bytes 5767168 | tf_op jit(solution)/shard_map/dot_general | solution.py:16
  92.4 2.1 convolution_convert_fusion.3
  96.5 10.9 %collective-permute-done.8 = bf16[256,1024]{1,0:T(8,128)(2,1)} collective-permute-done((bf16[256,1024]{1,0:T(8,128)(2,1)}, bf16[256,1024]{1,0:T(8,128)(2,1)}, u32[]{:S(2)}, u32[]{:S(2)}) %collective-permute-start.8) | collective-permute-done | bytes 524320 | tf_op jit(solution)/shard_map/ppermute | solution.py:117
  109.0 2.0 maximum_select_fusion.2
  111.0 3.5 %add_convert_fusion.1 = bf16[256,1024]{1,0:T(8,128)(2,1)} fusion(bf16[256,1024]{1,0:T(8,128)(2,1)} %collective-permute-done.8, bf16[256,2048]{1,0:T(8,128)(2,1)S(1)} %maximum_select_fusion.2, bf16[2048,1024]{1,0:T(8,128)(2,1)S(1)} %copy-done.26), kind=kOutput, calls=%fused_computation.20 | convolution fusion | flops 1074528256 | bytes 6291456 | tf_op jit(solution)/shard_map/dot_general | solution.py:16
  114.6 3.4 %convert_add_fusion.1.qm_ref = f32[256,1024]{1,0:T(8,128)} fusion(bf16[256,1024]{1,0:T(8,128)(2,1)} %collective-permute-done.10, bf16[256,2048]{1,0:T(8,128)(2,1)S(1)} %maximum_select_fusion.3, bf16[2048,1024]{1,0:T(8,128)(2,1)S(1)} %copy-done.26), kind=kOutput, calls=%fused_computation.19 | convolution fusion | flops 1074266112 | bytes 6815744 | tf_op jit(solution)/shard_map/dot_general | solution.py:16
  119.8 3.8 %convolution_convert_fusion.1 = bf16[256,1024]{1,0:T(8,128)(2,1)S(1)} fusion(bf16[2048,1024]{1,0:T(8,128)(2,1)} %all-gather.8.cloned.1.call-done, bf16[128,2048]{1,0:T(8,128)(2,1)} %get-tuple-element.123, bf16[128,2048]{1,0:T(8,128)(2,1)S(1)} %copy-done.24), kind=kOutput, calls=%fused_computation.1 | convolution fusion | flops 1076101120 | bytes 5767168 | tf_op jit(solution)/shard_map/dot_general | solution.py:16
  125.3 20.8 %collective-permute-done.12 = bf16[256,1024]{1,0:T(8,128)(2,1)} collective-permute-done((bf16[256,1024]{1,0:T(8,128)(2,1)}, bf16[256,1024]{1,0:T(8,128)(2,1)}, u32[]{:S(2)}, u32[]{:S(2)}) %collective-permute-start.12) | collective-permute-done | bytes 524320 | tf_op jit(solution)/shard_map/ppermute | solution.py:117
  146.1 2.3 %add_convert_fusion = bf16[256,1024]{1,0:T(8,128)(2,1)S(1)} fusion(bf16[256,1024]{1,0:T(8,128)(2,1)} %collective-permute-done.12, bf16[256,2048]{1,0:T(8,128)(2,1)S(1)} %maximum_select_fusion.2, bf16[2048,1024]{1,0:T(8,128)(2,1)S(1)} %copy-done.28), kind=kOutput, calls=%fused_computation.18 | convolution fusion | flops 1074528256 | bytes 6291456 | tf_op jit(solution)/shard_map/dot_general | solution.py:16
  151.1 2.5 %collective-permute-start.14 = (bf16[256,1024]{1,0:T(8,128)(2,1)S(1)}, bf16[256,1024]{1,0:T(8,128)(2,1)S(1)}, u32[]{:S(2)}, u32[]{:S(2)}) collective-permute-start(bf16[256,1024]{1,0:T(8,128)(2,1)S(1)} %convolution_convert_fusion), channel_id=1, source_target_pairs={{0,8},{2,10},{4,12},{6,14},{8,0},{10,2},{12,4},{14,6},{16,24},{18,... | collective-permute-start | bytes 1572872 | tf_op jit(solution)/shard_map/ppermute | solution.py:117
  153.6 4.6 %collective-permute-done.16 = bf16[256,1024]{1,0:T(8,128)(2,1)S(1)} collective-permute-done((bf16[256,1024]{1,0:T(8,128)(2,1)S(1)}, bf16[256,1024]{1,0:T(8,128)(2,1)S(1)}, u32[]{:S(2)}, u32[]{:S(2)}) %collective-permute-start.16) | collective-permute-done | bytes 524320 | tf_op jit(solution)/shard_map/ppermute | solution.py:117
  160.4 2.3 %convert_add_fusion.km_ref.vm_ref = f32[256,1024]{1,0:T(8,128)S(1)} fusion(bf16[256,1024]{1,0:T(8,128)(2,1)} %collective-permute-done.13, bf16[256,2048]{1,0:T(8,128)(2,1)S(1)} %maximum_select_fusion.3, bf16[2048,1024]{1,0:T(8,128)(2,1)S(1)} %copy-done.28), kind=kOutput, calls=%fused_computation.17 | convolution fusion | flops 1074266112 | bytes 6815744 | tf_op jit(solution)/shard_map/dot_general | solution.py:16
  162.8 15.1 %collective-permute-done.15.kt_ref.vt_ref = bf16[256,1024]{1,0:T(8,128)(2,1)S(1)} collective-permute-done((bf16[256,1024]{1,0:T(8,128)(2,1)S(1)}, bf16[256,1024]{1,0:T(8,128)(2,1)S(1)}, u32[]{:S(2)}, u32[]{:S(2)}) %collective-permute-start.15) | collective-permute-done | bytes 524320 | tf_op jit(solution)/shard_map/ppermute | solution.py:117
  178.7 2.6 %fusion.13.qm_ref = f32[128,1024]{1,0:T(8,128)} fusion(bf16[2048,1024]{1,0:T(8,128)(2,1)S(1)} %copy-done.11, bf16[256,2048]{1,0:T(8,128)(2,1)} %copy-done.14, bf16[256,1024]{1,0:T(8,128)(2,1)S(1)} %collective-permute-done.14), kind=kOutput, calls=%fused_computation.26 | convolution fusion | flops 537133056 | bytes 5505024 | tf_op jit(solution)/shard_map/dot_general | solution.py:16
  181.3 5.4 %attention.4 = (bf16[256,2048]{1,0:T(8,128)(2,1)}, bf16[1,1024]{1,0:T(2,128)(2,1)S(1)}) custom-call(s32[3]{0:T(128)S(1)} %get-tuple-element.129.place_ref, f32[256,1024]{1,0:T(8,128)S(1)} %copy-done.3, bf16[256,1024]{1,0:T(8,128)(2,1)S(1)} %copy-done.6, bf16[1792,512]{1,0:T(8,128)(2,1)S(1)} %copy-done, bf16[1792,512]{1,0:T(8,128)(2,1)S(1)} %copy-done.1, ...), custom_call_target="tpu_custom_call" | custom-call | bytes 1048576 | tf_op jit(solution)/shard_map/attention/pallas_call | solution.py:72
  186.7 5.4 %attention.5 = (bf16[256,2048]{1,0:T(8,128)(2,1)}, bf16[1,1024]{1,0:T(2,128)(2,1)S(1)}) custom-call(s32[3]{0:T(128)S(1)} %get-tuple-element.129.place_ref, f32[128,1024]{1,0:T(8,128)S(1)} %fusion.8.qm_ref, bf16[128,1024]{1,0:T(8,128)(2,1)S(1)} %collective-permute-done.18.qc_ref, bf16[1792,512]{1,0:T(8,128)(2,1)S(1)} %copy-done, ...), custom_call_target="tpu_custom_call", output_to_operand_aliasing={{0}: (9, {})} | custom-call | bytes 1048576 | tf_op jit(solution)/shard_map/attention/pallas_call | solution.py:72
  198.3 4.1 %collective-permute-start.22 = (bf16[4,1,2048]{2,0,1:T(4,128)(2,1)S(1)}, bf16[4,1,2048]{2,0,1:T(4,128)(2,1)S(1)}, u32[]{:S(2)}, u32[]{:S(2)}) collective-permute-start(bf16[4,1,2048]{2,0,1:T(4,128)(2,1)S(1)} %reshape.23), channel_id=1, source_target_pairs={{0,8},{2,10},{4,12},{6,14},{8,0},{10,2},{12,4},{14,6},{16,24},{18,... | collective-permute-start | bytes 49160 | tf_op jit(solution)/shard_map/ppermute | solution.py:117
  207.7 5.5 %attention.6 = (bf16[256,2048]{1,0:T(8,128)(2,1)}, bf16[1,1024]{1,0:T(2,128)(2,1)}) custom-call(s32[3]{0:T(128)S(1)} %get-tuple-element.128.place_ref, f32[256,1024]{1,0:T(8,128)S(1)} %copy-done.4, bf16[256,1024]{1,0:T(8,128)(2,1)S(1)} %copy-done.7, bf16[1792,512]{1,0:T(8,128)(2,1)S(1)} %copy-done, ...), custom_call_target="tpu_custom_call", output_to_operand_aliasing={{0}: (9, {})} | custom-call | bytes 1048576 | tf_op jit(solution)/shard_map/attention/pallas_call | solution.py:72
  213.2 5.5 %attention.7 = (bf16[256,2048]{1,0:T(8,128)(2,1)}, bf16[1,1024]{1,0:T(2,128)(2,1)}) custom-call(s32[3]{0:T(128)S(1)} %get-tuple-element.128.place_ref, f32[128,1024]{1,0:T(8,128)S(1)} %copy-done.8, bf16[128,1024]{1,0:T(8,128)(2,1)S(1)} %copy-done.10, bf16[1792,512]{1,0:T(8,128)(2,1)S(1)} %copy-done, ...), custom_call_target="tpu_custom_call", output_to_operand_aliasing={{0}: (9, {})} | custom-call | bytes 1048576 | tf_op jit(solution)/shard_map/attention/pallas_call | solution.py:72
  (131 shorter events, 46.8 us)
Async XLA Ops:
  7.2 57.7 %all-gather.4.cloned.1.call-start = ((), (), s32[]{:S(2)}) async-start(), calls=%async_computation | async-start | bytes 5242880 | tf_op jit(solution)/shard_map/all_gather | solution.py:147
  9.7 78.3 %all-gather.6.cloned.1.call-start = ((), (), s32[]{:S(2)}) async-start(), calls=%async_computation.1 | async-start | bytes 5242880 | tf_op jit(solution)/shard_map/all_gather | solution.py:147
  12.4 15.2 %collective-permute-start.1 = (bf16[256,1024]{1,0:T(8,128)(2,1)}, bf16[256,1024]{1,0:T(8,128)(2,1)}, u32[]{:S(2)}, u32[]{:S(2)}) collective-permute-start(bf16[256,1024]{1,0:T(8,128)(2,1)} %pad_maximum_fusion.1), channel_id=1, source_target_pairs={{0,1},{1,0},{2,3},{3,2},{4,5},{5,4},{6,7},{7,6},{8,9},{9,8},{10,11... | collective-permute-start | bytes 1572872 | tf_op jit(solution)/shard_map/ppermute | solution.py:123
  32.2 87.5 %all-gather.8.cloned.1.call-start = ((), (), s32[]{:S(2)}) async-start(), calls=%async_computation.2 | async-start | bytes 5242880 | tf_op jit(solution)/shard_map/all_gather | solution.py:147
  33.4 14.6 %collective-permute-start.3 = (bf16[256,1024]{1,0:T(8,128)(2,1)}, bf16[256,1024]{1,0:T(8,128)(2,1)S(1)}, u32[]{:S(2)}, u32[]{:S(2)}) collective-permute-start(bf16[256,1024]{1,0:T(8,128)(2,1)} %get-tuple-element.61), channel_id=1, source_target_pairs={{0,8},{2,10},{4,12},{6,14},{8,0},{10,2},{12,4},{14,6},{16,24},{18,... | collective-permute-start | bytes 1572872 | tf_op jit(solution)/shard_map/ppermute | solution.py:117
  35.3 24.8 %collective-permute-start.2 = (bf16[256,1024]{1,0:T(8,128)(2,1)}, bf16[256,1024]{1,0:T(8,128)(2,1)S(1)}, u32[]{:S(2)}, u32[]{:S(2)}) collective-permute-start(bf16[256,1024]{1,0:T(8,128)(2,1)} %get-tuple-element.60), channel_id=1, source_target_pairs={{0,24},{2,26},{4,28},{6,30},{8,16},{10,18},{12,20},{14,22},{16,8},... | collective-permute-start | bytes 1572872 | tf_op jit(solution)/shard_map/ppermute | solution.py:117
  37.7 23.8 %collective-permute-start = (bf16[256,1024]{1,0:T(8,128)(2,1)S(1)}, bf16[256,1024]{1,0:T(8,128)(2,1)S(1)}, u32[]{:S(2)}, u32[]{:S(2)}) collective-permute-start(bf16[256,1024]{1,0:T(8,128)(2,1)S(1)} %copy-done.21), channel_id=1, source_target_pairs={{0,1},{1,0},{2,3},{3,2},{4,5},{5,4},{6,7},{7,6},{8,9},{9,8},{10,11... | collective-permute-start | bytes 1572872 | tf_op jit(solution)/shard_map/ppermute | solution.py:123
  48.0 16.9 %collective-permute-start.6 = (bf16[256,1024]{1,0:T(8,128)(2,1)S(1)}, bf16[256,1024]{1,0:T(8,128)(2,1)}, u32[]{:S(2)}, u32[]{:S(2)}) collective-permute-start(bf16[256,1024]{1,0:T(8,128)(2,1)S(1)} %collective-permute-done.3), channel_id=1, source_target_pairs={{0,1},{1,0},{2,3},{3,2},{4,5},{5,4},{6,7},{7,6},{8,9},{9,8},{10,11... | collective-permute-start | bytes 1572872 | tf_op jit(solution)/shard_map/ppermute | solution.py:123
  60.0 15.0 %collective-permute-start.5 = (bf16[256,1024]{1,0:T(8,128)(2,1)S(1)}, bf16[256,1024]{1,0:T(8,128)(2,1)}, u32[]{:S(2)}, u32[]{:S(2)}) collective-permute-start(bf16[256,1024]{1,0:T(8,128)(2,1)S(1)} %collective-permute-done.2), channel_id=1, source_target_pairs={{0,1},{1,0},{2,3},{3,2},{4,5},{5,4},{6,7},{7,6},{8,9},{9,8},{10,11... | collective-permute-start | bytes 1572872 | tf_op jit(solution)/shard_map/ppermute | solution.py:123
  62.6 22.7 %collective-permute-start.4 = (bf16[256,1024]{1,0:T(8,128)(2,1)}, bf16[256,1024]{1,0:T(8,128)(2,1)S(1)}, u32[]{:S(2)}, u32[]{:S(2)}) collective-permute-start(bf16[256,1024]{1,0:T(8,128)(2,1)} %get-tuple-element.66), channel_id=1, source_target_pairs={{0,16},{2,18},{4,20},{6,22},{8,24},{10,26},{12,28},{14,30},{16,0},... | collective-permute-start | bytes 1572872 | tf_op jit(solution)/shard_map/ppermute | solution.py:117
  64.3 32.2 %collective-permute-start.9 = (bf16[256,1024]{1,0:T(8,128)(2,1)S(1)}, bf16[256,1024]{1,0:T(8,128)(2,1)}, u32[]{:S(2)}, u32[]{:S(2)}) collective-permute-start(bf16[256,1024]{1,0:T(8,128)(2,1)S(1)} %get-tuple-element.67), channel_id=1, source_target_pairs={{0,1},{1,0},{2,3},{3,2},{4,5},{5,4},{6,7},{7,6},{8,9},{9,8},{10,11... | collective-permute-start | bytes 1572872 | tf_op jit(solution)/shard_map/ppermute | solution.py:123
  71.4 24.8 %collective-permute-start.10 = (bf16[256,1024]{1,0:T(8,128)(2,1)}, bf16[256,1024]{1,0:T(8,128)(2,1)}, u32[]{:S(2)}, u32[]{:S(2)}) collective-permute-start(bf16[256,1024]{1,0:T(8,128)(2,1)} %convolution_convert_fusion.5), channel_id=1, source_target_pairs={{0,8},{2,10},{4,12},{6,14},{8,0},{10,2},{12,4},{14,6},{16,24},{18,... | collective-permute-start | bytes 1572872 | tf_op jit(solution)/shard_map/ppermute | solution.py:117
  79.0 28.3 %collective-permute-start.8 = (bf16[256,1024]{1,0:T(8,128)(2,1)}, bf16[256,1024]{1,0:T(8,128)(2,1)}, u32[]{:S(2)}, u32[]{:S(2)}) collective-permute-start(bf16[256,1024]{1,0:T(8,128)(2,1)} %convolution_convert_fusion.4), channel_id=1, source_target_pairs={{0,8},{2,10},{4,12},{6,14},{8,0},{10,2},{12,4},{14,6},{16,24},{18,... | collective-permute-start | bytes 1572872 | tf_op jit(solution)/shard_map/ppermute | solution.py:117
  85.3 22.1 %collective-permute-start.7 = (bf16[256,1024]{1,0:T(8,128)(2,1)S(1)}, bf16[256,1024]{1,0:T(8,128)(2,1)}, u32[]{:S(2)}, u32[]{:S(2)}) collective-permute-start(bf16[256,1024]{1,0:T(8,128)(2,1)S(1)} %collective-permute-done.4), channel_id=1, source_target_pairs={{0,1},{1,0},{2,3},{3,2},{4,5},{5,4},{6,7},{7,6},{8,9},{9,8},{10,11... | collective-permute-start | bytes 1572872 | tf_op jit(solution)/shard_map/ppermute | solution.py:123
  92.3 33.0 %collective-permute-start.13 = (bf16[256,1024]{1,0:T(8,128)(2,1)}, bf16[256,1024]{1,0:T(8,128)(2,1)}, u32[]{:S(2)}, u32[]{:S(2)}) collective-permute-start(bf16[256,1024]{1,0:T(8,128)(2,1)} %convolution_convert_fusion.2), channel_id=1, source_target_pairs={{0,8},{2,10},{4,12},{6,14},{8,0},{10,2},{12,4},{14,6},{16,24},{18,... | collective-permute-start | bytes 1572872 | tf_op jit(solution)/shard_map/ppermute | solution.py:117
  96.1 50.0 %collective-permute-start.12 = (bf16[256,1024]{1,0:T(8,128)(2,1)}, bf16[256,1024]{1,0:T(8,128)(2,1)}, u32[]{:S(2)}, u32[]{:S(2)}) collective-permute-start(bf16[256,1024]{1,0:T(8,128)(2,1)} %convolution_convert_fusion.3), channel_id=1, source_target_pairs={{0,8},{2,10},{4,12},{6,14},{8,0},{10,2},{12,4},{14,6},{16,24},{18,... | collective-permute-start | bytes 1572872 | tf_op jit(solution)/shard_map/ppermute | solution.py:117
  109.0 51.4 %copy-start.14 = (bf16[256,2048]{1,0:T(8,128)(2,1)}, bf16[256,2048]{1,0:T(8,128)(2,1)S(1)}, u32[]{:S(2)}) copy-start(bf16[256,2048]{1,0:T(8,128)(2,1)S(1)} %maximum_select_fusion.3) | copy-start | bytes 3145732
  111.0 48.1 %copy-start.12 = (bf16[256,2048]{1,0:T(8,128)(2,1)}, bf16[256,2048]{1,0:T(8,128)(2,1)S(1)}, u32[]{:S(2)}) copy-start(bf16[256,2048]{1,0:T(8,128)(2,1)S(1)} %maximum_select_fusion.2) | copy-start | bytes 3145732
  117.9 31.9 %collective-permute-start.11 = (bf16[256,1024]{1,0:T(8,128)(2,1)}, bf16[256,1024]{1,0:T(8,128)(2,1)S(1)}, u32[]{:S(2)}, u32[]{:S(2)}) collective-permute-start(bf16[256,1024]{1,0:T(8,128)(2,1)} %add_convert_fusion.1), channel_id=1, source_target_pairs={{0,16},{2,18},{4,20},{6,22},{8,24},{10,26},{12,28},{14,30},{16,0},... | collective-permute-start | bytes 1572872 | tf_op jit(solution)/shard_map/ppermute | solution.py:117
  119.7 26.4 %copy-start.28 = (bf16[2048,1024]{1,0:T(8,128)(2,1)S(1)}, bf16[2048,1024]{1,0:T(8,128)(2,1)}, u32[]{:S(2)}) copy-start(bf16[2048,1024]{1,0:T(8,128)(2,1)} %all-gather.6.cloned.1.call-done) | copy-start | bytes 12582916
  123.5 26.3 %copy-start.11 = (bf16[2048,1024]{1,0:T(8,128)(2,1)S(1)}, bf16[2048,1024]{1,0:T(8,128)(2,1)}, u32[]{:S(2)}) copy-start(bf16[2048,1024]{1,0:T(8,128)(2,1)} %all-gather.8.cloned.1.call-done) | copy-start | bytes 12582916
  123.6 34.6 %collective-permute-start.16 = (bf16[256,1024]{1,0:T(8,128)(2,1)S(1)}, bf16[256,1024]{1,0:T(8,128)(2,1)S(1)}, u32[]{:S(2)}, u32[]{:S(2)}) collective-permute-start(bf16[256,1024]{1,0:T(8,128)(2,1)S(1)} %convolution_convert_fusion.1), channel_id=1, source_target_pairs={{0,8},{2,10},{4,12},{6,14},{8,0},{10,2},{12,4},{14,6},{16,24},{18,... | collective-permute-start | bytes 1572872 | tf_op jit(solution)/shard_map/ppermute | solution.py:117
  148.4 29.4 %collective-permute-start.15 = (bf16[256,1024]{1,0:T(8,128)(2,1)S(1)}, bf16[256,1024]{1,0:T(8,128)(2,1)S(1)}, u32[]{:S(2)}, u32[]{:S(2)}) collective-permute-start(bf16[256,1024]{1,0:T(8,128)(2,1)S(1)} %add_convert_fusion), channel_id=1, source_target_pairs={{0,16},{2,18},{4,20},{6,22},{8,24},{10,26},{12,28},{14,30},{16,0},... | collective-permute-start | bytes 1572872 | tf_op jit(solution)/shard_map/ppermute | solution.py:117
  151.1 26.8 %collective-permute-start.14 = (bf16[256,1024]{1,0:T(8,128)(2,1)S(1)}, bf16[256,1024]{1,0:T(8,128)(2,1)S(1)}, u32[]{:S(2)}, u32[]{:S(2)}) collective-permute-start(bf16[256,1024]{1,0:T(8,128)(2,1)S(1)} %convolution_convert_fusion), channel_id=1, source_target_pairs={{0,8},{2,10},{4,12},{6,14},{8,0},{10,2},{12,4},{14,6},{16,24},{18,... | collective-permute-start | bytes 1572872 | tf_op jit(solution)/shard_map/ppermute | solution.py:117
  159.9 26.8 %collective-permute-start.18 = (bf16[128,1024]{1,0:T(8,128)(2,1)S(1)}, bf16[128,1024]{1,0:T(8,128)(2,1)S(1)}, u32[]{:S(2)}, u32[]{:S(2)}) collective-permute-start(bf16[128,1024]{1,0:T(8,128)(2,1)S(1)} %fusion.21), channel_id=1, source_target_pairs={{0,16},{2,18},{4,20},{6,22},{8,24},{10,26},{12,28},{14,30},{16,0},... | collective-permute-start | bytes 786440 | tf_op jit(solution)/shard_map/ppermute | solution.py:117
  178.6 13.6 %collective-permute-start.17 = (bf16[128,1024]{1,0:T(8,128)(2,1)S(1)}, bf16[128,1024]{1,0:T(8,128)(2,1)S(1)}, u32[]{:S(2)}, u32[]{:S(2)}) collective-permute-start(bf16[128,1024]{1,0:T(8,128)(2,1)S(1)} %fusion.29), channel_id=1, source_target_pairs={{0,16},{2,18},{4,20},{6,22},{8,24},{10,26},{12,28},{14,30},{16,0},... | collective-permute-start | bytes 786440 | tf_op jit(solution)/shard_map/ppermute | solution.py:117
  192.9 2.1 collective-permute-start.19
  192.9 3.1 %collective-permute-start.21 = (bf16[1,2048]{1,0:T(2,128)(2,1)S(1)}, bf16[1,2048]{1,0:T(2,128)(2,1)S(1)}, u32[]{:S(2)}, u32[]{:S(2)}) collective-permute-start(bf16[1,2048]{1,0:T(2,128)(2,1)S(1)} %pad_maximum_fusion.7), channel_id=1, source_target_pairs={{0,6},{2,4},{4,2},{6,0},{8,14},{10,12},{12,10},{14,8},{16,22},{18,... | collective-permute-start | bytes 12296 | tf_op jit(solution)/shard_map/ppermute | solution.py:117
  194.0 3.7 %collective-permute-start.20 = (bf16[1,2048]{1,0:T(2,128)(2,1)S(1)}, bf16[1,2048]{1,0:T(2,128)(2,1)S(1)}, u32[]{:S(2)}, u32[]{:S(2)}) collective-permute-start(bf16[1,2048]{1,0:T(2,128)(2,1)S(1)} %pad_maximum_fusion.7), channel_id=1, source_target_pairs={{0,4},{2,6},{4,0},{6,2},{8,12},{10,14},{12,8},{14,10},{16,20},{18,... | collective-permute-start | bytes 12296 | tf_op jit(solution)/shard_map/ppermute | solution.py:117
  198.3 20.4 %collective-permute-start.22 = (bf16[4,1,2048]{2,0,1:T(4,128)(2,1)S(1)}, bf16[4,1,2048]{2,0,1:T(4,128)(2,1)S(1)}, u32[]{:S(2)}, u32[]{:S(2)}) collective-permute-start(bf16[4,1,2048]{2,0,1:T(4,128)(2,1)S(1)} %reshape.23), channel_id=1, source_target_pairs={{0,8},{2,10},{4,12},{6,14},{8,0},{10,2},{12,4},{14,6},{16,24},{18,... | collective-permute-start | bytes 49160 | tf_op jit(solution)/shard_map/ppermute | solution.py:117
  202.4 16.3 %collective-permute-start.24 = (bf16[4,1,2048]{2,0,1:T(4,128)(2,1)S(1)}, bf16[4,1,2048]{2,0,1:T(4,128)(2,1)S(1)}, u32[]{:S(2)}, u32[]{:S(2)}) collective-permute-start(bf16[4,1,2048]{2,0,1:T(4,128)(2,1)S(1)} %reshape.23), channel_id=1, source_target_pairs={{0,24},{2,26},{4,28},{6,30},{8,16},{10,18},{12,20},{14,22},{16,8},... | collective-permute-start | bytes 49160 | tf_op jit(solution)/shard_map/ppermute | solution.py:117
  202.7 16.0 %collective-permute-start.23 = (bf16[4,1,2048]{2,0,1:T(4,128)(2,1)S(1)}, bf16[4,1,2048]{2,0,1:T(4,128)(2,1)S(1)}, u32[]{:S(2)}, u32[]{:S(2)}) collective-permute-start(bf16[4,1,2048]{2,0,1:T(4,128)(2,1)S(1)} %reshape.23), channel_id=1, source_target_pairs={{0,16},{2,18},{4,20},{6,22},{8,24},{10,26},{12,28},{14,30},{16,0},... | collective-permute-start | bytes 49160 | tf_op jit(solution)/shard_map/ppermute | solution.py:117
  (25 other events, 294.6 us)
Sparse Core Ops, SparseCore 0:
  9.8 37.1 all-gather.3
  48.6 34.4 all-gather.5
  85.2 34.4 all-gather.7

commit v5 on v4

--- a/solution.py
+++ b/solution.py
@@ -8,7 +8,7 @@
 HEAD_SIZE = 128
 QUERY_PER_GROUP = 4
 VMEM_LIMIT = 32 * 1024 * 1024
-COST = 1 << 20
+COST = 1 << 10
 INNER = 4
 
 
@@ -57,7 +57,7 @@
             )
 
 
-def attend(place, q, which, k_cache, v_cache, kv, start, shape, buffer):
+def attend(place, q, k_cache, v_cache, kv, start, shape, buffer):
     cols = q[0].shape[1]
     wide = QUERY_PER_GROUP * HEAD_SIZE
     cached, block = k_cache.shape[0], kv[0].shape[0]
@@ -67,7 +67,7 @@
     begin = start // wide
     column = lambda i, place: (0, begin + i)
     after = lambda i, place: (0, heads + begin + i)
-    mine = lambda i, place: (which, i)
+    mine = lambda i, place: (0, i)
     buffers = [] if buffer is None else [buffer]
     return pl.pallas_call(
         attention_kernel,
@@ -87,7 +87,7 @@
             + [pl.BlockSpec(memory_space=pl.ANY)] * len(buffers),
             out_specs=[
                 pl.BlockSpec((rows, wide), lambda i, place: (place[1], begin + i)),
-                pl.BlockSpec((1, wide), lambda i, place: (0, i)),
+                pl.BlockSpec((1, wide), mine),
             ],
         ),
         out_shape=[
@@ -148,14 +148,13 @@
 
     weights = {}
 
-    def gather_queries(piece, source):
-        weights[piece] = group_gather(source[:, piece * chunk : (piece + 1) * chunk])
-
-    def gather_others():
-        key, value, query = step(w_key, w_value, w_query)
-        weights["kv"] = group_gather(jnp.concatenate([key, value], axis=1))
-        if pieces == 2:
-            gather_queries(1, query)
+    weights["kv"] = group_gather(jnp.concatenate([w_key, w_value], axis=1))
+
+    def gather_queries():
+        source = step(w_query) if fast else w_query
+        for piece in range(pieces):
+            part_of = source[:, piece * chunk : (piece + 1) * chunk]
+            weights[piece] = group_gather(part_of)
 
     tokens = {}
     if fast:
@@ -170,7 +169,6 @@
                 axis=0,
             )
 
-        gather_queries(0, w_query)
         swap = {1: over_tp(step(cut(tokens_in, 1, 1 - x)))}
         source = step(tokens_in)
         swap[0] = over_tp(step(cut(source, 0, 1 - x)))
@@ -181,13 +179,14 @@
         send = {b: jnp.where(mine == (b < 2), own, swap[1]) for b in (1, 3)}
         send[1], send[3] = step(send[1], send[3])
         got = {b: over_outer(send[b], b) for b in (1, 3)}
-        gather_others()
+        gather_queries()
 
         def tp_exchange(b):
             held[b] = step(got[b])
             came[b] = over_tp(held[b])
 
         tp_exchange(1)
+        weights["kv"] = step(weights["kv"])
         tp_exchange(3)
         swap[0] = step(swap[0])
         own = cut(source, 0, x)
@@ -201,8 +200,7 @@
                 tokens[b] = (swapped_if(x == 1, held[b], step(came[b]), 1),)
 
     else:
-        gather_queries(0, w_query)
-        gather_others()
+        gather_queries()
         swapped = jnp.where(first == 1, jnp.roll(tokens_in, half, axis=0), tokens_in)
         own = swapped.reshape(rows, outer // n_tp, n_tp, part)
         parts = lax.all_to_all(own, "tp", 2, 1, tiled=True).reshape(rows, outer, part)
@@ -247,16 +245,25 @@
 
     def later_sends(h, name, come):
         weight = weights[name]
-        sums = {}
-        if h is not None:
+        for b in range(0, outer, 2):
+            arrived(b)
+        if h is None:
+            bits = list(come)
+            come = dict(zip(bits, step(*[come[b] for b in bits])))
+        else:
             whole = step(next(iter(come.values()))[0])
             come = {b: whole[i * half : (i + 1) * half] for b, (_, i) in come.items()}
-        for b in range(0, outer, 2):
-            if h is None:
-                come[b + 1] = step(come[b + 1])
-            arrived(b)
-        for b in range(0, outer, 2):
-            sums[b] = times(rows_of(tokens[b], h), weight) + come[b + 1].astype(jnp.float32)
+
+        def total(b, arrival):
+            return times(rows_of(tokens[b], h), weight) + arrival.astype(jnp.float32)
+
+        if outer == 4 and h is not None:
+            send, keep = step(total(2, come[3]).astype(jnp.bfloat16), total(0, come[1]))
+            return keep, over_outer(send, 2)
+        if outer == 4:
+            moved = over_outer(step(total(2, come[3]).astype(jnp.bfloat16)), 2)
+            return total(0, step(come[1])), moved
+        sums = {b: total(b, come[b + 1]) for b in range(0, outer, 2)}
         bit = 2
         while True:
             for b in sorted(sums):
@@ -267,10 +274,7 @@
                     sums[b ^ bit] = sums[b ^ bit] + moved.astype(jnp.float32)
             bit *= 2
 
-    if pieces == 2:
-        jobs = [(None, 0), (None, "kv"), (0, 1), (1, 1)]
-    else:
-        jobs = [(None, "kv"), (0, 0), (1, 0)]
+    jobs = [(None, "kv")] + [(h, piece) for piece in range(pieces) for h in (0, 1)]
     opened, parts_of, lasts = {}, {}, []
     attended = [None]
 
@@ -284,15 +288,13 @@
         came_in, mine = step(parts_of[n][1], parts_of[n][0])
         parts_of[n] = (mine, came_in)
 
-    def attention(n, h):
-        own_half, piece = jobs[n]
+    def attention(n):
+        h, piece = jobs[n]
         place = jnp.stack([prompt_len[0], h ^ first, first]).astype(jnp.int32)
-        which = h if own_half is None else 0
-        kv = parts_of[jobs.index((None, "kv"))]
         caches = (stored_key_cache, stored_value_cache)
         shape = (rows, heads * wide)
         attended[0], last = attend(
-            place, parts_of[n], which, *caches, kv, piece * chunk, shape, attended[0]
+            place, parts_of[n], *caches, parts_of[0], piece * chunk, shape, attended[0]
         )
         lasts.append(step(last))
 
@@ -309,35 +311,37 @@
     if fast:
         tp_exchange(2)
     start(1)
+    start(2)
     advance(0)
+    advance(1)
     if pieces == 2:
-        start(2)
-        advance(1)
-        arrive(0)
         start(3)
         advance(2)
+        start(4)
+        arrive(0)
         arrive(1)
         advance(3)
-        attention(0, 0)
+        attention(1)
         arrive(2)
-        attention(2, 0)
+        advance(4)
+        attention(2)
+        arrive(3)
+        attention(3)
+        arrive(4)
+        row = jnp.concatenate([lasts[0], lasts[2]], axis=1)
     else:
-        start(2)
-        advance(1)
+        advance(2)
         arrive(0)
-        advance(2)
         arrive(1)
-        attention(1, 0)
-    arrive(len(jobs) - 1)
-    row = step(jnp.concatenate(lasts, axis=1))
+        attention(1)
+        arrive(2)
+        row = lasts[0]
+    row = step(row)
     in_group = [row] + [over_inst(row, m) for m in range(1, INNER)]
-    if pieces == 2:
-        attention(0, 1)
+    attention(len(jobs) - 1)
     in_group[1] = step(in_group[1])
     in_group = from_xor_order(in_group, w)
     over_all = [in_group] + [over_outer(in_group, b) for b in range(1, outer)]
-    attention(len(jobs) - 1, 1)
-    over_all[1] = step(over_all[1])
     handoff = from_xor_order(over_all, z).reshape(n_inst, heads * wide)
     return (attended[0], handoff)
 

time: 227 us -> 225 us (level)
  matrix products: 34.6 us -> 29.5 us
  starting transfers between devices: 33.5 us -> 36.2 us
  waiting for transfers between devices: 93.3 us -> 95.9 us
    ppermute x6, waiting for transfers between devices: 13 us -> 18.6 us  [over_tp(): return lax.ppermute(value, 'tp', [(0, 1), (1, 0)])]
    ppermute x19 -> x20, waiting for transfers between devices: 79.5 us -> 74 us  [over_inst(): return lax.ppermute(value, 'inst', [(i, i ^ bits) for i in range(n_inst)])]
    dot_general x14 -> x16, matrix products: 34.6 us -> 29.5 us  [dot(): return jnp.dot(a, b, preferred_element_type=jnp.float32)]
    unnamed x58 -> x64, local copies, waits for them, and re-layouts: 4.57 us -> 7.84 us
    ppermute x19 -> x20, starting transfers between devices: 24.9 us -> 27.6 us  [over_inst(): return lax.ppermute(value, 'inst', [(i, i ^ bits) for i in range(n_inst)])]
  transfers between devices with their start and end apart: 28 -> 29, of which waited for: 13 -> 13; matrix products, arithmetic and copies ran while one was open for 24% -> 18% of each run, Pallas kernels for 10% -> 10%
where the time goes in v5:
time: 225 us
  waiting for transfers between devices  95.9 us (43%)
  starting transfers between devices  36.2 us (16%)
  matrix products  29.5 us (13%)
  Pallas kernels  21.8 us (10%)
  between operations  15 us (7%)
  other arithmetic  14 us (6%)
  local copies, waits for them, and re-layouts  11.9 us (5%)
    ppermute x20, waiting for transfers between devices, over_inst(): return lax.ppermute(value, 'inst', [(i, i ^ bits) for i in range(n_inst)])  74 us
    dot_general x16, matrix products, dot(): return jnp.dot(a, b, preferred_element_type=jnp.float32)  29.5 us
    ppermute x20, starting transfers between devices, over_inst(): return lax.ppermute(value, 'inst', [(i, i ^ bits) for i in range(n_inst)])  27.6 us
    pallas_call x4, Pallas kernels, attend(): pl.pallas_call(attention_kernel, grid_spec=pltpu.PrefetchScalarGridSpec(n...  21.8 us
    ppermute x6, waiting for transfers between devices, over_tp(): return lax.ppermute(value, 'tp', [(0, 1), (1, 0)])  18.6 us
    ppermute x6, starting transfers between devices, over_tp(): return lax.ppermute(value, 'tp', [(0, 1), (1, 0)])  8.5 us
    unnamed x64, local copies, waits for them, and re-layouts  7.84 us
    select_n x4, other arithmetic, swapped_if(): jnp.where(flag, jnp.concatenate([b, a], axis=axis), jnp.concatenate([a, b...  7.15 us
  transfers between devices with their start and end apart: 29, of which 13 were waited for; matrix products, arithmetic and copies ran while one was open for 18% of the time, Pallas kernels for 10%

profile of v5, /device:TPU:0, one launch (start us, length us, event | category | flops | bytes accessed | tf_op | source)
XLA Modules:
  0.0 224.5 jit_solution(5293767150584317313)
XLA Ops:
  7.2 2.4 %pad_maximum_fusion = bf16[512,1024]{1,0:T(8,128)(2,1)} fusion(bf16[512,512]{1,0:T(8,128)(2,1)} %param.10, bf16[512,512]{1,0:T(8,128)(2,1)} %param.9), kind=kLoop, calls=%fused_computation.7 | loop fusion | flops 2097152 | bytes 2097152 | tf_op jit(solution)/shard_map/concatenate | solution.py:151
  12.4 2.9 %collective-permute-start.1 = (bf16[256,1024]{1,0:T(8,128)(2,1)}, bf16[256,1024]{1,0:T(8,128)(2,1)}, u32[]{:S(2)}, u32[]{:S(2)}) collective-permute-start(bf16[256,1024]{1,0:T(8,128)(2,1)} %pad_maximum_fusion.7), channel_id=1, source_target_pairs={{0,1},{1,0},{2,3},{3,2},{4,5},{5,4},{6,7},{7,6},{8,9},{9,8},{10,11... | collective-permute-start | bytes 1572872 | tf_op jit(solution)/shard_map/ppermute | solution.py:123
  16.3 11.2 %collective-permute-done.1 = bf16[256,1024]{1,0:T(8,128)(2,1)} collective-permute-done((bf16[256,1024]{1,0:T(8,128)(2,1)}, bf16[256,1024]{1,0:T(8,128)(2,1)}, u32[]{:S(2)}, u32[]{:S(2)}) %collective-permute-start.1) | collective-permute-done | bytes 524320 | tf_op jit(solution)/shard_map/ppermute | solution.py:123
  27.5 2.3 %broadcast_select_fusion.3 = (bf16[256,1024]{1,0:T(8,128)(2,1)}, bf16[256,1024]{1,0:T(8,128)(2,1)}) fusion(bf16[256,1024]{1,0:T(8,128)(2,1)} %collective-permute-done.1, pred[]{:T(512)S(6)} %eq.37, bf16[128,1024]{1,0:T(8,128)(2,1)S(1)} %get-tuple-element.129, bf16[128,1024]{1,0:T(8,128)(2,1)S(1)} %get-tuple-element.130, pred[]{:T(512)S(6)} %eq.36), kind=kLoop, calls=%fused_computation.30 | loop fusion | flops 1572864 | bytes 2097154 | tf_op jit(solution)/shard_map/jit(_where)/select_n | solution.py:179
  34.0 2.5 %collective-permute-start.2 = (bf16[256,1024]{1,0:T(8,128)(2,1)}, bf16[256,1024]{1,0:T(8,128)(2,1)S(1)}, u32[]{:S(2)}, u32[]{:S(2)}) collective-permute-start(bf16[256,1024]{1,0:T(8,128)(2,1)} %get-tuple-element.68), channel_id=1, source_target_pairs={{0,24},{2,26},{4,28},{6,30},{8,16},{10,18},{12,20},{14,22},{16,8},... | collective-permute-start | bytes 1572872 | tf_op jit(solution)/shard_map/ppermute | solution.py:117
  38.0 8.7 %collective-permute-done.3 = bf16[256,1024]{1,0:T(8,128)(2,1)S(1)} collective-permute-done((bf16[256,1024]{1,0:T(8,128)(2,1)}, bf16[256,1024]{1,0:T(8,128)(2,1)S(1)}, u32[]{:S(2)}, u32[]{:S(2)}) %collective-permute-start.3) | collective-permute-done | bytes 524320 | tf_op jit(solution)/shard_map/ppermute | solution.py:117
  48.3 10.5 %collective-permute-done.2 = bf16[256,1024]{1,0:T(8,128)(2,1)S(1)} collective-permute-done((bf16[256,1024]{1,0:T(8,128)(2,1)}, bf16[256,1024]{1,0:T(8,128)(2,1)S(1)}, u32[]{:S(2)}, u32[]{:S(2)}) %collective-permute-start.2) | collective-permute-done | bytes 524320 | tf_op jit(solution)/shard_map/ppermute | solution.py:117
  62.9 2.0 maximum_select_fusion
  64.9 2.1 convolution_convert_fusion.5
  68.9 4.8 %collective-permute-done.5 = bf16[256,1024]{1,0:T(8,128)(2,1)S(1)} collective-permute-done((bf16[256,1024]{1,0:T(8,128)(2,1)S(1)}, bf16[256,1024]{1,0:T(8,128)(2,1)S(1)}, u32[]{:S(2)}, u32[]{:S(2)}) %collective-permute-start.5) | collective-permute-done | bytes 524320 | tf_op jit(solution)/shard_map/ppermute | solution.py:123
  75.3 2.1 convolution_convert_fusion.4
  78.9 4.3 %collective-permute-done.4 = bf16[256,1024]{1,0:T(8,128)(2,1)} collective-permute-done((bf16[256,1024]{1,0:T(8,128)(2,1)S(1)}, bf16[256,1024]{1,0:T(8,128)(2,1)}, u32[]{:S(2)}, u32[]{:S(2)}) %collective-permute-start.4) | collective-permute-done | bytes 524320 | tf_op jit(solution)/shard_map/ppermute | solution.py:117
  83.9 2.7 %copy-done.8 = bf16[2048,1024]{1,0:T(8,128)(2,1)S(1)} copy-done((bf16[2048,1024]{1,0:T(8,128)(2,1)S(1)}, bf16[2048,1024]{1,0:T(8,128)(2,1)}, u32[]{:S(2)}) %copy-start.8) | copy-done | bytes 4194328
  89.5 2.1 convolution_convert_fusion.2
  94.7 2.6 %collective-permute-done.7 = bf16[256,1024]{1,0:T(8,128)(2,1)} collective-permute-done((bf16[256,1024]{1,0:T(8,128)(2,1)}, bf16[256,1024]{1,0:T(8,128)(2,1)}, u32[]{:S(2)}, u32[]{:S(2)}) %collective-permute-start.7) | collective-permute-done | bytes 524320 | tf_op jit(solution)/shard_map/ppermute | solution.py:123
  99.2 3.8 %collective-permute-done.11 = bf16[256,1024]{1,0:T(8,128)(2,1)} collective-permute-done((bf16[256,1024]{1,0:T(8,128)(2,1)}, bf16[256,1024]{1,0:T(8,128)(2,1)}, u32[]{:S(2)}, u32[]{:S(2)}) %collective-permute-start.11) | collective-permute-done | bytes 524320 | tf_op jit(solution)/shard_map/ppermute | solution.py:117
  103.1 3.2 %add_convert_fusion = bf16[256,1024]{1,0:T(8,128)(2,1)} fusion(bf16[256,1024]{1,0:T(8,128)(2,1)} %collective-permute-done.11, bf16[256,2048]{1,0:T(8,128)(2,1)S(1)} %maximum_select_fusion.2, bf16[2048,1024]{1,0:T(8,128)(2,1)S(1)} %copy-done.29), kind=kOutput, calls=%fused_computation.14 | convolution fusion | flops 1074528256 | bytes 6291456 | tf_op jit(solution)/shard_map/dot_general | solution.py:16
  106.3 7.9 %collective-permute-done.9 = bf16[256,1024]{1,0:T(8,128)(2,1)S(1)} collective-permute-done((bf16[256,1024]{1,0:T(8,128)(2,1)S(1)}, bf16[256,1024]{1,0:T(8,128)(2,1)S(1)}, u32[]{:S(2)}, u32[]{:S(2)}) %collective-permute-start.9) | collective-permute-done | bytes 524320 | tf_op jit(solution)/shard_map/ppermute | solution.py:117
  117.2 2.6 %all-gather.8.cloned.1.call-done = bf16[2048,1024]{1,0:T(8,128)(2,1)} async-done(((bf16[512,1024]{1,0:T(8,128)(2,1)}), bf16[2048,1024]{1,0:T(8,128)(2,1)}) %all-gather.8.cloned.1.call-update) | async-done | bytes 4194320 | tf_op jit(solution)/shard_map/all_gather | solution.py:147
  119.8 3.6 %convolution_convert_fusion.1 = bf16[256,1024]{1,0:T(8,128)(2,1)S(1)} fusion(bf16[2048,1024]{1,0:T(8,128)(2,1)} %all-gather.8.cloned.1.call-done, bf16[128,2048]{1,0:T(8,128)(2,1)S(1)} %copy-done.27, bf16[128,2048]{1,0:T(8,128)(2,1)S(1)} %copy-done.25), kind=kOutput, calls=%fused_computation.2 | convolution fusion | flops 1076101120 | bytes 5767168 | tf_op jit(solution)/shard_map/dot_general | solution.py:16
  127.0 2.5 %collective-permute-start.16 = (bf16[256,1024]{1,0:T(8,128)(2,1)S(1)}, bf16[256,1024]{1,0:T(8,128)(2,1)S(1)}, u32[]{:S(2)}, u32[]{:S(2)}) collective-permute-start(bf16[256,1024]{1,0:T(8,128)(2,1)S(1)} %copy-done.31), channel_id=1, source_target_pairs={{0,16},{2,18},{4,20},{6,22},{8,24},{10,26},{12,28},{14,30},{16,0},... | collective-permute-start | bytes 1572872 | tf_op jit(solution)/shard_map/ppermute | solution.py:117
  131.5 2.4 %collective-permute-start.14 = (bf16[128,1024]{1,0:T(8,128)(2,1)S(1)}, bf16[128,1024]{1,0:T(8,128)(2,1)S(1)}, u32[]{:S(2)}, u32[]{:S(2)}) collective-permute-start(bf16[128,1024]{1,0:T(8,128)(2,1)S(1)} %add_convert_fusion.3), channel_id=1, source_target_pairs={{0,16},{2,18},{4,20},{6,22},{8,24},{10,26},{12,28},{14,30},{16,0},... | collective-permute-start | bytes 786440 | tf_op jit(solution)/shard_map/ppermute | solution.py:117
  136.0 2.3 %convolution_add_fusion.km_ref.vm_ref = f32[256,1024]{1,0:T(8,128)S(1)} fusion(bf16[256,2048]{1,0:T(8,128)(2,1)S(1)} %maximum_select_fusion.3, bf16[2048,1024]{1,0:T(8,128)(2,1)S(1)} %copy-done.30, bf16[256,1024]{1,0:T(8,128)(2,1)} %collective-permute-done.10), kind=kOutput, calls=%fused_computation | convolution fusion | flops 1074266112 | bytes 6815744 | tf_op jit(solution)/shard_map/dot_general | solution.py:16
  138.4 21.7 %collective-permute-done.16.kt_ref.vt_ref = bf16[256,1024]{1,0:T(8,128)(2,1)S(1)} collective-permute-done((bf16[256,1024]{1,0:T(8,128)(2,1)S(1)}, bf16[256,1024]{1,0:T(8,128)(2,1)S(1)}, u32[]{:S(2)}, u32[]{:S(2)}) %collective-permute-start.16) | collective-permute-done | bytes 524320 | tf_op jit(solution)/shard_map/ppermute | solution.py:117
  160.1 10.9 %collective-permute-done.15.qc_ref = bf16[128,1024]{1,0:T(8,128)(2,1)S(1)} collective-permute-done((bf16[128,1024]{1,0:T(8,128)(2,1)}, bf16[128,1024]{1,0:T(8,128)(2,1)S(1)}, u32[]{:S(2)}, u32[]{:S(2)}) %collective-permute-start.15) | collective-permute-done | bytes 262176 | tf_op jit(solution)/shard_map/ppermute | solution.py:117
  173.6 5.4 %attention.4 = (bf16[256,2048]{1,0:T(8,128)(2,1)}, bf16[1,1024]{1,0:T(2,128)(2,1)S(1)}) custom-call(s32[3]{0:T(128)S(1)} %get-tuple-element.147.place_ref, f32[128,1024]{1,0:T(8,128)S(1)} %copy-done.4, bf16[128,1024]{1,0:T(8,128)(2,1)S(1)} %collective-permute-done.15.qc_ref, bf16[1792,512]{1,0:T(8,128)(2,1)S(1)} %copy-done, bf16[1792,512]{1,0:T(8,128)(2,1)S(1)} %copy-done.1, ...), custom_call_target="tpu_custom_call" | custom-call | bytes 1024 | tf_op jit(solution)/shard_map/attention/pallas_call | solution.py:72
  181.4 3.0 %collective-permute-start.18 = (bf16[128,1024]{1,0:T(8,128)(2,1)S(1)}, bf16[128,1024]{1,0:T(8,128)(2,1)S(1)}, u32[]{:S(2)}, u32[]{:S(2)}) collective-permute-start(bf16[128,1024]{1,0:T(8,128)(2,1)S(1)} %add_convert_fusion.1), channel_id=1, source_target_pairs={{0,16},{2,18},{4,20},{6,22},{8,24},{10,26},{12,28},{14,30},{16,0},... | collective-permute-start | bytes 786440 | tf_op jit(solution)/shard_map/ppermute | solution.py:117
  184.4 5.5 %attention.5 = (bf16[256,2048]{1,0:T(8,128)(2,1)}, bf16[1,1024]{1,0:T(2,128)(2,1)}) custom-call(s32[3]{0:T(128)S(1)} %get-tuple-element.146.place_ref, f32[128,1024]{1,0:T(8,128)S(1)} %convert_add_fusion.2.qm_ref, bf16[128,1024]{1,0:T(8,128)(2,1)S(1)} %collective-permute-done.14.qc_ref, ...), custom_call_target="tpu_custom_call", output_to_operand_aliasing={{0}: (9, {})} | custom-call | bytes 1024 | tf_op jit(solution)/shard_map/attention/pallas_call | solution.py:72
  189.8 4.3 %collective-permute-done.19.qc_ref = bf16[128,1024]{1,0:T(8,128)(2,1)S(1)} collective-permute-done((bf16[128,1024]{1,0:T(8,128)(2,1)S(1)}, bf16[128,1024]{1,0:T(8,128)(2,1)S(1)}, u32[]{:S(2)}, u32[]{:S(2)}) %collective-permute-start.19) | collective-permute-done | bytes 262176 | tf_op jit(solution)/shard_map/ppermute | solution.py:117
  194.1 5.4 %attention.6 = (bf16[256,2048]{1,0:T(8,128)(2,1)}, bf16[1,1024]{1,0:T(2,128)(2,1)S(1)}) custom-call(s32[3]{0:T(128)S(1)} %get-tuple-element.147.place_ref, f32[128,1024]{1,0:T(8,128)S(1)} %convert_add_fusion.1.qm_ref, bf16[128,1024]{1,0:T(8,128)(2,1)S(1)} %collective-permute-done.19.qc_ref, ...), custom_call_target="tpu_custom_call", output_to_operand_aliasing={{0}: (9, {})} | custom-call | bytes 1024 | tf_op jit(solution)/shard_map/attention/pallas_call | solution.py:72
  204.7 2.2 collective-permute-start.25
  211.6 5.5 %attention.7 = (bf16[256,2048]{1,0:T(8,128)(2,1)}, bf16[1,1024]{1,0:T(2,128)(2,1)}) custom-call(s32[3]{0:T(128)S(1)} %get-tuple-element.146.place_ref, f32[128,1024]{1,0:T(8,128)S(1)} %copy-done.3, bf16[128,1024]{1,0:T(8,128)(2,1)S(1)} %copy-done.6, bf16[1792,512]{1,0:T(8,128)(2,1)S(1)} %copy-done, ...), custom_call_target="tpu_custom_call", output_to_operand_aliasing={{0}: (9, {})} | custom-call | bytes 1024 | tf_op jit(solution)/shard_map/attention/pallas_call | solution.py:72
  (139 shorter events, 54.0 us)
Async XLA Ops:
  7.2 41.1 %all-gather.4.cloned.1.call-start = ((), (), s32[]{:S(2)}) async-start(), calls=%async_computation | async-start | bytes 5242880 | tf_op jit(solution)/shard_map/all_gather | solution.py:147
  9.7 74.0 %all-gather.6.cloned.1.call-start = ((), (), s32[]{:S(2)}) async-start(), calls=%async_computation.1 | async-start | bytes 5242880 | tf_op jit(solution)/shard_map/all_gather | solution.py:147
  12.4 15.2 %collective-permute-start.1 = (bf16[256,1024]{1,0:T(8,128)(2,1)}, bf16[256,1024]{1,0:T(8,128)(2,1)}, u32[]{:S(2)}, u32[]{:S(2)}) collective-permute-start(bf16[256,1024]{1,0:T(8,128)(2,1)} %pad_maximum_fusion.7), channel_id=1, source_target_pairs={{0,1},{1,0},{2,3},{3,2},{4,5},{5,4},{6,7},{7,6},{8,9},{9,8},{10,11... | collective-permute-start | bytes 1572872 | tf_op jit(solution)/shard_map/ppermute | solution.py:123
  31.4 88.4 %all-gather.8.cloned.1.call-start = ((), (), s32[]{:S(2)}) async-start(), calls=%async_computation.2 | async-start | bytes 5242880 | tf_op jit(solution)/shard_map/all_gather | solution.py:147
  32.1 14.6 %collective-permute-start.3 = (bf16[256,1024]{1,0:T(8,128)(2,1)}, bf16[256,1024]{1,0:T(8,128)(2,1)S(1)}, u32[]{:S(2)}, u32[]{:S(2)}) collective-permute-start(bf16[256,1024]{1,0:T(8,128)(2,1)} %get-tuple-element.69), channel_id=1, source_target_pairs={{0,8},{2,10},{4,12},{6,14},{8,0},{10,2},{12,4},{14,6},{16,24},{18,... | collective-permute-start | bytes 1572872 | tf_op jit(solution)/shard_map/ppermute | solution.py:117
  34.0 24.8 %collective-permute-start.2 = (bf16[256,1024]{1,0:T(8,128)(2,1)}, bf16[256,1024]{1,0:T(8,128)(2,1)S(1)}, u32[]{:S(2)}, u32[]{:S(2)}) collective-permute-start(bf16[256,1024]{1,0:T(8,128)(2,1)} %get-tuple-element.68), channel_id=1, source_target_pairs={{0,24},{2,26},{4,28},{6,30},{8,16},{10,18},{12,20},{14,22},{16,8},... | collective-permute-start | bytes 1572872 | tf_op jit(solution)/shard_map/ppermute | solution.py:117
  36.5 23.8 %collective-permute-start = (bf16[256,1024]{1,0:T(8,128)(2,1)S(1)}, bf16[256,1024]{1,0:T(8,128)(2,1)S(1)}, u32[]{:S(2)}, u32[]{:S(2)}) collective-permute-start(bf16[256,1024]{1,0:T(8,128)(2,1)S(1)} %copy-done.19), channel_id=1, source_target_pairs={{0,1},{1,0},{2,3},{3,2},{4,5},{5,4},{6,7},{7,6},{8,9},{9,8},{10,11... | collective-permute-start | bytes 1572872 | tf_op jit(solution)/shard_map/ppermute | solution.py:123
  46.7 16.2 %collective-permute-start.6 = (bf16[256,1024]{1,0:T(8,128)(2,1)S(1)}, bf16[256,1024]{1,0:T(8,128)(2,1)}, u32[]{:S(2)}, u32[]{:S(2)}) collective-permute-start(bf16[256,1024]{1,0:T(8,128)(2,1)S(1)} %collective-permute-done.3), channel_id=1, source_target_pairs={{0,1},{1,0},{2,3},{3,2},{4,5},{5,4},{6,7},{7,6},{8,9},{9,8},{10,11... | collective-permute-start | bytes 1572872 | tf_op jit(solution)/shard_map/ppermute | solution.py:123
  58.8 14.9 %collective-permute-start.5 = (bf16[256,1024]{1,0:T(8,128)(2,1)S(1)}, bf16[256,1024]{1,0:T(8,128)(2,1)S(1)}, u32[]{:S(2)}, u32[]{:S(2)}) collective-permute-start(bf16[256,1024]{1,0:T(8,128)(2,1)S(1)} %collective-permute-done.2), channel_id=1, source_target_pairs={{0,1},{1,0},{2,3},{3,2},{4,5},{5,4},{6,7},{7,6},{8,9},{9,8},{10,11... | collective-permute-start | bytes 1572872 | tf_op jit(solution)/shard_map/ppermute | solution.py:123
  60.5 22.6 %collective-permute-start.4 = (bf16[256,1024]{1,0:T(8,128)(2,1)S(1)}, bf16[256,1024]{1,0:T(8,128)(2,1)}, u32[]{:S(2)}, u32[]{:S(2)}) collective-permute-start(bf16[256,1024]{1,0:T(8,128)(2,1)S(1)} %get-tuple-element.75), channel_id=1, source_target_pairs={{0,16},{2,18},{4,20},{6,22},{8,24},{10,26},{12,28},{14,30},{16,0},... | collective-permute-start | bytes 1572872 | tf_op jit(solution)/shard_map/ppermute | solution.py:117
  62.4 29.2 %collective-permute-start.8 = (bf16[256,1024]{1,0:T(8,128)(2,1)S(1)}, bf16[256,1024]{1,0:T(8,128)(2,1)S(1)}, u32[]{:S(2)}, u32[]{:S(2)}) collective-permute-start(bf16[256,1024]{1,0:T(8,128)(2,1)S(1)} %get-tuple-element.76), channel_id=1, source_target_pairs={{0,1},{1,0},{2,3},{3,2},{4,5},{5,4},{6,7},{7,6},{8,9},{9,8},{10,11... | collective-permute-start | bytes 1572872 | tf_op jit(solution)/shard_map/ppermute | solution.py:123
  67.0 32.2 %collective-permute-start.10 = (bf16[256,1024]{1,0:T(8,128)(2,1)}, bf16[256,1024]{1,0:T(8,128)(2,1)}, u32[]{:S(2)}, u32[]{:S(2)}) collective-permute-start(bf16[256,1024]{1,0:T(8,128)(2,1)} %convolution_convert_fusion.5), channel_id=1, source_target_pairs={{0,8},{2,10},{4,12},{6,14},{8,0},{10,2},{12,4},{14,6},{16,24},{18,... | collective-permute-start | bytes 1572872 | tf_op jit(solution)/shard_map/ppermute | solution.py:117
  77.4 25.7 %collective-permute-start.11 = (bf16[256,1024]{1,0:T(8,128)(2,1)}, bf16[256,1024]{1,0:T(8,128)(2,1)}, u32[]{:S(2)}, u32[]{:S(2)}) collective-permute-start(bf16[256,1024]{1,0:T(8,128)(2,1)} %convolution_convert_fusion.4), channel_id=1, source_target_pairs={{0,8},{2,10},{4,12},{6,14},{8,0},{10,2},{12,4},{14,6},{16,24},{18,... | collective-permute-start | bytes 1572872 | tf_op jit(solution)/shard_map/ppermute | solution.py:117
  83.2 14.1 %collective-permute-start.7 = (bf16[256,1024]{1,0:T(8,128)(2,1)}, bf16[256,1024]{1,0:T(8,128)(2,1)}, u32[]{:S(2)}, u32[]{:S(2)}) collective-permute-start(bf16[256,1024]{1,0:T(8,128)(2,1)} %collective-permute-done.4), channel_id=1, source_target_pairs={{0,1},{1,0},{2,3},{3,2},{4,5},{5,4},{6,7},{7,6},{8,9},{9,8},{10,11... | collective-permute-start | bytes 1572872 | tf_op jit(solution)/shard_map/ppermute | solution.py:123
  88.0 26.2 %collective-permute-start.9 = (bf16[256,1024]{1,0:T(8,128)(2,1)S(1)}, bf16[256,1024]{1,0:T(8,128)(2,1)S(1)}, u32[]{:S(2)}, u32[]{:S(2)}) collective-permute-start(bf16[256,1024]{1,0:T(8,128)(2,1)S(1)} %convolution_convert_fusion.3), channel_id=1, source_target_pairs={{0,8},{2,10},{4,12},{6,14},{8,0},{10,2},{12,4},{14,6},{16,24},{18,... | collective-permute-start | bytes 1572872 | tf_op jit(solution)/shard_map/ppermute | solution.py:117
  92.4 31.1 %collective-permute-start.12 = (bf16[256,1024]{1,0:T(8,128)(2,1)}, bf16[256,1024]{1,0:T(8,128)(2,1)}, u32[]{:S(2)}, u32[]{:S(2)}) collective-permute-start(bf16[256,1024]{1,0:T(8,128)(2,1)} %convolution_convert_fusion.2), channel_id=1, source_target_pairs={{0,8},{2,10},{4,12},{6,14},{8,0},{10,2},{12,4},{14,6},{16,24},{18,... | collective-permute-start | bytes 1572872 | tf_op jit(solution)/shard_map/ppermute | solution.py:117
  94.6 41.4 %copy-start.12 = (bf16[256,2048]{1,0:T(8,128)(2,1)}, bf16[256,2048]{1,0:T(8,128)(2,1)S(1)}, u32[]{:S(2)}) copy-start(bf16[256,2048]{1,0:T(8,128)(2,1)S(1)} %maximum_select_fusion.3) | copy-start | bytes 3145732
  127.0 33.1 %collective-permute-start.16 = (bf16[256,1024]{1,0:T(8,128)(2,1)S(1)}, bf16[256,1024]{1,0:T(8,128)(2,1)S(1)}, u32[]{:S(2)}, u32[]{:S(2)}) collective-permute-start(bf16[256,1024]{1,0:T(8,128)(2,1)S(1)} %copy-done.31), channel_id=1, source_target_pairs={{0,16},{2,18},{4,20},{6,22},{8,24},{10,26},{12,28},{14,30},{16,0},... | collective-permute-start | bytes 1572872 | tf_op jit(solution)/shard_map/ppermute | solution.py:117
  129.5 41.5 %collective-permute-start.15 = (bf16[128,1024]{1,0:T(8,128)(2,1)}, bf16[128,1024]{1,0:T(8,128)(2,1)S(1)}, u32[]{:S(2)}, u32[]{:S(2)}) collective-permute-start(bf16[128,1024]{1,0:T(8,128)(2,1)} %add_convert_fusion.4), channel_id=1, source_target_pairs={{0,16},{2,18},{4,20},{6,22},{8,24},{10,26},{12,28},{14,30},{16,0},... | collective-permute-start | bytes 786440 | tf_op jit(solution)/shard_map/ppermute | solution.py:117
  130.0 41.0 %collective-permute-start.17 = (bf16[256,1024]{1,0:T(8,128)(2,1)S(1)}, bf16[256,1024]{1,0:T(8,128)(2,1)S(1)}, u32[]{:S(2)}, u32[]{:S(2)}) collective-permute-start(bf16[256,1024]{1,0:T(8,128)(2,1)S(1)} %convolution_convert_fusion.1), channel_id=1, source_target_pairs={{0,8},{2,10},{4,12},{6,14},{8,0},{10,2},{12,4},{14,6},{16,24},{18,... | collective-permute-start | bytes 1572872 | tf_op jit(solution)/shard_map/ppermute | solution.py:117
  131.5 47.5 %collective-permute-start.14 = (bf16[128,1024]{1,0:T(8,128)(2,1)S(1)}, bf16[128,1024]{1,0:T(8,128)(2,1)S(1)}, u32[]{:S(2)}, u32[]{:S(2)}) collective-permute-start(bf16[128,1024]{1,0:T(8,128)(2,1)S(1)} %add_convert_fusion.3), channel_id=1, source_target_pairs={{0,16},{2,18},{4,20},{6,22},{8,24},{10,26},{12,28},{14,30},{16,0},... | collective-permute-start | bytes 786440 | tf_op jit(solution)/shard_map/ppermute | solution.py:117
  135.4 43.7 %collective-permute-start.13 = (bf16[256,1024]{1,0:T(8,128)(2,1)S(1)}, bf16[256,1024]{1,0:T(8,128)(2,1)S(1)}, u32[]{:S(2)}, u32[]{:S(2)}) collective-permute-start(bf16[256,1024]{1,0:T(8,128)(2,1)S(1)} %convolution_convert_fusion), channel_id=1, source_target_pairs={{0,8},{2,10},{4,12},{6,14},{8,0},{10,2},{12,4},{14,6},{16,24},{18,... | collective-permute-start | bytes 1572872 | tf_op jit(solution)/shard_map/ppermute | solution.py:117
  138.4 35.3 %copy-start = (bf16[1792,512]{1,0:T(8,128)(2,1)S(1)}, bf16[1792,512]{1,0:T(8,128)(2,1)}, u32[]{:S(2)}) copy-start(bf16[1792,512]{1,0:T(8,128)(2,1)} %kc_ref.7) | copy-start | bytes 5505028
  138.4 35.3 %copy-start.1 = (bf16[1792,512]{1,0:T(8,128)(2,1)S(1)}, bf16[1792,512]{1,0:T(8,128)(2,1)}, u32[]{:S(2)}) copy-start(bf16[1792,512]{1,0:T(8,128)(2,1)} %vc_ref.7) | copy-start | bytes 5505028
  173.5 20.6 %collective-permute-start.19 = (bf16[128,1024]{1,0:T(8,128)(2,1)S(1)}, bf16[128,1024]{1,0:T(8,128)(2,1)S(1)}, u32[]{:S(2)}, u32[]{:S(2)}) collective-permute-start(bf16[128,1024]{1,0:T(8,128)(2,1)S(1)} %add_convert_fusion.2), channel_id=1, source_target_pairs={{0,16},{2,18},{4,20},{6,22},{8,24},{10,26},{12,28},{14,30},{16,0},... | collective-permute-start | bytes 786440 | tf_op jit(solution)/shard_map/ppermute | solution.py:117
  181.4 18.1 %collective-permute-start.18 = (bf16[128,1024]{1,0:T(8,128)(2,1)S(1)}, bf16[128,1024]{1,0:T(8,128)(2,1)S(1)}, u32[]{:S(2)}, u32[]{:S(2)}) collective-permute-start(bf16[128,1024]{1,0:T(8,128)(2,1)S(1)} %add_convert_fusion.1), channel_id=1, source_target_pairs={{0,16},{2,18},{4,20},{6,22},{8,24},{10,26},{12,28},{14,30},{16,0},... | collective-permute-start | bytes 786440 | tf_op jit(solution)/shard_map/ppermute | solution.py:117
  200.3 1.9 collective-permute-start.20
  200.3 3.7 %collective-permute-start.21 = (bf16[1,2048]{1,0:T(2,128)(2,1)S(1)}, bf16[1,2048]{1,0:T(2,128)(2,1)S(1)}, u32[]{:S(2)}, u32[]{:S(2)}) collective-permute-start(bf16[1,2048]{1,0:T(2,128)(2,1)S(1)} %pad_maximum_fusion.13), channel_id=1, source_target_pairs={{0,4},{2,6},{4,0},{6,2},{8,12},{10,14},{12,8},{14,10},{16,20},{18,... | collective-permute-start | bytes 12296 | tf_op jit(solution)/shard_map/ppermute | solution.py:117
  200.8 3.2 %collective-permute-start.22 = (bf16[1,2048]{1,0:T(2,128)(2,1)S(1)}, bf16[1,2048]{1,0:T(2,128)(2,1)S(1)}, u32[]{:S(2)}, u32[]{:S(2)}) collective-permute-start(bf16[1,2048]{1,0:T(2,128)(2,1)S(1)} %pad_maximum_fusion.13), channel_id=1, source_target_pairs={{0,6},{2,4},{4,2},{6,0},{8,14},{10,12},{12,10},{14,8},{16,22},{18,... | collective-permute-start | bytes 12296 | tf_op jit(solution)/shard_map/ppermute | solution.py:117
  204.6 12.6 %collective-permute-start.24 = (bf16[4,1,2048]{2,0,1:T(4,128)(2,1)S(1)}, bf16[4,1,2048]{2,0,1:T(4,128)(2,1)S(1)}, u32[]{:S(2)}, u32[]{:S(2)}) collective-permute-start(bf16[4,1,2048]{2,0,1:T(4,128)(2,1)S(1)} %reshape.23), channel_id=1, source_target_pairs={{0,16},{2,18},{4,20},{6,22},{8,24},{10,26},{12,28},{14,30},{16,0},... | collective-permute-start | bytes 49160 | tf_op jit(solution)/shard_map/ppermute | solution.py:117
  204.7 12.5 %collective-permute-start.25 = (bf16[4,1,2048]{2,0,1:T(4,128)(2,1)S(1)}, bf16[4,1,2048]{2,0,1:T(4,128)(2,1)S(1)}, u32[]{:S(2)}, u32[]{:S(2)}) collective-permute-start(bf16[4,1,2048]{2,0,1:T(4,128)(2,1)S(1)} %reshape.23), channel_id=1, source_target_pairs={{0,24},{2,26},{4,28},{6,30},{8,16},{10,18},{12,20},{14,22},{16,8},... | collective-permute-start | bytes 49160 | tf_op jit(solution)/shard_map/ppermute | solution.py:117
  206.9 10.3 %collective-permute-start.23 = (bf16[4,1,2048]{2,0,1:T(4,128)(2,1)S(1)}, bf16[4,1,2048]{2,0,1:T(4,128)(2,1)S(1)}, u32[]{:S(2)}, u32[]{:S(2)}) collective-permute-start(bf16[4,1,2048]{2,0,1:T(4,128)(2,1)S(1)} %reshape.23), channel_id=1, source_target_pairs={{0,8},{2,10},{4,12},{6,14},{8,0},{10,2},{12,4},{14,6},{16,24},{18,... | collective-permute-start | bytes 49160 | tf_op jit(solution)/shard_map/ppermute | solution.py:117
  (29 other events, 300.5 us)
Sparse Core Ops, SparseCore 0:
  9.8 37.1 all-gather.3
  49.2 34.4 all-gather.5
  85.2 34.4 all-gather.7

commit v6 on v5

--- a/solution.py
+++ b/solution.py
@@ -14,6 +14,43 @@
 
 def dot(a, b):
     return jnp.dot(a, b, preferred_element_type=jnp.float32)
+
+
+def first_kernel(low_ref, high_ref, w_ref, send_ref):
+    t = jnp.concatenate([low_ref[...], high_ref[...]], axis=0)
+    send_ref[...] = dot(t, w_ref[...]).astype(send_ref.dtype)
+
+
+def later_kernel(low_ref, high_ref, w_ref, came_ref, send_ref, keep_ref):
+    t = jnp.concatenate([low_ref[...], high_ref[...]], axis=0)
+    out = dot(t, w_ref[...]) + came_ref[...].astype(jnp.float32)
+    n = keep_ref.shape[0]
+    keep_ref[...] = out[:n]
+    send_ref[...] = out[n:].astype(send_ref.dtype)
+
+
+def half_product(low, high, h, weight, came=None, tile=512):
+    half, features, columns = low.shape[0] // 2, low.shape[1], weight.shape[1]
+    tile = min(tile, columns)
+    column = lambda i: (0, i)
+    rows = pl.BlockSpec((half, features), lambda i: (h, 0))
+    both = pl.BlockSpec((2 * half, tile), column)
+    one = pl.BlockSpec((half, tile), column)
+    shape = lambda n, dtype: jax.ShapeDtypeStruct((n, columns), dtype)
+    first = came is None
+    cost = 2 * features * columns * 2 if first else COST
+    return pl.pallas_call(
+        first_kernel if first else later_kernel,
+        grid=(columns // tile,),
+        in_specs=[rows, rows, pl.BlockSpec((features, tile), column)] + ([] if first else [both]),
+        out_specs=both if first else [one, one],
+        out_shape=shape(2 * half, jnp.bfloat16)
+        if first
+        else [shape(half, jnp.bfloat16), shape(half, jnp.float32)],
+        compiler_params=pltpu.CompilerParams(vmem_limit_bytes=VMEM_LIMIT),
+        cost_estimate=pl.CostEstimate(flops=0, bytes_accessed=cost, transcendentals=0),
+        name="half_product",
+    )(low, high, weight, *([] if first else [came]))
 
 
 def attention_kernel(
@@ -57,7 +94,7 @@
             )
 
 
-def attend(place, q, k_cache, v_cache, kv, start, shape, buffer):
+def attend(place, q, which, k_cache, v_cache, kv, start, shape, buffer, limit):
     cols = q[0].shape[1]
     wide = QUERY_PER_GROUP * HEAD_SIZE
     cached, block = k_cache.shape[0], kv[0].shape[0]
@@ -67,7 +104,7 @@
     begin = start // wide
     column = lambda i, place: (0, begin + i)
     after = lambda i, place: (0, heads + begin + i)
-    mine = lambda i, place: (0, i)
+    mine = lambda i, place: (which, i)
     buffers = [] if buffer is None else [buffer]
     return pl.pallas_call(
         attention_kernel,
@@ -87,7 +124,7 @@
             + [pl.BlockSpec(memory_space=pl.ANY)] * len(buffers),
             out_specs=[
                 pl.BlockSpec((rows, wide), lambda i, place: (place[1], begin + i)),
-                pl.BlockSpec((1, wide), mine),
+                pl.BlockSpec((1, wide), lambda i, place: (0, i)),
             ],
         ),
         out_shape=[
@@ -95,7 +132,7 @@
             jax.ShapeDtypeStruct((1, cols), jnp.bfloat16),
         ],
         input_output_aliases={9: 0} if buffers else {},
-        compiler_params=pltpu.CompilerParams(vmem_limit_bytes=VMEM_LIMIT),
+        compiler_params=pltpu.CompilerParams(vmem_limit_bytes=limit),
         cost_estimate=pl.CostEstimate(flops=0, bytes_accessed=COST, transcendentals=0),
         name="attention",
     )(place, *q, k_cache, v_cache, *kv, *kv, *buffers)
@@ -239,17 +276,24 @@
                 arrived(b)
                 come[b] = over_outer(step(times(tokens[b], weight).astype(jnp.bfloat16)), 1)
             return come
+        if fast:
+            send = half_product(tokens[1][0], tokens[3][0], h, weight)
+            return over_outer(step(send), 1)
         joined = [jnp.concatenate(same) for same in zip(*[rows_of(tokens[b], h) for b in bits])]
         come = over_outer(step(times(joined, weight).astype(jnp.bfloat16)), 1)
         return {b: (come, i) for i, b in enumerate(bits)}
 
     def later_sends(h, name, come):
         weight = weights[name]
-        for b in range(0, outer, 2):
-            arrived(b)
+        arrived(0)
+        if fast and h is not None:
+            send, keep = half_product(tokens[0][0], tokens[2][0], h, weight, step(come))
+            send, keep = step(send, keep)
+            return keep, over_outer(send, 2)
         if h is None:
             bits = list(come)
             come = dict(zip(bits, step(*[come[b] for b in bits])))
+            arrived(2)
         else:
             whole = step(next(iter(come.values()))[0])
             come = {b: whole[i * half : (i + 1) * half] for b, (_, i) in come.items()}
@@ -257,9 +301,6 @@
         def total(b, arrival):
             return times(rows_of(tokens[b], h), weight) + arrival.astype(jnp.float32)
 
-        if outer == 4 and h is not None:
-            send, keep = step(total(2, come[3]).astype(jnp.bfloat16), total(0, come[1]))
-            return keep, over_outer(send, 2)
         if outer == 4:
             moved = over_outer(step(total(2, come[3]).astype(jnp.bfloat16)), 2)
             return total(0, step(come[1])), moved
@@ -274,7 +315,8 @@
                     sums[b ^ bit] = sums[b ^ bit] + moved.astype(jnp.float32)
             bit *= 2
 
-    jobs = [(None, "kv")] + [(h, piece) for piece in range(pieces) for h in (0, 1)]
+    jobs = [(None, "kv")] + ([(None, 0)] if pieces == 2 else [])
+    jobs += [(0, pieces - 1), (1, pieces - 1)]
     opened, parts_of, lasts = {}, {}, []
     attended = [None]
 
@@ -288,14 +330,15 @@
         came_in, mine = step(parts_of[n][1], parts_of[n][0])
         parts_of[n] = (mine, came_in)
 
-    def attention(n):
-        h, piece = jobs[n]
+    def attention(n, h):
+        own_half, piece = jobs[n]
+        which = h if own_half is None else 0
         place = jnp.stack([prompt_len[0], h ^ first, first]).astype(jnp.int32)
         caches = (stored_key_cache, stored_value_cache)
         shape = (rows, heads * wide)
-        attended[0], last = attend(
-            place, parts_of[n], *caches, parts_of[0], piece * chunk, shape, attended[0]
-        )
+        limit = VMEM_LIMIT if n < len(jobs) - 1 else 56 * 1024 * 1024
+        where = (piece * chunk, shape, attended[0], limit)
+        attended[0], last = attend(place, parts_of[n], which, *caches, parts_of[0], *where)
         lasts.append(step(last))
 
     def from_xor_order(values, index):
@@ -311,34 +354,34 @@
     if fast:
         tp_exchange(2)
     start(1)
-    start(2)
     advance(0)
-    advance(1)
     if pieces == 2:
+        weights[1] = step(weights[1])
+        start(2)
+        advance(1)
+        arrive(0)
+        advance(2)
         start(3)
-        advance(2)
-        start(4)
-        arrive(0)
         arrive(1)
+        attention(1, 0)
         advance(3)
-        attention(1)
+        attention(1, 1)
         arrive(2)
-        advance(4)
-        attention(2)
+        attention(2, 0)
         arrive(3)
-        attention(3)
-        arrive(4)
         row = jnp.concatenate([lasts[0], lasts[2]], axis=1)
     else:
+        start(2)
+        advance(1)
+        arrive(0)
         advance(2)
-        arrive(0)
         arrive(1)
-        attention(1)
+        attention(1, 0)
         arrive(2)
         row = lasts[0]
     row = step(row)
     in_group = [row] + [over_inst(row, m) for m in range(1, INNER)]
-    attention(len(jobs) - 1)
+    attention(len(jobs) - 1, 1)
     in_group[1] = step(in_group[1])
     in_group = from_xor_order(in_group, w)
     over_all = [in_group] + [over_outer(in_group, b) for b in range(1, outer)]

time: 225 us -> 215 us (0.956)
  waiting for transfers between devices: 95.9 us -> 85.9 us
  matrix products: 29.5 us -> 20.5 us
  Pallas kernels: 21.8 us -> 30 us
  local copies, waits for them, and re-layouts: 11.9 us -> 5.47 us
  starting transfers between devices: 36.2 us -> 41 us
  other arithmetic: 14 us -> 16.5 us
    dot_general x16 -> x8, matrix products: 29.5 us -> 20.5 us  [dot(): return jnp.dot(a, b, preferred_element_type=jnp.float32)]
    pallas_call x0 -> x4, Pallas kernels: none -> 7.14 us  [half_product(): pl.pallas_call(first_kernel if first else later_kernel, grid=(columns //...]
    ppermute x20 -> x19, waiting for transfers between devices: 74 us -> 67.1 us  [over_inst(): return lax.ppermute(value, 'inst', [(i, i ^ bits) for i in range(n_inst)])]
    unnamed x64 -> x52, local copies, waits for them, and re-layouts: 7.84 us -> 2.56 us
    ppermute x20 -> x19, starting transfers between devices: 27.6 us -> 32.3 us  [over_inst(): return lax.ppermute(value, 'inst', [(i, i ^ bits) for i in range(n_inst)])]
    ppermute x6, waiting for transfers between devices: 18.6 us -> 14.9 us  [over_tp(): return lax.ppermute(value, 'tp', [(0, 1), (1, 0)])]
  transfers between devices with their start and end apart: 29 -> 28, of which waited for: 13 -> 13; matrix products, arithmetic and copies ran while one was open for 18% -> 17% of each run, Pallas kernels for 10% -> 14%
where the time goes in v6:
time: 215 us; the launch traced here: 214 us
  waiting for transfers between devices  85.9 us (40%)
  starting transfers between devices  41 us (19%)
  Pallas kernels  30 us (14%)
  matrix products  20.5 us (10%)
  other arithmetic  16.5 us (8%)
  between operations  15 us (7%)
  local copies, waits for them, and re-layouts  5.47 us (3%)
    ppermute x19, waiting for transfers between devices, over_inst(): return lax.ppermute(value, 'inst', [(i, i ^ bits) for i in range(n_inst)])  67.1 us
    ppermute x19, starting transfers between devices, over_inst(): return lax.ppermute(value, 'inst', [(i, i ^ bits) for i in range(n_inst)])  32.3 us
    pallas_call x4, Pallas kernels, attend(): pl.pallas_call(attention_kernel, grid_spec=pltpu.PrefetchScalarGridSpec(n...  22.9 us
    dot_general x8, matrix products, dot(): return jnp.dot(a, b, preferred_element_type=jnp.float32)  20.5 us
    ppermute x6, waiting for transfers between devices, over_tp(): return lax.ppermute(value, 'tp', [(0, 1), (1, 0)])  14.9 us
    ppermute x6, starting transfers between devices, over_tp(): return lax.ppermute(value, 'tp', [(0, 1), (1, 0)])  8.54 us
    select_n x4, other arithmetic, swapped_if(): jnp.where(flag, jnp.concatenate([b, a], axis=axis), jnp.concatenate([a, b...  8.4 us
    pallas_call x4, Pallas kernels, half_product(): pl.pallas_call(first_kernel if first else later_kernel, grid=(columns //...  7.14 us
  transfers between devices with their start and end apart: 28, of which 13 were waited for; matrix products, arithmetic and copies ran while one was open for 17% of the time, Pallas kernels for 14%

profile of v6, /device:TPU:0, one launch (start us, length us, event | category | flops | bytes accessed | tf_op | source)
XLA Modules:
  0.0 214.3 jit_solution(3880042783623930721)
XLA Ops:
  7.2 2.4 %pad_maximum_fusion = bf16[512,1024]{1,0:T(8,128)(2,1)} fusion(bf16[512,512]{1,0:T(8,128)(2,1)} %param.10, bf16[512,512]{1,0:T(8,128)(2,1)} %param.9), kind=kLoop, calls=%fused_computation.6 | loop fusion | flops 2097152 | bytes 2097152 | tf_op jit(solution)/shard_map/concatenate | solution.py:188
  11.4 2.9 %collective-permute-start.1 = (bf16[256,1024]{1,0:T(8,128)(2,1)}, bf16[256,1024]{1,0:T(8,128)(2,1)}, u32[]{:S(2)}, u32[]{:S(2)}) collective-permute-start(bf16[256,1024]{1,0:T(8,128)(2,1)} %pad_maximum_fusion.1), channel_id=1, source_target_pairs={{0,1},{1,0},{2,3},{3,2},{4,5},{5,4},{6,7},{7,6},{8,9},{9,8},{10,11... | collective-permute-start | bytes 1572872 | tf_op jit(solution)/shard_map/ppermute | solution.py:160
  15.3 11.2 %collective-permute-done.1 = bf16[256,1024]{1,0:T(8,128)(2,1)} collective-permute-done((bf16[256,1024]{1,0:T(8,128)(2,1)}, bf16[256,1024]{1,0:T(8,128)(2,1)}, u32[]{:S(2)}, u32[]{:S(2)}) %collective-permute-start.1) | collective-permute-done | bytes 524320 | tf_op jit(solution)/shard_map/ppermute | solution.py:160
  26.5 2.3 %broadcast_select_fusion.1 = (bf16[256,1024]{1,0:T(8,128)(2,1)}, bf16[256,1024]{1,0:T(8,128)(2,1)}) fusion(bf16[256,1024]{1,0:T(8,128)(2,1)} %collective-permute-done.1, pred[]{:T(512)S(6)} %eq.37, bf16[128,1024]{1,0:T(8,128)(2,1)S(1)} %get-tuple-element.129, bf16[128,1024]{1,0:T(8,128)(2,1)S(1)} %get-tuple-element.130, pred[]{:T(512)S(6)} %eq.36), kind=kLoop, calls=%fused_computation.18 | loop fusion | flops 1572864 | bytes 2097154 | tf_op jit(solution)/shard_map/jit(_where)/select_n | solution.py:216
  33.2 2.5 %collective-permute-start.2 = (bf16[256,1024]{1,0:T(8,128)(2,1)S(1)}, bf16[256,1024]{1,0:T(8,128)(2,1)S(1)}, u32[]{:S(2)}, u32[]{:S(2)}) collective-permute-start(bf16[256,1024]{1,0:T(8,128)(2,1)S(1)} %copy-done.18), channel_id=1, source_target_pairs={{0,24},{2,26},{4,28},{6,30},{8,16},{10,18},{12,20},{14,22},{16,8},... | collective-permute-start | bytes 1572872 | tf_op jit(solution)/shard_map/ppermute | solution.py:154
  37.2 8.4 %collective-permute-done.3 = bf16[256,1024]{1,0:T(8,128)(2,1)S(1)} collective-permute-done((bf16[256,1024]{1,0:T(8,128)(2,1)S(1)}, bf16[256,1024]{1,0:T(8,128)(2,1)S(1)}, u32[]{:S(2)}, u32[]{:S(2)}) %collective-permute-start.3) | collective-permute-done | bytes 524320 | tf_op jit(solution)/shard_map/ppermute | solution.py:154
  47.1 10.7 %collective-permute-done.2 = bf16[256,1024]{1,0:T(8,128)(2,1)S(1)} collective-permute-done((bf16[256,1024]{1,0:T(8,128)(2,1)S(1)}, bf16[256,1024]{1,0:T(8,128)(2,1)S(1)}, u32[]{:S(2)}, u32[]{:S(2)}) %collective-permute-start.2) | collective-permute-done | bytes 524320 | tf_op jit(solution)/shard_map/ppermute | solution.py:154
  65.2 2.1 convolution_convert_fusion.3
  69.0 3.7 %collective-permute-done.5 = bf16[256,1024]{1,0:T(8,128)(2,1)S(1)} collective-permute-done((bf16[256,1024]{1,0:T(8,128)(2,1)S(1)}, bf16[256,1024]{1,0:T(8,128)(2,1)S(1)}, u32[]{:S(2)}, u32[]{:S(2)}) %collective-permute-start.5) | collective-permute-done | bytes 524320 | tf_op jit(solution)/shard_map/ppermute | solution.py:160
  74.3 2.1 convolution_convert_fusion.2
  77.9 5.5 %collective-permute-done.7 = bf16[256,1024]{1,0:T(8,128)(2,1)S(1)} collective-permute-done((bf16[256,1024]{1,0:T(8,128)(2,1)S(1)}, bf16[256,1024]{1,0:T(8,128)(2,1)S(1)}, u32[]{:S(2)}, u32[]{:S(2)}) %collective-permute-start.7) | collective-permute-done | bytes 524320 | tf_op jit(solution)/shard_map/ppermute | solution.py:154
  83.8 4.4 %convolution_convert_fusion = bf16[256,1024]{1,0:T(8,128)(2,1)} fusion(bf16[256,2048]{1,0:T(8,128)(2,1)S(1)} %maximum_select_fusion.low_ref, bf16[2048,1024]{1,0:T(8,128)(2,1)} %all-gather.6.cloned.1.call-done), kind=kOutput, calls=%fused_computation.2 | convolution fusion | flops 1074003968 | bytes 5767168 | tf_op jit(solution)/shard_map/dot_general | solution.py:16
  92.3 3.3 %maximum_select_fusion.2.low_ref = bf16[256,2048]{1,0:T(8,128)(2,1)} fusion(bf16[256,1024]{1,0:T(8,128)(2,1)S(1)} %get-tuple-element.75, bf16[256,1024]{1,0:T(8,128)(2,1)} %collective-permute-done.4, pred[]{:T(512)S(6)} %eq.35), kind=kLoop, calls=%fused_computation.9 | loop fusion | flops 4718592 | bytes 2097153 | tf_op jit(solution)/shard_map/jit(_where)/select_n | solution.py:163
  95.7 7.8 %collective-permute-done.10 = bf16[256,1024]{1,0:T(8,128)(2,1)} collective-permute-done((bf16[256,1024]{1,0:T(8,128)(2,1)}, bf16[256,1024]{1,0:T(8,128)(2,1)}, u32[]{:S(2)}, u32[]{:S(2)}) %collective-permute-start.10) | collective-permute-done | bytes 524320 | tf_op jit(solution)/shard_map/ppermute | solution.py:154
  105.0 2.7 %add_convert_fusion.1 = bf16[256,1024]{1,0:T(8,128)(2,1)S(1)} fusion(bf16[256,1024]{1,0:T(8,128)(2,1)} %collective-permute-done.10, bf16[256,2048]{1,0:T(8,128)(2,1)S(1)} %maximum_select_fusion.3.high_ref, bf16[2048,1024]{1,0:T(8,128)(2,1)S(1)} %copy-done.22), kind=kOutput, calls=%fused_computation.12 | convolution fusion | flops 1074528256 | bytes 6291456 | tf_op jit(solution)/shard_map/dot_general | solution.py:16
  107.8 8.9 %collective-permute-start.12 = (bf16[256,1024]{1,0:T(8,128)(2,1)S(1)}, bf16[256,1024]{1,0:T(8,128)(2,1)S(1)}, u32[]{:S(2)}, u32[]{:S(2)}) collective-permute-start(bf16[256,1024]{1,0:T(8,128)(2,1)S(1)} %add_convert_fusion.1), channel_id=1, source_target_pairs={{0,16},{2,18},{4,20},{6,22},{8,24},{10,26},{12,28},{14,30},{16,0},... | collective-permute-start | bytes 1572872 | tf_op jit(solution)/shard_map/ppermute | solution.py:154
  116.6 3.1 %all-gather.8.cloned.1.call-done.w_ref = bf16[2048,1024]{1,0:T(8,128)(2,1)} async-done(((bf16[512,1024]{1,0:T(8,128)(2,1)}), bf16[2048,1024]{1,0:T(8,128)(2,1)}) %all-gather.8.cloned.1.call-update) | async-done | bytes 4194320 | tf_op jit(solution)/shard_map/all_gather | solution.py:184
  119.8 2.2 %copy-done.1 = bf16[2048,1024]{1,0:T(8,128)(2,1)S(1)} copy-done((bf16[2048,1024]{1,0:T(8,128)(2,1)S(1)}, bf16[2048,1024]{1,0:T(8,128)(2,1)}, u32[]{:S(2)}) %copy-start.1) | copy-done | bytes 4194328
  125.3 15.1 %collective-permute-done.14 = bf16[256,1024]{1,0:T(8,128)(2,1)} collective-permute-done((bf16[256,1024]{1,0:T(8,128)(2,1)}, bf16[256,1024]{1,0:T(8,128)(2,1)}, u32[]{:S(2)}, u32[]{:S(2)}) %collective-permute-start.14) | collective-permute-done | bytes 524320 | tf_op jit(solution)/shard_map/ppermute | solution.py:154
  140.4 2.3 %add_convert_fusion = bf16[256,1024]{1,0:T(8,128)(2,1)S(1)} fusion(bf16[256,1024]{1,0:T(8,128)(2,1)} %collective-permute-done.14, bf16[256,2048]{1,0:T(8,128)(2,1)S(1)} %copy-done.10, bf16[2048,1024]{1,0:T(8,128)(2,1)S(1)} %copy-done.25), kind=kOutput, calls=%fused_computation.11 | convolution fusion | flops 1074528256 | bytes 6291456 | tf_op jit(solution)/shard_map/dot_general | solution.py:16
  142.9 2.5 %convolution_add_fusion.1.km_ref.vm_ref = f32[256,1024]{1,0:T(8,128)S(1)} fusion(bf16[256,2048]{1,0:T(8,128)(2,1)S(1)} %copy-done.8, bf16[2048,1024]{1,0:T(8,128)(2,1)S(1)} %copy-done.23, bf16[256,1024]{1,0:T(8,128)(2,1)} %collective-permute-done.9), kind=kOutput, calls=%fused_computation.1 | convolution fusion | flops 1074266112 | bytes 6815744 | tf_op jit(solution)/shard_map/dot_general | solution.py:16
  145.4 4.9 %collective-permute-done.11.came_ref = bf16[256,1024]{1,0:T(8,128)(2,1)S(1)} collective-permute-done((bf16[256,1024]{1,0:T(8,128)(2,1)S(1)}, bf16[256,1024]{1,0:T(8,128)(2,1)S(1)}, u32[]{:S(2)}, u32[]{:S(2)}) %collective-permute-start.11) | collective-permute-done | bytes 524320 | tf_op jit(solution)/shard_map/ppermute | solution.py:154
  154.1 3.3 %collective-permute-start.18 = (bf16[128,1024]{1,0:T(8,128)(2,1)S(1)}, bf16[128,1024]{1,0:T(8,128)(2,1)S(1)}, u32[]{:S(2)}, u32[]{:S(2)}) collective-permute-start(bf16[128,1024]{1,0:T(8,128)(2,1)S(1)} %get-tuple-element.101), channel_id=1, source_target_pairs={{0,16},{2,18},{4,20},{6,22},{8,24},{10,26},{12,28},{14,30},{16,0},... | collective-permute-start | bytes 786440 | tf_op jit(solution)/shard_map/ppermute | solution.py:154
  157.4 2.3 %convolution_add_fusion.qm_ref = f32[256,1024]{1,0:T(8,128)S(1)} fusion(bf16[256,2048]{1,0:T(8,128)(2,1)S(1)} %copy-done.8, bf16[2048,1024]{1,0:T(8,128)(2,1)S(1)} %copy-done.25, bf16[256,1024]{1,0:T(8,128)(2,1)} %collective-permute-done.13), kind=kOutput, calls=%fused_computation | convolution fusion | flops 1074266112 | bytes 6815744 | tf_op jit(solution)/shard_map/dot_general | solution.py:16
  159.7 5.4 %attention.4 = (bf16[256,2048]{1,0:T(8,128)(2,1)}, bf16[1,1024]{1,0:T(2,128)(2,1)S(1)}) custom-call(s32[3]{0:T(128)S(1)} %get-tuple-element.141.place_ref, f32[256,1024]{1,0:T(8,128)S(1)} %convolution_add_fusion.qm_ref, bf16[256,1024]{1,0:T(8,128)(2,1)S(1)} %collective-permute-done.16.qc_ref, bf16[1792,512]{1,0:T(8,128)(2,1)S(1)} %copy-done.4, ...), custom_call_target="tpu_custom_call" | custom-call | bytes 1024 | tf_op jit(solution)/shard_map/attention/pallas_call | solution.py:109
  165.2 9.1 %collective-permute-done.15.came_ref = bf16[256,1024]{1,0:T(8,128)(2,1)S(1)} collective-permute-done((bf16[256,1024]{1,0:T(8,128)(2,1)S(1)}, bf16[256,1024]{1,0:T(8,128)(2,1)S(1)}, u32[]{:S(2)}, u32[]{:S(2)}) %collective-permute-start.15) | collective-permute-done | bytes 524320 | tf_op jit(solution)/shard_map/ppermute | solution.py:154
  176.2 5.5 %attention.5 = (bf16[256,2048]{1,0:T(8,128)(2,1)}, bf16[1,1024]{1,0:T(2,128)(2,1)}) custom-call(s32[3]{0:T(128)S(1)} %get-tuple-element.140.place_ref, f32[256,1024]{1,0:T(8,128)S(1)} %convolution_add_fusion.qm_ref, bf16[256,1024]{1,0:T(8,128)(2,1)S(1)} %collective-permute-done.16.qc_ref, ...), custom_call_target="tpu_custom_call", output_to_operand_aliasing={{0}: (9, {})} | custom-call | bytes 1024 | tf_op jit(solution)/shard_map/attention/pallas_call | solution.py:109
  181.7 5.4 %attention.6 = (bf16[256,2048]{1,0:T(8,128)(2,1)}, bf16[1,1024]{1,0:T(2,128)(2,1)S(1)}) custom-call(s32[3]{0:T(128)S(1)} %get-tuple-element.141.place_ref, f32[128,1024]{1,0:T(8,128)S(1)} %get-tuple-element.115.qm_ref, bf16[128,1024]{1,0:T(8,128)(2,1)S(1)} %collective-permute-done.18.qc_ref, ...), custom_call_target="tpu_custom_call", output_to_operand_aliasing={{0}: (9, {})} | custom-call | bytes 1024 | tf_op jit(solution)/shard_map/attention/pallas_call | solution.py:109
  187.1 2.6 %collective-permute-done.17.qc_ref = bf16[128,1024]{1,0:T(8,128)(2,1)S(1)} collective-permute-done((bf16[128,1024]{1,0:T(8,128)(2,1)S(1)}, bf16[128,1024]{1,0:T(8,128)(2,1)S(1)}, u32[]{:S(2)}, u32[]{:S(2)}) %collective-permute-start.17) | collective-permute-done | bytes 262176 | tf_op jit(solution)/shard_map/ppermute | solution.py:154
  189.8 3.3 %collective-permute-start.20 = (bf16[1,2048]{1,0:T(2,128)(2,1)S(1)}, bf16[1,2048]{1,0:T(2,128)(2,1)S(1)}, u32[]{:S(2)}, u32[]{:S(2)}) collective-permute-start(bf16[1,2048]{1,0:T(2,128)(2,1)S(1)} %pad_maximum_fusion.7), channel_id=1, source_target_pairs={{0,4},{2,6},{4,0},{6,2},{8,12},{10,14},{12,8},{14,10},{16,20},{18,... | collective-permute-start | bytes 12296 | tf_op jit(solution)/shard_map/ppermute | solution.py:154
  197.9 2.5 %collective-permute-start.22 = (bf16[4,1,2048]{2,0,1:T(4,128)(2,1)S(1)}, bf16[4,1,2048]{2,0,1:T(4,128)(2,1)S(1)}, u32[]{:S(2)}, u32[]{:S(2)}) collective-permute-start(bf16[4,1,2048]{2,0,1:T(4,128)(2,1)S(1)} %reshape.23), channel_id=1, source_target_pairs={{0,8},{2,10},{4,12},{6,14},{8,0},{10,2},{12,4},{14,6},{16,24},{18,... | collective-permute-start | bytes 49160 | tf_op jit(solution)/shard_map/ppermute | solution.py:154
  200.4 6.5 %attention.7 = (bf16[256,2048]{1,0:T(8,128)(2,1)}, bf16[1,1024]{1,0:T(2,128)(2,1)}) custom-call(s32[3]{0:T(128)} %copy-done.12, f32[128,1024]{1,0:T(8,128)} %copy-done.11, bf16[128,1024]{1,0:T(8,128)(2,1)} %copy-done.20, bf16[1792,512]{1,0:T(8,128)(2,1)} %kc_ref.7, bf16[1792,512]{1,0:T(8,128)(2,1)} %vc_ref.7, ...), custom_call_target="tpu_custom_call", output_to_operand_aliasing={{0}: (9, {})} | custom-call | bytes 1024 | tf_op jit(solution)/shard_map/attention/pallas_call | solution.py:109
  (120 shorter events, 42.2 us)
Async XLA Ops:
  7.2 39.9 %all-gather.4.cloned.1.call-start = ((), (), s32[]{:S(2)}) async-start(), calls=%async_computation | async-start | bytes 5242880 | tf_op jit(solution)/shard_map/all_gather | solution.py:184
  9.7 74.1 %all-gather.6.cloned.1.call-start = ((), (), s32[]{:S(2)}) async-start(), calls=%async_computation.1 | async-start | bytes 5242880 | tf_op jit(solution)/shard_map/all_gather | solution.py:184
  11.4 15.2 %collective-permute-start.1 = (bf16[256,1024]{1,0:T(8,128)(2,1)}, bf16[256,1024]{1,0:T(8,128)(2,1)}, u32[]{:S(2)}, u32[]{:S(2)}) collective-permute-start(bf16[256,1024]{1,0:T(8,128)(2,1)} %pad_maximum_fusion.1), channel_id=1, source_target_pairs={{0,1},{1,0},{2,3},{3,2},{4,5},{5,4},{6,7},{7,6},{8,9},{9,8},{10,11... | collective-permute-start | bytes 1572872 | tf_op jit(solution)/shard_map/ppermute | solution.py:160
  30.4 89.4 %all-gather.8.cloned.1.call-start = ((), (), s32[]{:S(2)}) async-start(), calls=%async_computation.2 | async-start | bytes 5242880 | tf_op jit(solution)/shard_map/all_gather | solution.py:184
  31.4 14.2 %collective-permute-start.3 = (bf16[256,1024]{1,0:T(8,128)(2,1)S(1)}, bf16[256,1024]{1,0:T(8,128)(2,1)S(1)}, u32[]{:S(2)}, u32[]{:S(2)}) collective-permute-start(bf16[256,1024]{1,0:T(8,128)(2,1)S(1)} %copy-done.19), channel_id=1, source_target_pairs={{0,8},{2,10},{4,12},{6,14},{8,0},{10,2},{12,4},{14,6},{16,24},{18,... | collective-permute-start | bytes 1572872 | tf_op jit(solution)/shard_map/ppermute | solution.py:154
  33.2 24.6 %collective-permute-start.2 = (bf16[256,1024]{1,0:T(8,128)(2,1)S(1)}, bf16[256,1024]{1,0:T(8,128)(2,1)S(1)}, u32[]{:S(2)}, u32[]{:S(2)}) collective-permute-start(bf16[256,1024]{1,0:T(8,128)(2,1)S(1)} %copy-done.18), channel_id=1, source_target_pairs={{0,24},{2,26},{4,28},{6,30},{8,16},{10,18},{12,20},{14,22},{16,8},... | collective-permute-start | bytes 1572872 | tf_op jit(solution)/shard_map/ppermute | solution.py:154
  35.7 23.6 %collective-permute-start = (bf16[256,1024]{1,0:T(8,128)(2,1)S(1)}, bf16[256,1024]{1,0:T(8,128)(2,1)}, u32[]{:S(2)}, u32[]{:S(2)}) collective-permute-start(bf16[256,1024]{1,0:T(8,128)(2,1)S(1)} %copy-done.17), channel_id=1, source_target_pairs={{0,1},{1,0},{2,3},{3,2},{4,5},{5,4},{6,7},{7,6},{8,9},{9,8},{10,11... | collective-permute-start | bytes 1572872 | tf_op jit(solution)/shard_map/ppermute | solution.py:160
  45.6 17.7 %collective-permute-start.6 = (bf16[256,1024]{1,0:T(8,128)(2,1)S(1)}, bf16[256,1024]{1,0:T(8,128)(2,1)}, u32[]{:S(2)}, u32[]{:S(2)}) collective-permute-start(bf16[256,1024]{1,0:T(8,128)(2,1)S(1)} %collective-permute-done.3), channel_id=1, source_target_pairs={{0,1},{1,0},{2,3},{3,2},{4,5},{5,4},{6,7},{7,6},{8,9},{9,8},{10,11... | collective-permute-start | bytes 1572872 | tf_op jit(solution)/shard_map/ppermute | solution.py:160
  57.8 14.9 %collective-permute-start.5 = (bf16[256,1024]{1,0:T(8,128)(2,1)S(1)}, bf16[256,1024]{1,0:T(8,128)(2,1)S(1)}, u32[]{:S(2)}, u32[]{:S(2)}) collective-permute-start(bf16[256,1024]{1,0:T(8,128)(2,1)S(1)} %collective-permute-done.2), channel_id=1, source_target_pairs={{0,1},{1,0},{2,3},{3,2},{4,5},{5,4},{6,7},{7,6},{8,9},{9,8},{10,11... | collective-permute-start | bytes 1572872 | tf_op jit(solution)/shard_map/ppermute | solution.py:160
  60.7 22.6 %collective-permute-start.7 = (bf16[256,1024]{1,0:T(8,128)(2,1)S(1)}, bf16[256,1024]{1,0:T(8,128)(2,1)S(1)}, u32[]{:S(2)}, u32[]{:S(2)}) collective-permute-start(bf16[256,1024]{1,0:T(8,128)(2,1)S(1)} %get-tuple-element.74), channel_id=1, source_target_pairs={{0,16},{2,18},{4,20},{6,22},{8,24},{10,26},{12,28},{14,30},{16,0},... | collective-permute-start | bytes 1572872 | tf_op jit(solution)/shard_map/ppermute | solution.py:154
  62.6 29.0 %collective-permute-start.4 = (bf16[256,1024]{1,0:T(8,128)(2,1)S(1)}, bf16[256,1024]{1,0:T(8,128)(2,1)}, u32[]{:S(2)}, u32[]{:S(2)}) collective-permute-start(bf16[256,1024]{1,0:T(8,128)(2,1)S(1)} %get-tuple-element.75), channel_id=1, source_target_pairs={{0,1},{1,0},{2,3},{3,2},{4,5},{5,4},{6,7},{7,6},{8,9},{9,8},{10,11... | collective-permute-start | bytes 1572872 | tf_op jit(solution)/shard_map/ppermute | solution.py:160
  67.3 28.4 %collective-permute-start.9 = (bf16[256,1024]{1,0:T(8,128)(2,1)}, bf16[256,1024]{1,0:T(8,128)(2,1)}, u32[]{:S(2)}, u32[]{:S(2)}) collective-permute-start(bf16[256,1024]{1,0:T(8,128)(2,1)} %convolution_convert_fusion.3), channel_id=1, source_target_pairs={{0,8},{2,10},{4,12},{6,14},{8,0},{10,2},{12,4},{14,6},{16,24},{18,... | collective-permute-start | bytes 1572872 | tf_op jit(solution)/shard_map/ppermute | solution.py:154
  74.3 45.5 %copy-start.6 = (bf16[256,2048]{1,0:T(8,128)(2,1)}, bf16[256,2048]{1,0:T(8,128)(2,1)S(1)}, u32[]{:S(2)}) copy-start(bf16[256,2048]{1,0:T(8,128)(2,1)S(1)} %maximum_select_fusion.1.high_ref) | copy-start | bytes 3145732
  76.4 27.0 %collective-permute-start.10 = (bf16[256,1024]{1,0:T(8,128)(2,1)}, bf16[256,1024]{1,0:T(8,128)(2,1)}, u32[]{:S(2)}, u32[]{:S(2)}) collective-permute-start(bf16[256,1024]{1,0:T(8,128)(2,1)} %convolution_convert_fusion.2), channel_id=1, source_target_pairs={{0,8},{2,10},{4,12},{6,14},{8,0},{10,2},{12,4},{14,6},{16,24},{18,... | collective-permute-start | bytes 1572872 | tf_op jit(solution)/shard_map/ppermute | solution.py:154
  83.3 20.1 %collective-permute-start.8 = (bf16[256,1024]{1,0:T(8,128)(2,1)S(1)}, bf16[256,1024]{1,0:T(8,128)(2,1)}, u32[]{:S(2)}, u32[]{:S(2)}) collective-permute-start(bf16[256,1024]{1,0:T(8,128)(2,1)S(1)} %collective-permute-done.7), channel_id=1, source_target_pairs={{0,1},{1,0},{2,3},{3,2},{4,5},{5,4},{6,7},{7,6},{8,9},{9,8},{10,11... | collective-permute-start | bytes 1572872 | tf_op jit(solution)/shard_map/ppermute | solution.py:160
  88.2 52.2 %collective-permute-start.13 = (bf16[256,1024]{1,0:T(8,128)(2,1)}, bf16[256,1024]{1,0:T(8,128)(2,1)}, u32[]{:S(2)}, u32[]{:S(2)}) collective-permute-start(bf16[256,1024]{1,0:T(8,128)(2,1)} %convolution_convert_fusion), channel_id=1, source_target_pairs={{0,8},{2,10},{4,12},{6,14},{8,0},{10,2},{12,4},{14,6},{16,24},{18,... | collective-permute-start | bytes 1572872 | tf_op jit(solution)/shard_map/ppermute | solution.py:154
  91.6 48.8 %collective-permute-start.14 = (bf16[256,1024]{1,0:T(8,128)(2,1)}, bf16[256,1024]{1,0:T(8,128)(2,1)}, u32[]{:S(2)}, u32[]{:S(2)}) collective-permute-start(bf16[256,1024]{1,0:T(8,128)(2,1)} %convolution_convert_fusion.1), channel_id=1, source_target_pairs={{0,8},{2,10},{4,12},{6,14},{8,0},{10,2},{12,4},{14,6},{16,24},{18,... | collective-permute-start | bytes 1572872 | tf_op jit(solution)/shard_map/ppermute | solution.py:154
  107.8 37.6 %collective-permute-start.12 = (bf16[256,1024]{1,0:T(8,128)(2,1)S(1)}, bf16[256,1024]{1,0:T(8,128)(2,1)S(1)}, u32[]{:S(2)}, u32[]{:S(2)}) collective-permute-start(bf16[256,1024]{1,0:T(8,128)(2,1)S(1)} %add_convert_fusion.1), channel_id=1, source_target_pairs={{0,16},{2,18},{4,20},{6,22},{8,24},{10,26},{12,28},{14,30},{16,0},... | collective-permute-start | bytes 1572872 | tf_op jit(solution)/shard_map/ppermute | solution.py:154
  123.7 26.6 %collective-permute-start.11 = (bf16[256,1024]{1,0:T(8,128)(2,1)S(1)}, bf16[256,1024]{1,0:T(8,128)(2,1)S(1)}, u32[]{:S(2)}, u32[]{:S(2)}) collective-permute-start(bf16[256,1024]{1,0:T(8,128)(2,1)S(1)} %half_product.4), channel_id=1, source_target_pairs={{0,8},{2,10},{4,12},{6,14},{8,0},{10,2},{12,4},{14,6},{16,24},{18,... | collective-permute-start | bytes 1572872 | tf_op jit(solution)/shard_map/ppermute | solution.py:154
  142.8 16.9 %collective-permute-start.16 = (bf16[256,1024]{1,0:T(8,128)(2,1)S(1)}, bf16[256,1024]{1,0:T(8,128)(2,1)S(1)}, u32[]{:S(2)}, u32[]{:S(2)}) collective-permute-start(bf16[256,1024]{1,0:T(8,128)(2,1)S(1)} %add_convert_fusion), channel_id=1, source_target_pairs={{0,16},{2,18},{4,20},{6,22},{8,24},{10,26},{12,28},{14,30},{16,0},... | collective-permute-start | bytes 1572872 | tf_op jit(solution)/shard_map/ppermute | solution.py:154
  145.4 36.3 %copy-start = (f32[256,1024]{1,0:T(8,128)}, f32[256,1024]{1,0:T(8,128)S(1)}, u32[]{:S(2)}) copy-start(f32[256,1024]{1,0:T(8,128)S(1)} %convolution_add_fusion.1.km_ref.vm_ref) | copy-start | bytes 3145732
  145.4 36.3 %copy-start.3 = (bf16[256,1024]{1,0:T(8,128)(2,1)}, bf16[256,1024]{1,0:T(8,128)(2,1)S(1)}, u32[]{:S(2)}) copy-start(bf16[256,1024]{1,0:T(8,128)(2,1)S(1)} %collective-permute-done.12.kt_ref.vt_ref) | copy-start | bytes 1572868
  153.9 20.3 %collective-permute-start.15 = (bf16[256,1024]{1,0:T(8,128)(2,1)S(1)}, bf16[256,1024]{1,0:T(8,128)(2,1)S(1)}, u32[]{:S(2)}, u32[]{:S(2)}) collective-permute-start(bf16[256,1024]{1,0:T(8,128)(2,1)S(1)} %half_product.6), channel_id=1, source_target_pairs={{0,8},{2,10},{4,12},{6,14},{8,0},{10,2},{12,4},{14,6},{16,24},{18,... | collective-permute-start | bytes 1572872 | tf_op jit(solution)/shard_map/ppermute | solution.py:154
  154.1 22.0 %copy-start.12 = (s32[3]{0:T(128)}, s32[3]{0:T(128)S(1)}, u32[]{:S(2)}) copy-start(s32[3]{0:T(128)S(1)} %get-tuple-element.140.place_ref) | copy-start | bytes 40
  154.1 27.5 %collective-permute-start.18 = (bf16[128,1024]{1,0:T(8,128)(2,1)S(1)}, bf16[128,1024]{1,0:T(8,128)(2,1)S(1)}, u32[]{:S(2)}, u32[]{:S(2)}) collective-permute-start(bf16[128,1024]{1,0:T(8,128)(2,1)S(1)} %get-tuple-element.101), channel_id=1, source_target_pairs={{0,16},{2,18},{4,20},{6,22},{8,24},{10,26},{12,28},{14,30},{16,0},... | collective-permute-start | bytes 786440 | tf_op jit(solution)/shard_map/ppermute | solution.py:154
  176.1 13.7 %collective-permute-start.17 = (bf16[128,1024]{1,0:T(8,128)(2,1)S(1)}, bf16[128,1024]{1,0:T(8,128)(2,1)S(1)}, u32[]{:S(2)}, u32[]{:S(2)}) collective-permute-start(bf16[128,1024]{1,0:T(8,128)(2,1)S(1)} %get-tuple-element.112), channel_id=1, source_target_pairs={{0,16},{2,18},{4,20},{6,22},{8,24},{10,26},{12,28},{14,30},{16,0},... | collective-permute-start | bytes 786440 | tf_op jit(solution)/shard_map/ppermute | solution.py:154
  189.8 3.5 %collective-permute-start.19 = (bf16[1,2048]{1,0:T(2,128)(2,1)S(1)}, bf16[1,2048]{1,0:T(2,128)(2,1)S(1)}, u32[]{:S(2)}, u32[]{:S(2)}) collective-permute-start(bf16[1,2048]{1,0:T(2,128)(2,1)S(1)} %pad_maximum_fusion.7), channel_id=1, source_target_pairs={{0,2},{2,0},{4,6},{6,4},{8,10},{10,8},{12,14},{14,12},{16,18},{18,... | collective-permute-start | bytes 12296 | tf_op jit(solution)/shard_map/ppermute | solution.py:154
  189.8 4.9 %collective-permute-start.20 = (bf16[1,2048]{1,0:T(2,128)(2,1)S(1)}, bf16[1,2048]{1,0:T(2,128)(2,1)S(1)}, u32[]{:S(2)}, u32[]{:S(2)}) collective-permute-start(bf16[1,2048]{1,0:T(2,128)(2,1)S(1)} %pad_maximum_fusion.7), channel_id=1, source_target_pairs={{0,4},{2,6},{4,0},{6,2},{8,12},{10,14},{12,8},{14,10},{16,20},{18,... | collective-permute-start | bytes 12296 | tf_op jit(solution)/shard_map/ppermute | solution.py:154
  193.1 3.1 %collective-permute-start.21 = (bf16[1,2048]{1,0:T(2,128)(2,1)S(1)}, bf16[1,2048]{1,0:T(2,128)(2,1)S(1)}, u32[]{:S(2)}, u32[]{:S(2)}) collective-permute-start(bf16[1,2048]{1,0:T(2,128)(2,1)S(1)} %pad_maximum_fusion.7), channel_id=1, source_target_pairs={{0,6},{2,4},{4,2},{6,0},{8,14},{10,12},{12,10},{14,8},{16,22},{18,... | collective-permute-start | bytes 12296 | tf_op jit(solution)/shard_map/ppermute | solution.py:154
  196.8 10.1 %collective-permute-start.23 = (bf16[4,1,2048]{2,0,1:T(4,128)(2,1)S(1)}, bf16[4,1,2048]{2,0,1:T(4,128)(2,1)S(1)}, u32[]{:S(2)}, u32[]{:S(2)}) collective-permute-start(bf16[4,1,2048]{2,0,1:T(4,128)(2,1)S(1)} %reshape.23), channel_id=1, source_target_pairs={{0,16},{2,18},{4,20},{6,22},{8,24},{10,26},{12,28},{14,30},{16,0},... | collective-permute-start | bytes 49160 | tf_op jit(solution)/shard_map/ppermute | solution.py:154
  197.2 9.7 %collective-permute-start.24 = (bf16[4,1,2048]{2,0,1:T(4,128)(2,1)S(1)}, bf16[4,1,2048]{2,0,1:T(4,128)(2,1)S(1)}, u32[]{:S(2)}, u32[]{:S(2)}) collective-permute-start(bf16[4,1,2048]{2,0,1:T(4,128)(2,1)S(1)} %reshape.23), channel_id=1, source_target_pairs={{0,24},{2,26},{4,28},{6,30},{8,16},{10,18},{12,20},{14,22},{16,8},... | collective-permute-start | bytes 49160 | tf_op jit(solution)/shard_map/ppermute | solution.py:154
  197.9 9.0 %collective-permute-start.22 = (bf16[4,1,2048]{2,0,1:T(4,128)(2,1)S(1)}, bf16[4,1,2048]{2,0,1:T(4,128)(2,1)S(1)}, u32[]{:S(2)}, u32[]{:S(2)}) collective-permute-start(bf16[4,1,2048]{2,0,1:T(4,128)(2,1)S(1)} %reshape.23), channel_id=1, source_target_pairs={{0,8},{2,10},{4,12},{6,14},{8,0},{10,2},{12,4},{14,6},{16,24},{18,... | collective-permute-start | bytes 49160 | tf_op jit(solution)/shard_map/ppermute | solution.py:154
  (22 other events, 198.9 us)
Sparse Core Ops, SparseCore 0:
  9.8 37.1 all-gather.3
  49.2 34.4 all-gather.5
  85.2 34.4 all-gather.7

commit v7 on v6

--- a/solution.py
+++ b/solution.py
@@ -230,7 +230,6 @@
         send = {b: jnp.where(mine == (b < 2), own, swap[0]) for b in (2, 0)}
         send[2] = step(send[2])
         got[2], got[0] = over_outer(send[2], 2), send[0]
-        tp_exchange(0)
 
         def arrived(b):
             if b not in tokens:
@@ -352,24 +351,24 @@
 
     start(0)
     if fast:
+        tp_exchange(0)
         tp_exchange(2)
     start(1)
     advance(0)
     if pieces == 2:
         weights[1] = step(weights[1])
+        advance(1)
         start(2)
-        advance(1)
         arrive(0)
+        arrive(1)
         advance(2)
         start(3)
-        arrive(1)
         attention(1, 0)
+        attention(1, 1)
         advance(3)
-        attention(1, 1)
         arrive(2)
         attention(2, 0)
-        arrive(3)
-        row = jnp.concatenate([lasts[0], lasts[2]], axis=1)
+        row = jnp.concatenate([lasts[0] + lasts[1], lasts[2]], axis=1)
     else:
         start(2)
         advance(1)
@@ -377,14 +376,15 @@
         advance(2)
         arrive(1)
         attention(1, 0)
-        arrive(2)
         row = lasts[0]
     row = step(row)
     in_group = [row] + [over_inst(row, m) for m in range(1, INNER)]
-    attention(len(jobs) - 1, 1)
+    arrive(len(jobs) - 1)
     in_group[1] = step(in_group[1])
     in_group = from_xor_order(in_group, w)
     over_all = [in_group] + [over_outer(in_group, b) for b in range(1, outer)]
+    attention(len(jobs) - 1, 1)
+    over_all[1] = step(over_all[1])
     handoff = from_xor_order(over_all, z).reshape(n_inst, heads * wide)
     return (attended[0], handoff)
 

time: 215 us -> 217 us (level)
  starting transfers between devices: 41 us -> 37.3 us
  Pallas kernels: 30 us -> 33.3 us
  matrix products: 20.5 us -> 23.7 us
  local copies, waits for them, and re-layouts: 5.47 us -> 7.88 us
    ppermute x19, waiting for transfers between devices: 67.1 us -> 61.6 us  [over_inst(): return lax.ppermute(value, 'inst', [(i, i ^ bits) for i in range(n_inst)])]
    all_gather x3, waiting for transfers between devices: 3.13 us -> 8.16 us  [group_gather(): lax.all_gather(value, 'inst', axis=0, tiled=True, axis_index_groups=groups)]
    ppermute x19, starting transfers between devices: 32.3 us -> 27.8 us  [over_inst(): return lax.ppermute(value, 'inst', [(i, i ^ bits) for i in range(n_inst)])]
    dot_general x8, matrix products: 20.5 us -> 23.7 us  [dot(): return jnp.dot(a, b, preferred_element_type=jnp.float32)]
    pallas_call x4, Pallas kernels: 7.14 us -> 10 us  [half_product(): pl.pallas_call(first_kernel if first else later_kernel, grid=(columns //...]
    unnamed x52 -> x70, local copies, waits for them, and re-layouts: 2.56 us -> 4.95 us
  transfers between devices with their start and end apart: 28 -> 28, of which waited for: 13 -> 13; matrix products, arithmetic and copies ran while one was open for 17% -> 17% of each run, Pallas kernels for 14% -> 13%
where the time goes in v7:
time: 217 us
  waiting for transfers between devices  84.6 us (39%)
  starting transfers between devices  37.3 us (17%)
  Pallas kernels  33.3 us (15%)
  matrix products  23.7 us (11%)
  between operations  14.9 us (7%)
  other arithmetic  14.8 us (7%)
  local copies, waits for them, and re-layouts  7.88 us (4%)
    ppermute x19, waiting for transfers between devices, over_inst(): return lax.ppermute(value, 'inst', [(i, i ^ bits) for i in range(n_inst)])  61.6 us
    ppermute x19, starting transfers between devices, over_inst(): return lax.ppermute(value, 'inst', [(i, i ^ bits) for i in range(n_inst)])  27.8 us
    dot_general x8, matrix products, dot(): return jnp.dot(a, b, preferred_element_type=jnp.float32)  23.7 us
    pallas_call x4, Pallas kernels, attend(): pl.pallas_call(attention_kernel, grid_spec=pltpu.PrefetchScalarGridSpec(n...  23.2 us
    ppermute x6, waiting for transfers between devices, over_tp(): return lax.ppermute(value, 'tp', [(0, 1), (1, 0)])  14.2 us
    pallas_call x4, Pallas kernels, half_product(): pl.pallas_call(first_kernel if first else later_kernel, grid=(columns //...  10 us
    ppermute x6, starting transfers between devices, over_tp(): return lax.ppermute(value, 'tp', [(0, 1), (1, 0)])  9.42 us
    all_gather x3, waiting for transfers between devices, group_gather(): lax.all_gather(value, 'inst', axis=0, tiled=True, axis_index_groups=groups)  8.16 us
  transfers between devices with their start and end apart: 28, of which 13 were waited for; matrix products, arithmetic and copies ran while one was open for 17% of the time, Pallas kernels for 13%

profile of v7, /device:TPU:0, one launch (start us, length us, event | category | flops | bytes accessed | tf_op | source)
XLA Modules:
  0.0 216.5 jit_solution(13275002551879971881)
XLA Ops:
  7.2 2.4 %pad_maximum_fusion = bf16[512,1024]{1,0:T(8,128)(2,1)} fusion(bf16[512,512]{1,0:T(8,128)(2,1)} %param.10, bf16[512,512]{1,0:T(8,128)(2,1)} %param.9), kind=kLoop, calls=%fused_computation.6 | loop fusion | flops 2097152 | bytes 2097152 | tf_op jit(solution)/shard_map/concatenate | solution.py:188
  11.3 2.9 %collective-permute-start.1 = (bf16[256,1024]{1,0:T(8,128)(2,1)}, bf16[256,1024]{1,0:T(8,128)(2,1)}, u32[]{:S(2)}, u32[]{:S(2)}) collective-permute-start(bf16[256,1024]{1,0:T(8,128)(2,1)} %pad_maximum_fusion.1), channel_id=1, source_target_pairs={{0,1},{1,0},{2,3},{3,2},{4,5},{5,4},{6,7},{7,6},{8,9},{9,8},{10,11... | collective-permute-start | bytes 1572872 | tf_op jit(solution)/shard_map/ppermute | solution.py:160
  15.3 11.2 %collective-permute-done.1 = bf16[256,1024]{1,0:T(8,128)(2,1)} collective-permute-done((bf16[256,1024]{1,0:T(8,128)(2,1)}, bf16[256,1024]{1,0:T(8,128)(2,1)}, u32[]{:S(2)}, u32[]{:S(2)}) %collective-permute-start.1) | collective-permute-done | bytes 524320 | tf_op jit(solution)/shard_map/ppermute | solution.py:160
  26.5 2.3 %broadcast_select_fusion.1 = (bf16[256,1024]{1,0:T(8,128)(2,1)}, bf16[256,1024]{1,0:T(8,128)(2,1)}) fusion(bf16[256,1024]{1,0:T(8,128)(2,1)} %collective-permute-done.1, pred[]{:T(512)S(6)} %eq.37, bf16[128,1024]{1,0:T(8,128)(2,1)S(1)} %get-tuple-element.137, bf16[128,1024]{1,0:T(8,128)(2,1)S(1)} %get-tuple-element.138, pred[]{:T(512)S(6)} %eq.36), kind=kLoop, calls=%fused_computation.18 | loop fusion | flops 1572864 | bytes 2097154 | tf_op jit(solution)/shard_map/jit(_where)/select_n | solution.py:216
  33.2 2.5 %collective-permute-start.2 = (bf16[256,1024]{1,0:T(8,128)(2,1)S(1)}, bf16[256,1024]{1,0:T(8,128)(2,1)S(1)}, u32[]{:S(2)}, u32[]{:S(2)}) collective-permute-start(bf16[256,1024]{1,0:T(8,128)(2,1)S(1)} %copy-done.28), channel_id=1, source_target_pairs={{0,24},{2,26},{4,28},{6,30},{8,16},{10,18},{12,20},{14,22},{16,8},... | collective-permute-start | bytes 1572872 | tf_op jit(solution)/shard_map/ppermute | solution.py:154
  37.2 8.4 %collective-permute-done.3 = bf16[256,1024]{1,0:T(8,128)(2,1)S(1)} collective-permute-done((bf16[256,1024]{1,0:T(8,128)(2,1)S(1)}, bf16[256,1024]{1,0:T(8,128)(2,1)S(1)}, u32[]{:S(2)}, u32[]{:S(2)}) %collective-permute-start.3) | collective-permute-done | bytes 524320 | tf_op jit(solution)/shard_map/ppermute | solution.py:154
  47.1 10.7 %collective-permute-done.2 = bf16[256,1024]{1,0:T(8,128)(2,1)S(1)} collective-permute-done((bf16[256,1024]{1,0:T(8,128)(2,1)S(1)}, bf16[256,1024]{1,0:T(8,128)(2,1)S(1)}, u32[]{:S(2)}, u32[]{:S(2)}) %collective-permute-start.2) | collective-permute-done | bytes 524320 | tf_op jit(solution)/shard_map/ppermute | solution.py:154
  67.5 2.9 %collective-permute-done.4 = bf16[256,1024]{1,0:T(8,128)(2,1)S(1)} collective-permute-done((bf16[256,1024]{1,0:T(8,128)(2,1)S(1)}, bf16[256,1024]{1,0:T(8,128)(2,1)S(1)}, u32[]{:S(2)}, u32[]{:S(2)}) %collective-permute-start.4) | collective-permute-done | bytes 524320 | tf_op jit(solution)/shard_map/ppermute | solution.py:160
  72.0 2.1 convolution_convert_fusion.2
  76.3 7.0 %collective-permute-done.7 = bf16[256,1024]{1,0:T(8,128)(2,1)S(1)} collective-permute-done((bf16[256,1024]{1,0:T(8,128)(2,1)S(1)}, bf16[256,1024]{1,0:T(8,128)(2,1)S(1)}, u32[]{:S(2)}, u32[]{:S(2)}) %collective-permute-start.7) | collective-permute-done | bytes 524320 | tf_op jit(solution)/shard_map/ppermute | solution.py:154
  83.9 4.4 %convolution_convert_fusion = bf16[256,1024]{1,0:T(8,128)(2,1)} fusion(bf16[256,2048]{1,0:T(8,128)(2,1)S(1)} %maximum_select_fusion.low_ref, bf16[2048,1024]{1,0:T(8,128)(2,1)} %all-gather.6.cloned.1.call-done), kind=kOutput, calls=%fused_computation.2 | convolution fusion | flops 1074003968 | bytes 5767168 | tf_op jit(solution)/shard_map/dot_general | solution.py:16
  92.4 10.7 %collective-permute-done.10 = bf16[256,1024]{1,0:T(8,128)(2,1)} collective-permute-done((bf16[256,1024]{1,0:T(8,128)(2,1)}, bf16[256,1024]{1,0:T(8,128)(2,1)}, u32[]{:S(2)}, u32[]{:S(2)}) %collective-permute-start.10) | collective-permute-done | bytes 524320 | tf_op jit(solution)/shard_map/ppermute | solution.py:154
  104.7 3.5 %add_convert_fusion.1 = bf16[256,1024]{1,0:T(8,128)(2,1)} fusion(bf16[256,1024]{1,0:T(8,128)(2,1)} %collective-permute-done.10, bf16[256,2048]{1,0:T(8,128)(2,1)S(1)} %maximum_select_fusion.3.high_ref, bf16[2048,1024]{1,0:T(8,128)(2,1)S(1)} %copy-done.31), kind=kOutput, calls=%fused_computation.12 | convolution fusion | flops 1074528256 | bytes 6291456 | tf_op jit(solution)/shard_map/dot_general | solution.py:16
  108.3 3.3 %collective-permute-start.15 = (bf16[256,1024]{1,0:T(8,128)(2,1)}, bf16[256,1024]{1,0:T(8,128)(2,1)S(1)}, u32[]{:S(2)}, u32[]{:S(2)}) collective-permute-start(bf16[256,1024]{1,0:T(8,128)(2,1)} %add_convert_fusion.1), channel_id=1, source_target_pairs={{0,16},{2,18},{4,20},{6,22},{8,24},{10,26},{12,28},{14,30},{16,0},... | collective-permute-start | bytes 1572872 | tf_op jit(solution)/shard_map/ppermute | solution.py:154
  111.6 8.2 %all-gather.8.cloned.1.call-done.w_ref = bf16[2048,1024]{1,0:T(8,128)(2,1)} async-done(((bf16[512,1024]{1,0:T(8,128)(2,1)}), bf16[2048,1024]{1,0:T(8,128)(2,1)}) %all-gather.8.cloned.1.call-update) | async-done | bytes 4194320 | tf_op jit(solution)/shard_map/all_gather | solution.py:184
  121.4 11.9 %collective-permute-done.12 = bf16[256,1024]{1,0:T(8,128)(2,1)} collective-permute-done((bf16[256,1024]{1,0:T(8,128)(2,1)}, bf16[256,1024]{1,0:T(8,128)(2,1)}, u32[]{:S(2)}, u32[]{:S(2)}) %collective-permute-start.12) | collective-permute-done | bytes 524320 | tf_op jit(solution)/shard_map/ppermute | solution.py:154
  133.4 3.6 %add_convert_fusion = bf16[256,1024]{1,0:T(8,128)(2,1)S(1)} fusion(bf16[256,1024]{1,0:T(8,128)(2,1)} %collective-permute-done.12, bf16[256,2048]{1,0:T(8,128)(2,1)S(1)} %copy-done.11, bf16[2048,1024]{1,0:T(8,128)(2,1)} %all-gather.6.cloned.1.call-done), kind=kOutput, calls=%fused_computation.11 | convolution fusion | flops 1074528256 | bytes 6291456 | tf_op jit(solution)/shard_map/dot_general | solution.py:16
  136.9 2.1 collective-permute-start.14
  141.0 2.5 %collective-permute-start.13 = (bf16[256,1024]{1,0:T(8,128)(2,1)S(1)}, bf16[256,1024]{1,0:T(8,128)(2,1)S(1)}, u32[]{:S(2)}, u32[]{:S(2)}) collective-permute-start(bf16[256,1024]{1,0:T(8,128)(2,1)S(1)} %half_product.4), channel_id=1, source_target_pairs={{0,8},{2,10},{4,12},{6,14},{8,0},{10,2},{12,4},{14,6},{16,24},{18,... | collective-permute-start | bytes 1572872 | tf_op jit(solution)/shard_map/ppermute | solution.py:154
  143.6 2.3 %convolution_add_fusion.km_ref.vm_ref = f32[256,1024]{1,0:T(8,128)S(1)} fusion(bf16[256,2048]{1,0:T(8,128)(2,1)S(1)} %maximum_select_fusion.2.low_ref, bf16[2048,1024]{1,0:T(8,128)(2,1)S(1)} %copy-done.32, bf16[256,1024]{1,0:T(8,128)(2,1)} %collective-permute-done.9), kind=kOutput, calls=%fused_computation | convolution fusion | flops 1074266112 | bytes 6815744 | tf_op jit(solution)/shard_map/dot_general | solution.py:16
  145.9 3.7 %convolution_add_fusion.1.qm_ref = f32[256,1024]{1,0:T(8,128)} fusion(bf16[256,2048]{1,0:T(8,128)(2,1)S(1)} %maximum_select_fusion.2.low_ref, bf16[2048,1024]{1,0:T(8,128)(2,1)S(1)} %copy-done.34, bf16[256,1024]{1,0:T(8,128)(2,1)} %collective-permute-done.11), kind=kOutput, calls=%fused_computation.1 | convolution fusion | flops 1074266112 | bytes 6815744 | tf_op jit(solution)/shard_map/dot_general | solution.py:16
  149.6 7.2 %collective-permute-done.14.qc_ref = bf16[256,1024]{1,0:T(8,128)(2,1)S(1)} collective-permute-done((bf16[256,1024]{1,0:T(8,128)(2,1)S(1)}, bf16[256,1024]{1,0:T(8,128)(2,1)S(1)}, u32[]{:S(2)}, u32[]{:S(2)}) %collective-permute-start.14) | collective-permute-done | bytes 524320 | tf_op jit(solution)/shard_map/ppermute | solution.py:154
  158.8 2.4 %half_product.5 = (bf16[128,1024]{1,0:T(8,128)(2,1)}, f32[128,1024]{1,0:T(8,128)S(1)}) custom-call(bf16[256,2048]{1,0:T(8,128)(2,1)S(1)} %maximum_select_fusion.2.low_ref, bf16[256,2048]{1,0:T(8,128)(2,1)S(1)} %copy-done.11, bf16[2048,1024]{1,0:T(8,128)(2,1)S(1)} %copy-done.1, bf16[256,1024]{1,0:T(8,128)(2,1)S(1)} %collective-permute-done.13.came_ref), custom_call_target="tpu_custom_call" | custom-call | bytes 1024 | tf_op jit(solution)/shard_map/half_product/pallas_call | solution.py:42
  161.2 2.4 %half_product.6 = bf16[256,1024]{1,0:T(8,128)(2,1)} custom-call(bf16[256,2048]{1,0:T(8,128)(2,1)S(1)} %copy-done.7, bf16[256,2048]{1,0:T(8,128)(2,1)S(1)} %copy-done.9, bf16[2048,1024]{1,0:T(8,128)(2,1)S(1)} %copy-done.1), custom_call_target="tpu_custom_call" | custom-call | bytes 8388608 | tf_op jit(solution)/shard_map/half_product/pallas_call | solution.py:42
  168.5 5.4 %attention.4 = (bf16[256,2048]{1,0:T(8,128)(2,1)}, bf16[1,1024]{1,0:T(2,128)(2,1)S(1)}) custom-call(s32[3]{0:T(128)S(1)} %get-tuple-element.149.place_ref, f32[256,1024]{1,0:T(8,128)S(1)} %copy-done.15, bf16[256,1024]{1,0:T(8,128)(2,1)S(1)} %copy-done.18, bf16[1792,512]{1,0:T(8,128)(2,1)S(1)} %copy-done.4, bf16[1792,512]{1,0:T(8,128)(2,1)S(1)} %copy-done.5, ...), custom_call_target="tpu_custom_call" | custom-call | bytes 1024 | tf_op jit(solution)/shard_map/attention/pallas_call | solution.py:109
  174.0 5.4 %attention.5 = (bf16[256,2048]{1,0:T(8,128)(2,1)}, bf16[1,1024]{1,0:T(2,128)(2,1)S(1)}) custom-call(s32[3]{0:T(128)S(1)} %get-tuple-element.148.place_ref, f32[256,1024]{1,0:T(8,128)S(1)} %copy-done.16, bf16[256,1024]{1,0:T(8,128)(2,1)S(1)} %copy-done.18, bf16[1792,512]{1,0:T(8,128)(2,1)S(1)} %copy-done.4, ...), custom_call_target="tpu_custom_call", output_to_operand_aliasing={{0}: (9, {})} | custom-call | bytes 1024 | tf_op jit(solution)/shard_map/attention/pallas_call | solution.py:109
  180.7 3.2 %half_product.7 = (bf16[128,1024]{1,0:T(8,128)(2,1)}, f32[128,1024]{1,0:T(8,128)S(1)}) custom-call(bf16[256,2048]{1,0:T(8,128)(2,1)S(1)} %copy-done.14, bf16[256,2048]{1,0:T(8,128)(2,1)S(1)} %copy-done.12, bf16[2048,1024]{1,0:T(8,128)(2,1)S(1)} %copy-done.2, bf16[256,1024]{1,0:T(8,128)(2,1)} %collective-permute-done.16.came_ref), custom_call_target="tpu_custom_call" | custom-call | bytes 1024 | tf_op jit(solution)/shard_map/half_product/pallas_call | solution.py:42
  184.7 5.8 %attention.6 = (bf16[256,2048]{1,0:T(8,128)(2,1)}, bf16[1,1024]{1,0:T(2,128)(2,1)S(1)}) custom-call(s32[3]{0:T(128)S(1)} %get-tuple-element.149.place_ref, f32[128,1024]{1,0:T(8,128)S(1)} %copy-done.21, bf16[128,1024]{1,0:T(8,128)(2,1)} %collective-permute-done.18.qc_ref, bf16[1792,512]{1,0:T(8,128)(2,1)S(1)} %copy-done.4, ...), custom_call_target="tpu_custom_call", output_to_operand_aliasing={{0}: (9, {})} | custom-call | bytes 1024 | tf_op jit(solution)/shard_map/attention/pallas_call | solution.py:109
  190.6 3.8 %collective-permute-start.20 = (bf16[1,2048]{1,0:T(2,128)(2,1)S(1)}, bf16[1,2048]{1,0:T(2,128)(2,1)S(1)}, u32[]{:S(2)}, u32[]{:S(2)}) collective-permute-start(bf16[1,2048]{1,0:T(2,128)(2,1)S(1)} %pad_maximum_fusion.7), channel_id=1, source_target_pairs={{0,4},{2,6},{4,0},{6,2},{8,12},{10,14},{12,8},{14,10},{16,20},{18,... | collective-permute-start | bytes 12296 | tf_op jit(solution)/shard_map/ppermute | solution.py:154
  194.4 2.6 %collective-permute-done.17.qc_ref = bf16[128,1024]{1,0:T(8,128)(2,1)} collective-permute-done((bf16[128,1024]{1,0:T(8,128)(2,1)}, bf16[128,1024]{1,0:T(8,128)(2,1)}, u32[]{:S(2)}, u32[]{:S(2)}) %collective-permute-start.17) | collective-permute-done | bytes 262176 | tf_op jit(solution)/shard_map/ppermute | solution.py:154
  200.2 2.4 %collective-permute-start.24 = (bf16[4,1,2048]{2,0,1:T(4,128)(2,1)S(1)}, bf16[4,1,2048]{2,0,1:T(4,128)(2,1)S(1)}, u32[]{:S(2)}, u32[]{:S(2)}) collective-permute-start(bf16[4,1,2048]{2,0,1:T(4,128)(2,1)S(1)} %reshape.23), channel_id=1, source_target_pairs={{0,24},{2,26},{4,28},{6,30},{8,16},{10,18},{12,20},{14,22},{16,8},... | collective-permute-start | bytes 49160 | tf_op jit(solution)/shard_map/ppermute | solution.py:154
  202.6 6.5 %attention.7 = (bf16[256,2048]{1,0:T(8,128)(2,1)}, bf16[1,1024]{1,0:T(2,128)(2,1)}) custom-call(s32[3]{0:T(128)} %copy-done.22, f32[128,1024]{1,0:T(8,128)} %copy-done.19, bf16[128,1024]{1,0:T(8,128)(2,1)} %collective-permute-done.17.qc_ref, bf16[1792,512]{1,0:T(8,128)(2,1)} %kc_ref.7, bf16[1792,512]{1,0:T(8,128)(2,1)} %vc_ref.7, ...), custom_call_target="tpu_custom_call", output_to_operand_aliasing={{0}: (9, {})} | custom-call | bytes 1024 | tf_op jit(solution)/shard_map/attention/pallas_call | solution.py:109
  (139 shorter events, 45.5 us)
Async XLA Ops:
  7.2 39.9 %all-gather.4.cloned.1.call-start = ((), (), s32[]{:S(2)}) async-start(), calls=%async_computation | async-start | bytes 5242880 | tf_op jit(solution)/shard_map/all_gather | solution.py:184
  9.7 74.2 %all-gather.6.cloned.1.call-start = ((), (), s32[]{:S(2)}) async-start(), calls=%async_computation.1 | async-start | bytes 5242880 | tf_op jit(solution)/shard_map/all_gather | solution.py:184
  11.3 15.2 %collective-permute-start.1 = (bf16[256,1024]{1,0:T(8,128)(2,1)}, bf16[256,1024]{1,0:T(8,128)(2,1)}, u32[]{:S(2)}, u32[]{:S(2)}) collective-permute-start(bf16[256,1024]{1,0:T(8,128)(2,1)} %pad_maximum_fusion.1), channel_id=1, source_target_pairs={{0,1},{1,0},{2,3},{3,2},{4,5},{5,4},{6,7},{7,6},{8,9},{9,8},{10,11... | collective-permute-start | bytes 1572872 | tf_op jit(solution)/shard_map/ppermute | solution.py:160
  30.4 89.4 %all-gather.8.cloned.1.call-start = ((), (), s32[]{:S(2)}) async-start(), calls=%async_computation.2 | async-start | bytes 5242880 | tf_op jit(solution)/shard_map/all_gather | solution.py:184
  31.4 14.2 %collective-permute-start.3 = (bf16[256,1024]{1,0:T(8,128)(2,1)S(1)}, bf16[256,1024]{1,0:T(8,128)(2,1)S(1)}, u32[]{:S(2)}, u32[]{:S(2)}) collective-permute-start(bf16[256,1024]{1,0:T(8,128)(2,1)S(1)} %copy-done.29), channel_id=1, source_target_pairs={{0,8},{2,10},{4,12},{6,14},{8,0},{10,2},{12,4},{14,6},{16,24},{18,... | collective-permute-start | bytes 1572872 | tf_op jit(solution)/shard_map/ppermute | solution.py:154
  33.2 24.6 %collective-permute-start.2 = (bf16[256,1024]{1,0:T(8,128)(2,1)S(1)}, bf16[256,1024]{1,0:T(8,128)(2,1)S(1)}, u32[]{:S(2)}, u32[]{:S(2)}) collective-permute-start(bf16[256,1024]{1,0:T(8,128)(2,1)S(1)} %copy-done.28), channel_id=1, source_target_pairs={{0,24},{2,26},{4,28},{6,30},{8,16},{10,18},{12,20},{14,22},{16,8},... | collective-permute-start | bytes 1572872 | tf_op jit(solution)/shard_map/ppermute | solution.py:154
  35.7 23.6 %collective-permute-start = (bf16[256,1024]{1,0:T(8,128)(2,1)S(1)}, bf16[256,1024]{1,0:T(8,128)(2,1)}, u32[]{:S(2)}, u32[]{:S(2)}) collective-permute-start(bf16[256,1024]{1,0:T(8,128)(2,1)S(1)} %copy-done.27), channel_id=1, source_target_pairs={{0,1},{1,0},{2,3},{3,2},{4,5},{5,4},{6,7},{7,6},{8,9},{9,8},{10,11... | collective-permute-start | bytes 1572872 | tf_op jit(solution)/shard_map/ppermute | solution.py:160
  45.6 17.0 %collective-permute-start.5 = (bf16[256,1024]{1,0:T(8,128)(2,1)S(1)}, bf16[256,1024]{1,0:T(8,128)(2,1)}, u32[]{:S(2)}, u32[]{:S(2)}) collective-permute-start(bf16[256,1024]{1,0:T(8,128)(2,1)S(1)} %collective-permute-done.3), channel_id=1, source_target_pairs={{0,1},{1,0},{2,3},{3,2},{4,5},{5,4},{6,7},{7,6},{8,9},{9,8},{10,11... | collective-permute-start | bytes 1572872 | tf_op jit(solution)/shard_map/ppermute | solution.py:160
  57.8 12.6 %collective-permute-start.4 = (bf16[256,1024]{1,0:T(8,128)(2,1)S(1)}, bf16[256,1024]{1,0:T(8,128)(2,1)S(1)}, u32[]{:S(2)}, u32[]{:S(2)}) collective-permute-start(bf16[256,1024]{1,0:T(8,128)(2,1)S(1)} %collective-permute-done.2), channel_id=1, source_target_pairs={{0,1},{1,0},{2,3},{3,2},{4,5},{5,4},{6,7},{7,6},{8,9},{9,8},{10,11... | collective-permute-start | bytes 1572872 | tf_op jit(solution)/shard_map/ppermute | solution.py:160
  60.7 22.6 %collective-permute-start.7 = (bf16[256,1024]{1,0:T(8,128)(2,1)S(1)}, bf16[256,1024]{1,0:T(8,128)(2,1)S(1)}, u32[]{:S(2)}, u32[]{:S(2)}) collective-permute-start(bf16[256,1024]{1,0:T(8,128)(2,1)S(1)} %get-tuple-element.78), channel_id=1, source_target_pairs={{0,16},{2,18},{4,20},{6,22},{8,24},{10,26},{12,28},{14,30},{16,0},... | collective-permute-start | bytes 1572872 | tf_op jit(solution)/shard_map/ppermute | solution.py:154
  64.5 74.6 %copy-start.6 = (bf16[256,2048]{1,0:T(8,128)(2,1)}, bf16[256,2048]{1,0:T(8,128)(2,1)S(1)}, u32[]{:S(2)}) copy-start(bf16[256,2048]{1,0:T(8,128)(2,1)S(1)} %maximum_select_fusion.low_ref) | copy-start | bytes 3145732
  66.6 25.8 %collective-permute-start.9 = (bf16[256,1024]{1,0:T(8,128)(2,1)}, bf16[256,1024]{1,0:T(8,128)(2,1)}, u32[]{:S(2)}, u32[]{:S(2)}) collective-permute-start(bf16[256,1024]{1,0:T(8,128)(2,1)} %convolution_convert_fusion.3), channel_id=1, source_target_pairs={{0,8},{2,10},{4,12},{6,14},{8,0},{10,2},{12,4},{14,6},{16,24},{18,... | collective-permute-start | bytes 1572872 | tf_op jit(solution)/shard_map/ppermute | solution.py:154
  72.0 67.1 %copy-start.8 = (bf16[256,2048]{1,0:T(8,128)(2,1)}, bf16[256,2048]{1,0:T(8,128)(2,1)S(1)}, u32[]{:S(2)}) copy-start(bf16[256,2048]{1,0:T(8,128)(2,1)S(1)} %maximum_select_fusion.1.high_ref) | copy-start | bytes 3145732
  74.1 29.0 %collective-permute-start.10 = (bf16[256,1024]{1,0:T(8,128)(2,1)}, bf16[256,1024]{1,0:T(8,128)(2,1)}, u32[]{:S(2)}, u32[]{:S(2)}) collective-permute-start(bf16[256,1024]{1,0:T(8,128)(2,1)} %convolution_convert_fusion.2), channel_id=1, source_target_pairs={{0,8},{2,10},{4,12},{6,14},{8,0},{10,2},{12,4},{14,6},{16,24},{18,... | collective-permute-start | bytes 1572872 | tf_op jit(solution)/shard_map/ppermute | solution.py:154
  74.8 16.2 %collective-permute-start.6 = (bf16[256,1024]{1,0:T(8,128)(2,1)S(1)}, bf16[256,1024]{1,0:T(8,128)(2,1)}, u32[]{:S(2)}, u32[]{:S(2)}) collective-permute-start(bf16[256,1024]{1,0:T(8,128)(2,1)S(1)} %get-tuple-element.84), channel_id=1, source_target_pairs={{0,1},{1,0},{2,3},{3,2},{4,5},{5,4},{6,7},{7,6},{8,9},{9,8},{10,11... | collective-permute-start | bytes 1572872 | tf_op jit(solution)/shard_map/ppermute | solution.py:160
  83.3 19.8 %collective-permute-start.8 = (bf16[256,1024]{1,0:T(8,128)(2,1)S(1)}, bf16[256,1024]{1,0:T(8,128)(2,1)}, u32[]{:S(2)}, u32[]{:S(2)}) collective-permute-start(bf16[256,1024]{1,0:T(8,128)(2,1)S(1)} %collective-permute-done.7), channel_id=1, source_target_pairs={{0,1},{1,0},{2,3},{3,2},{4,5},{5,4},{6,7},{7,6},{8,9},{9,8},{10,11... | collective-permute-start | bytes 1572872 | tf_op jit(solution)/shard_map/ppermute | solution.py:160
  88.2 45.1 %collective-permute-start.11 = (bf16[256,1024]{1,0:T(8,128)(2,1)}, bf16[256,1024]{1,0:T(8,128)(2,1)}, u32[]{:S(2)}, u32[]{:S(2)}) collective-permute-start(bf16[256,1024]{1,0:T(8,128)(2,1)} %convolution_convert_fusion), channel_id=1, source_target_pairs={{0,8},{2,10},{4,12},{6,14},{8,0},{10,2},{12,4},{14,6},{16,24},{18,... | collective-permute-start | bytes 1572872 | tf_op jit(solution)/shard_map/ppermute | solution.py:154
  91.0 42.3 %collective-permute-start.12 = (bf16[256,1024]{1,0:T(8,128)(2,1)}, bf16[256,1024]{1,0:T(8,128)(2,1)}, u32[]{:S(2)}, u32[]{:S(2)}) collective-permute-start(bf16[256,1024]{1,0:T(8,128)(2,1)} %convolution_convert_fusion.1), channel_id=1, source_target_pairs={{0,8},{2,10},{4,12},{6,14},{8,0},{10,2},{12,4},{14,6},{16,24},{18,... | collective-permute-start | bytes 1572872 | tf_op jit(solution)/shard_map/ppermute | solution.py:154
  108.3 41.4 %collective-permute-start.15 = (bf16[256,1024]{1,0:T(8,128)(2,1)}, bf16[256,1024]{1,0:T(8,128)(2,1)S(1)}, u32[]{:S(2)}, u32[]{:S(2)}) collective-permute-start(bf16[256,1024]{1,0:T(8,128)(2,1)} %add_convert_fusion.1), channel_id=1, source_target_pairs={{0,16},{2,18},{4,20},{6,22},{8,24},{10,26},{12,28},{14,30},{16,0},... | collective-permute-start | bytes 1572872 | tf_op jit(solution)/shard_map/ppermute | solution.py:154
  121.4 37.4 %copy-start.13 = (bf16[256,2048]{1,0:T(8,128)(2,1)}, bf16[256,2048]{1,0:T(8,128)(2,1)S(1)}, u32[]{:S(2)}) copy-start(bf16[256,2048]{1,0:T(8,128)(2,1)S(1)} %maximum_select_fusion.2.low_ref) | copy-start | bytes 3145732
  136.9 19.9 %collective-permute-start.14 = (bf16[256,1024]{1,0:T(8,128)(2,1)S(1)}, bf16[256,1024]{1,0:T(8,128)(2,1)S(1)}, u32[]{:S(2)}, u32[]{:S(2)}) collective-permute-start(bf16[256,1024]{1,0:T(8,128)(2,1)S(1)} %add_convert_fusion), channel_id=1, source_target_pairs={{0,16},{2,18},{4,20},{6,22},{8,24},{10,26},{12,28},{14,30},{16,0},... | collective-permute-start | bytes 1572872 | tf_op jit(solution)/shard_map/ppermute | solution.py:154
  141.0 17.8 %collective-permute-start.13 = (bf16[256,1024]{1,0:T(8,128)(2,1)S(1)}, bf16[256,1024]{1,0:T(8,128)(2,1)S(1)}, u32[]{:S(2)}, u32[]{:S(2)}) collective-permute-start(bf16[256,1024]{1,0:T(8,128)(2,1)S(1)} %half_product.4), channel_id=1, source_target_pairs={{0,8},{2,10},{4,12},{6,14},{8,0},{10,2},{12,4},{14,6},{16,24},{18,... | collective-permute-start | bytes 1572872 | tf_op jit(solution)/shard_map/ppermute | solution.py:154
  145.9 38.8 %copy-start = (f32[256,1024]{1,0:T(8,128)}, f32[256,1024]{1,0:T(8,128)S(1)}, u32[]{:S(2)}) copy-start(f32[256,1024]{1,0:T(8,128)S(1)} %convolution_add_fusion.km_ref.vm_ref) | copy-start | bytes 3145732
  163.7 17.0 %collective-permute-start.16 = (bf16[256,1024]{1,0:T(8,128)(2,1)}, bf16[256,1024]{1,0:T(8,128)(2,1)}, u32[]{:S(2)}, u32[]{:S(2)}) collective-permute-start(bf16[256,1024]{1,0:T(8,128)(2,1)} %half_product.6), channel_id=1, source_target_pairs={{0,8},{2,10},{4,12},{6,14},{8,0},{10,2},{12,4},{14,6},{16,24},{18,... | collective-permute-start | bytes 1572872 | tf_op jit(solution)/shard_map/ppermute | solution.py:154
  163.7 20.9 %collective-permute-start.18 = (bf16[128,1024]{1,0:T(8,128)(2,1)}, bf16[128,1024]{1,0:T(8,128)(2,1)}, u32[]{:S(2)}, u32[]{:S(2)}) collective-permute-start(bf16[128,1024]{1,0:T(8,128)(2,1)} %get-tuple-element.107), channel_id=1, source_target_pairs={{0,16},{2,18},{4,20},{6,22},{8,24},{10,26},{12,28},{14,30},{16,0},... | collective-permute-start | bytes 786440 | tf_op jit(solution)/shard_map/ppermute | solution.py:154
  184.0 13.1 %collective-permute-start.17 = (bf16[128,1024]{1,0:T(8,128)(2,1)}, bf16[128,1024]{1,0:T(8,128)(2,1)}, u32[]{:S(2)}, u32[]{:S(2)}) collective-permute-start(bf16[128,1024]{1,0:T(8,128)(2,1)} %get-tuple-element.120), channel_id=1, source_target_pairs={{0,16},{2,18},{4,20},{6,22},{8,24},{10,26},{12,28},{14,30},{16,0},... | collective-permute-start | bytes 786440 | tf_op jit(solution)/shard_map/ppermute | solution.py:154
  190.5 6.5 %collective-permute-start.19 = (bf16[1,2048]{1,0:T(2,128)(2,1)S(1)}, bf16[1,2048]{1,0:T(2,128)(2,1)S(1)}, u32[]{:S(2)}, u32[]{:S(2)}) collective-permute-start(bf16[1,2048]{1,0:T(2,128)(2,1)S(1)} %pad_maximum_fusion.7), channel_id=1, source_target_pairs={{0,2},{2,0},{4,6},{6,4},{8,10},{10,8},{12,14},{14,12},{16,18},{18,... | collective-permute-start | bytes 12296 | tf_op jit(solution)/shard_map/ppermute | solution.py:154
  190.6 6.4 %collective-permute-start.20 = (bf16[1,2048]{1,0:T(2,128)(2,1)S(1)}, bf16[1,2048]{1,0:T(2,128)(2,1)S(1)}, u32[]{:S(2)}, u32[]{:S(2)}) collective-permute-start(bf16[1,2048]{1,0:T(2,128)(2,1)S(1)} %pad_maximum_fusion.7), channel_id=1, source_target_pairs={{0,4},{2,6},{4,0},{6,2},{8,12},{10,14},{12,8},{14,10},{16,20},{18,... | collective-permute-start | bytes 12296 | tf_op jit(solution)/shard_map/ppermute | solution.py:154
  194.4 3.1 %collective-permute-start.21 = (bf16[1,2048]{1,0:T(2,128)(2,1)S(1)}, bf16[1,2048]{1,0:T(2,128)(2,1)S(1)}, u32[]{:S(2)}, u32[]{:S(2)}) collective-permute-start(bf16[1,2048]{1,0:T(2,128)(2,1)S(1)} %pad_maximum_fusion.7), channel_id=1, source_target_pairs={{0,6},{2,4},{4,2},{6,0},{8,14},{10,12},{12,10},{14,8},{16,22},{18,... | collective-permute-start | bytes 12296 | tf_op jit(solution)/shard_map/ppermute | solution.py:154
  198.1 11.1 %collective-permute-start.22 = (bf16[4,1,2048]{2,0,1:T(4,128)(2,1)S(1)}, bf16[4,1,2048]{2,0,1:T(4,128)(2,1)S(1)}, u32[]{:S(2)}, u32[]{:S(2)}) collective-permute-start(bf16[4,1,2048]{2,0,1:T(4,128)(2,1)S(1)} %reshape.23), channel_id=1, source_target_pairs={{0,8},{2,10},{4,12},{6,14},{8,0},{10,2},{12,4},{14,6},{16,24},{18,... | collective-permute-start | bytes 49160 | tf_op jit(solution)/shard_map/ppermute | solution.py:154
  200.2 9.0 %collective-permute-start.23 = (bf16[4,1,2048]{2,0,1:T(4,128)(2,1)S(1)}, bf16[4,1,2048]{2,0,1:T(4,128)(2,1)S(1)}, u32[]{:S(2)}, u32[]{:S(2)}) collective-permute-start(bf16[4,1,2048]{2,0,1:T(4,128)(2,1)S(1)} %reshape.23), channel_id=1, source_target_pairs={{0,16},{2,18},{4,20},{6,22},{8,24},{10,26},{12,28},{14,30},{16,0},... | collective-permute-start | bytes 49160 | tf_op jit(solution)/shard_map/ppermute | solution.py:154
  200.2 9.0 %collective-permute-start.24 = (bf16[4,1,2048]{2,0,1:T(4,128)(2,1)S(1)}, bf16[4,1,2048]{2,0,1:T(4,128)(2,1)S(1)}, u32[]{:S(2)}, u32[]{:S(2)}) collective-permute-start(bf16[4,1,2048]{2,0,1:T(4,128)(2,1)S(1)} %reshape.23), channel_id=1, source_target_pairs={{0,24},{2,26},{4,28},{6,30},{8,16},{10,18},{12,20},{14,22},{16,8},... | collective-permute-start | bytes 49160 | tf_op jit(solution)/shard_map/ppermute | solution.py:154
  (31 other events, 238.5 us)
Sparse Core Ops, SparseCore 0:
  9.8 37.1 all-gather.3
  48.6 34.4 all-gather.5
  85.2 34.4 all-gather.7

commit v8 on v7

--- a/solution.py
+++ b/solution.py
@@ -357,12 +357,12 @@
     advance(0)
     if pieces == 2:
         weights[1] = step(weights[1])
+        start(2)
         advance(1)
-        start(2)
         arrive(0)
-        arrive(1)
         advance(2)
         start(3)
+        arrive(1)
         attention(1, 0)
         attention(1, 1)
         advance(3)

time: 217 us -> 209 us (0.963)
  waiting for transfers between devices: 84.6 us -> 94 us
  starting transfers between devices: 37.3 us -> 31.2 us
  other arithmetic: 14.8 us -> 11.1 us
  Pallas kernels: 33.3 us -> 30.8 us
  local copies, waits for them, and re-layouts: 7.88 us -> 5.46 us
  matrix products: 23.7 us -> 21.3 us
    ppermute x19, starting transfers between devices: 27.8 us -> 21.7 us  [over_inst(): return lax.ppermute(value, 'inst', [(i, i ^ bits) for i in range(n_inst)])]
    ppermute x19, waiting for transfers between devices: 61.6 us -> 66.7 us  [over_inst(): return lax.ppermute(value, 'inst', [(i, i ^ bits) for i in range(n_inst)])]
    select_n x4, other arithmetic: 6.77 us -> 3.04 us  [swapped_if(): jnp.where(flag, jnp.concatenate([b, a], axis=axis), jnp.concatenate([a, b...]
    all_gather x3, waiting for transfers between devices: 8.16 us -> 10.8 us  [group_gather(): lax.all_gather(value, 'inst', axis=0, tiled=True, axis_index_groups=groups)]
    dot_general x8, matrix products: 23.7 us -> 21.3 us  [dot(): return jnp.dot(a, b, preferred_element_type=jnp.float32)]
    unnamed x70 -> x48, local copies, waits for them, and re-layouts: 4.95 us -> 2.55 us
    pallas_call x4, Pallas kernels: 10 us -> 7.75 us  [half_product(): pl.pallas_call(first_kernel if first else later_kernel, grid=(columns //...]
  transfers between devices with their start and end apart: 28 -> 28, of which waited for: 13 -> 12; matrix products, arithmetic and copies ran while one was open for 17% -> 15% of each run, Pallas kernels for 13% -> 15%
where the time goes in v8:
time: 209 us
  waiting for transfers between devices  94 us (45%)
  starting transfers between devices  31.2 us (15%)
  Pallas kernels  30.8 us (15%)
  matrix products  21.3 us (10%)
  between operations  14.9 us (7%)
  other arithmetic  11.1 us (5%)
  local copies, waits for them, and re-layouts  5.46 us (3%)
    ppermute x19, waiting for transfers between devices, over_inst(): return lax.ppermute(value, 'inst', [(i, i ^ bits) for i in range(n_inst)])  66.7 us
    pallas_call x4, Pallas kernels, attend(): pl.pallas_call(attention_kernel, grid_spec=pltpu.PrefetchScalarGridSpec(n...  23 us
    ppermute x19, starting transfers between devices, over_inst(): return lax.ppermute(value, 'inst', [(i, i ^ bits) for i in range(n_inst)])  21.7 us
    dot_general x8, matrix products, dot(): return jnp.dot(a, b, preferred_element_type=jnp.float32)  21.3 us
    ppermute x6, waiting for transfers between devices, over_tp(): return lax.ppermute(value, 'tp', [(0, 1), (1, 0)])  15.7 us
    all_gather x3, waiting for transfers between devices, group_gather(): lax.all_gather(value, 'inst', axis=0, tiled=True, axis_index_groups=groups)  10.8 us
    ppermute x6, starting transfers between devices, over_tp(): return lax.ppermute(value, 'tp', [(0, 1), (1, 0)])  9.38 us
    pallas_call x4, Pallas kernels, half_product(): pl.pallas_call(first_kernel if first else later_kernel, grid=(columns //...  7.75 us
  transfers between devices with their start and end apart: 28, of which 12 were waited for; matrix products, arithmetic and copies ran while one was open for 15% of the time, Pallas kernels for 15%

profile of v8, /device:TPU:0, one launch (start us, length us, event | category | flops | bytes accessed | tf_op | source)
XLA Modules:
  0.0 208.8 jit_solution(15811924301400850436)
XLA Ops:
  7.2 2.5 %pad_maximum_fusion = bf16[512,1024]{1,0:T(8,128)(2,1)} fusion(bf16[512,512]{1,0:T(8,128)(2,1)} %param.10, bf16[512,512]{1,0:T(8,128)(2,1)} %param.9), kind=kLoop, calls=%fused_computation.6 | loop fusion | flops 2097152 | bytes 2097152 | tf_op jit(solution)/shard_map/concatenate | solution.py:188
  11.4 2.9 %collective-permute-start.1 = (bf16[256,1024]{1,0:T(8,128)(2,1)}, bf16[256,1024]{1,0:T(8,128)(2,1)}, u32[]{:S(2)}, u32[]{:S(2)}) collective-permute-start(bf16[256,1024]{1,0:T(8,128)(2,1)} %pad_maximum_fusion.1), channel_id=1, source_target_pairs={{0,1},{1,0},{2,3},{3,2},{4,5},{5,4},{6,7},{7,6},{8,9},{9,8},{10,11... | collective-permute-start | bytes 1572872 | tf_op jit(solution)/shard_map/ppermute | solution.py:160
  15.3 11.2 %collective-permute-done.1 = bf16[256,1024]{1,0:T(8,128)(2,1)} collective-permute-done((bf16[256,1024]{1,0:T(8,128)(2,1)}, bf16[256,1024]{1,0:T(8,128)(2,1)}, u32[]{:S(2)}, u32[]{:S(2)}) %collective-permute-start.1) | collective-permute-done | bytes 524320 | tf_op jit(solution)/shard_map/ppermute | solution.py:160
  26.6 2.3 %broadcast_select_fusion.1 = (bf16[256,1024]{1,0:T(8,128)(2,1)}, bf16[256,1024]{1,0:T(8,128)(2,1)}) fusion(bf16[256,1024]{1,0:T(8,128)(2,1)} %collective-permute-done.1, pred[]{:T(512)S(6)} %eq.37, bf16[128,1024]{1,0:T(8,128)(2,1)S(1)} %get-tuple-element.135, bf16[128,1024]{1,0:T(8,128)(2,1)S(1)} %get-tuple-element.136, pred[]{:T(512)S(6)} %eq.36), kind=kLoop, calls=%fused_computation.18 | loop fusion | flops 1572864 | bytes 2097154 | tf_op jit(solution)/shard_map/jit(_where)/select_n | solution.py:216
  33.2 2.5 %collective-permute-start.2 = (bf16[256,1024]{1,0:T(8,128)(2,1)S(1)}, bf16[256,1024]{1,0:T(8,128)(2,1)S(1)}, u32[]{:S(2)}, u32[]{:S(2)}) collective-permute-start(bf16[256,1024]{1,0:T(8,128)(2,1)S(1)} %copy-done.17), channel_id=1, source_target_pairs={{0,24},{2,26},{4,28},{6,30},{8,16},{10,18},{12,20},{14,22},{16,8},... | collective-permute-start | bytes 1572872 | tf_op jit(solution)/shard_map/ppermute | solution.py:154
  37.2 8.4 %collective-permute-done.3 = bf16[256,1024]{1,0:T(8,128)(2,1)S(1)} collective-permute-done((bf16[256,1024]{1,0:T(8,128)(2,1)S(1)}, bf16[256,1024]{1,0:T(8,128)(2,1)S(1)}, u32[]{:S(2)}, u32[]{:S(2)}) %collective-permute-start.3) | collective-permute-done | bytes 524320 | tf_op jit(solution)/shard_map/ppermute | solution.py:154
  47.1 10.7 %collective-permute-done.2 = bf16[256,1024]{1,0:T(8,128)(2,1)S(1)} collective-permute-done((bf16[256,1024]{1,0:T(8,128)(2,1)S(1)}, bf16[256,1024]{1,0:T(8,128)(2,1)S(1)}, u32[]{:S(2)}, u32[]{:S(2)}) %collective-permute-start.2) | collective-permute-done | bytes 524320 | tf_op jit(solution)/shard_map/ppermute | solution.py:154
  63.0 2.1 convolution_convert_fusion.3
  66.0 4.5 %collective-permute-done.4 = bf16[256,1024]{1,0:T(8,128)(2,1)S(1)} collective-permute-done((bf16[256,1024]{1,0:T(8,128)(2,1)S(1)}, bf16[256,1024]{1,0:T(8,128)(2,1)S(1)}, u32[]{:S(2)}, u32[]{:S(2)}) %collective-permute-start.4) | collective-permute-done | bytes 524320 | tf_op jit(solution)/shard_map/ppermute | solution.py:160
  70.8 2.1 %convolution_convert_fusion.2 = bf16[256,1024]{1,0:T(8,128)(2,1)} fusion(bf16[256,2048]{1,0:T(8,128)(2,1)S(1)} %maximum_select_fusion.1.high_ref, bf16[2048,1024]{1,0:T(8,128)(2,1)S(1)} %copy-done.19), kind=kOutput, calls=%fused_computation.4 | convolution fusion | flops 1074003968 | bytes 5767168 | tf_op jit(solution)/shard_map/dot_general | solution.py:16
  75.1 8.4 %collective-permute-done.7 = bf16[256,1024]{1,0:T(8,128)(2,1)} collective-permute-done((bf16[256,1024]{1,0:T(8,128)(2,1)S(1)}, bf16[256,1024]{1,0:T(8,128)(2,1)}, u32[]{:S(2)}, u32[]{:S(2)}) %collective-permute-start.7) | collective-permute-done | bytes 524320 | tf_op jit(solution)/shard_map/ppermute | solution.py:154
  83.9 4.4 %convolution_convert_fusion = bf16[256,1024]{1,0:T(8,128)(2,1)} fusion(bf16[256,2048]{1,0:T(8,128)(2,1)S(1)} %maximum_select_fusion.low_ref, bf16[2048,1024]{1,0:T(8,128)(2,1)} %all-gather.6.cloned.1.call-done), kind=kOutput, calls=%fused_computation.2 | convolution fusion | flops 1074003968 | bytes 5767168 | tf_op jit(solution)/shard_map/dot_general | solution.py:16
  89.6 2.1 convolution_convert_fusion.1
  92.5 9.9 %collective-permute-done.10 = bf16[256,1024]{1,0:T(8,128)(2,1)} collective-permute-done((bf16[256,1024]{1,0:T(8,128)(2,1)}, bf16[256,1024]{1,0:T(8,128)(2,1)}, u32[]{:S(2)}, u32[]{:S(2)}) %collective-permute-start.10) | collective-permute-done | bytes 524320 | tf_op jit(solution)/shard_map/ppermute | solution.py:154
  104.3 3.5 %add_convert_fusion.1 = bf16[256,1024]{1,0:T(8,128)(2,1)} fusion(bf16[256,1024]{1,0:T(8,128)(2,1)} %collective-permute-done.10, bf16[256,2048]{1,0:T(8,128)(2,1)S(1)} %maximum_select_fusion.3.high_ref, bf16[2048,1024]{1,0:T(8,128)(2,1)S(1)} %copy-done.20), kind=kOutput, calls=%fused_computation.12 | convolution fusion | flops 1074528256 | bytes 6291456 | tf_op jit(solution)/shard_map/dot_general | solution.py:16
  108.9 10.8 %all-gather.8.cloned.1.call-done.w_ref = bf16[2048,1024]{1,0:T(8,128)(2,1)} async-done(((bf16[512,1024]{1,0:T(8,128)(2,1)}), bf16[2048,1024]{1,0:T(8,128)(2,1)}) %all-gather.8.cloned.1.call-update) | async-done | bytes 4194320 | tf_op jit(solution)/shard_map/all_gather | solution.py:184
  119.8 2.2 %copy-done.1 = bf16[2048,1024]{1,0:T(8,128)(2,1)S(1)} copy-done((bf16[2048,1024]{1,0:T(8,128)(2,1)S(1)}, bf16[2048,1024]{1,0:T(8,128)(2,1)}, u32[]{:S(2)}) %copy-start.1) | copy-done | bytes 4194328
  125.3 16.0 %collective-permute-done.14 = bf16[256,1024]{1,0:T(8,128)(2,1)} collective-permute-done((bf16[256,1024]{1,0:T(8,128)(2,1)}, bf16[256,1024]{1,0:T(8,128)(2,1)}, u32[]{:S(2)}, u32[]{:S(2)}) %collective-permute-start.14) | collective-permute-done | bytes 524320 | tf_op jit(solution)/shard_map/ppermute | solution.py:154
  141.3 2.4 %add_convert_fusion = bf16[256,1024]{1,0:T(8,128)(2,1)S(1)} fusion(bf16[256,1024]{1,0:T(8,128)(2,1)} %collective-permute-done.14, bf16[256,2048]{1,0:T(8,128)(2,1)S(1)} %copy-done.9, bf16[2048,1024]{1,0:T(8,128)(2,1)S(1)} %copy-done.23), kind=kOutput, calls=%fused_computation.11 | convolution fusion | flops 1074528256 | bytes 6291456 | tf_op jit(solution)/shard_map/dot_general | solution.py:16
  144.3 2.4 %convolution_add_fusion.1.km_ref.vm_ref = f32[256,1024]{1,0:T(8,128)S(1)} fusion(bf16[256,2048]{1,0:T(8,128)(2,1)S(1)} %maximum_select_fusion.2.low_ref, bf16[2048,1024]{1,0:T(8,128)(2,1)S(1)} %copy-done.21, bf16[256,1024]{1,0:T(8,128)(2,1)} %collective-permute-done.9), kind=kOutput, calls=%fused_computation.1 | convolution fusion | flops 1074266112 | bytes 6815744 | tf_op jit(solution)/shard_map/dot_general | solution.py:16
  146.8 2.5 %collective-permute-done.11.came_ref = bf16[256,1024]{1,0:T(8,128)(2,1)S(1)} collective-permute-done((bf16[256,1024]{1,0:T(8,128)(2,1)S(1)}, bf16[256,1024]{1,0:T(8,128)(2,1)S(1)}, u32[]{:S(2)}, u32[]{:S(2)}) %collective-permute-start.11) | collective-permute-done | bytes 524320 | tf_op jit(solution)/shard_map/ppermute | solution.py:154
  153.1 2.7 %collective-permute-start.18 = (bf16[128,1024]{1,0:T(8,128)(2,1)S(1)}, bf16[128,1024]{1,0:T(8,128)(2,1)S(1)}, u32[]{:S(2)}, u32[]{:S(2)}) collective-permute-start(bf16[128,1024]{1,0:T(8,128)(2,1)S(1)} %get-tuple-element.104), channel_id=1, source_target_pairs={{0,16},{2,18},{4,20},{6,22},{8,24},{10,26},{12,28},{14,30},{16,0},... | collective-permute-start | bytes 786440 | tf_op jit(solution)/shard_map/ppermute | solution.py:154
  155.8 2.3 %convolution_add_fusion.qm_ref = f32[256,1024]{1,0:T(8,128)S(1)} fusion(bf16[256,2048]{1,0:T(8,128)(2,1)S(1)} %maximum_select_fusion.2.low_ref, bf16[2048,1024]{1,0:T(8,128)(2,1)S(1)} %copy-done.23, bf16[256,1024]{1,0:T(8,128)(2,1)} %collective-permute-done.13), kind=kOutput, calls=%fused_computation | convolution fusion | flops 1074266112 | bytes 6815744 | tf_op jit(solution)/shard_map/dot_general | solution.py:16
  158.1 4.2 %collective-permute-done.16.qc_ref = bf16[256,1024]{1,0:T(8,128)(2,1)S(1)} collective-permute-done((bf16[256,1024]{1,0:T(8,128)(2,1)S(1)}, bf16[256,1024]{1,0:T(8,128)(2,1)S(1)}, u32[]{:S(2)}, u32[]{:S(2)}) %collective-permute-start.16) | collective-permute-done | bytes 524320 | tf_op jit(solution)/shard_map/ppermute | solution.py:154
  162.3 5.4 %attention.4 = (bf16[256,2048]{1,0:T(8,128)(2,1)}, bf16[1,1024]{1,0:T(2,128)(2,1)S(1)}) custom-call(s32[3]{0:T(128)S(1)} %get-tuple-element.147.place_ref, f32[256,1024]{1,0:T(8,128)S(1)} %convolution_add_fusion.qm_ref, bf16[256,1024]{1,0:T(8,128)(2,1)S(1)} %collective-permute-done.16.qc_ref, bf16[1792,512]{1,0:T(8,128)(2,1)S(1)} %copy-done.4, ...), custom_call_target="tpu_custom_call" | custom-call | bytes 1024 | tf_op jit(solution)/shard_map/attention/pallas_call | solution.py:109
  167.7 5.4 %attention.5 = (bf16[256,2048]{1,0:T(8,128)(2,1)}, bf16[1,1024]{1,0:T(2,128)(2,1)S(1)}) custom-call(s32[3]{0:T(128)S(1)} %get-tuple-element.146.place_ref, f32[256,1024]{1,0:T(8,128)S(1)} %convolution_add_fusion.qm_ref, bf16[256,1024]{1,0:T(8,128)(2,1)S(1)} %collective-permute-done.16.qc_ref, ...), custom_call_target="tpu_custom_call", output_to_operand_aliasing={{0}: (9, {})} | custom-call | bytes 1024 | tf_op jit(solution)/shard_map/attention/pallas_call | solution.py:109
  174.1 2.4 %half_product.7 = (bf16[128,1024]{1,0:T(8,128)(2,1)}, f32[128,1024]{1,0:T(8,128)S(1)}) custom-call(bf16[256,2048]{1,0:T(8,128)(2,1)S(1)} %maximum_select_fusion.2.low_ref, bf16[256,2048]{1,0:T(8,128)(2,1)S(1)} %copy-done.9, bf16[2048,1024]{1,0:T(8,128)(2,1)S(1)} %copy-done.2, bf16[256,1024]{1,0:T(8,128)(2,1)S(1)} %collective-permute-done.15.came_ref), custom_call_target="tpu_custom_call" | custom-call | bytes 1024 | tf_op jit(solution)/shard_map/half_product/pallas_call | solution.py:42
  176.6 5.7 %attention.6 = (bf16[256,2048]{1,0:T(8,128)(2,1)}, bf16[1,1024]{1,0:T(2,128)(2,1)S(1)}) custom-call(s32[3]{0:T(128)S(1)} %get-tuple-element.147.place_ref, f32[128,1024]{1,0:T(8,128)S(1)} %get-tuple-element.121.qm_ref, bf16[128,1024]{1,0:T(8,128)(2,1)S(1)} %collective-permute-done.18.qc_ref, ...), custom_call_target="tpu_custom_call", output_to_operand_aliasing={{0}: (9, {})} | custom-call | bytes 1024 | tf_op jit(solution)/shard_map/attention/pallas_call | solution.py:109
  184.2 5.5 %collective-permute-done.17.qc_ref = bf16[128,1024]{1,0:T(8,128)(2,1)} collective-permute-done((bf16[128,1024]{1,0:T(8,128)(2,1)}, bf16[128,1024]{1,0:T(8,128)(2,1)}, u32[]{:S(2)}, u32[]{:S(2)}) %collective-permute-start.17) | collective-permute-done | bytes 262176 | tf_op jit(solution)/shard_map/ppermute | solution.py:154
  190.5 2.2 %collective-permute-start.23 = (bf16[4,1,2048]{2,0,1:T(4,128)(2,1)S(1)}, bf16[4,1,2048]{2,0,1:T(4,128)(2,1)S(1)}, u32[]{:S(2)}, u32[]{:S(2)}) collective-permute-start(bf16[4,1,2048]{2,0,1:T(4,128)(2,1)S(1)} %reshape.23), channel_id=1, source_target_pairs={{0,16},{2,18},{4,20},{6,22},{8,24},{10,26},{12,28},{14,30},{16,0},... | collective-permute-start | bytes 49160 | tf_op jit(solution)/shard_map/ppermute | solution.py:154
  192.7 2.2 %collective-permute-start.24 = (bf16[4,1,2048]{2,0,1:T(4,128)(2,1)S(1)}, bf16[4,1,2048]{2,0,1:T(4,128)(2,1)S(1)}, u32[]{:S(2)}, u32[]{:S(2)}) collective-permute-start(bf16[4,1,2048]{2,0,1:T(4,128)(2,1)S(1)} %reshape.23), channel_id=1, source_target_pairs={{0,24},{2,26},{4,28},{6,30},{8,16},{10,18},{12,20},{14,22},{16,8},... | collective-permute-start | bytes 49160 | tf_op jit(solution)/shard_map/ppermute | solution.py:154
  194.9 6.5 %attention.7 = (bf16[256,2048]{1,0:T(8,128)(2,1)}, bf16[1,1024]{1,0:T(2,128)(2,1)}) custom-call(s32[3]{0:T(128)} %copy-done.11, f32[128,1024]{1,0:T(8,128)} %copy-done.10, bf16[128,1024]{1,0:T(8,128)(2,1)} %collective-permute-done.17.qc_ref, bf16[1792,512]{1,0:T(8,128)(2,1)} %kc_ref.7, bf16[1792,512]{1,0:T(8,128)(2,1)} %vc_ref.7, ...), custom_call_target="tpu_custom_call", output_to_operand_aliasing={{0}: (9, {})} | custom-call | bytes 1024 | tf_op jit(solution)/shard_map/attention/pallas_call | solution.py:109
  (117 shorter events, 35.4 us)
Async XLA Ops:
  7.2 39.9 %all-gather.4.cloned.1.call-start = ((), (), s32[]{:S(2)}) async-start(), calls=%async_computation | async-start | bytes 5242880 | tf_op jit(solution)/shard_map/all_gather | solution.py:184
  9.7 74.2 %all-gather.6.cloned.1.call-start = ((), (), s32[]{:S(2)}) async-start(), calls=%async_computation.1 | async-start | bytes 5242880 | tf_op jit(solution)/shard_map/all_gather | solution.py:184
  11.4 15.2 %collective-permute-start.1 = (bf16[256,1024]{1,0:T(8,128)(2,1)}, bf16[256,1024]{1,0:T(8,128)(2,1)}, u32[]{:S(2)}, u32[]{:S(2)}) collective-permute-start(bf16[256,1024]{1,0:T(8,128)(2,1)} %pad_maximum_fusion.1), channel_id=1, source_target_pairs={{0,1},{1,0},{2,3},{3,2},{4,5},{5,4},{6,7},{7,6},{8,9},{9,8},{10,11... | collective-permute-start | bytes 1572872 | tf_op jit(solution)/shard_map/ppermute | solution.py:160
  30.4 89.4 %all-gather.8.cloned.1.call-start = ((), (), s32[]{:S(2)}) async-start(), calls=%async_computation.2 | async-start | bytes 5242880 | tf_op jit(solution)/shard_map/all_gather | solution.py:184
  31.4 14.2 %collective-permute-start.3 = (bf16[256,1024]{1,0:T(8,128)(2,1)S(1)}, bf16[256,1024]{1,0:T(8,128)(2,1)S(1)}, u32[]{:S(2)}, u32[]{:S(2)}) collective-permute-start(bf16[256,1024]{1,0:T(8,128)(2,1)S(1)} %copy-done.18), channel_id=1, source_target_pairs={{0,8},{2,10},{4,12},{6,14},{8,0},{10,2},{12,4},{14,6},{16,24},{18,... | collective-permute-start | bytes 1572872 | tf_op jit(solution)/shard_map/ppermute | solution.py:154
  33.2 24.6 %collective-permute-start.2 = (bf16[256,1024]{1,0:T(8,128)(2,1)S(1)}, bf16[256,1024]{1,0:T(8,128)(2,1)S(1)}, u32[]{:S(2)}, u32[]{:S(2)}) collective-permute-start(bf16[256,1024]{1,0:T(8,128)(2,1)S(1)} %copy-done.17), channel_id=1, source_target_pairs={{0,24},{2,26},{4,28},{6,30},{8,16},{10,18},{12,20},{14,22},{16,8},... | collective-permute-start | bytes 1572872 | tf_op jit(solution)/shard_map/ppermute | solution.py:154
  35.7 23.6 %collective-permute-start = (bf16[256,1024]{1,0:T(8,128)(2,1)S(1)}, bf16[256,1024]{1,0:T(8,128)(2,1)}, u32[]{:S(2)}, u32[]{:S(2)}) collective-permute-start(bf16[256,1024]{1,0:T(8,128)(2,1)S(1)} %copy-done.16), channel_id=1, source_target_pairs={{0,1},{1,0},{2,3},{3,2},{4,5},{5,4},{6,7},{7,6},{8,9},{9,8},{10,11... | collective-permute-start | bytes 1572872 | tf_op jit(solution)/shard_map/ppermute | solution.py:160
  45.6 17.0 %collective-permute-start.5 = (bf16[256,1024]{1,0:T(8,128)(2,1)S(1)}, bf16[256,1024]{1,0:T(8,128)(2,1)S(1)}, u32[]{:S(2)}, u32[]{:S(2)}) collective-permute-start(bf16[256,1024]{1,0:T(8,128)(2,1)S(1)} %collective-permute-done.3), channel_id=1, source_target_pairs={{0,1},{1,0},{2,3},{3,2},{4,5},{5,4},{6,7},{7,6},{8,9},{9,8},{10,11... | collective-permute-start | bytes 1572872 | tf_op jit(solution)/shard_map/ppermute | solution.py:160
  57.9 12.6 %collective-permute-start.4 = (bf16[256,1024]{1,0:T(8,128)(2,1)S(1)}, bf16[256,1024]{1,0:T(8,128)(2,1)S(1)}, u32[]{:S(2)}, u32[]{:S(2)}) collective-permute-start(bf16[256,1024]{1,0:T(8,128)(2,1)S(1)} %collective-permute-done.2), channel_id=1, source_target_pairs={{0,1},{1,0},{2,3},{3,2},{4,5},{5,4},{6,7},{7,6},{8,9},{9,8},{10,11... | collective-permute-start | bytes 1572872 | tf_op jit(solution)/shard_map/ppermute | solution.py:160
  60.8 22.7 %collective-permute-start.7 = (bf16[256,1024]{1,0:T(8,128)(2,1)S(1)}, bf16[256,1024]{1,0:T(8,128)(2,1)}, u32[]{:S(2)}, u32[]{:S(2)}) collective-permute-start(bf16[256,1024]{1,0:T(8,128)(2,1)S(1)} %get-tuple-element.77), channel_id=1, source_target_pairs={{0,16},{2,18},{4,20},{6,22},{8,24},{10,26},{12,28},{14,30},{16,0},... | collective-permute-start | bytes 1572872 | tf_op jit(solution)/shard_map/ppermute | solution.py:154
  65.1 27.4 %collective-permute-start.9 = (bf16[256,1024]{1,0:T(8,128)(2,1)}, bf16[256,1024]{1,0:T(8,128)(2,1)}, u32[]{:S(2)}, u32[]{:S(2)}) collective-permute-start(bf16[256,1024]{1,0:T(8,128)(2,1)} %convolution_convert_fusion.3), channel_id=1, source_target_pairs={{0,8},{2,10},{4,12},{6,14},{8,0},{10,2},{12,4},{14,6},{16,24},{18,... | collective-permute-start | bytes 1572872 | tf_op jit(solution)/shard_map/ppermute | solution.py:154
  70.8 48.9 %copy-start.6 = (bf16[256,2048]{1,0:T(8,128)(2,1)}, bf16[256,2048]{1,0:T(8,128)(2,1)S(1)}, u32[]{:S(2)}) copy-start(bf16[256,2048]{1,0:T(8,128)(2,1)S(1)} %maximum_select_fusion.1.high_ref) | copy-start | bytes 3145732
  72.9 29.4 %collective-permute-start.10 = (bf16[256,1024]{1,0:T(8,128)(2,1)}, bf16[256,1024]{1,0:T(8,128)(2,1)}, u32[]{:S(2)}, u32[]{:S(2)}) collective-permute-start(bf16[256,1024]{1,0:T(8,128)(2,1)} %convolution_convert_fusion.2), channel_id=1, source_target_pairs={{0,8},{2,10},{4,12},{6,14},{8,0},{10,2},{12,4},{14,6},{16,24},{18,... | collective-permute-start | bytes 1572872 | tf_op jit(solution)/shard_map/ppermute | solution.py:154
  73.6 18.0 %collective-permute-start.6 = (bf16[256,1024]{1,0:T(8,128)(2,1)S(1)}, bf16[256,1024]{1,0:T(8,128)(2,1)S(1)}, u32[]{:S(2)}, u32[]{:S(2)}) collective-permute-start(bf16[256,1024]{1,0:T(8,128)(2,1)S(1)} %get-tuple-element.83), channel_id=1, source_target_pairs={{0,1},{1,0},{2,3},{3,2},{4,5},{5,4},{6,7},{7,6},{8,9},{9,8},{10,11... | collective-permute-start | bytes 1572872 | tf_op jit(solution)/shard_map/ppermute | solution.py:160
  83.5 18.9 %collective-permute-start.8 = (bf16[256,1024]{1,0:T(8,128)(2,1)}, bf16[256,1024]{1,0:T(8,128)(2,1)}, u32[]{:S(2)}, u32[]{:S(2)}) collective-permute-start(bf16[256,1024]{1,0:T(8,128)(2,1)} %collective-permute-done.7), channel_id=1, source_target_pairs={{0,1},{1,0},{2,3},{3,2},{4,5},{5,4},{6,7},{7,6},{8,9},{9,8},{10,11... | collective-permute-start | bytes 1572872 | tf_op jit(solution)/shard_map/ppermute | solution.py:160
  88.3 53.0 %collective-permute-start.13 = (bf16[256,1024]{1,0:T(8,128)(2,1)}, bf16[256,1024]{1,0:T(8,128)(2,1)}, u32[]{:S(2)}, u32[]{:S(2)}) collective-permute-start(bf16[256,1024]{1,0:T(8,128)(2,1)} %convolution_convert_fusion), channel_id=1, source_target_pairs={{0,8},{2,10},{4,12},{6,14},{8,0},{10,2},{12,4},{14,6},{16,24},{18,... | collective-permute-start | bytes 1572872 | tf_op jit(solution)/shard_map/ppermute | solution.py:154
  91.7 49.7 %collective-permute-start.14 = (bf16[256,1024]{1,0:T(8,128)(2,1)}, bf16[256,1024]{1,0:T(8,128)(2,1)}, u32[]{:S(2)}, u32[]{:S(2)}) collective-permute-start(bf16[256,1024]{1,0:T(8,128)(2,1)} %convolution_convert_fusion.1), channel_id=1, source_target_pairs={{0,8},{2,10},{4,12},{6,14},{8,0},{10,2},{12,4},{14,6},{16,24},{18,... | collective-permute-start | bytes 1572872 | tf_op jit(solution)/shard_map/ppermute | solution.py:154
  107.8 39.0 %collective-permute-start.12 = (bf16[256,1024]{1,0:T(8,128)(2,1)}, bf16[256,1024]{1,0:T(8,128)(2,1)S(1)}, u32[]{:S(2)}, u32[]{:S(2)}) collective-permute-start(bf16[256,1024]{1,0:T(8,128)(2,1)} %add_convert_fusion.1), channel_id=1, source_target_pairs={{0,16},{2,18},{4,20},{6,22},{8,24},{10,26},{12,28},{14,30},{16,0},... | collective-permute-start | bytes 1572872 | tf_op jit(solution)/shard_map/ppermute | solution.py:154
  123.7 20.1 %copy-start.15 = (bf16[256,1024]{1,0:T(8,128)(2,1)S(1)}, bf16[256,1024]{1,0:T(8,128)(2,1)}, u32[]{:S(2)}) copy-start(bf16[256,1024]{1,0:T(8,128)(2,1)} %copy-done.14) | copy-start | bytes 1572868
  123.7 25.6 %collective-permute-start.11 = (bf16[256,1024]{1,0:T(8,128)(2,1)S(1)}, bf16[256,1024]{1,0:T(8,128)(2,1)S(1)}, u32[]{:S(2)}, u32[]{:S(2)}) collective-permute-start(bf16[256,1024]{1,0:T(8,128)(2,1)S(1)} %half_product.4), channel_id=1, source_target_pairs={{0,8},{2,10},{4,12},{6,14},{8,0},{10,2},{12,4},{14,6},{16,24},{18,... | collective-permute-start | bytes 1572872 | tf_op jit(solution)/shard_map/ppermute | solution.py:154
  144.2 18.1 %collective-permute-start.16 = (bf16[256,1024]{1,0:T(8,128)(2,1)S(1)}, bf16[256,1024]{1,0:T(8,128)(2,1)S(1)}, u32[]{:S(2)}, u32[]{:S(2)}) collective-permute-start(bf16[256,1024]{1,0:T(8,128)(2,1)S(1)} %add_convert_fusion), channel_id=1, source_target_pairs={{0,16},{2,18},{4,20},{6,22},{8,24},{10,26},{12,28},{14,30},{16,0},... | collective-permute-start | bytes 1572872 | tf_op jit(solution)/shard_map/ppermute | solution.py:154
  146.7 29.9 %copy-start = (f32[256,1024]{1,0:T(8,128)}, f32[256,1024]{1,0:T(8,128)S(1)}, u32[]{:S(2)}) copy-start(f32[256,1024]{1,0:T(8,128)S(1)} %convolution_add_fusion.1.km_ref.vm_ref) | copy-start | bytes 3145732
  146.8 29.8 %copy-start.3 = (bf16[256,1024]{1,0:T(8,128)(2,1)}, bf16[256,1024]{1,0:T(8,128)(2,1)S(1)}, u32[]{:S(2)}) copy-start(bf16[256,1024]{1,0:T(8,128)(2,1)S(1)} %collective-permute-done.12.kt_ref.vt_ref) | copy-start | bytes 1572868
  152.9 21.2 %collective-permute-start.15 = (bf16[256,1024]{1,0:T(8,128)(2,1)S(1)}, bf16[256,1024]{1,0:T(8,128)(2,1)S(1)}, u32[]{:S(2)}, u32[]{:S(2)}) collective-permute-start(bf16[256,1024]{1,0:T(8,128)(2,1)S(1)} %half_product.6), channel_id=1, source_target_pairs={{0,8},{2,10},{4,12},{6,14},{8,0},{10,2},{12,4},{14,6},{16,24},{18,... | collective-permute-start | bytes 1572872 | tf_op jit(solution)/shard_map/ppermute | solution.py:154
  153.1 23.5 %collective-permute-start.18 = (bf16[128,1024]{1,0:T(8,128)(2,1)S(1)}, bf16[128,1024]{1,0:T(8,128)(2,1)S(1)}, u32[]{:S(2)}, u32[]{:S(2)}) collective-permute-start(bf16[128,1024]{1,0:T(8,128)(2,1)S(1)} %get-tuple-element.104), channel_id=1, source_target_pairs={{0,16},{2,18},{4,20},{6,22},{8,24},{10,26},{12,28},{14,30},{16,0},... | collective-permute-start | bytes 786440 | tf_op jit(solution)/shard_map/ppermute | solution.py:154
  176.6 13.2 %collective-permute-start.17 = (bf16[128,1024]{1,0:T(8,128)(2,1)}, bf16[128,1024]{1,0:T(8,128)(2,1)}, u32[]{:S(2)}, u32[]{:S(2)}) collective-permute-start(bf16[128,1024]{1,0:T(8,128)(2,1)} %get-tuple-element.118), channel_id=1, source_target_pairs={{0,16},{2,18},{4,20},{6,22},{8,24},{10,26},{12,28},{14,30},{16,0},... | collective-permute-start | bytes 786440 | tf_op jit(solution)/shard_map/ppermute | solution.py:154
  182.3 7.5 %collective-permute-start.19 = (bf16[1,2048]{1,0:T(2,128)(2,1)S(1)}, bf16[1,2048]{1,0:T(2,128)(2,1)S(1)}, u32[]{:S(2)}, u32[]{:S(2)}) collective-permute-start(bf16[1,2048]{1,0:T(2,128)(2,1)S(1)} %pad_maximum_fusion.7), channel_id=1, source_target_pairs={{0,2},{2,0},{4,6},{6,4},{8,10},{10,8},{12,14},{14,12},{16,18},{18,... | collective-permute-start | bytes 12296 | tf_op jit(solution)/shard_map/ppermute | solution.py:154
  182.4 7.4 %collective-permute-start.20 = (bf16[1,2048]{1,0:T(2,128)(2,1)S(1)}, bf16[1,2048]{1,0:T(2,128)(2,1)S(1)}, u32[]{:S(2)}, u32[]{:S(2)}) collective-permute-start(bf16[1,2048]{1,0:T(2,128)(2,1)S(1)} %pad_maximum_fusion.7), channel_id=1, source_target_pairs={{0,4},{2,6},{4,0},{6,2},{8,12},{10,14},{12,8},{14,10},{16,20},{18,... | collective-permute-start | bytes 12296 | tf_op jit(solution)/shard_map/ppermute | solution.py:154
  183.8 6.0 %collective-permute-start.21 = (bf16[1,2048]{1,0:T(2,128)(2,1)S(1)}, bf16[1,2048]{1,0:T(2,128)(2,1)S(1)}, u32[]{:S(2)}, u32[]{:S(2)}) collective-permute-start(bf16[1,2048]{1,0:T(2,128)(2,1)S(1)} %pad_maximum_fusion.7), channel_id=1, source_target_pairs={{0,6},{2,4},{4,2},{6,0},{8,14},{10,12},{12,10},{14,8},{16,22},{18,... | collective-permute-start | bytes 12296 | tf_op jit(solution)/shard_map/ppermute | solution.py:154
  190.4 11.0 %collective-permute-start.22 = (bf16[4,1,2048]{2,0,1:T(4,128)(2,1)S(1)}, bf16[4,1,2048]{2,0,1:T(4,128)(2,1)S(1)}, u32[]{:S(2)}, u32[]{:S(2)}) collective-permute-start(bf16[4,1,2048]{2,0,1:T(4,128)(2,1)S(1)} %reshape.23), channel_id=1, source_target_pairs={{0,8},{2,10},{4,12},{6,14},{8,0},{10,2},{12,4},{14,6},{16,24},{18,... | collective-permute-start | bytes 49160 | tf_op jit(solution)/shard_map/ppermute | solution.py:154
  190.5 10.9 %collective-permute-start.23 = (bf16[4,1,2048]{2,0,1:T(4,128)(2,1)S(1)}, bf16[4,1,2048]{2,0,1:T(4,128)(2,1)S(1)}, u32[]{:S(2)}, u32[]{:S(2)}) collective-permute-start(bf16[4,1,2048]{2,0,1:T(4,128)(2,1)S(1)} %reshape.23), channel_id=1, source_target_pairs={{0,16},{2,18},{4,20},{6,22},{8,24},{10,26},{12,28},{14,30},{16,0},... | collective-permute-start | bytes 49160 | tf_op jit(solution)/shard_map/ppermute | solution.py:154
  192.7 8.8 %collective-permute-start.24 = (bf16[4,1,2048]{2,0,1:T(4,128)(2,1)S(1)}, bf16[4,1,2048]{2,0,1:T(4,128)(2,1)S(1)}, u32[]{:S(2)}, u32[]{:S(2)}) collective-permute-start(bf16[4,1,2048]{2,0,1:T(4,128)(2,1)S(1)} %reshape.23), channel_id=1, source_target_pairs={{0,24},{2,26},{4,28},{6,30},{8,16},{10,18},{12,20},{14,22},{16,8},... | collective-permute-start | bytes 49160 | tf_op jit(solution)/shard_map/ppermute | solution.py:154
  (20 other events, 159.2 us)
Sparse Core Ops, SparseCore 0:
  9.8 37.1 all-gather.3
  49.2 34.4 all-gather.5
  85.3 34.4 all-gather.7

commit v9 on v8

--- a/solution.py
+++ b/solution.py
@@ -285,6 +285,7 @@
     def later_sends(h, name, come):
         weight = weights[name]
         arrived(0)
+        arrived(2)
         if fast and h is not None:
             send, keep = half_product(tokens[0][0], tokens[2][0], h, weight, step(come))
             send, keep = step(send, keep)
@@ -292,7 +293,6 @@
         if h is None:
             bits = list(come)
             come = dict(zip(bits, step(*[come[b] for b in bits])))
-            arrived(2)
         else:
             whole = step(next(iter(come.values()))[0])
             come = {b: whole[i * half : (i + 1) * half] for b, (_, i) in come.items()}
@@ -359,13 +359,13 @@
         weights[1] = step(weights[1])
         start(2)
         advance(1)
+        start(3)
         arrive(0)
         advance(2)
-        start(3)
         arrive(1)
         attention(1, 0)
+        advance(3)
         attention(1, 1)
-        advance(3)
         arrive(2)
         attention(2, 0)
         row = jnp.concatenate([lasts[0] + lasts[1], lasts[2]], axis=1)

time: 209 us -> 210 us (level)
    ppermute x19, waiting for transfers between devices: 66.7 us -> 61.7 us  [over_inst(): return lax.ppermute(value, 'inst', [(i, i ^ bits) for i in range(n_inst)])]
    ppermute x6, waiting for transfers between devices: 15.7 us -> 19.3 us  [over_tp(): return lax.ppermute(value, 'tp', [(0, 1), (1, 0)])]
  transfers between devices with their start and end apart: 28 -> 28, of which waited for: 12 -> 14; matrix products, arithmetic and copies ran while one was open for 15% -> 15% of each run, Pallas kernels for 15% -> 15%
where the time goes in v9:
time: 210 us
  waiting for transfers between devices  91.9 us (44%)
  starting transfers between devices  32.7 us (16%)
  Pallas kernels  30.8 us (15%)
  matrix products  20.8 us (10%)
  between operations  14.9 us (7%)
  other arithmetic  12.4 us (6%)
  local copies, waits for them, and re-layouts  6.44 us (3%)
    ppermute x19, waiting for transfers between devices, over_inst(): return lax.ppermute(value, 'inst', [(i, i ^ bits) for i in range(n_inst)])  61.7 us
    ppermute x19, starting transfers between devices, over_inst(): return lax.ppermute(value, 'inst', [(i, i ^ bits) for i in range(n_inst)])  23.1 us
    pallas_call x4, Pallas kernels, attend(): pl.pallas_call(attention_kernel, grid_spec=pltpu.PrefetchScalarGridSpec(n...  23 us
    dot_general x8, matrix products, dot(): return jnp.dot(a, b, preferred_element_type=jnp.float32)  20.8 us
    ppermute x6, waiting for transfers between devices, over_tp(): return lax.ppermute(value, 'tp', [(0, 1), (1, 0)])  19.3 us
    all_gather x3, waiting for transfers between devices, group_gather(): lax.all_gather(value, 'inst', axis=0, tiled=True, axis_index_groups=groups)  10.3 us
    ppermute x6, starting transfers between devices, over_tp(): return lax.ppermute(value, 'tp', [(0, 1), (1, 0)])  9.42 us
    pallas_call x4, Pallas kernels, half_product(): pl.pallas_call(first_kernel if first else later_kernel, grid=(columns //...  7.78 us
  transfers between devices with their start and end apart: 28, of which 14 were waited for; matrix products, arithmetic and copies ran while one was open for 15% of the time, Pallas kernels for 15%

profile of v9, /device:TPU:0, one launch (start us, length us, event | category | flops | bytes accessed | tf_op | source)
XLA Modules:
  0.0 209.9 jit_solution(11857339236413671368)
XLA Ops:
  7.2 2.4 %pad_maximum_fusion = bf16[512,1024]{1,0:T(8,128)(2,1)} fusion(bf16[512,512]{1,0:T(8,128)(2,1)} %param.10, bf16[512,512]{1,0:T(8,128)(2,1)} %param.9), kind=kLoop, calls=%fused_computation.6 | loop fusion | flops 2097152 | bytes 2097152 | tf_op jit(solution)/shard_map/concatenate | solution.py:188
  11.4 2.9 %collective-permute-start.1 = (bf16[256,1024]{1,0:T(8,128)(2,1)}, bf16[256,1024]{1,0:T(8,128)(2,1)}, u32[]{:S(2)}, u32[]{:S(2)}) collective-permute-start(bf16[256,1024]{1,0:T(8,128)(2,1)} %pad_maximum_fusion.1), channel_id=1, source_target_pairs={{0,1},{1,0},{2,3},{3,2},{4,5},{5,4},{6,7},{7,6},{8,9},{9,8},{10,11... | collective-permute-start | bytes 1572872 | tf_op jit(solution)/shard_map/ppermute | solution.py:160
  15.3 11.2 %collective-permute-done.1 = bf16[256,1024]{1,0:T(8,128)(2,1)} collective-permute-done((bf16[256,1024]{1,0:T(8,128)(2,1)}, bf16[256,1024]{1,0:T(8,128)(2,1)}, u32[]{:S(2)}, u32[]{:S(2)}) %collective-permute-start.1) | collective-permute-done | bytes 524320 | tf_op jit(solution)/shard_map/ppermute | solution.py:160
  26.5 2.3 %broadcast_select_fusion.1 = (bf16[256,1024]{1,0:T(8,128)(2,1)}, bf16[256,1024]{1,0:T(8,128)(2,1)}) fusion(bf16[256,1024]{1,0:T(8,128)(2,1)} %collective-permute-done.1, pred[]{:T(512)S(6)} %eq.37, bf16[128,1024]{1,0:T(8,128)(2,1)S(1)} %get-tuple-element.135, bf16[128,1024]{1,0:T(8,128)(2,1)S(1)} %get-tuple-element.136, pred[]{:T(512)S(6)} %eq.36), kind=kLoop, calls=%fused_computation.18 | loop fusion | flops 1572864 | bytes 2097154 | tf_op jit(solution)/shard_map/jit(_where)/select_n | solution.py:216
  33.0 2.5 %collective-permute-start.2 = (bf16[256,1024]{1,0:T(8,128)(2,1)S(1)}, bf16[256,1024]{1,0:T(8,128)(2,1)S(1)}, u32[]{:S(2)}, u32[]{:S(2)}) collective-permute-start(bf16[256,1024]{1,0:T(8,128)(2,1)S(1)} %copy-done.17), channel_id=1, source_target_pairs={{0,24},{2,26},{4,28},{6,30},{8,16},{10,18},{12,20},{14,22},{16,8},... | collective-permute-start | bytes 1572872 | tf_op jit(solution)/shard_map/ppermute | solution.py:154
  37.0 8.7 %collective-permute-done.3 = bf16[256,1024]{1,0:T(8,128)(2,1)S(1)} collective-permute-done((bf16[256,1024]{1,0:T(8,128)(2,1)}, bf16[256,1024]{1,0:T(8,128)(2,1)S(1)}, u32[]{:S(2)}, u32[]{:S(2)}) %collective-permute-start.3) | collective-permute-done | bytes 524320 | tf_op jit(solution)/shard_map/ppermute | solution.py:154
  47.3 10.5 %collective-permute-done.2 = bf16[256,1024]{1,0:T(8,128)(2,1)S(1)} collective-permute-done((bf16[256,1024]{1,0:T(8,128)(2,1)S(1)}, bf16[256,1024]{1,0:T(8,128)(2,1)S(1)}, u32[]{:S(2)}, u32[]{:S(2)}) %collective-permute-start.2) | collective-permute-done | bytes 524320 | tf_op jit(solution)/shard_map/ppermute | solution.py:154
  64.1 2.1 convolution_convert_fusion.3
  67.3 3.0 %collective-permute-done.4 = bf16[256,1024]{1,0:T(8,128)(2,1)S(1)} collective-permute-done((bf16[256,1024]{1,0:T(8,128)(2,1)S(1)}, bf16[256,1024]{1,0:T(8,128)(2,1)S(1)}, u32[]{:S(2)}, u32[]{:S(2)}) %collective-permute-start.4) | collective-permute-done | bytes 524320 | tf_op jit(solution)/shard_map/ppermute | solution.py:160
  70.7 2.1 convolution_convert_fusion.2
  74.9 8.6 %collective-permute-done.7 = bf16[256,1024]{1,0:T(8,128)(2,1)} collective-permute-done((bf16[256,1024]{1,0:T(8,128)(2,1)S(1)}, bf16[256,1024]{1,0:T(8,128)(2,1)}, u32[]{:S(2)}, u32[]{:S(2)}) %collective-permute-start.7) | collective-permute-done | bytes 524320 | tf_op jit(solution)/shard_map/ppermute | solution.py:154
  84.0 4.4 %convolution_convert_fusion = bf16[256,1024]{1,0:T(8,128)(2,1)} fusion(bf16[256,2048]{1,0:T(8,128)(2,1)S(1)} %maximum_select_fusion.low_ref, bf16[2048,1024]{1,0:T(8,128)(2,1)} %all-gather.6.cloned.1.call-done), kind=kOutput, calls=%fused_computation.2 | convolution fusion | flops 1074003968 | bytes 5767168 | tf_op jit(solution)/shard_map/dot_general | solution.py:16
  89.0 2.1 convolution_convert_fusion.1
  92.5 5.1 %collective-permute-done.8 = bf16[256,1024]{1,0:T(8,128)(2,1)} collective-permute-done((bf16[256,1024]{1,0:T(8,128)(2,1)}, bf16[256,1024]{1,0:T(8,128)(2,1)}, u32[]{:S(2)}, u32[]{:S(2)}) %collective-permute-start.8) | collective-permute-done | bytes 524320 | tf_op jit(solution)/shard_map/ppermute | solution.py:160
  97.6 1.9 maximum_select_fusion.3.high_ref
  99.5 3.4 %collective-permute-done.10 = bf16[256,1024]{1,0:T(8,128)(2,1)} collective-permute-done((bf16[256,1024]{1,0:T(8,128)(2,1)}, bf16[256,1024]{1,0:T(8,128)(2,1)}, u32[]{:S(2)}, u32[]{:S(2)}) %collective-permute-start.10) | collective-permute-done | bytes 524320 | tf_op jit(solution)/shard_map/ppermute | solution.py:154
  102.9 3.1 %add_convert_fusion.1 = bf16[256,1024]{1,0:T(8,128)(2,1)} fusion(bf16[256,1024]{1,0:T(8,128)(2,1)} %collective-permute-done.10, bf16[256,2048]{1,0:T(8,128)(2,1)S(1)} %maximum_select_fusion.3.high_ref, bf16[2048,1024]{1,0:T(8,128)(2,1)S(1)} %copy-done.20), kind=kOutput, calls=%fused_computation.12 | convolution fusion | flops 1074528256 | bytes 6291456 | tf_op jit(solution)/shard_map/dot_general | solution.py:16
  106.1 3.4 %collective-permute-start.16 = (bf16[256,1024]{1,0:T(8,128)(2,1)}, bf16[256,1024]{1,0:T(8,128)(2,1)S(1)}, u32[]{:S(2)}, u32[]{:S(2)}) collective-permute-start(bf16[256,1024]{1,0:T(8,128)(2,1)} %add_convert_fusion.1), channel_id=1, source_target_pairs={{0,16},{2,18},{4,20},{6,22},{8,24},{10,26},{12,28},{14,30},{16,0},... | collective-permute-start | bytes 1572872 | tf_op jit(solution)/shard_map/ppermute | solution.py:154
  109.5 10.3 %all-gather.8.cloned.1.call-done.w_ref = bf16[2048,1024]{1,0:T(8,128)(2,1)} async-done(((bf16[512,1024]{1,0:T(8,128)(2,1)}), bf16[2048,1024]{1,0:T(8,128)(2,1)}) %all-gather.8.cloned.1.call-update) | async-done | bytes 4194320 | tf_op jit(solution)/shard_map/all_gather | solution.py:184
  119.8 2.2 %copy-done.1 = bf16[2048,1024]{1,0:T(8,128)(2,1)S(1)} copy-done((bf16[2048,1024]{1,0:T(8,128)(2,1)S(1)}, bf16[2048,1024]{1,0:T(8,128)(2,1)}, u32[]{:S(2)}) %copy-start.1) | copy-done | bytes 4194328
  126.5 15.4 %collective-permute-done.12 = bf16[256,1024]{1,0:T(8,128)(2,1)} collective-permute-done((bf16[256,1024]{1,0:T(8,128)(2,1)}, bf16[256,1024]{1,0:T(8,128)(2,1)}, u32[]{:S(2)}, u32[]{:S(2)}) %collective-permute-start.12) | collective-permute-done | bytes 524320 | tf_op jit(solution)/shard_map/ppermute | solution.py:154
  141.8 2.3 %add_convert_fusion = bf16[256,1024]{1,0:T(8,128)(2,1)S(1)} fusion(bf16[256,1024]{1,0:T(8,128)(2,1)} %collective-permute-done.12, bf16[256,2048]{1,0:T(8,128)(2,1)S(1)} %maximum_select_fusion.3.high_ref, bf16[2048,1024]{1,0:T(8,128)(2,1)S(1)} %copy-done.23), kind=kOutput, calls=%fused_computation.11 | convolution fusion | flops 1074528256 | bytes 6291456 | tf_op jit(solution)/shard_map/dot_general | solution.py:16
  147.6 2.3 %convolution_add_fusion.km_ref.vm_ref = f32[256,1024]{1,0:T(8,128)S(1)} fusion(bf16[256,2048]{1,0:T(8,128)(2,1)S(1)} %maximum_select_fusion.2.low_ref, bf16[2048,1024]{1,0:T(8,128)(2,1)S(1)} %copy-done.21, bf16[256,1024]{1,0:T(8,128)(2,1)} %collective-permute-done.9), kind=kOutput, calls=%fused_computation | convolution fusion | flops 1074266112 | bytes 6815744 | tf_op jit(solution)/shard_map/dot_general | solution.py:16
  149.9 7.4 %collective-permute-done.15.came_ref = bf16[256,1024]{1,0:T(8,128)(2,1)S(1)} collective-permute-done((bf16[256,1024]{1,0:T(8,128)(2,1)S(1)}, bf16[256,1024]{1,0:T(8,128)(2,1)S(1)}, u32[]{:S(2)}, u32[]{:S(2)}) %collective-permute-start.15) | collective-permute-done | bytes 524320 | tf_op jit(solution)/shard_map/ppermute | solution.py:154
  159.3 2.4 %convolution_add_fusion.1.qm_ref = f32[256,1024]{1,0:T(8,128)S(1)} fusion(bf16[256,2048]{1,0:T(8,128)(2,1)S(1)} %maximum_select_fusion.2.low_ref, bf16[2048,1024]{1,0:T(8,128)(2,1)S(1)} %copy-done.23, bf16[256,1024]{1,0:T(8,128)(2,1)} %collective-permute-done.11), kind=kOutput, calls=%fused_computation.1 | convolution fusion | flops 1074266112 | bytes 6815744 | tf_op jit(solution)/shard_map/dot_general | solution.py:16
  161.7 3.5 %collective-permute-done.14.qc_ref = bf16[256,1024]{1,0:T(8,128)(2,1)S(1)} collective-permute-done((bf16[256,1024]{1,0:T(8,128)(2,1)S(1)}, bf16[256,1024]{1,0:T(8,128)(2,1)S(1)}, u32[]{:S(2)}, u32[]{:S(2)}) %collective-permute-start.14) | collective-permute-done | bytes 524320 | tf_op jit(solution)/shard_map/ppermute | solution.py:154
  165.3 5.4 %attention.4 = (bf16[256,2048]{1,0:T(8,128)(2,1)}, bf16[1,1024]{1,0:T(2,128)(2,1)S(1)}) custom-call(s32[3]{0:T(128)S(1)} %get-tuple-element.147.place_ref, f32[256,1024]{1,0:T(8,128)S(1)} %convolution_add_fusion.1.qm_ref, bf16[256,1024]{1,0:T(8,128)(2,1)S(1)} %collective-permute-done.14.qc_ref, bf16[1792,512]{1,0:T(8,128)(2,1)S(1)} %copy-done.4, ...), custom_call_target="tpu_custom_call" | custom-call | bytes 1024 | tf_op jit(solution)/shard_map/attention/pallas_call | solution.py:109
  172.2 2.5 %half_product.7 = (bf16[128,1024]{1,0:T(8,128)(2,1)}, f32[128,1024]{1,0:T(8,128)S(1)}) custom-call(bf16[256,2048]{1,0:T(8,128)(2,1)S(1)} %maximum_select_fusion.2.low_ref, bf16[256,2048]{1,0:T(8,128)(2,1)S(1)} %copy-done.7, bf16[2048,1024]{1,0:T(8,128)(2,1)S(1)} %copy-done.2, bf16[256,1024]{1,0:T(8,128)(2,1)S(1)} %collective-permute-done.13.came_ref), custom_call_target="tpu_custom_call" | custom-call | bytes 1024 | tf_op jit(solution)/shard_map/half_product/pallas_call | solution.py:42
  174.8 5.4 %attention.5 = (bf16[256,2048]{1,0:T(8,128)(2,1)}, bf16[1,1024]{1,0:T(2,128)(2,1)S(1)}) custom-call(s32[3]{0:T(128)S(1)} %get-tuple-element.146.place_ref, f32[256,1024]{1,0:T(8,128)S(1)} %convolution_add_fusion.1.qm_ref, bf16[256,1024]{1,0:T(8,128)(2,1)S(1)} %collective-permute-done.14.qc_ref, ...), custom_call_target="tpu_custom_call", output_to_operand_aliasing={{0}: (9, {})} | custom-call | bytes 1024 | tf_op jit(solution)/shard_map/attention/pallas_call | solution.py:109
  180.2 5.7 %attention.6 = (bf16[256,2048]{1,0:T(8,128)(2,1)}, bf16[1,1024]{1,0:T(2,128)(2,1)S(1)}) custom-call(s32[3]{0:T(128)S(1)} %get-tuple-element.147.place_ref, f32[128,1024]{1,0:T(8,128)S(1)} %get-tuple-element.121.qm_ref, bf16[128,1024]{1,0:T(8,128)(2,1)S(1)} %collective-permute-done.18.qc_ref, ...), custom_call_target="tpu_custom_call", output_to_operand_aliasing={{0}: (9, {})} | custom-call | bytes 1024 | tf_op jit(solution)/shard_map/attention/pallas_call | solution.py:109
  191.2 2.4 %collective-permute-start.22 = (bf16[4,1,2048]{2,0,1:T(4,128)(2,1)S(1)}, bf16[4,1,2048]{2,0,1:T(4,128)(2,1)S(1)}, u32[]{:S(2)}, u32[]{:S(2)}) collective-permute-start(bf16[4,1,2048]{2,0,1:T(4,128)(2,1)S(1)} %reshape.23), channel_id=1, source_target_pairs={{0,8},{2,10},{4,12},{6,14},{8,0},{10,2},{12,4},{14,6},{16,24},{18,... | collective-permute-start | bytes 49160 | tf_op jit(solution)/shard_map/ppermute | solution.py:154
  196.0 6.5 %attention.7 = (bf16[256,2048]{1,0:T(8,128)(2,1)}, bf16[1,1024]{1,0:T(2,128)(2,1)}) custom-call(s32[3]{0:T(128)} %copy-done.11, f32[128,1024]{1,0:T(8,128)} %copy-done.10, bf16[128,1024]{1,0:T(8,128)(2,1)} %copy-done.18, bf16[1792,512]{1,0:T(8,128)(2,1)} %kc_ref.7, bf16[1792,512]{1,0:T(8,128)(2,1)} %vc_ref.7, ...), custom_call_target="tpu_custom_call", output_to_operand_aliasing={{0}: (9, {})} | custom-call | bytes 1024 | tf_op jit(solution)/shard_map/attention/pallas_call | solution.py:109
  (117 shorter events, 41.7 us)
Async XLA Ops:
  7.2 40.1 %all-gather.4.cloned.1.call-start = ((), (), s32[]{:S(2)}) async-start(), calls=%async_computation | async-start | bytes 5242880 | tf_op jit(solution)/shard_map/all_gather | solution.py:184
  9.7 74.3 %all-gather.6.cloned.1.call-start = ((), (), s32[]{:S(2)}) async-start(), calls=%async_computation.1 | async-start | bytes 5242880 | tf_op jit(solution)/shard_map/all_gather | solution.py:184
  11.4 15.2 %collective-permute-start.1 = (bf16[256,1024]{1,0:T(8,128)(2,1)}, bf16[256,1024]{1,0:T(8,128)(2,1)}, u32[]{:S(2)}, u32[]{:S(2)}) collective-permute-start(bf16[256,1024]{1,0:T(8,128)(2,1)} %pad_maximum_fusion.1), channel_id=1, source_target_pairs={{0,1},{1,0},{2,3},{3,2},{4,5},{5,4},{6,7},{7,6},{8,9},{9,8},{10,11... | collective-permute-start | bytes 1572872 | tf_op jit(solution)/shard_map/ppermute | solution.py:160
  30.4 89.4 %all-gather.8.cloned.1.call-start = ((), (), s32[]{:S(2)}) async-start(), calls=%async_computation.2 | async-start | bytes 5242880 | tf_op jit(solution)/shard_map/all_gather | solution.py:184
  31.1 14.6 %collective-permute-start.3 = (bf16[256,1024]{1,0:T(8,128)(2,1)}, bf16[256,1024]{1,0:T(8,128)(2,1)S(1)}, u32[]{:S(2)}, u32[]{:S(2)}) collective-permute-start(bf16[256,1024]{1,0:T(8,128)(2,1)} %get-tuple-element.71), channel_id=1, source_target_pairs={{0,8},{2,10},{4,12},{6,14},{8,0},{10,2},{12,4},{14,6},{16,24},{18,... | collective-permute-start | bytes 1572872 | tf_op jit(solution)/shard_map/ppermute | solution.py:154
  33.0 24.7 %collective-permute-start.2 = (bf16[256,1024]{1,0:T(8,128)(2,1)S(1)}, bf16[256,1024]{1,0:T(8,128)(2,1)S(1)}, u32[]{:S(2)}, u32[]{:S(2)}) collective-permute-start(bf16[256,1024]{1,0:T(8,128)(2,1)S(1)} %copy-done.17), channel_id=1, source_target_pairs={{0,24},{2,26},{4,28},{6,30},{8,16},{10,18},{12,20},{14,22},{16,8},... | collective-permute-start | bytes 1572872 | tf_op jit(solution)/shard_map/ppermute | solution.py:154
  35.5 23.7 %collective-permute-start = (bf16[256,1024]{1,0:T(8,128)(2,1)S(1)}, bf16[256,1024]{1,0:T(8,128)(2,1)}, u32[]{:S(2)}, u32[]{:S(2)}) collective-permute-start(bf16[256,1024]{1,0:T(8,128)(2,1)S(1)} %copy-done.16), channel_id=1, source_target_pairs={{0,1},{1,0},{2,3},{3,2},{4,5},{5,4},{6,7},{7,6},{8,9},{9,8},{10,11... | collective-permute-start | bytes 1572872 | tf_op jit(solution)/shard_map/ppermute | solution.py:160
  45.7 16.7 %collective-permute-start.5 = (bf16[256,1024]{1,0:T(8,128)(2,1)S(1)}, bf16[256,1024]{1,0:T(8,128)(2,1)}, u32[]{:S(2)}, u32[]{:S(2)}) collective-permute-start(bf16[256,1024]{1,0:T(8,128)(2,1)S(1)} %collective-permute-done.3), channel_id=1, source_target_pairs={{0,1},{1,0},{2,3},{3,2},{4,5},{5,4},{6,7},{7,6},{8,9},{9,8},{10,11... | collective-permute-start | bytes 1572872 | tf_op jit(solution)/shard_map/ppermute | solution.py:160
  47.3 127.5 %copy-start.11 = (s32[3]{0:T(128)}, s32[3]{0:T(128)S(1)}, u32[]{:S(2)}) copy-start(s32[3]{0:T(128)S(1)} %get-tuple-element.146.place_ref) | copy-start | bytes 40
  57.7 12.5 %collective-permute-start.4 = (bf16[256,1024]{1,0:T(8,128)(2,1)S(1)}, bf16[256,1024]{1,0:T(8,128)(2,1)S(1)}, u32[]{:S(2)}, u32[]{:S(2)}) collective-permute-start(bf16[256,1024]{1,0:T(8,128)(2,1)S(1)} %collective-permute-done.2), channel_id=1, source_target_pairs={{0,1},{1,0},{2,3},{3,2},{4,5},{5,4},{6,7},{7,6},{8,9},{9,8},{10,11... | collective-permute-start | bytes 1572872 | tf_op jit(solution)/shard_map/ppermute | solution.py:160
  60.7 22.8 %collective-permute-start.7 = (bf16[256,1024]{1,0:T(8,128)(2,1)S(1)}, bf16[256,1024]{1,0:T(8,128)(2,1)}, u32[]{:S(2)}, u32[]{:S(2)}) collective-permute-start(bf16[256,1024]{1,0:T(8,128)(2,1)S(1)} %get-tuple-element.77), channel_id=1, source_target_pairs={{0,16},{2,18},{4,20},{6,22},{8,24},{10,26},{12,28},{14,30},{16,0},... | collective-permute-start | bytes 1572872 | tf_op jit(solution)/shard_map/ppermute | solution.py:154
  66.1 33.4 %collective-permute-start.9 = (bf16[256,1024]{1,0:T(8,128)(2,1)}, bf16[256,1024]{1,0:T(8,128)(2,1)}, u32[]{:S(2)}, u32[]{:S(2)}) collective-permute-start(bf16[256,1024]{1,0:T(8,128)(2,1)} %convolution_convert_fusion.3), channel_id=1, source_target_pairs={{0,8},{2,10},{4,12},{6,14},{8,0},{10,2},{12,4},{14,6},{16,24},{18,... | collective-permute-start | bytes 1572872 | tf_op jit(solution)/shard_map/ppermute | solution.py:154
  72.7 30.2 %collective-permute-start.10 = (bf16[256,1024]{1,0:T(8,128)(2,1)}, bf16[256,1024]{1,0:T(8,128)(2,1)}, u32[]{:S(2)}, u32[]{:S(2)}) collective-permute-start(bf16[256,1024]{1,0:T(8,128)(2,1)} %convolution_convert_fusion.2), channel_id=1, source_target_pairs={{0,8},{2,10},{4,12},{6,14},{8,0},{10,2},{12,4},{14,6},{16,24},{18,... | collective-permute-start | bytes 1572872 | tf_op jit(solution)/shard_map/ppermute | solution.py:154
  73.4 17.7 %collective-permute-start.6 = (bf16[256,1024]{1,0:T(8,128)(2,1)S(1)}, bf16[256,1024]{1,0:T(8,128)(2,1)S(1)}, u32[]{:S(2)}, u32[]{:S(2)}) collective-permute-start(bf16[256,1024]{1,0:T(8,128)(2,1)S(1)} %get-tuple-element.83), channel_id=1, source_target_pairs={{0,1},{1,0},{2,3},{3,2},{4,5},{5,4},{6,7},{7,6},{8,9},{9,8},{10,11... | collective-permute-start | bytes 1572872 | tf_op jit(solution)/shard_map/ppermute | solution.py:160
  83.5 14.1 %collective-permute-start.8 = (bf16[256,1024]{1,0:T(8,128)(2,1)}, bf16[256,1024]{1,0:T(8,128)(2,1)}, u32[]{:S(2)}, u32[]{:S(2)}) collective-permute-start(bf16[256,1024]{1,0:T(8,128)(2,1)} %collective-permute-done.7), channel_id=1, source_target_pairs={{0,1},{1,0},{2,3},{3,2},{4,5},{5,4},{6,7},{7,6},{8,9},{9,8},{10,11... | collective-permute-start | bytes 1572872 | tf_op jit(solution)/shard_map/ppermute | solution.py:160
  88.4 53.4 %collective-permute-start.11 = (bf16[256,1024]{1,0:T(8,128)(2,1)}, bf16[256,1024]{1,0:T(8,128)(2,1)}, u32[]{:S(2)}, u32[]{:S(2)}) collective-permute-start(bf16[256,1024]{1,0:T(8,128)(2,1)} %convolution_convert_fusion), channel_id=1, source_target_pairs={{0,8},{2,10},{4,12},{6,14},{8,0},{10,2},{12,4},{14,6},{16,24},{18,... | collective-permute-start | bytes 1572872 | tf_op jit(solution)/shard_map/ppermute | solution.py:154
  91.1 50.8 %collective-permute-start.12 = (bf16[256,1024]{1,0:T(8,128)(2,1)}, bf16[256,1024]{1,0:T(8,128)(2,1)}, u32[]{:S(2)}, u32[]{:S(2)}) collective-permute-start(bf16[256,1024]{1,0:T(8,128)(2,1)} %convolution_convert_fusion.1), channel_id=1, source_target_pairs={{0,8},{2,10},{4,12},{6,14},{8,0},{10,2},{12,4},{14,6},{16,24},{18,... | collective-permute-start | bytes 1572872 | tf_op jit(solution)/shard_map/ppermute | solution.py:154
  99.5 57.8 %copy-start.6 = (bf16[256,2048]{1,0:T(8,128)(2,1)}, bf16[256,2048]{1,0:T(8,128)(2,1)S(1)}, u32[]{:S(2)}) copy-start(bf16[256,2048]{1,0:T(8,128)(2,1)S(1)} %maximum_select_fusion.3.high_ref) | copy-start | bytes 3145732
  106.1 43.8 %collective-permute-start.16 = (bf16[256,1024]{1,0:T(8,128)(2,1)}, bf16[256,1024]{1,0:T(8,128)(2,1)S(1)}, u32[]{:S(2)}, u32[]{:S(2)}) collective-permute-start(bf16[256,1024]{1,0:T(8,128)(2,1)} %add_convert_fusion.1), channel_id=1, source_target_pairs={{0,16},{2,18},{4,20},{6,22},{8,24},{10,26},{12,28},{14,30},{16,0},... | collective-permute-start | bytes 1572872 | tf_op jit(solution)/shard_map/ppermute | solution.py:154
  124.9 32.4 %collective-permute-start.15 = (bf16[256,1024]{1,0:T(8,128)(2,1)S(1)}, bf16[256,1024]{1,0:T(8,128)(2,1)S(1)}, u32[]{:S(2)}, u32[]{:S(2)}) collective-permute-start(bf16[256,1024]{1,0:T(8,128)(2,1)S(1)} %half_product.4), channel_id=1, source_target_pairs={{0,8},{2,10},{4,12},{6,14},{8,0},{10,2},{12,4},{14,6},{16,24},{18,... | collective-permute-start | bytes 1572872 | tf_op jit(solution)/shard_map/ppermute | solution.py:154
  144.5 20.7 %collective-permute-start.14 = (bf16[256,1024]{1,0:T(8,128)(2,1)S(1)}, bf16[256,1024]{1,0:T(8,128)(2,1)S(1)}, u32[]{:S(2)}, u32[]{:S(2)}) collective-permute-start(bf16[256,1024]{1,0:T(8,128)(2,1)S(1)} %add_convert_fusion), channel_id=1, source_target_pairs={{0,16},{2,18},{4,20},{6,22},{8,24},{10,26},{12,28},{14,30},{16,0},... | collective-permute-start | bytes 1572872 | tf_op jit(solution)/shard_map/ppermute | solution.py:154
  146.4 25.8 %collective-permute-start.13 = (bf16[256,1024]{1,0:T(8,128)(2,1)S(1)}, bf16[256,1024]{1,0:T(8,128)(2,1)S(1)}, u32[]{:S(2)}, u32[]{:S(2)}) collective-permute-start(bf16[256,1024]{1,0:T(8,128)(2,1)S(1)} %half_product.5), channel_id=1, source_target_pairs={{0,8},{2,10},{4,12},{6,14},{8,0},{10,2},{12,4},{14,6},{16,24},{18,... | collective-permute-start | bytes 1572872 | tf_op jit(solution)/shard_map/ppermute | solution.py:154
  149.9 30.3 %copy-start = (f32[256,1024]{1,0:T(8,128)}, f32[256,1024]{1,0:T(8,128)S(1)}, u32[]{:S(2)}) copy-start(f32[256,1024]{1,0:T(8,128)S(1)} %convolution_add_fusion.km_ref.vm_ref) | copy-start | bytes 3145732
  149.9 30.3 %copy-start.3 = (bf16[256,1024]{1,0:T(8,128)(2,1)}, bf16[256,1024]{1,0:T(8,128)(2,1)S(1)}, u32[]{:S(2)}) copy-start(bf16[256,1024]{1,0:T(8,128)(2,1)S(1)} %collective-permute-done.16.kt_ref.vt_ref) | copy-start | bytes 1572868
  159.2 21.0 %collective-permute-start.18 = (bf16[128,1024]{1,0:T(8,128)(2,1)S(1)}, bf16[128,1024]{1,0:T(8,128)(2,1)S(1)}, u32[]{:S(2)}, u32[]{:S(2)}) collective-permute-start(bf16[128,1024]{1,0:T(8,128)(2,1)S(1)} %get-tuple-element.106), channel_id=1, source_target_pairs={{0,16},{2,18},{4,20},{6,22},{8,24},{10,26},{12,28},{14,30},{16,0},... | collective-permute-start | bytes 786440 | tf_op jit(solution)/shard_map/ppermute | solution.py:154
  174.7 13.2 %collective-permute-start.17 = (bf16[128,1024]{1,0:T(8,128)(2,1)}, bf16[128,1024]{1,0:T(8,128)(2,1)S(1)}, u32[]{:S(2)}, u32[]{:S(2)}) collective-permute-start(bf16[128,1024]{1,0:T(8,128)(2,1)} %get-tuple-element.115), channel_id=1, source_target_pairs={{0,16},{2,18},{4,20},{6,22},{8,24},{10,26},{12,28},{14,30},{16,0},... | collective-permute-start | bytes 786440 | tf_op jit(solution)/shard_map/ppermute | solution.py:154
  185.9 1.9 collective-permute-start.19
  186.0 3.7 %collective-permute-start.20 = (bf16[1,2048]{1,0:T(2,128)(2,1)S(1)}, bf16[1,2048]{1,0:T(2,128)(2,1)S(1)}, u32[]{:S(2)}, u32[]{:S(2)}) collective-permute-start(bf16[1,2048]{1,0:T(2,128)(2,1)S(1)} %pad_maximum_fusion.7), channel_id=1, source_target_pairs={{0,4},{2,6},{4,0},{6,2},{8,12},{10,14},{12,8},{14,10},{16,20},{18,... | collective-permute-start | bytes 12296 | tf_op jit(solution)/shard_map/ppermute | solution.py:154
  187.5 3.1 %collective-permute-start.21 = (bf16[1,2048]{1,0:T(2,128)(2,1)S(1)}, bf16[1,2048]{1,0:T(2,128)(2,1)S(1)}, u32[]{:S(2)}, u32[]{:S(2)}) collective-permute-start(bf16[1,2048]{1,0:T(2,128)(2,1)S(1)} %pad_maximum_fusion.7), channel_id=1, source_target_pairs={{0,6},{2,4},{4,2},{6,0},{8,14},{10,12},{12,10},{14,8},{16,22},{18,... | collective-permute-start | bytes 12296 | tf_op jit(solution)/shard_map/ppermute | solution.py:154
  191.2 11.4 %collective-permute-start.22 = (bf16[4,1,2048]{2,0,1:T(4,128)(2,1)S(1)}, bf16[4,1,2048]{2,0,1:T(4,128)(2,1)S(1)}, u32[]{:S(2)}, u32[]{:S(2)}) collective-permute-start(bf16[4,1,2048]{2,0,1:T(4,128)(2,1)S(1)} %reshape.23), channel_id=1, source_target_pairs={{0,8},{2,10},{4,12},{6,14},{8,0},{10,2},{12,4},{14,6},{16,24},{18,... | collective-permute-start | bytes 49160 | tf_op jit(solution)/shard_map/ppermute | solution.py:154
  193.6 9.0 %collective-permute-start.23 = (bf16[4,1,2048]{2,0,1:T(4,128)(2,1)S(1)}, bf16[4,1,2048]{2,0,1:T(4,128)(2,1)S(1)}, u32[]{:S(2)}, u32[]{:S(2)}) collective-permute-start(bf16[4,1,2048]{2,0,1:T(4,128)(2,1)S(1)} %reshape.23), channel_id=1, source_target_pairs={{0,16},{2,18},{4,20},{6,22},{8,24},{10,26},{12,28},{14,30},{16,0},... | collective-permute-start | bytes 49160 | tf_op jit(solution)/shard_map/ppermute | solution.py:154
  194.2 8.4 %collective-permute-start.24 = (bf16[4,1,2048]{2,0,1:T(4,128)(2,1)S(1)}, bf16[4,1,2048]{2,0,1:T(4,128)(2,1)S(1)}, u32[]{:S(2)}, u32[]{:S(2)}) collective-permute-start(bf16[4,1,2048]{2,0,1:T(4,128)(2,1)S(1)} %reshape.23), channel_id=1, source_target_pairs={{0,24},{2,26},{4,28},{6,30},{8,16},{10,18},{12,20},{14,22},{16,8},... | collective-permute-start | bytes 49160 | tf_op jit(solution)/shard_map/ppermute | solution.py:154
  (20 other events, 157.1 us)
Sparse Core Ops, SparseCore 0:
  9.8 37.1 all-gather.3
  48.6 34.4 all-gather.5
  85.2 34.4 all-gather.7

commit v10 on v9

--- a/solution.py
+++ b/solution.py
@@ -207,7 +207,7 @@
             )
 
         swap = {1: over_tp(step(cut(tokens_in, 1, 1 - x)))}
-        source = step(tokens_in)
+        source = tokens_in
         swap[0] = over_tp(step(cut(source, 0, 1 - x)))
         mine = z // 2 == x
         held, came = {}, {}
@@ -357,12 +357,12 @@
     advance(0)
     if pieces == 2:
         weights[1] = step(weights[1])
+        advance(1)
         start(2)
-        advance(1)
         start(3)
         arrive(0)
+        arrive(1)
         advance(2)
-        arrive(1)
         attention(1, 0)
         advance(3)
         attention(1, 1)

time: 210 us -> 219 us (1.043)
  waiting for transfers between devices: 91.9 us -> 85.6 us
  starting transfers between devices: 32.7 us -> 37.1 us
  local copies, waits for them, and re-layouts: 6.44 us -> 9.52 us
  matrix products: 20.8 us -> 23.4 us
  Pallas kernels: 30.8 us -> 33.1 us
  other arithmetic: 12.4 us -> 14.7 us
    ppermute x19, starting transfers between devices: 23.1 us -> 27.6 us  [over_inst(): return lax.ppermute(value, 'inst', [(i, i ^ bits) for i in range(n_inst)])]
    ppermute x19, waiting for transfers between devices: 61.7 us -> 58.1 us  [over_inst(): return lax.ppermute(value, 'inst', [(i, i ^ bits) for i in range(n_inst)])]
    all_gather x3, waiting for transfers between devices: 10.3 us -> 7.58 us  [group_gather(): lax.all_gather(value, 'inst', axis=0, tiled=True, axis_index_groups=groups)]
    dot_general x8, matrix products: 20.8 us -> 23.4 us  [dot(): return jnp.dot(a, b, preferred_element_type=jnp.float32)]
    select_n x4, other arithmetic: 4.3 us -> 6.78 us  [swapped_if(): jnp.where(flag, jnp.concatenate([b, a], axis=axis), jnp.concatenate([a, b...]
    unnamed x48 -> x66, local copies, waits for them, and re-layouts: 3.5 us -> 5.86 us
  transfers between devices with their start and end apart: 28 -> 28, of which waited for: 14 -> 13; matrix products, arithmetic and copies ran while one was open for 15% -> 17% of each run, Pallas kernels for 15% -> 15%
where the time goes in v10:
time: 219 us; the launch traced here: 218 us
  waiting for transfers between devices  85.6 us (39%)
  starting transfers between devices  37.1 us (17%)
  Pallas kernels  33.1 us (15%)
  matrix products  23.4 us (11%)
  between operations  14.9 us (7%)
  other arithmetic  14.7 us (7%)
  local copies, waits for them, and re-layouts  9.52 us (4%)
    ppermute x19, waiting for transfers between devices, over_inst(): return lax.ppermute(value, 'inst', [(i, i ^ bits) for i in range(n_inst)])  58.1 us
    ppermute x19, starting transfers between devices, over_inst(): return lax.ppermute(value, 'inst', [(i, i ^ bits) for i in range(n_inst)])  27.6 us
    dot_general x8, matrix products, dot(): return jnp.dot(a, b, preferred_element_type=jnp.float32)  23.4 us
    pallas_call x4, Pallas kernels, attend(): pl.pallas_call(attention_kernel, grid_spec=pltpu.PrefetchScalarGridSpec(n...  23.2 us
    ppermute x6, waiting for transfers between devices, over_tp(): return lax.ppermute(value, 'tp', [(0, 1), (1, 0)])  19.2 us
    pallas_call x4, Pallas kernels, half_product(): pl.pallas_call(first_kernel if first else later_kernel, grid=(columns //...  9.93 us
    ppermute x6, starting transfers between devices, over_tp(): return lax.ppermute(value, 'tp', [(0, 1), (1, 0)])  9.39 us
    all_gather x3, waiting for transfers between devices, group_gather(): lax.all_gather(value, 'inst', axis=0, tiled=True, axis_index_groups=groups)  7.58 us
  transfers between devices with their start and end apart: 28, of which 13 were waited for; matrix products, arithmetic and copies ran while one was open for 17% of the time, Pallas kernels for 15%

profile of v10, /device:TPU:0, one launch (start us, length us, event | category | flops | bytes accessed | tf_op | source)
XLA Modules:
  0.0 218.3 jit_solution(9442101817429620743)
XLA Ops:
  7.2 2.4 %pad_maximum_fusion = bf16[512,1024]{1,0:T(8,128)(2,1)} fusion(bf16[512,512]{1,0:T(8,128)(2,1)} %param.10, bf16[512,512]{1,0:T(8,128)(2,1)} %param.9), kind=kLoop, calls=%fused_computation.6 | loop fusion | flops 2097152 | bytes 2097152 | tf_op jit(solution)/shard_map/concatenate | solution.py:188
  12.3 2.9 %collective-permute-start.1 = (bf16[256,1024]{1,0:T(8,128)(2,1)}, bf16[256,1024]{1,0:T(8,128)(2,1)}, u32[]{:S(2)}, u32[]{:S(2)}) collective-permute-start(bf16[256,1024]{1,0:T(8,128)(2,1)} %pad_maximum_fusion.3), channel_id=1, source_target_pairs={{0,1},{1,0},{2,3},{3,2},{4,5},{5,4},{6,7},{7,6},{8,9},{9,8},{10,11... | collective-permute-start | bytes 1572872 | tf_op jit(solution)/shard_map/ppermute | solution.py:160
  16.1 11.4 %collective-permute-done.1 = bf16[256,1024]{1,0:T(8,128)(2,1)} collective-permute-done((bf16[256,1024]{1,0:T(8,128)(2,1)}, bf16[256,1024]{1,0:T(8,128)(2,1)}, u32[]{:S(2)}, u32[]{:S(2)}) %collective-permute-start.1) | collective-permute-done | bytes 524320 | tf_op jit(solution)/shard_map/ppermute | solution.py:160
  27.4 2.1 broadcast_select_fusion.1
  34.0 2.5 %collective-permute-start.2 = (bf16[256,1024]{1,0:T(8,128)(2,1)S(1)}, bf16[256,1024]{1,0:T(8,128)(2,1)S(1)}, u32[]{:S(2)}, u32[]{:S(2)}) collective-permute-start(bf16[256,1024]{1,0:T(8,128)(2,1)S(1)} %get-tuple-element.69), channel_id=1, source_target_pairs={{0,24},{2,26},{4,28},{6,30},{8,16},{10,18},{12,20},{14,22},{16,8},... | collective-permute-start | bytes 1572872 | tf_op jit(solution)/shard_map/ppermute | solution.py:154
  37.9 8.4 %collective-permute-done.3 = bf16[256,1024]{1,0:T(8,128)(2,1)S(1)} collective-permute-done((bf16[256,1024]{1,0:T(8,128)(2,1)S(1)}, bf16[256,1024]{1,0:T(8,128)(2,1)S(1)}, u32[]{:S(2)}, u32[]{:S(2)}) %collective-permute-start.3) | collective-permute-done | bytes 524320 | tf_op jit(solution)/shard_map/ppermute | solution.py:154
  47.8 10.7 %collective-permute-done.2 = bf16[256,1024]{1,0:T(8,128)(2,1)S(1)} collective-permute-done((bf16[256,1024]{1,0:T(8,128)(2,1)S(1)}, bf16[256,1024]{1,0:T(8,128)(2,1)S(1)}, u32[]{:S(2)}, u32[]{:S(2)}) %collective-permute-start.2) | collective-permute-done | bytes 524320 | tf_op jit(solution)/shard_map/ppermute | solution.py:154
  68.1 3.0 %collective-permute-done.4 = bf16[256,1024]{1,0:T(8,128)(2,1)S(1)} collective-permute-done((bf16[256,1024]{1,0:T(8,128)(2,1)S(1)}, bf16[256,1024]{1,0:T(8,128)(2,1)S(1)}, u32[]{:S(2)}, u32[]{:S(2)}) %collective-permute-start.4) | collective-permute-done | bytes 524320 | tf_op jit(solution)/shard_map/ppermute | solution.py:160
  72.7 2.1 convolution_convert_fusion.2
  77.0 7.0 %collective-permute-done.7 = bf16[256,1024]{1,0:T(8,128)(2,1)S(1)} collective-permute-done((bf16[256,1024]{1,0:T(8,128)(2,1)S(1)}, bf16[256,1024]{1,0:T(8,128)(2,1)S(1)}, u32[]{:S(2)}, u32[]{:S(2)}) %collective-permute-start.7) | collective-permute-done | bytes 524320 | tf_op jit(solution)/shard_map/ppermute | solution.py:154
  84.6 4.4 %convolution_convert_fusion = bf16[256,1024]{1,0:T(8,128)(2,1)} fusion(bf16[256,2048]{1,0:T(8,128)(2,1)S(1)} %maximum_select_fusion.low_ref, bf16[2048,1024]{1,0:T(8,128)(2,1)} %all-gather.6.cloned.1.call-done), kind=kOutput, calls=%fused_computation.2 | convolution fusion | flops 1074003968 | bytes 5767168 | tf_op jit(solution)/shard_map/dot_general | solution.py:16
  93.1 4.9 %collective-permute-done.8 = bf16[256,1024]{1,0:T(8,128)(2,1)} collective-permute-done((bf16[256,1024]{1,0:T(8,128)(2,1)S(1)}, bf16[256,1024]{1,0:T(8,128)(2,1)}, u32[]{:S(2)}, u32[]{:S(2)}) %collective-permute-start.8) | collective-permute-done | bytes 524320 | tf_op jit(solution)/shard_map/ppermute | solution.py:160
  98.0 5.5 %collective-permute-done.10 = bf16[256,1024]{1,0:T(8,128)(2,1)} collective-permute-done((bf16[256,1024]{1,0:T(8,128)(2,1)}, bf16[256,1024]{1,0:T(8,128)(2,1)}, u32[]{:S(2)}, u32[]{:S(2)}) %collective-permute-start.10) | collective-permute-done | bytes 524320 | tf_op jit(solution)/shard_map/ppermute | solution.py:154
  105.1 3.5 %add_convert_fusion.1 = bf16[256,1024]{1,0:T(8,128)(2,1)} fusion(bf16[256,1024]{1,0:T(8,128)(2,1)} %collective-permute-done.10, bf16[256,2048]{1,0:T(8,128)(2,1)S(1)} %maximum_select_fusion.3.high_ref, bf16[2048,1024]{1,0:T(8,128)(2,1)S(1)} %copy-done.29), kind=kOutput, calls=%fused_computation.12 | convolution fusion | flops 1074528256 | bytes 6291456 | tf_op jit(solution)/shard_map/dot_general | solution.py:16
  108.7 3.5 %collective-permute-start.15 = (bf16[256,1024]{1,0:T(8,128)(2,1)}, bf16[256,1024]{1,0:T(8,128)(2,1)S(1)}, u32[]{:S(2)}, u32[]{:S(2)}) collective-permute-start(bf16[256,1024]{1,0:T(8,128)(2,1)} %add_convert_fusion.1), channel_id=1, source_target_pairs={{0,16},{2,18},{4,20},{6,22},{8,24},{10,26},{12,28},{14,30},{16,0},... | collective-permute-start | bytes 1572872 | tf_op jit(solution)/shard_map/ppermute | solution.py:154
  112.2 7.6 %all-gather.8.cloned.1.call-done.w_ref = bf16[2048,1024]{1,0:T(8,128)(2,1)} async-done(((bf16[512,1024]{1,0:T(8,128)(2,1)}), bf16[2048,1024]{1,0:T(8,128)(2,1)}) %all-gather.8.cloned.1.call-update) | async-done | bytes 4194320 | tf_op jit(solution)/shard_map/all_gather | solution.py:184
  121.5 12.1 %collective-permute-done.12 = bf16[256,1024]{1,0:T(8,128)(2,1)} collective-permute-done((bf16[256,1024]{1,0:T(8,128)(2,1)}, bf16[256,1024]{1,0:T(8,128)(2,1)}, u32[]{:S(2)}, u32[]{:S(2)}) %collective-permute-start.12) | collective-permute-done | bytes 524320 | tf_op jit(solution)/shard_map/ppermute | solution.py:154
  133.6 3.6 %add_convert_fusion = bf16[256,1024]{1,0:T(8,128)(2,1)S(1)} fusion(bf16[256,1024]{1,0:T(8,128)(2,1)} %collective-permute-done.12, bf16[256,2048]{1,0:T(8,128)(2,1)S(1)} %copy-done.9, bf16[2048,1024]{1,0:T(8,128)(2,1)} %all-gather.6.cloned.1.call-done), kind=kOutput, calls=%fused_computation.11 | convolution fusion | flops 1074528256 | bytes 6291456 | tf_op jit(solution)/shard_map/dot_general | solution.py:16
  137.2 2.5 %collective-permute-start.14 = (bf16[256,1024]{1,0:T(8,128)(2,1)S(1)}, bf16[256,1024]{1,0:T(8,128)(2,1)S(1)}, u32[]{:S(2)}, u32[]{:S(2)}) collective-permute-start(bf16[256,1024]{1,0:T(8,128)(2,1)S(1)} %add_convert_fusion), channel_id=1, source_target_pairs={{0,16},{2,18},{4,20},{6,22},{8,24},{10,26},{12,28},{14,30},{16,0},... | collective-permute-start | bytes 1572872 | tf_op jit(solution)/shard_map/ppermute | solution.py:154
  141.4 2.5 %collective-permute-start.16 = (bf16[256,1024]{1,0:T(8,128)(2,1)S(1)}, bf16[256,1024]{1,0:T(8,128)(2,1)S(1)}, u32[]{:S(2)}, u32[]{:S(2)}) collective-permute-start(bf16[256,1024]{1,0:T(8,128)(2,1)S(1)} %half_product.4), channel_id=1, source_target_pairs={{0,8},{2,10},{4,12},{6,14},{8,0},{10,2},{12,4},{14,6},{16,24},{18,... | collective-permute-start | bytes 1572872 | tf_op jit(solution)/shard_map/ppermute | solution.py:154
  144.0 2.3 %convolution_add_fusion.km_ref.vm_ref = f32[256,1024]{1,0:T(8,128)S(1)} fusion(bf16[256,2048]{1,0:T(8,128)(2,1)S(1)} %maximum_select_fusion.2.low_ref, bf16[2048,1024]{1,0:T(8,128)(2,1)S(1)} %copy-done.30, bf16[256,1024]{1,0:T(8,128)(2,1)} %collective-permute-done.9), kind=kOutput, calls=%fused_computation | convolution fusion | flops 1074266112 | bytes 6815744 | tf_op jit(solution)/shard_map/dot_general | solution.py:16
  146.3 2.5 %half_product.5 = bf16[256,1024]{1,0:T(8,128)(2,1)} custom-call(bf16[256,2048]{1,0:T(8,128)(2,1)S(1)} %maximum_select_fusion.low_ref, bf16[256,2048]{1,0:T(8,128)(2,1)S(1)} %copy-done.7, bf16[2048,1024]{1,0:T(8,128)(2,1)S(1)} %copy-done.1), custom_call_target="tpu_custom_call" | custom-call | bytes 8388608 | tf_op jit(solution)/shard_map/half_product/pallas_call | solution.py:42
  148.9 3.3 %convolution_add_fusion.1.qm_ref = f32[256,1024]{1,0:T(8,128)} fusion(bf16[256,2048]{1,0:T(8,128)(2,1)S(1)} %maximum_select_fusion.2.low_ref, bf16[2048,1024]{1,0:T(8,128)(2,1)S(1)} %copy-done.32, bf16[256,1024]{1,0:T(8,128)(2,1)} %collective-permute-done.11), kind=kOutput, calls=%fused_computation.1 | convolution fusion | flops 1074266112 | bytes 6815744 | tf_op jit(solution)/shard_map/dot_general | solution.py:16
  152.2 4.7 %collective-permute-done.14.qc_ref = bf16[256,1024]{1,0:T(8,128)(2,1)S(1)} collective-permute-done((bf16[256,1024]{1,0:T(8,128)(2,1)S(1)}, bf16[256,1024]{1,0:T(8,128)(2,1)S(1)}, u32[]{:S(2)}, u32[]{:S(2)}) %collective-permute-start.14) | collective-permute-done | bytes 524320 | tf_op jit(solution)/shard_map/ppermute | solution.py:154
  157.7 6.7 %collective-permute-done.16.came_ref = bf16[256,1024]{1,0:T(8,128)(2,1)S(1)} collective-permute-done((bf16[256,1024]{1,0:T(8,128)(2,1)S(1)}, bf16[256,1024]{1,0:T(8,128)(2,1)S(1)}, u32[]{:S(2)}, u32[]{:S(2)}) %collective-permute-start.16) | collective-permute-done | bytes 524320 | tf_op jit(solution)/shard_map/ppermute | solution.py:154
  164.4 2.4 %half_product.6 = (bf16[128,1024]{1,0:T(8,128)(2,1)}, f32[128,1024]{1,0:T(8,128)S(1)}) custom-call(bf16[256,2048]{1,0:T(8,128)(2,1)S(1)} %maximum_select_fusion.2.low_ref, bf16[256,2048]{1,0:T(8,128)(2,1)S(1)} %copy-done.9, bf16[2048,1024]{1,0:T(8,128)(2,1)S(1)} %copy-done.1, bf16[256,1024]{1,0:T(8,128)(2,1)S(1)} %collective-permute-done.16.came_ref), custom_call_target="tpu_custom_call" | custom-call | bytes 1024 | tf_op jit(solution)/shard_map/half_product/pallas_call | solution.py:42
  172.9 5.4 %attention.4 = (bf16[256,2048]{1,0:T(8,128)(2,1)}, bf16[1,1024]{1,0:T(2,128)(2,1)S(1)}) custom-call(s32[3]{0:T(128)S(1)} %get-tuple-element.147.place_ref, f32[256,1024]{1,0:T(8,128)S(1)} %copy-done.13, bf16[256,1024]{1,0:T(8,128)(2,1)S(1)} %copy-done.16, bf16[1792,512]{1,0:T(8,128)(2,1)S(1)} %copy-done.4, bf16[1792,512]{1,0:T(8,128)(2,1)S(1)} %copy-done.5, ...), custom_call_target="tpu_custom_call" | custom-call | bytes 1024 | tf_op jit(solution)/shard_map/attention/pallas_call | solution.py:109
  178.4 3.3 %half_product.7 = (bf16[128,1024]{1,0:T(8,128)(2,1)}, f32[128,1024]{1,0:T(8,128)S(1)}) custom-call(bf16[256,2048]{1,0:T(8,128)(2,1)S(1)} %copy-done.12, bf16[256,2048]{1,0:T(8,128)(2,1)S(1)} %copy-done.10, bf16[2048,1024]{1,0:T(8,128)(2,1)S(1)} %copy-done.2, bf16[256,1024]{1,0:T(8,128)(2,1)} %collective-permute-done.13.came_ref), custom_call_target="tpu_custom_call" | custom-call | bytes 1024 | tf_op jit(solution)/shard_map/half_product/pallas_call | solution.py:42
  183.2 5.4 %attention.5 = (bf16[256,2048]{1,0:T(8,128)(2,1)}, bf16[1,1024]{1,0:T(2,128)(2,1)S(1)}) custom-call(s32[3]{0:T(128)S(1)} %get-tuple-element.146.place_ref, f32[256,1024]{1,0:T(8,128)S(1)} %copy-done.14, bf16[256,1024]{1,0:T(8,128)(2,1)S(1)} %copy-done.16, bf16[1792,512]{1,0:T(8,128)(2,1)S(1)} %copy-done.4, ...), custom_call_target="tpu_custom_call", output_to_operand_aliasing={{0}: (9, {})} | custom-call | bytes 1024 | tf_op jit(solution)/shard_map/attention/pallas_call | solution.py:109
  188.7 5.8 %attention.6 = (bf16[256,2048]{1,0:T(8,128)(2,1)}, bf16[1,1024]{1,0:T(2,128)(2,1)S(1)}) custom-call(s32[3]{0:T(128)S(1)} %get-tuple-element.147.place_ref, f32[128,1024]{1,0:T(8,128)S(1)} %copy-done.19, bf16[128,1024]{1,0:T(8,128)(2,1)} %collective-permute-done.18.qc_ref, bf16[1792,512]{1,0:T(8,128)(2,1)S(1)} %copy-done.4, ...), custom_call_target="tpu_custom_call", output_to_operand_aliasing={{0}: (9, {})} | custom-call | bytes 1024 | tf_op jit(solution)/shard_map/attention/pallas_call | solution.py:109
  200.2 2.9 %collective-permute-start.23 = (bf16[4,1,2048]{2,0,1:T(4,128)(2,1)S(1)}, bf16[4,1,2048]{2,0,1:T(4,128)(2,1)S(1)}, u32[]{:S(2)}, u32[]{:S(2)}) collective-permute-start(bf16[4,1,2048]{2,0,1:T(4,128)(2,1)S(1)} %reshape.23), channel_id=1, source_target_pairs={{0,16},{2,18},{4,20},{6,22},{8,24},{10,26},{12,28},{14,30},{16,0},... | collective-permute-start | bytes 49160 | tf_op jit(solution)/shard_map/ppermute | solution.py:154
  204.4 6.5 %attention.7 = (bf16[256,2048]{1,0:T(8,128)(2,1)}, bf16[1,1024]{1,0:T(2,128)(2,1)}) custom-call(s32[3]{0:T(128)} %copy-done.20, f32[128,1024]{1,0:T(8,128)} %copy-done.17, bf16[128,1024]{1,0:T(8,128)(2,1)} %collective-permute-done.17.qc_ref, bf16[1792,512]{1,0:T(8,128)(2,1)} %kc_ref.7, bf16[1792,512]{1,0:T(8,128)(2,1)} %vc_ref.7, ...), custom_call_target="tpu_custom_call", output_to_operand_aliasing={{0}: (9, {})} | custom-call | bytes 1024 | tf_op jit(solution)/shard_map/attention/pallas_call | solution.py:109
  (134 shorter events, 49.5 us)
Async XLA Ops:
  7.2 40.6 %all-gather.4.cloned.1.call-start = ((), (), s32[]{:S(2)}) async-start(), calls=%async_computation | async-start | bytes 5242880 | tf_op jit(solution)/shard_map/all_gather | solution.py:184
  9.7 74.9 %all-gather.6.cloned.1.call-start = ((), (), s32[]{:S(2)}) async-start(), calls=%async_computation.1 | async-start | bytes 5242880 | tf_op jit(solution)/shard_map/all_gather | solution.py:184
  12.3 15.2 %collective-permute-start.1 = (bf16[256,1024]{1,0:T(8,128)(2,1)}, bf16[256,1024]{1,0:T(8,128)(2,1)}, u32[]{:S(2)}, u32[]{:S(2)}) collective-permute-start(bf16[256,1024]{1,0:T(8,128)(2,1)} %pad_maximum_fusion.3), channel_id=1, source_target_pairs={{0,1},{1,0},{2,3},{3,2},{4,5},{5,4},{6,7},{7,6},{8,9},{9,8},{10,11... | collective-permute-start | bytes 1572872 | tf_op jit(solution)/shard_map/ppermute | solution.py:160
  31.1 88.6 %all-gather.8.cloned.1.call-start = ((), (), s32[]{:S(2)}) async-start(), calls=%async_computation.2 | async-start | bytes 5242880 | tf_op jit(solution)/shard_map/all_gather | solution.py:184
  32.1 14.2 %collective-permute-start.3 = (bf16[256,1024]{1,0:T(8,128)(2,1)S(1)}, bf16[256,1024]{1,0:T(8,128)(2,1)S(1)}, u32[]{:S(2)}, u32[]{:S(2)}) collective-permute-start(bf16[256,1024]{1,0:T(8,128)(2,1)S(1)} %copy-done.27), channel_id=1, source_target_pairs={{0,8},{2,10},{4,12},{6,14},{8,0},{10,2},{12,4},{14,6},{16,24},{18,... | collective-permute-start | bytes 1572872 | tf_op jit(solution)/shard_map/ppermute | solution.py:154
  34.0 24.6 %collective-permute-start.2 = (bf16[256,1024]{1,0:T(8,128)(2,1)S(1)}, bf16[256,1024]{1,0:T(8,128)(2,1)S(1)}, u32[]{:S(2)}, u32[]{:S(2)}) collective-permute-start(bf16[256,1024]{1,0:T(8,128)(2,1)S(1)} %get-tuple-element.69), channel_id=1, source_target_pairs={{0,24},{2,26},{4,28},{6,30},{8,16},{10,18},{12,20},{14,22},{16,8},... | collective-permute-start | bytes 1572872 | tf_op jit(solution)/shard_map/ppermute | solution.py:154
  36.4 23.6 %collective-permute-start = (bf16[256,1024]{1,0:T(8,128)(2,1)S(1)}, bf16[256,1024]{1,0:T(8,128)(2,1)}, u32[]{:S(2)}, u32[]{:S(2)}) collective-permute-start(bf16[256,1024]{1,0:T(8,128)(2,1)S(1)} %copy-done.26), channel_id=1, source_target_pairs={{0,1},{1,0},{2,3},{3,2},{4,5},{5,4},{6,7},{7,6},{8,9},{9,8},{10,11... | collective-permute-start | bytes 1572872 | tf_op jit(solution)/shard_map/ppermute | solution.py:160
  46.3 16.9 %collective-permute-start.5 = (bf16[256,1024]{1,0:T(8,128)(2,1)S(1)}, bf16[256,1024]{1,0:T(8,128)(2,1)}, u32[]{:S(2)}, u32[]{:S(2)}) collective-permute-start(bf16[256,1024]{1,0:T(8,128)(2,1)S(1)} %collective-permute-done.3), channel_id=1, source_target_pairs={{0,1},{1,0},{2,3},{3,2},{4,5},{5,4},{6,7},{7,6},{8,9},{9,8},{10,11... | collective-permute-start | bytes 1572872 | tf_op jit(solution)/shard_map/ppermute | solution.py:160
  58.5 12.6 %collective-permute-start.4 = (bf16[256,1024]{1,0:T(8,128)(2,1)S(1)}, bf16[256,1024]{1,0:T(8,128)(2,1)S(1)}, u32[]{:S(2)}, u32[]{:S(2)}) collective-permute-start(bf16[256,1024]{1,0:T(8,128)(2,1)S(1)} %collective-permute-done.2), channel_id=1, source_target_pairs={{0,1},{1,0},{2,3},{3,2},{4,5},{5,4},{6,7},{7,6},{8,9},{9,8},{10,11... | collective-permute-start | bytes 1572872 | tf_op jit(solution)/shard_map/ppermute | solution.py:160
  61.4 22.6 %collective-permute-start.7 = (bf16[256,1024]{1,0:T(8,128)(2,1)S(1)}, bf16[256,1024]{1,0:T(8,128)(2,1)S(1)}, u32[]{:S(2)}, u32[]{:S(2)}) collective-permute-start(bf16[256,1024]{1,0:T(8,128)(2,1)S(1)} %get-tuple-element.76), channel_id=1, source_target_pairs={{0,16},{2,18},{4,20},{6,22},{8,24},{10,26},{12,28},{14,30},{16,0},... | collective-permute-start | bytes 1572872 | tf_op jit(solution)/shard_map/ppermute | solution.py:154
  67.3 30.7 %collective-permute-start.9 = (bf16[256,1024]{1,0:T(8,128)(2,1)}, bf16[256,1024]{1,0:T(8,128)(2,1)}, u32[]{:S(2)}, u32[]{:S(2)}) collective-permute-start(bf16[256,1024]{1,0:T(8,128)(2,1)} %convolution_convert_fusion.3), channel_id=1, source_target_pairs={{0,8},{2,10},{4,12},{6,14},{8,0},{10,2},{12,4},{14,6},{16,24},{18,... | collective-permute-start | bytes 1572872 | tf_op jit(solution)/shard_map/ppermute | solution.py:154
  72.7 66.9 %copy-start.6 = (bf16[256,2048]{1,0:T(8,128)(2,1)}, bf16[256,2048]{1,0:T(8,128)(2,1)S(1)}, u32[]{:S(2)}) copy-start(bf16[256,2048]{1,0:T(8,128)(2,1)S(1)} %maximum_select_fusion.1.high_ref) | copy-start | bytes 3145732
  74.9 28.6 %collective-permute-start.10 = (bf16[256,1024]{1,0:T(8,128)(2,1)}, bf16[256,1024]{1,0:T(8,128)(2,1)}, u32[]{:S(2)}, u32[]{:S(2)}) collective-permute-start(bf16[256,1024]{1,0:T(8,128)(2,1)} %convolution_convert_fusion.2), channel_id=1, source_target_pairs={{0,8},{2,10},{4,12},{6,14},{8,0},{10,2},{12,4},{14,6},{16,24},{18,... | collective-permute-start | bytes 1572872 | tf_op jit(solution)/shard_map/ppermute | solution.py:154
  75.5 15.6 %collective-permute-start.6 = (bf16[256,1024]{1,0:T(8,128)(2,1)S(1)}, bf16[256,1024]{1,0:T(8,128)(2,1)}, u32[]{:S(2)}, u32[]{:S(2)}) collective-permute-start(bf16[256,1024]{1,0:T(8,128)(2,1)S(1)} %get-tuple-element.82), channel_id=1, source_target_pairs={{0,1},{1,0},{2,3},{3,2},{4,5},{5,4},{6,7},{7,6},{8,9},{9,8},{10,11... | collective-permute-start | bytes 1572872 | tf_op jit(solution)/shard_map/ppermute | solution.py:160
  84.1 13.9 %collective-permute-start.8 = (bf16[256,1024]{1,0:T(8,128)(2,1)S(1)}, bf16[256,1024]{1,0:T(8,128)(2,1)}, u32[]{:S(2)}, u32[]{:S(2)}) collective-permute-start(bf16[256,1024]{1,0:T(8,128)(2,1)S(1)} %collective-permute-done.7), channel_id=1, source_target_pairs={{0,1},{1,0},{2,3},{3,2},{4,5},{5,4},{6,7},{7,6},{8,9},{9,8},{10,11... | collective-permute-start | bytes 1572872 | tf_op jit(solution)/shard_map/ppermute | solution.py:160
  89.0 44.6 %collective-permute-start.11 = (bf16[256,1024]{1,0:T(8,128)(2,1)}, bf16[256,1024]{1,0:T(8,128)(2,1)}, u32[]{:S(2)}, u32[]{:S(2)}) collective-permute-start(bf16[256,1024]{1,0:T(8,128)(2,1)} %convolution_convert_fusion), channel_id=1, source_target_pairs={{0,8},{2,10},{4,12},{6,14},{8,0},{10,2},{12,4},{14,6},{16,24},{18,... | collective-permute-start | bytes 1572872 | tf_op jit(solution)/shard_map/ppermute | solution.py:154
  91.1 42.5 %collective-permute-start.12 = (bf16[256,1024]{1,0:T(8,128)(2,1)}, bf16[256,1024]{1,0:T(8,128)(2,1)}, u32[]{:S(2)}, u32[]{:S(2)}) collective-permute-start(bf16[256,1024]{1,0:T(8,128)(2,1)} %convolution_convert_fusion.1), channel_id=1, source_target_pairs={{0,8},{2,10},{4,12},{6,14},{8,0},{10,2},{12,4},{14,6},{16,24},{18,... | collective-permute-start | bytes 1572872 | tf_op jit(solution)/shard_map/ppermute | solution.py:154
  108.7 43.6 %collective-permute-start.15 = (bf16[256,1024]{1,0:T(8,128)(2,1)}, bf16[256,1024]{1,0:T(8,128)(2,1)S(1)}, u32[]{:S(2)}, u32[]{:S(2)}) collective-permute-start(bf16[256,1024]{1,0:T(8,128)(2,1)} %add_convert_fusion.1), channel_id=1, source_target_pairs={{0,16},{2,18},{4,20},{6,22},{8,24},{10,26},{12,28},{14,30},{16,0},... | collective-permute-start | bytes 1572872 | tf_op jit(solution)/shard_map/ppermute | solution.py:154
  121.4 43.0 %copy-start.11 = (bf16[256,2048]{1,0:T(8,128)(2,1)}, bf16[256,2048]{1,0:T(8,128)(2,1)S(1)}, u32[]{:S(2)}) copy-start(bf16[256,2048]{1,0:T(8,128)(2,1)S(1)} %maximum_select_fusion.2.low_ref) | copy-start | bytes 3145732
  137.2 19.7 %collective-permute-start.14 = (bf16[256,1024]{1,0:T(8,128)(2,1)S(1)}, bf16[256,1024]{1,0:T(8,128)(2,1)S(1)}, u32[]{:S(2)}, u32[]{:S(2)}) collective-permute-start(bf16[256,1024]{1,0:T(8,128)(2,1)S(1)} %add_convert_fusion), channel_id=1, source_target_pairs={{0,16},{2,18},{4,20},{6,22},{8,24},{10,26},{12,28},{14,30},{16,0},... | collective-permute-start | bytes 1572872 | tf_op jit(solution)/shard_map/ppermute | solution.py:154
  141.4 23.0 %collective-permute-start.16 = (bf16[256,1024]{1,0:T(8,128)(2,1)S(1)}, bf16[256,1024]{1,0:T(8,128)(2,1)S(1)}, u32[]{:S(2)}, u32[]{:S(2)}) collective-permute-start(bf16[256,1024]{1,0:T(8,128)(2,1)S(1)} %half_product.4), channel_id=1, source_target_pairs={{0,8},{2,10},{4,12},{6,14},{8,0},{10,2},{12,4},{14,6},{16,24},{18,... | collective-permute-start | bytes 1572872 | tf_op jit(solution)/shard_map/ppermute | solution.py:154
  146.3 42.4 %copy-start = (f32[256,1024]{1,0:T(8,128)}, f32[256,1024]{1,0:T(8,128)S(1)}, u32[]{:S(2)}) copy-start(f32[256,1024]{1,0:T(8,128)S(1)} %convolution_add_fusion.km_ref.vm_ref) | copy-start | bytes 3145732
  148.7 29.6 %collective-permute-start.13 = (bf16[256,1024]{1,0:T(8,128)(2,1)}, bf16[256,1024]{1,0:T(8,128)(2,1)}, u32[]{:S(2)}, u32[]{:S(2)}) collective-permute-start(bf16[256,1024]{1,0:T(8,128)(2,1)} %half_product.5), channel_id=1, source_target_pairs={{0,8},{2,10},{4,12},{6,14},{8,0},{10,2},{12,4},{14,6},{16,24},{18,... | collective-permute-start | bytes 1572872 | tf_op jit(solution)/shard_map/ppermute | solution.py:154
  152.2 36.5 %copy-start.3 = (bf16[256,1024]{1,0:T(8,128)(2,1)}, bf16[256,1024]{1,0:T(8,128)(2,1)S(1)}, u32[]{:S(2)}) copy-start(bf16[256,1024]{1,0:T(8,128)(2,1)S(1)} %collective-permute-done.15.kt_ref.vt_ref) | copy-start | bytes 1572868
  167.7 21.0 %collective-permute-start.18 = (bf16[128,1024]{1,0:T(8,128)(2,1)}, bf16[128,1024]{1,0:T(8,128)(2,1)}, u32[]{:S(2)}, u32[]{:S(2)}) collective-permute-start(bf16[128,1024]{1,0:T(8,128)(2,1)} %get-tuple-element.110), channel_id=1, source_target_pairs={{0,16},{2,18},{4,20},{6,22},{8,24},{10,26},{12,28},{14,30},{16,0},... | collective-permute-start | bytes 786440 | tf_op jit(solution)/shard_map/ppermute | solution.py:154
  181.7 14.8 %collective-permute-start.17 = (bf16[128,1024]{1,0:T(8,128)(2,1)}, bf16[128,1024]{1,0:T(8,128)(2,1)}, u32[]{:S(2)}, u32[]{:S(2)}) collective-permute-start(bf16[128,1024]{1,0:T(8,128)(2,1)} %get-tuple-element.115), channel_id=1, source_target_pairs={{0,16},{2,18},{4,20},{6,22},{8,24},{10,26},{12,28},{14,30},{16,0},... | collective-permute-start | bytes 786440 | tf_op jit(solution)/shard_map/ppermute | solution.py:154
  194.5 1.9 collective-permute-start.19
  194.6 3.7 %collective-permute-start.20 = (bf16[1,2048]{1,0:T(2,128)(2,1)S(1)}, bf16[1,2048]{1,0:T(2,128)(2,1)S(1)}, u32[]{:S(2)}, u32[]{:S(2)}) collective-permute-start(bf16[1,2048]{1,0:T(2,128)(2,1)S(1)} %pad_maximum_fusion.7), channel_id=1, source_target_pairs={{0,4},{2,6},{4,0},{6,2},{8,12},{10,14},{12,8},{14,10},{16,20},{18,... | collective-permute-start | bytes 12296 | tf_op jit(solution)/shard_map/ppermute | solution.py:154
  196.3 3.1 %collective-permute-start.21 = (bf16[1,2048]{1,0:T(2,128)(2,1)S(1)}, bf16[1,2048]{1,0:T(2,128)(2,1)S(1)}, u32[]{:S(2)}, u32[]{:S(2)}) collective-permute-start(bf16[1,2048]{1,0:T(2,128)(2,1)S(1)} %pad_maximum_fusion.7), channel_id=1, source_target_pairs={{0,6},{2,4},{4,2},{6,0},{8,14},{10,12},{12,10},{14,8},{16,22},{18,... | collective-permute-start | bytes 12296 | tf_op jit(solution)/shard_map/ppermute | solution.py:154
  200.0 11.0 %collective-permute-start.22 = (bf16[4,1,2048]{2,0,1:T(4,128)(2,1)S(1)}, bf16[4,1,2048]{2,0,1:T(4,128)(2,1)S(1)}, u32[]{:S(2)}, u32[]{:S(2)}) collective-permute-start(bf16[4,1,2048]{2,0,1:T(4,128)(2,1)S(1)} %reshape.23), channel_id=1, source_target_pairs={{0,8},{2,10},{4,12},{6,14},{8,0},{10,2},{12,4},{14,6},{16,24},{18,... | collective-permute-start | bytes 49160 | tf_op jit(solution)/shard_map/ppermute | solution.py:154
  200.2 10.8 %collective-permute-start.23 = (bf16[4,1,2048]{2,0,1:T(4,128)(2,1)S(1)}, bf16[4,1,2048]{2,0,1:T(4,128)(2,1)S(1)}, u32[]{:S(2)}, u32[]{:S(2)}) collective-permute-start(bf16[4,1,2048]{2,0,1:T(4,128)(2,1)S(1)} %reshape.23), channel_id=1, source_target_pairs={{0,16},{2,18},{4,20},{6,22},{8,24},{10,26},{12,28},{14,30},{16,0},... | collective-permute-start | bytes 49160 | tf_op jit(solution)/shard_map/ppermute | solution.py:154
  203.1 7.9 %collective-permute-start.24 = (bf16[4,1,2048]{2,0,1:T(4,128)(2,1)S(1)}, bf16[4,1,2048]{2,0,1:T(4,128)(2,1)S(1)}, u32[]{:S(2)}, u32[]{:S(2)}) collective-permute-start(bf16[4,1,2048]{2,0,1:T(4,128)(2,1)S(1)} %reshape.23), channel_id=1, source_target_pairs={{0,24},{2,26},{4,28},{6,30},{8,16},{10,18},{12,20},{14,22},{16,8},... | collective-permute-start | bytes 49160 | tf_op jit(solution)/shard_map/ppermute | solution.py:154
  (29 other events, 228.9 us)
Sparse Core Ops, SparseCore 0:
  9.8 37.1 all-gather.3
  48.6 34.4 all-gather.5
  85.2 34.4 all-gather.7

commit v11 on v8

--- a/solution.py
+++ b/solution.py
@@ -51,6 +51,25 @@
         cost_estimate=pl.CostEstimate(flops=0, bytes_accessed=cost, transcendentals=0),
         name="half_product",
     )(low, high, weight, *([] if first else [came]))
+
+
+def order_kernel(index_ref, *refs):
+    out_ref = refs[-1]
+    for m, ref in enumerate(refs[:-1]):
+        out_ref[index_ref[0] ^ m] = ref[...]
+
+
+def from_xor_order(values, index):
+    shape = values[0].shape
+    return pl.pallas_call(
+        order_kernel,
+        in_specs=[pl.BlockSpec(memory_space=pltpu.SMEM)]
+        + [pl.BlockSpec(memory_space=pltpu.VMEM)] * len(values),
+        out_specs=pl.BlockSpec(memory_space=pltpu.VMEM),
+        out_shape=jax.ShapeDtypeStruct((len(values), *shape), values[0].dtype),
+        cost_estimate=pl.CostEstimate(flops=0, bytes_accessed=COST, transcendentals=0),
+        name="order",
+    )(index[None].astype(jnp.int32), *values)
 
 
 def attention_kernel(
@@ -340,15 +359,6 @@
         attended[0], last = attend(place, parts_of[n], which, *caches, parts_of[0], *where)
         lasts.append(step(last))
 
-    def from_xor_order(values, index):
-        out = jnp.stack(values)
-        shape = out.shape
-        bits = len(values).bit_length() - 1
-        for bit in range(bits):
-            out = out.reshape(len(values) >> (bit + 1), 2, 1 << bit, *shape[1:])
-            out = jnp.where((index >> bit) % 2 == 1, out[:, ::-1], out)
-        return out.reshape(shape)
-
     start(0)
     if fast:
         tp_exchange(0)
@@ -379,12 +389,10 @@
         row = lasts[0]
     row = step(row)
     in_group = [row] + [over_inst(row, m) for m in range(1, INNER)]
-    arrive(len(jobs) - 1)
-    in_group[1] = step(in_group[1])
     in_group = from_xor_order(in_group, w)
     over_all = [in_group] + [over_outer(in_group, b) for b in range(1, outer)]
+    arrive(len(jobs) - 1)
     attention(len(jobs) - 1, 1)
-    over_all[1] = step(over_all[1])
     handoff = from_xor_order(over_all, z).reshape(n_inst, heads * wide)
     return (attended[0], handoff)
 

time: 209 us -> 214 us (1.024)
  Pallas kernels: 30.8 us -> 33.6 us
    pallas_call x0 -> x2, Pallas kernels: none -> 2.85 us  [from_xor_order(): pl.pallas_call(order_kernel, in_specs=[pl.BlockSpec(memory_space=pltpu.SM...]
  transfers between devices with their start and end apart: 28 -> 28, of which waited for: 12 -> 16; matrix products, arithmetic and copies ran while one was open for 15% -> 16% of each run, Pallas kernels for 15% -> 13%
where the time goes in v11:
time: 214 us
  waiting for transfers between devices  94.3 us (44%)
  Pallas kernels  33.6 us (16%)
  starting transfers between devices  31.2 us (15%)
  matrix products  21.4 us (10%)
  between operations  14.8 us (7%)
  other arithmetic  12.3 us (6%)
  local copies, waits for them, and re-layouts  6.12 us (3%)
    ppermute x19, waiting for transfers between devices, over_inst(): return lax.ppermute(value, 'inst', [(i, i ^ bits) for i in range(n_inst)])  67.1 us
    pallas_call x4, Pallas kernels, attend(): pl.pallas_call(attention_kernel, grid_spec=pltpu.PrefetchScalarGridSpec(n...  23 us
    ppermute x19, starting transfers between devices, over_inst(): return lax.ppermute(value, 'inst', [(i, i ^ bits) for i in range(n_inst)])  21.7 us
    dot_general x8, matrix products, dot(): return jnp.dot(a, b, preferred_element_type=jnp.float32)  21.4 us
    ppermute x6, waiting for transfers between devices, over_tp(): return lax.ppermute(value, 'tp', [(0, 1), (1, 0)])  15.7 us
    all_gather x3, waiting for transfers between devices, group_gather(): lax.all_gather(value, 'inst', axis=0, tiled=True, axis_index_groups=groups)  10.8 us
    ppermute x6, starting transfers between devices, over_tp(): return lax.ppermute(value, 'tp', [(0, 1), (1, 0)])  9.38 us
    pallas_call x4, Pallas kernels, half_product(): pl.pallas_call(first_kernel if first else later_kernel, grid=(columns //...  7.75 us
  transfers between devices with their start and end apart: 28, of which 16 were waited for; matrix products, arithmetic and copies ran while one was open for 16% of the time, Pallas kernels for 13%

profile of v11, /device:TPU:0, one launch (start us, length us, event | category | flops | bytes accessed | tf_op | source)
XLA Modules:
  0.0 213.8 jit_solution(18102062348720147334)
XLA Ops:
  7.2 2.4 %pad_maximum_fusion = bf16[512,1024]{1,0:T(8,128)(2,1)} fusion(bf16[512,512]{1,0:T(8,128)(2,1)} %param.10, bf16[512,512]{1,0:T(8,128)(2,1)} %param.9), kind=kLoop, calls=%fused_computation.6 | loop fusion | flops 2097152 | bytes 2097152 | tf_op jit(solution)/shard_map/concatenate | solution.py:207
  11.4 2.9 %collective-permute-start.1 = (bf16[256,1024]{1,0:T(8,128)(2,1)}, bf16[256,1024]{1,0:T(8,128)(2,1)}, u32[]{:S(2)}, u32[]{:S(2)}) collective-permute-start(bf16[256,1024]{1,0:T(8,128)(2,1)} %pad_maximum_fusion.1), channel_id=1, source_target_pairs={{0,1},{1,0},{2,3},{3,2},{4,5},{5,4},{6,7},{7,6},{8,9},{9,8},{10,11... | collective-permute-start | bytes 1572872 | tf_op jit(solution)/shard_map/ppermute | solution.py:179
  15.3 11.2 %collective-permute-done.1 = bf16[256,1024]{1,0:T(8,128)(2,1)} collective-permute-done((bf16[256,1024]{1,0:T(8,128)(2,1)}, bf16[256,1024]{1,0:T(8,128)(2,1)}, u32[]{:S(2)}, u32[]{:S(2)}) %collective-permute-start.1) | collective-permute-done | bytes 524320 | tf_op jit(solution)/shard_map/ppermute | solution.py:179
  26.5 2.3 %broadcast_select_fusion.1 = (bf16[256,1024]{1,0:T(8,128)(2,1)}, bf16[256,1024]{1,0:T(8,128)(2,1)}) fusion(bf16[256,1024]{1,0:T(8,128)(2,1)} %collective-permute-done.1, pred[]{:T(512)S(6)} %eq.21, bf16[128,1024]{1,0:T(8,128)(2,1)S(1)} %get-tuple-element.133, bf16[128,1024]{1,0:T(8,128)(2,1)S(1)} %get-tuple-element.134, pred[]{:T(512)S(6)} %eq.20), kind=kLoop, calls=%fused_computation.18 | loop fusion | flops 1572864 | bytes 2097154 | tf_op jit(solution)/shard_map/jit(_where)/select_n | solution.py:235
  33.2 2.5 %collective-permute-start.2 = (bf16[256,1024]{1,0:T(8,128)(2,1)S(1)}, bf16[256,1024]{1,0:T(8,128)(2,1)S(1)}, u32[]{:S(2)}, u32[]{:S(2)}) collective-permute-start(bf16[256,1024]{1,0:T(8,128)(2,1)S(1)} %copy-done.17), channel_id=1, source_target_pairs={{0,24},{2,26},{4,28},{6,30},{8,16},{10,18},{12,20},{14,22},{16,8},... | collective-permute-start | bytes 1572872 | tf_op jit(solution)/shard_map/ppermute | solution.py:173
  37.2 8.4 %collective-permute-done.3 = bf16[256,1024]{1,0:T(8,128)(2,1)S(1)} collective-permute-done((bf16[256,1024]{1,0:T(8,128)(2,1)S(1)}, bf16[256,1024]{1,0:T(8,128)(2,1)S(1)}, u32[]{:S(2)}, u32[]{:S(2)}) %collective-permute-start.3) | collective-permute-done | bytes 524320 | tf_op jit(solution)/shard_map/ppermute | solution.py:173
  47.1 10.7 %collective-permute-done.2 = bf16[256,1024]{1,0:T(8,128)(2,1)S(1)} collective-permute-done((bf16[256,1024]{1,0:T(8,128)(2,1)S(1)}, bf16[256,1024]{1,0:T(8,128)(2,1)S(1)}, u32[]{:S(2)}, u32[]{:S(2)}) %collective-permute-start.2) | collective-permute-done | bytes 524320 | tf_op jit(solution)/shard_map/ppermute | solution.py:173
  60.7 1.9 collective-permute-start.7
  63.0 2.1 convolution_convert_fusion.3
  66.0 4.5 %collective-permute-done.4 = bf16[256,1024]{1,0:T(8,128)(2,1)S(1)} collective-permute-done((bf16[256,1024]{1,0:T(8,128)(2,1)S(1)}, bf16[256,1024]{1,0:T(8,128)(2,1)S(1)}, u32[]{:S(2)}, u32[]{:S(2)}) %collective-permute-start.4) | collective-permute-done | bytes 524320 | tf_op jit(solution)/shard_map/ppermute | solution.py:179
  70.8 2.1 convolution_convert_fusion.2
  75.1 8.4 %collective-permute-done.7 = bf16[256,1024]{1,0:T(8,128)(2,1)} collective-permute-done((bf16[256,1024]{1,0:T(8,128)(2,1)S(1)}, bf16[256,1024]{1,0:T(8,128)(2,1)}, u32[]{:S(2)}, u32[]{:S(2)}) %collective-permute-start.7) | collective-permute-done | bytes 524320 | tf_op jit(solution)/shard_map/ppermute | solution.py:173
  83.9 4.4 %convolution_convert_fusion = bf16[256,1024]{1,0:T(8,128)(2,1)} fusion(bf16[256,2048]{1,0:T(8,128)(2,1)S(1)} %maximum_select_fusion.low_ref, bf16[2048,1024]{1,0:T(8,128)(2,1)} %all-gather.6.cloned.1.call-done), kind=kOutput, calls=%fused_computation.2 | convolution fusion | flops 1074003968 | bytes 5767168 | tf_op jit(solution)/shard_map/dot_general | solution.py:16
  89.6 2.1 convolution_convert_fusion.1
  92.5 9.8 %collective-permute-done.10 = bf16[256,1024]{1,0:T(8,128)(2,1)} collective-permute-done((bf16[256,1024]{1,0:T(8,128)(2,1)}, bf16[256,1024]{1,0:T(8,128)(2,1)}, u32[]{:S(2)}, u32[]{:S(2)}) %collective-permute-start.10) | collective-permute-done | bytes 524320 | tf_op jit(solution)/shard_map/ppermute | solution.py:173
  102.3 2.0 maximum_select_fusion.3.high_ref
  104.3 3.5 %add_convert_fusion.1 = bf16[256,1024]{1,0:T(8,128)(2,1)} fusion(bf16[256,1024]{1,0:T(8,128)(2,1)} %collective-permute-done.10, bf16[256,2048]{1,0:T(8,128)(2,1)S(1)} %maximum_select_fusion.3.high_ref, bf16[2048,1024]{1,0:T(8,128)(2,1)S(1)} %copy-done.27), kind=kOutput, calls=%fused_computation.12 | convolution fusion | flops 1074528256 | bytes 6291456 | tf_op jit(solution)/shard_map/dot_general | solution.py:16
  109.0 10.8 %all-gather.8.cloned.1.call-done.w_ref = bf16[2048,1024]{1,0:T(8,128)(2,1)} async-done(((bf16[512,1024]{1,0:T(8,128)(2,1)}), bf16[2048,1024]{1,0:T(8,128)(2,1)}) %all-gather.8.cloned.1.call-update) | async-done | bytes 4194320 | tf_op jit(solution)/shard_map/all_gather | solution.py:203
  119.8 2.2 %copy-done.1 = bf16[2048,1024]{1,0:T(8,128)(2,1)S(1)} copy-done((bf16[2048,1024]{1,0:T(8,128)(2,1)S(1)}, bf16[2048,1024]{1,0:T(8,128)(2,1)}, u32[]{:S(2)}) %copy-start.1) | copy-done | bytes 4194328
  125.3 16.1 %collective-permute-done.14 = bf16[256,1024]{1,0:T(8,128)(2,1)} collective-permute-done((bf16[256,1024]{1,0:T(8,128)(2,1)}, bf16[256,1024]{1,0:T(8,128)(2,1)}, u32[]{:S(2)}, u32[]{:S(2)}) %collective-permute-start.14) | collective-permute-done | bytes 524320 | tf_op jit(solution)/shard_map/ppermute | solution.py:173
  141.4 2.4 %add_convert_fusion = bf16[256,1024]{1,0:T(8,128)(2,1)S(1)} fusion(bf16[256,1024]{1,0:T(8,128)(2,1)} %collective-permute-done.14, bf16[256,2048]{1,0:T(8,128)(2,1)S(1)} %copy-done.9, bf16[2048,1024]{1,0:T(8,128)(2,1)S(1)} %copy-done.30), kind=kOutput, calls=%fused_computation.11 | convolution fusion | flops 1074528256 | bytes 6291456 | tf_op jit(solution)/shard_map/dot_general | solution.py:16
  144.4 2.4 %convolution_add_fusion.1.km_ref.vm_ref = f32[256,1024]{1,0:T(8,128)S(1)} fusion(bf16[256,2048]{1,0:T(8,128)(2,1)S(1)} %maximum_select_fusion.2.low_ref, bf16[2048,1024]{1,0:T(8,128)(2,1)S(1)} %copy-done.28, bf16[256,1024]{1,0:T(8,128)(2,1)} %collective-permute-done.9), kind=kOutput, calls=%fused_computation.1 | convolution fusion | flops 1074266112 | bytes 6815744 | tf_op jit(solution)/shard_map/dot_general | solution.py:16
  146.8 2.4 %collective-permute-done.11.came_ref = bf16[256,1024]{1,0:T(8,128)(2,1)S(1)} collective-permute-done((bf16[256,1024]{1,0:T(8,128)(2,1)S(1)}, bf16[256,1024]{1,0:T(8,128)(2,1)S(1)}, u32[]{:S(2)}, u32[]{:S(2)}) %collective-permute-start.11) | collective-permute-done | bytes 524320 | tf_op jit(solution)/shard_map/ppermute | solution.py:173
  153.0 2.8 %collective-permute-start.18 = (bf16[128,1024]{1,0:T(8,128)(2,1)S(1)}, bf16[128,1024]{1,0:T(8,128)(2,1)S(1)}, u32[]{:S(2)}, u32[]{:S(2)}) collective-permute-start(bf16[128,1024]{1,0:T(8,128)(2,1)S(1)} %get-tuple-element.103), channel_id=1, source_target_pairs={{0,16},{2,18},{4,20},{6,22},{8,24},{10,26},{12,28},{14,30},{16,0},... | collective-permute-start | bytes 786440 | tf_op jit(solution)/shard_map/ppermute | solution.py:173
  155.9 2.3 %convolution_add_fusion.qm_ref = f32[256,1024]{1,0:T(8,128)S(1)} fusion(bf16[256,2048]{1,0:T(8,128)(2,1)S(1)} %maximum_select_fusion.2.low_ref, bf16[2048,1024]{1,0:T(8,128)(2,1)S(1)} %copy-done.30, bf16[256,1024]{1,0:T(8,128)(2,1)} %collective-permute-done.13), kind=kOutput, calls=%fused_computation | convolution fusion | flops 1074266112 | bytes 6815744 | tf_op jit(solution)/shard_map/dot_general | solution.py:16
  158.2 4.2 %collective-permute-done.16.qc_ref = bf16[256,1024]{1,0:T(8,128)(2,1)S(1)} collective-permute-done((bf16[256,1024]{1,0:T(8,128)(2,1)S(1)}, bf16[256,1024]{1,0:T(8,128)(2,1)S(1)}, u32[]{:S(2)}, u32[]{:S(2)}) %collective-permute-start.16) | collective-permute-done | bytes 524320 | tf_op jit(solution)/shard_map/ppermute | solution.py:173
  162.4 5.4 %attention.4 = (bf16[256,2048]{1,0:T(8,128)(2,1)}, bf16[1,1024]{1,0:T(2,128)(2,1)S(1)}) custom-call(s32[3]{0:T(128)S(1)} %get-tuple-element.145.place_ref, f32[256,1024]{1,0:T(8,128)S(1)} %convolution_add_fusion.qm_ref, bf16[256,1024]{1,0:T(8,128)(2,1)S(1)} %collective-permute-done.16.qc_ref, bf16[1792,512]{1,0:T(8,128)(2,1)S(1)} %copy-done.4, ...), custom_call_target="tpu_custom_call" | custom-call | bytes 1024 | tf_op jit(solution)/shard_map/attention/pallas_call | solution.py:128
  167.8 5.4 %attention.5 = (bf16[256,2048]{1,0:T(8,128)(2,1)}, bf16[1,1024]{1,0:T(2,128)(2,1)S(1)}) custom-call(s32[3]{0:T(128)S(1)} %get-tuple-element.144.place_ref, f32[256,1024]{1,0:T(8,128)S(1)} %convolution_add_fusion.qm_ref, bf16[256,1024]{1,0:T(8,128)(2,1)S(1)} %collective-permute-done.16.qc_ref, ...), custom_call_target="tpu_custom_call", output_to_operand_aliasing={{0}: (9, {})} | custom-call | bytes 1024 | tf_op jit(solution)/shard_map/attention/pallas_call | solution.py:128
  174.2 2.4 %half_product.7 = (bf16[128,1024]{1,0:T(8,128)(2,1)}, f32[128,1024]{1,0:T(8,128)S(1)}) custom-call(bf16[256,2048]{1,0:T(8,128)(2,1)S(1)} %maximum_select_fusion.2.low_ref, bf16[256,2048]{1,0:T(8,128)(2,1)S(1)} %copy-done.9, bf16[2048,1024]{1,0:T(8,128)(2,1)S(1)} %copy-done.2, bf16[256,1024]{1,0:T(8,128)(2,1)S(1)} %collective-permute-done.15.came_ref), custom_call_target="tpu_custom_call" | custom-call | bytes 1024 | tf_op jit(solution)/shard_map/half_product/pallas_call | solution.py:42
  176.7 5.7 %attention.6 = (bf16[256,2048]{1,0:T(8,128)(2,1)}, bf16[1,1024]{1,0:T(2,128)(2,1)S(1)}) custom-call(s32[3]{0:T(128)S(1)} %get-tuple-element.145.place_ref, f32[128,1024]{1,0:T(8,128)S(1)} %get-tuple-element.120.qm_ref, bf16[128,1024]{1,0:T(8,128)(2,1)S(1)} %collective-permute-done.18.qc_ref, ...), custom_call_target="tpu_custom_call", output_to_operand_aliasing={{0}: (9, {})} | custom-call | bytes 1024 | tf_op jit(solution)/shard_map/attention/pallas_call | solution.py:128
  188.7 2.2 %collective-permute-start.24 = (bf16[4,1,2048]{2,1,0:T(2,128)(2,1)}, bf16[4,1,2048]{2,1,0:T(2,128)(2,1)S(1)}, u32[]{:S(2)}, u32[]{:S(2)}) collective-permute-start(bf16[4,1,2048]{2,1,0:T(2,128)(2,1)} %order.2.refs_0_), channel_id=1, source_target_pairs={{0,24},{2,26},{4,28},{6,30},{8,16},{10,18},{12,20},{14,22},{16,8},... | collective-permute-start | bytes 49160 | tf_op jit(solution)/shard_map/ppermute | solution.py:173
  200.8 6.5 %attention.7 = (bf16[256,2048]{1,0:T(8,128)(2,1)}, bf16[1,1024]{1,0:T(2,128)(2,1)}) custom-call(s32[3]{0:T(128)} %copy-done.11, f32[128,1024]{1,0:T(8,128)} %copy-done.10, bf16[128,1024]{1,0:T(8,128)(2,1)} %collective-permute-done.17.qc_ref, bf16[1792,512]{1,0:T(8,128)(2,1)} %kc_ref.7, bf16[1792,512]{1,0:T(8,128)(2,1)} %vc_ref.7, ...), custom_call_target="tpu_custom_call", output_to_operand_aliasing={{0}: (9, {})} | custom-call | bytes 1024 | tf_op jit(solution)/shard_map/attention/pallas_call | solution.py:128
  (124 shorter events, 44.4 us)
Async XLA Ops:
  7.2 39.9 %all-gather.4.cloned.1.call-start = ((), (), s32[]{:S(2)}) async-start(), calls=%async_computation | async-start | bytes 5242880 | tf_op jit(solution)/shard_map/all_gather | solution.py:203
  9.7 74.2 %all-gather.6.cloned.1.call-start = ((), (), s32[]{:S(2)}) async-start(), calls=%async_computation.1 | async-start | bytes 5242880 | tf_op jit(solution)/shard_map/all_gather | solution.py:203
  11.4 15.2 %collective-permute-start.1 = (bf16[256,1024]{1,0:T(8,128)(2,1)}, bf16[256,1024]{1,0:T(8,128)(2,1)}, u32[]{:S(2)}, u32[]{:S(2)}) collective-permute-start(bf16[256,1024]{1,0:T(8,128)(2,1)} %pad_maximum_fusion.1), channel_id=1, source_target_pairs={{0,1},{1,0},{2,3},{3,2},{4,5},{5,4},{6,7},{7,6},{8,9},{9,8},{10,11... | collective-permute-start | bytes 1572872 | tf_op jit(solution)/shard_map/ppermute | solution.py:179
  30.4 89.4 %all-gather.8.cloned.1.call-start = ((), (), s32[]{:S(2)}) async-start(), calls=%async_computation.2 | async-start | bytes 5242880 | tf_op jit(solution)/shard_map/all_gather | solution.py:203
  31.4 14.2 %collective-permute-start.3 = (bf16[256,1024]{1,0:T(8,128)(2,1)S(1)}, bf16[256,1024]{1,0:T(8,128)(2,1)S(1)}, u32[]{:S(2)}, u32[]{:S(2)}) collective-permute-start(bf16[256,1024]{1,0:T(8,128)(2,1)S(1)} %copy-done.18), channel_id=1, source_target_pairs={{0,8},{2,10},{4,12},{6,14},{8,0},{10,2},{12,4},{14,6},{16,24},{18,... | collective-permute-start | bytes 1572872 | tf_op jit(solution)/shard_map/ppermute | solution.py:173
  33.2 24.6 %collective-permute-start.2 = (bf16[256,1024]{1,0:T(8,128)(2,1)S(1)}, bf16[256,1024]{1,0:T(8,128)(2,1)S(1)}, u32[]{:S(2)}, u32[]{:S(2)}) collective-permute-start(bf16[256,1024]{1,0:T(8,128)(2,1)S(1)} %copy-done.17), channel_id=1, source_target_pairs={{0,24},{2,26},{4,28},{6,30},{8,16},{10,18},{12,20},{14,22},{16,8},... | collective-permute-start | bytes 1572872 | tf_op jit(solution)/shard_map/ppermute | solution.py:173
  35.7 23.6 %collective-permute-start = (bf16[256,1024]{1,0:T(8,128)(2,1)S(1)}, bf16[256,1024]{1,0:T(8,128)(2,1)}, u32[]{:S(2)}, u32[]{:S(2)}) collective-permute-start(bf16[256,1024]{1,0:T(8,128)(2,1)S(1)} %copy-done.16), channel_id=1, source_target_pairs={{0,1},{1,0},{2,3},{3,2},{4,5},{5,4},{6,7},{7,6},{8,9},{9,8},{10,11... | collective-permute-start | bytes 1572872 | tf_op jit(solution)/shard_map/ppermute | solution.py:179
  45.6 17.0 %collective-permute-start.5 = (bf16[256,1024]{1,0:T(8,128)(2,1)S(1)}, bf16[256,1024]{1,0:T(8,128)(2,1)S(1)}, u32[]{:S(2)}, u32[]{:S(2)}) collective-permute-start(bf16[256,1024]{1,0:T(8,128)(2,1)S(1)} %collective-permute-done.3), channel_id=1, source_target_pairs={{0,1},{1,0},{2,3},{3,2},{4,5},{5,4},{6,7},{7,6},{8,9},{9,8},{10,11... | collective-permute-start | bytes 1572872 | tf_op jit(solution)/shard_map/ppermute | solution.py:179
  57.8 12.6 %collective-permute-start.4 = (bf16[256,1024]{1,0:T(8,128)(2,1)S(1)}, bf16[256,1024]{1,0:T(8,128)(2,1)S(1)}, u32[]{:S(2)}, u32[]{:S(2)}) collective-permute-start(bf16[256,1024]{1,0:T(8,128)(2,1)S(1)} %collective-permute-done.2), channel_id=1, source_target_pairs={{0,1},{1,0},{2,3},{3,2},{4,5},{5,4},{6,7},{7,6},{8,9},{9,8},{10,11... | collective-permute-start | bytes 1572872 | tf_op jit(solution)/shard_map/ppermute | solution.py:179
  60.7 22.7 %collective-permute-start.7 = (bf16[256,1024]{1,0:T(8,128)(2,1)S(1)}, bf16[256,1024]{1,0:T(8,128)(2,1)}, u32[]{:S(2)}, u32[]{:S(2)}) collective-permute-start(bf16[256,1024]{1,0:T(8,128)(2,1)S(1)} %get-tuple-element.76), channel_id=1, source_target_pairs={{0,16},{2,18},{4,20},{6,22},{8,24},{10,26},{12,28},{14,30},{16,0},... | collective-permute-start | bytes 1572872 | tf_op jit(solution)/shard_map/ppermute | solution.py:173
  65.1 27.4 %collective-permute-start.9 = (bf16[256,1024]{1,0:T(8,128)(2,1)}, bf16[256,1024]{1,0:T(8,128)(2,1)}, u32[]{:S(2)}, u32[]{:S(2)}) collective-permute-start(bf16[256,1024]{1,0:T(8,128)(2,1)} %convolution_convert_fusion.3), channel_id=1, source_target_pairs={{0,8},{2,10},{4,12},{6,14},{8,0},{10,2},{12,4},{14,6},{16,24},{18,... | collective-permute-start | bytes 1572872 | tf_op jit(solution)/shard_map/ppermute | solution.py:173
  70.8 48.9 %copy-start.6 = (bf16[256,2048]{1,0:T(8,128)(2,1)}, bf16[256,2048]{1,0:T(8,128)(2,1)S(1)}, u32[]{:S(2)}) copy-start(bf16[256,2048]{1,0:T(8,128)(2,1)S(1)} %maximum_select_fusion.1.high_ref) | copy-start | bytes 3145732
  72.9 29.4 %collective-permute-start.10 = (bf16[256,1024]{1,0:T(8,128)(2,1)}, bf16[256,1024]{1,0:T(8,128)(2,1)}, u32[]{:S(2)}, u32[]{:S(2)}) collective-permute-start(bf16[256,1024]{1,0:T(8,128)(2,1)} %convolution_convert_fusion.2), channel_id=1, source_target_pairs={{0,8},{2,10},{4,12},{6,14},{8,0},{10,2},{12,4},{14,6},{16,24},{18,... | collective-permute-start | bytes 1572872 | tf_op jit(solution)/shard_map/ppermute | solution.py:173
  73.6 18.1 %collective-permute-start.6 = (bf16[256,1024]{1,0:T(8,128)(2,1)S(1)}, bf16[256,1024]{1,0:T(8,128)(2,1)S(1)}, u32[]{:S(2)}, u32[]{:S(2)}) collective-permute-start(bf16[256,1024]{1,0:T(8,128)(2,1)S(1)} %get-tuple-element.82), channel_id=1, source_target_pairs={{0,1},{1,0},{2,3},{3,2},{4,5},{5,4},{6,7},{7,6},{8,9},{9,8},{10,11... | collective-permute-start | bytes 1572872 | tf_op jit(solution)/shard_map/ppermute | solution.py:179
  83.4 18.9 %collective-permute-start.8 = (bf16[256,1024]{1,0:T(8,128)(2,1)}, bf16[256,1024]{1,0:T(8,128)(2,1)}, u32[]{:S(2)}, u32[]{:S(2)}) collective-permute-start(bf16[256,1024]{1,0:T(8,128)(2,1)} %collective-permute-done.7), channel_id=1, source_target_pairs={{0,1},{1,0},{2,3},{3,2},{4,5},{5,4},{6,7},{7,6},{8,9},{9,8},{10,11... | collective-permute-start | bytes 1572872 | tf_op jit(solution)/shard_map/ppermute | solution.py:179
  88.3 53.0 %collective-permute-start.13 = (bf16[256,1024]{1,0:T(8,128)(2,1)}, bf16[256,1024]{1,0:T(8,128)(2,1)}, u32[]{:S(2)}, u32[]{:S(2)}) collective-permute-start(bf16[256,1024]{1,0:T(8,128)(2,1)} %convolution_convert_fusion), channel_id=1, source_target_pairs={{0,8},{2,10},{4,12},{6,14},{8,0},{10,2},{12,4},{14,6},{16,24},{18,... | collective-permute-start | bytes 1572872 | tf_op jit(solution)/shard_map/ppermute | solution.py:173
  91.7 49.7 %collective-permute-start.14 = (bf16[256,1024]{1,0:T(8,128)(2,1)}, bf16[256,1024]{1,0:T(8,128)(2,1)}, u32[]{:S(2)}, u32[]{:S(2)}) collective-permute-start(bf16[256,1024]{1,0:T(8,128)(2,1)} %convolution_convert_fusion.1), channel_id=1, source_target_pairs={{0,8},{2,10},{4,12},{6,14},{8,0},{10,2},{12,4},{14,6},{16,24},{18,... | collective-permute-start | bytes 1572872 | tf_op jit(solution)/shard_map/ppermute | solution.py:173
  107.9 39.0 %collective-permute-start.12 = (bf16[256,1024]{1,0:T(8,128)(2,1)}, bf16[256,1024]{1,0:T(8,128)(2,1)S(1)}, u32[]{:S(2)}, u32[]{:S(2)}) collective-permute-start(bf16[256,1024]{1,0:T(8,128)(2,1)} %add_convert_fusion.1), channel_id=1, source_target_pairs={{0,16},{2,18},{4,20},{6,22},{8,24},{10,26},{12,28},{14,30},{16,0},... | collective-permute-start | bytes 1572872 | tf_op jit(solution)/shard_map/ppermute | solution.py:173
  123.7 20.2 %copy-start.15 = (bf16[256,1024]{1,0:T(8,128)(2,1)S(1)}, bf16[256,1024]{1,0:T(8,128)(2,1)}, u32[]{:S(2)}) copy-start(bf16[256,1024]{1,0:T(8,128)(2,1)} %copy-done.14) | copy-start | bytes 1572868
  123.7 25.6 %collective-permute-start.11 = (bf16[256,1024]{1,0:T(8,128)(2,1)S(1)}, bf16[256,1024]{1,0:T(8,128)(2,1)S(1)}, u32[]{:S(2)}, u32[]{:S(2)}) collective-permute-start(bf16[256,1024]{1,0:T(8,128)(2,1)S(1)} %half_product.4), channel_id=1, source_target_pairs={{0,8},{2,10},{4,12},{6,14},{8,0},{10,2},{12,4},{14,6},{16,24},{18,... | collective-permute-start | bytes 1572872 | tf_op jit(solution)/shard_map/ppermute | solution.py:173
  144.3 18.1 %collective-permute-start.16 = (bf16[256,1024]{1,0:T(8,128)(2,1)S(1)}, bf16[256,1024]{1,0:T(8,128)(2,1)S(1)}, u32[]{:S(2)}, u32[]{:S(2)}) collective-permute-start(bf16[256,1024]{1,0:T(8,128)(2,1)S(1)} %add_convert_fusion), channel_id=1, source_target_pairs={{0,16},{2,18},{4,20},{6,22},{8,24},{10,26},{12,28},{14,30},{16,0},... | collective-permute-start | bytes 1572872 | tf_op jit(solution)/shard_map/ppermute | solution.py:173
  146.8 29.9 %copy-start = (f32[256,1024]{1,0:T(8,128)}, f32[256,1024]{1,0:T(8,128)S(1)}, u32[]{:S(2)}) copy-start(f32[256,1024]{1,0:T(8,128)S(1)} %convolution_add_fusion.1.km_ref.vm_ref) | copy-start | bytes 3145732
  146.8 29.8 %copy-start.3 = (bf16[256,1024]{1,0:T(8,128)(2,1)}, bf16[256,1024]{1,0:T(8,128)(2,1)S(1)}, u32[]{:S(2)}) copy-start(bf16[256,1024]{1,0:T(8,128)(2,1)S(1)} %collective-permute-done.12.kt_ref.vt_ref) | copy-start | bytes 1572868
  152.9 21.3 %collective-permute-start.15 = (bf16[256,1024]{1,0:T(8,128)(2,1)S(1)}, bf16[256,1024]{1,0:T(8,128)(2,1)S(1)}, u32[]{:S(2)}, u32[]{:S(2)}) collective-permute-start(bf16[256,1024]{1,0:T(8,128)(2,1)S(1)} %half_product.6), channel_id=1, source_target_pairs={{0,8},{2,10},{4,12},{6,14},{8,0},{10,2},{12,4},{14,6},{16,24},{18,... | collective-permute-start | bytes 1572872 | tf_op jit(solution)/shard_map/ppermute | solution.py:173
  153.0 23.6 %collective-permute-start.18 = (bf16[128,1024]{1,0:T(8,128)(2,1)S(1)}, bf16[128,1024]{1,0:T(8,128)(2,1)S(1)}, u32[]{:S(2)}, u32[]{:S(2)}) collective-permute-start(bf16[128,1024]{1,0:T(8,128)(2,1)S(1)} %get-tuple-element.103), channel_id=1, source_target_pairs={{0,16},{2,18},{4,20},{6,22},{8,24},{10,26},{12,28},{14,30},{16,0},... | collective-permute-start | bytes 786440 | tf_op jit(solution)/shard_map/ppermute | solution.py:173
  176.6 24.1 %collective-permute-start.17 = (bf16[128,1024]{1,0:T(8,128)(2,1)}, bf16[128,1024]{1,0:T(8,128)(2,1)}, u32[]{:S(2)}, u32[]{:S(2)}) collective-permute-start(bf16[128,1024]{1,0:T(8,128)(2,1)} %get-tuple-element.117), channel_id=1, source_target_pairs={{0,16},{2,18},{4,20},{6,22},{8,24},{10,26},{12,28},{14,30},{16,0},... | collective-permute-start | bytes 786440 | tf_op jit(solution)/shard_map/ppermute | solution.py:173
  182.4 3.1 %collective-permute-start.21 = (bf16[1,2048]{1,0:T(2,128)(2,1)S(1)}, bf16[1,2048]{1,0:T(2,128)(2,1)S(1)}, u32[]{:S(2)}, u32[]{:S(2)}) collective-permute-start(bf16[1,2048]{1,0:T(2,128)(2,1)S(1)} %pad_maximum_fusion.5.refs_0_), channel_id=1, source_target_pairs={{0,6},{2,4},{4,2},{6,0},{8,14},{10,12},{12,10},{14,8},{16,22},{18,... | collective-permute-start | bytes 12296 | tf_op jit(solution)/shard_map/ppermute | solution.py:173
  183.0 3.7 %collective-permute-start.20 = (bf16[1,2048]{1,0:T(2,128)(2,1)S(1)}, bf16[1,2048]{1,0:T(2,128)(2,1)S(1)}, u32[]{:S(2)}, u32[]{:S(2)}) collective-permute-start(bf16[1,2048]{1,0:T(2,128)(2,1)S(1)} %pad_maximum_fusion.5.refs_0_), channel_id=1, source_target_pairs={{0,4},{2,6},{4,0},{6,2},{8,12},{10,14},{12,8},{14,10},{16,20},{18,... | collective-permute-start | bytes 12296 | tf_op jit(solution)/shard_map/ppermute | solution.py:173
  183.8 2.9 %collective-permute-start.19 = (bf16[1,2048]{1,0:T(2,128)(2,1)S(1)}, bf16[1,2048]{1,0:T(2,128)(2,1)S(1)}, u32[]{:S(2)}, u32[]{:S(2)}) collective-permute-start(bf16[1,2048]{1,0:T(2,128)(2,1)S(1)} %pad_maximum_fusion.5.refs_0_), channel_id=1, source_target_pairs={{0,2},{2,0},{4,6},{6,4},{8,10},{10,8},{12,14},{14,12},{16,18},{18,... | collective-permute-start | bytes 12296 | tf_op jit(solution)/shard_map/ppermute | solution.py:173
  188.7 6.0 %collective-permute-start.24 = (bf16[4,1,2048]{2,1,0:T(2,128)(2,1)}, bf16[4,1,2048]{2,1,0:T(2,128)(2,1)S(1)}, u32[]{:S(2)}, u32[]{:S(2)}) collective-permute-start(bf16[4,1,2048]{2,1,0:T(2,128)(2,1)} %order.2.refs_0_), channel_id=1, source_target_pairs={{0,24},{2,26},{4,28},{6,30},{8,16},{10,18},{12,20},{14,22},{16,8},... | collective-permute-start | bytes 49160 | tf_op jit(solution)/shard_map/ppermute | solution.py:173
  190.9 5.4 %collective-permute-start.23 = (bf16[4,1,2048]{2,1,0:T(2,128)(2,1)}, bf16[4,1,2048]{2,1,0:T(2,128)(2,1)S(1)}, u32[]{:S(2)}, u32[]{:S(2)}) collective-permute-start(bf16[4,1,2048]{2,1,0:T(2,128)(2,1)} %order.2.refs_0_), channel_id=1, source_target_pairs={{0,16},{2,18},{4,20},{6,22},{8,24},{10,26},{12,28},{14,30},{16,0},... | collective-permute-start | bytes 49160 | tf_op jit(solution)/shard_map/ppermute | solution.py:173
  192.6 4.1 %collective-permute-start.22 = (bf16[4,1,2048]{2,1,0:T(2,128)(2,1)}, bf16[4,1,2048]{2,1,0:T(2,128)(2,1)S(1)}, u32[]{:S(2)}, u32[]{:S(2)}) collective-permute-start(bf16[4,1,2048]{2,1,0:T(2,128)(2,1)} %order.2.refs_0_), channel_id=1, source_target_pairs={{0,8},{2,10},{4,12},{6,14},{8,0},{10,2},{12,4},{14,6},{16,24},{18,... | collective-permute-start | bytes 49160 | tf_op jit(solution)/shard_map/ppermute | solution.py:173
  (27 other events, 169.7 us)
Sparse Core Ops, SparseCore 0:
  9.8 37.1 all-gather.3
  49.1 34.4 all-gather.5
  85.2 34.4 all-gather.7

commit v12 on v11

--- a/solution.py
+++ b/solution.py
@@ -59,14 +59,13 @@
         out_ref[index_ref[0] ^ m] = ref[...]
 
 
-def from_xor_order(values, index):
-    shape = values[0].shape
+def ordered(values, index):
     return pl.pallas_call(
         order_kernel,
         in_specs=[pl.BlockSpec(memory_space=pltpu.SMEM)]
         + [pl.BlockSpec(memory_space=pltpu.VMEM)] * len(values),
         out_specs=pl.BlockSpec(memory_space=pltpu.VMEM),
-        out_shape=jax.ShapeDtypeStruct((len(values), *shape), values[0].dtype),
+        out_shape=jax.ShapeDtypeStruct((len(values), *values[0].shape), values[0].dtype),
         cost_estimate=pl.CostEstimate(flops=0, bytes_accessed=COST, transcendentals=0),
         name="order",
     )(index[None].astype(jnp.int32), *values)
@@ -95,13 +94,14 @@
         each = [
             slice((member + i) * HEAD_SIZE, (member + i + 1) * HEAD_SIZE) for i in range(stack)
         ]
-        q = jnp.concatenate([total(qm_ref[:, cols], qc_ref[:, cols]) for cols in each], axis=0)
+        q = [qm_ref[:, cols] + qc_ref[:, cols].astype(jnp.float32) for cols in each]
+        q = (jnp.concatenate(q, axis=0) * factor).astype(jnp.bfloat16)
         s1 = lax.dot_general(q, kc_ref[...], contract, preferred_element_type=jnp.float32)
         s2 = lax.dot_general(q, keys, contract, preferred_element_type=jnp.float32)
         s2 = jnp.where(allowed, s2, -jnp.inf)
         top = jnp.maximum(jnp.max(s1, axis=1, keepdims=True), jnp.max(s2, axis=1, keepdims=True))
-        p1 = jnp.exp2((s1 - top) * factor)
-        p2 = jnp.exp2((s2 - top) * factor)
+        p1 = jnp.exp2(s1 - top)
+        p2 = jnp.exp2(s2 - top)
         norm = jnp.sum(p1, axis=1, keepdims=True) + jnp.sum(p2, axis=1, keepdims=True)
         both = dot(p1.astype(jnp.bfloat16), vc_ref[...]) + dot(p2.astype(jnp.bfloat16), values)
         both = both / norm
@@ -359,6 +359,15 @@
         attended[0], last = attend(place, parts_of[n], which, *caches, parts_of[0], *where)
         lasts.append(step(last))
 
+    def from_xor_order(values, index):
+        out = jnp.stack(values)
+        shape = out.shape
+        bits = len(values).bit_length() - 1
+        for bit in range(bits):
+            out = out.reshape(len(values) >> (bit + 1), 2, 1 << bit, *shape[1:])
+            out = jnp.where((index >> bit) % 2 == 1, out[:, ::-1], out)
+        return out.reshape(shape)
+
     start(0)
     if fast:
         tp_exchange(0)
@@ -389,10 +398,11 @@
         row = lasts[0]
     row = step(row)
     in_group = [row] + [over_inst(row, m) for m in range(1, INNER)]
-    in_group = from_xor_order(in_group, w)
+    in_group = ordered(in_group, w)
     over_all = [in_group] + [over_outer(in_group, b) for b in range(1, outer)]
     arrive(len(jobs) - 1)
     attention(len(jobs) - 1, 1)
+    attended[0], *over_all[1:] = step(attended[0], *over_all[1:])
     handoff = from_xor_order(over_all, z).reshape(n_inst, heads * wide)
     return (attended[0], handoff)
 

time: 214 us -> 208 us (0.972)
  waiting for transfers between devices: 94.3 us -> 90.5 us
    ppermute x19, waiting for transfers between devices: 67.1 us -> 63.4 us  [over_inst(): return lax.ppermute(value, 'inst', [(i, i ^ bits) for i in range(n_inst)])]
  transfers between devices with their start and end apart: 28 -> 28, of which waited for: 16 -> 13; matrix products, arithmetic and copies ran while one was open for 16% -> 16% of each run, Pallas kernels for 13% -> 15%
where the time goes in v12:
time: 208 us
  waiting for transfers between devices  90.5 us (44%)
  Pallas kernels  32.2 us (15%)
  starting transfers between devices  31.2 us (15%)
  matrix products  21.4 us (10%)
  between operations  14.9 us (7%)
  other arithmetic  11.1 us (5%)
  local copies, waits for them, and re-layouts  6.37 us (3%)
    ppermute x19, waiting for transfers between devices, over_inst(): return lax.ppermute(value, 'inst', [(i, i ^ bits) for i in range(n_inst)])  63.4 us
    pallas_call x4, Pallas kernels, attend(): pl.pallas_call(attention_kernel, grid_spec=pltpu.PrefetchScalarGridSpec(n...  23.1 us
    ppermute x19, starting transfers between devices, over_inst(): return lax.ppermute(value, 'inst', [(i, i ^ bits) for i in range(n_inst)])  21.8 us
    dot_general x8, matrix products, dot(): return jnp.dot(a, b, preferred_element_type=jnp.float32)  21.4 us
    ppermute x6, waiting for transfers between devices, over_tp(): return lax.ppermute(value, 'tp', [(0, 1), (1, 0)])  15.7 us
    all_gather x3, waiting for transfers between devices, group_gather(): lax.all_gather(value, 'inst', axis=0, tiled=True, axis_index_groups=groups)  10.8 us
    ppermute x6, starting transfers between devices, over_tp(): return lax.ppermute(value, 'tp', [(0, 1), (1, 0)])  9.37 us
    pallas_call x4, Pallas kernels, half_product(): pl.pallas_call(first_kernel if first else later_kernel, grid=(columns //...  7.74 us
  transfers between devices with their start and end apart: 28, of which 13 were waited for; matrix products, arithmetic and copies ran while one was open for 16% of the time, Pallas kernels for 15%

profile of v12, /device:TPU:0, one launch (start us, length us, event | category | flops | bytes accessed | tf_op | source)
XLA Modules:
  0.0 207.7 jit_solution(17189020134257750151)
XLA Ops:
  7.2 2.4 %pad_maximum_fusion = bf16[512,1024]{1,0:T(8,128)(2,1)} fusion(bf16[512,512]{1,0:T(8,128)(2,1)} %param.10, bf16[512,512]{1,0:T(8,128)(2,1)} %param.9), kind=kLoop, calls=%fused_computation.6 | loop fusion | flops 2097152 | bytes 2097152 | tf_op jit(solution)/shard_map/concatenate | solution.py:207
  11.4 2.9 %collective-permute-start.1 = (bf16[256,1024]{1,0:T(8,128)(2,1)}, bf16[256,1024]{1,0:T(8,128)(2,1)}, u32[]{:S(2)}, u32[]{:S(2)}) collective-permute-start(bf16[256,1024]{1,0:T(8,128)(2,1)} %pad_maximum_fusion.1), channel_id=1, source_target_pairs={{0,1},{1,0},{2,3},{3,2},{4,5},{5,4},{6,7},{7,6},{8,9},{9,8},{10,11... | collective-permute-start | bytes 1572872 | tf_op jit(solution)/shard_map/ppermute | solution.py:179
  15.3 11.2 %collective-permute-done.1 = bf16[256,1024]{1,0:T(8,128)(2,1)} collective-permute-done((bf16[256,1024]{1,0:T(8,128)(2,1)}, bf16[256,1024]{1,0:T(8,128)(2,1)}, u32[]{:S(2)}, u32[]{:S(2)}) %collective-permute-start.1) | collective-permute-done | bytes 524320 | tf_op jit(solution)/shard_map/ppermute | solution.py:179
  26.5 2.3 %broadcast_select_fusion.1 = (bf16[256,1024]{1,0:T(8,128)(2,1)}, bf16[256,1024]{1,0:T(8,128)(2,1)}) fusion(bf16[256,1024]{1,0:T(8,128)(2,1)} %collective-permute-done.1, pred[]{:T(512)S(6)} %eq.29, bf16[128,1024]{1,0:T(8,128)(2,1)S(1)} %get-tuple-element.141, bf16[128,1024]{1,0:T(8,128)(2,1)S(1)} %get-tuple-element.142, pred[]{:T(512)S(6)} %eq.28), kind=kLoop, calls=%fused_computation.18 | loop fusion | flops 1572864 | bytes 2097154 | tf_op jit(solution)/shard_map/jit(_where)/select_n | solution.py:235
  33.2 2.5 %collective-permute-start.2 = (bf16[256,1024]{1,0:T(8,128)(2,1)S(1)}, bf16[256,1024]{1,0:T(8,128)(2,1)S(1)}, u32[]{:S(2)}, u32[]{:S(2)}) collective-permute-start(bf16[256,1024]{1,0:T(8,128)(2,1)S(1)} %copy-done.17), channel_id=1, source_target_pairs={{0,24},{2,26},{4,28},{6,30},{8,16},{10,18},{12,20},{14,22},{16,8},... | collective-permute-start | bytes 1572872 | tf_op jit(solution)/shard_map/ppermute | solution.py:173
  37.2 8.4 %collective-permute-done.3 = bf16[256,1024]{1,0:T(8,128)(2,1)S(1)} collective-permute-done((bf16[256,1024]{1,0:T(8,128)(2,1)S(1)}, bf16[256,1024]{1,0:T(8,128)(2,1)S(1)}, u32[]{:S(2)}, u32[]{:S(2)}) %collective-permute-start.3) | collective-permute-done | bytes 524320 | tf_op jit(solution)/shard_map/ppermute | solution.py:173
  47.1 10.7 %collective-permute-done.2 = bf16[256,1024]{1,0:T(8,128)(2,1)S(1)} collective-permute-done((bf16[256,1024]{1,0:T(8,128)(2,1)S(1)}, bf16[256,1024]{1,0:T(8,128)(2,1)S(1)}, u32[]{:S(2)}, u32[]{:S(2)}) %collective-permute-start.2) | collective-permute-done | bytes 524320 | tf_op jit(solution)/shard_map/ppermute | solution.py:173
  60.7 1.9 collective-permute-start.7
  63.0 2.1 %convolution_convert_fusion.3 = bf16[256,1024]{1,0:T(8,128)(2,1)} fusion(bf16[256,2048]{1,0:T(8,128)(2,1)S(1)} %maximum_select_fusion.low_ref, bf16[2048,1024]{1,0:T(8,128)(2,1)S(1)} %copy-done.23), kind=kOutput, calls=%fused_computation.5 | convolution fusion | flops 1074003968 | bytes 5767168 | tf_op jit(solution)/shard_map/dot_general | solution.py:16
  66.0 4.5 %collective-permute-done.4 = bf16[256,1024]{1,0:T(8,128)(2,1)S(1)} collective-permute-done((bf16[256,1024]{1,0:T(8,128)(2,1)S(1)}, bf16[256,1024]{1,0:T(8,128)(2,1)S(1)}, u32[]{:S(2)}, u32[]{:S(2)}) %collective-permute-start.4) | collective-permute-done | bytes 524320 | tf_op jit(solution)/shard_map/ppermute | solution.py:179
  70.8 2.1 %convolution_convert_fusion.2 = bf16[256,1024]{1,0:T(8,128)(2,1)} fusion(bf16[256,2048]{1,0:T(8,128)(2,1)S(1)} %maximum_select_fusion.1.high_ref, bf16[2048,1024]{1,0:T(8,128)(2,1)S(1)} %copy-done.23), kind=kOutput, calls=%fused_computation.4 | convolution fusion | flops 1074003968 | bytes 5767168 | tf_op jit(solution)/shard_map/dot_general | solution.py:16
  75.1 8.4 %collective-permute-done.7 = bf16[256,1024]{1,0:T(8,128)(2,1)} collective-permute-done((bf16[256,1024]{1,0:T(8,128)(2,1)S(1)}, bf16[256,1024]{1,0:T(8,128)(2,1)}, u32[]{:S(2)}, u32[]{:S(2)}) %collective-permute-start.7) | collective-permute-done | bytes 524320 | tf_op jit(solution)/shard_map/ppermute | solution.py:173
  83.9 4.4 %convolution_convert_fusion = bf16[256,1024]{1,0:T(8,128)(2,1)} fusion(bf16[256,2048]{1,0:T(8,128)(2,1)S(1)} %maximum_select_fusion.low_ref, bf16[2048,1024]{1,0:T(8,128)(2,1)} %all-gather.6.cloned.1.call-done), kind=kOutput, calls=%fused_computation.2 | convolution fusion | flops 1074003968 | bytes 5767168 | tf_op jit(solution)/shard_map/dot_general | solution.py:16
  89.6 2.1 %convolution_convert_fusion.1 = bf16[256,1024]{1,0:T(8,128)(2,1)} fusion(bf16[256,2048]{1,0:T(8,128)(2,1)S(1)} %maximum_select_fusion.1.high_ref, bf16[2048,1024]{1,0:T(8,128)(2,1)S(1)} %copy-done.26), kind=kOutput, calls=%fused_computation.3 | convolution fusion | flops 1074003968 | bytes 5767168 | tf_op jit(solution)/shard_map/dot_general | solution.py:16
  92.4 9.9 %collective-permute-done.10 = bf16[256,1024]{1,0:T(8,128)(2,1)} collective-permute-done((bf16[256,1024]{1,0:T(8,128)(2,1)}, bf16[256,1024]{1,0:T(8,128)(2,1)}, u32[]{:S(2)}, u32[]{:S(2)}) %collective-permute-start.10) | collective-permute-done | bytes 524320 | tf_op jit(solution)/shard_map/ppermute | solution.py:173
  102.3 2.0 maximum_select_fusion.3.high_ref
  104.3 3.5 %add_convert_fusion.1 = bf16[256,1024]{1,0:T(8,128)(2,1)} fusion(bf16[256,1024]{1,0:T(8,128)(2,1)} %collective-permute-done.10, bf16[256,2048]{1,0:T(8,128)(2,1)S(1)} %maximum_select_fusion.3.high_ref, bf16[2048,1024]{1,0:T(8,128)(2,1)S(1)} %copy-done.24), kind=kOutput, calls=%fused_computation.12 | convolution fusion | flops 1074528256 | bytes 6291456 | tf_op jit(solution)/shard_map/dot_general | solution.py:16
  109.0 10.8 %all-gather.8.cloned.1.call-done.w_ref = bf16[2048,1024]{1,0:T(8,128)(2,1)} async-done(((bf16[512,1024]{1,0:T(8,128)(2,1)}), bf16[2048,1024]{1,0:T(8,128)(2,1)}) %all-gather.8.cloned.1.call-update) | async-done | bytes 4194320 | tf_op jit(solution)/shard_map/all_gather | solution.py:203
  119.8 2.2 %copy-done.1 = bf16[2048,1024]{1,0:T(8,128)(2,1)S(1)} copy-done((bf16[2048,1024]{1,0:T(8,128)(2,1)S(1)}, bf16[2048,1024]{1,0:T(8,128)(2,1)}, u32[]{:S(2)}) %copy-start.1) | copy-done | bytes 4194328
  125.3 16.1 %collective-permute-done.14 = bf16[256,1024]{1,0:T(8,128)(2,1)} collective-permute-done((bf16[256,1024]{1,0:T(8,128)(2,1)}, bf16[256,1024]{1,0:T(8,128)(2,1)}, u32[]{:S(2)}, u32[]{:S(2)}) %collective-permute-start.14) | collective-permute-done | bytes 524320 | tf_op jit(solution)/shard_map/ppermute | solution.py:173
  141.4 2.4 %add_convert_fusion = bf16[256,1024]{1,0:T(8,128)(2,1)S(1)} fusion(bf16[256,1024]{1,0:T(8,128)(2,1)} %collective-permute-done.14, bf16[256,2048]{1,0:T(8,128)(2,1)S(1)} %copy-done.9, bf16[2048,1024]{1,0:T(8,128)(2,1)S(1)} %copy-done.27), kind=kOutput, calls=%fused_computation.11 | convolution fusion | flops 1074528256 | bytes 6291456 | tf_op jit(solution)/shard_map/dot_general | solution.py:16
  144.4 2.4 %convolution_add_fusion.1.km_ref.vm_ref = f32[256,1024]{1,0:T(8,128)S(1)} fusion(bf16[256,2048]{1,0:T(8,128)(2,1)S(1)} %maximum_select_fusion.2.low_ref, bf16[2048,1024]{1,0:T(8,128)(2,1)S(1)} %copy-done.25, bf16[256,1024]{1,0:T(8,128)(2,1)} %collective-permute-done.9), kind=kOutput, calls=%fused_computation.1 | convolution fusion | flops 1074266112 | bytes 6815744 | tf_op jit(solution)/shard_map/dot_general | solution.py:16
  146.8 2.4 %collective-permute-done.11.came_ref = bf16[256,1024]{1,0:T(8,128)(2,1)S(1)} collective-permute-done((bf16[256,1024]{1,0:T(8,128)(2,1)S(1)}, bf16[256,1024]{1,0:T(8,128)(2,1)S(1)}, u32[]{:S(2)}, u32[]{:S(2)}) %collective-permute-start.11) | collective-permute-done | bytes 524320 | tf_op jit(solution)/shard_map/ppermute | solution.py:173
  153.0 2.9 %collective-permute-start.18 = (bf16[128,1024]{1,0:T(8,128)(2,1)S(1)}, bf16[128,1024]{1,0:T(8,128)(2,1)S(1)}, u32[]{:S(2)}, u32[]{:S(2)}) collective-permute-start(bf16[128,1024]{1,0:T(8,128)(2,1)S(1)} %get-tuple-element.107), channel_id=1, source_target_pairs={{0,16},{2,18},{4,20},{6,22},{8,24},{10,26},{12,28},{14,30},{16,0},... | collective-permute-start | bytes 786440 | tf_op jit(solution)/shard_map/ppermute | solution.py:173
  155.9 2.3 %convolution_add_fusion.qm_ref = f32[256,1024]{1,0:T(8,128)S(1)} fusion(bf16[256,2048]{1,0:T(8,128)(2,1)S(1)} %maximum_select_fusion.2.low_ref, bf16[2048,1024]{1,0:T(8,128)(2,1)S(1)} %copy-done.27, bf16[256,1024]{1,0:T(8,128)(2,1)} %collective-permute-done.13), kind=kOutput, calls=%fused_computation | convolution fusion | flops 1074266112 | bytes 6815744 | tf_op jit(solution)/shard_map/dot_general | solution.py:16
  158.2 4.2 %collective-permute-done.16.qc_ref = bf16[256,1024]{1,0:T(8,128)(2,1)S(1)} collective-permute-done((bf16[256,1024]{1,0:T(8,128)(2,1)S(1)}, bf16[256,1024]{1,0:T(8,128)(2,1)S(1)}, u32[]{:S(2)}, u32[]{:S(2)}) %collective-permute-start.16) | collective-permute-done | bytes 524320 | tf_op jit(solution)/shard_map/ppermute | solution.py:173
  162.4 5.4 %attention.4 = (bf16[256,2048]{1,0:T(8,128)(2,1)}, bf16[1,1024]{1,0:T(2,128)(2,1)S(1)}) custom-call(s32[3]{0:T(128)S(1)} %get-tuple-element.153.place_ref, f32[256,1024]{1,0:T(8,128)S(1)} %convolution_add_fusion.qm_ref, bf16[256,1024]{1,0:T(8,128)(2,1)S(1)} %collective-permute-done.16.qc_ref, bf16[1792,512]{1,0:T(8,128)(2,1)S(1)} %copy-done.4, ...), custom_call_target="tpu_custom_call" | custom-call | bytes 1024 | tf_op jit(solution)/shard_map/attention/pallas_call | solution.py:128
  167.9 5.4 %attention.5 = (bf16[256,2048]{1,0:T(8,128)(2,1)}, bf16[1,1024]{1,0:T(2,128)(2,1)S(1)}) custom-call(s32[3]{0:T(128)S(1)} %get-tuple-element.152.place_ref, f32[256,1024]{1,0:T(8,128)S(1)} %convolution_add_fusion.qm_ref, bf16[256,1024]{1,0:T(8,128)(2,1)S(1)} %collective-permute-done.16.qc_ref, ...), custom_call_target="tpu_custom_call", output_to_operand_aliasing={{0}: (9, {})} | custom-call | bytes 1024 | tf_op jit(solution)/shard_map/attention/pallas_call | solution.py:128
  174.2 2.4 %half_product.7 = (bf16[128,1024]{1,0:T(8,128)(2,1)}, f32[128,1024]{1,0:T(8,128)S(1)}) custom-call(bf16[256,2048]{1,0:T(8,128)(2,1)S(1)} %maximum_select_fusion.2.low_ref, bf16[256,2048]{1,0:T(8,128)(2,1)S(1)} %copy-done.9, bf16[2048,1024]{1,0:T(8,128)(2,1)S(1)} %copy-done.2, bf16[256,1024]{1,0:T(8,128)(2,1)S(1)} %collective-permute-done.15.came_ref), custom_call_target="tpu_custom_call" | custom-call | bytes 1024 | tf_op jit(solution)/shard_map/half_product/pallas_call | solution.py:42
  176.7 5.7 %attention.6 = (bf16[256,2048]{1,0:T(8,128)(2,1)}, bf16[1,1024]{1,0:T(2,128)(2,1)S(1)}) custom-call(s32[3]{0:T(128)S(1)} %get-tuple-element.153.place_ref, f32[128,1024]{1,0:T(8,128)S(1)} %get-tuple-element.124.qm_ref, bf16[128,1024]{1,0:T(8,128)(2,1)S(1)} %collective-permute-done.18.qc_ref, ...), custom_call_target="tpu_custom_call", output_to_operand_aliasing={{0}: (9, {})} | custom-call | bytes 1024 | tf_op jit(solution)/shard_map/attention/pallas_call | solution.py:128
  188.6 2.2 %collective-permute-start.24 = (bf16[4,1,2048]{2,1,0:T(2,128)(2,1)}, bf16[4,1,2048]{2,1,0:T(2,128)(2,1)S(1)}, u32[]{:S(2)}, u32[]{:S(2)}) collective-permute-start(bf16[4,1,2048]{2,1,0:T(2,128)(2,1)} %order.1), channel_id=1, source_target_pairs={{0,24},{2,26},{4,28},{6,30},{8,16},{10,18},{12,20},{14,22},{16,8},... | collective-permute-start | bytes 49160 | tf_op jit(solution)/shard_map/ppermute | solution.py:173
  193.8 6.5 %attention.7 = (bf16[256,2048]{1,0:T(8,128)(2,1)}, bf16[1,1024]{1,0:T(2,128)(2,1)}) custom-call(s32[3]{0:T(128)} %copy-done.11, f32[128,1024]{1,0:T(8,128)} %copy-done.10, bf16[128,1024]{1,0:T(8,128)(2,1)} %collective-permute-done.17.qc_ref, bf16[1792,512]{1,0:T(8,128)(2,1)} %kc_ref.7, bf16[1792,512]{1,0:T(8,128)(2,1)} %vc_ref.7, ...), custom_call_target="tpu_custom_call", output_to_operand_aliasing={{0}: (9, {})} | custom-call | bytes 1024 | tf_op jit(solution)/shard_map/attention/pallas_call | solution.py:128
  (123 shorter events, 38.2 us)
Async XLA Ops:
  7.2 39.9 %all-gather.4.cloned.1.call-start = ((), (), s32[]{:S(2)}) async-start(), calls=%async_computation | async-start | bytes 5242880 | tf_op jit(solution)/shard_map/all_gather | solution.py:203
  9.7 74.2 %all-gather.6.cloned.1.call-start = ((), (), s32[]{:S(2)}) async-start(), calls=%async_computation.1 | async-start | bytes 5242880 | tf_op jit(solution)/shard_map/all_gather | solution.py:203
  11.4 15.2 %collective-permute-start.1 = (bf16[256,1024]{1,0:T(8,128)(2,1)}, bf16[256,1024]{1,0:T(8,128)(2,1)}, u32[]{:S(2)}, u32[]{:S(2)}) collective-permute-start(bf16[256,1024]{1,0:T(8,128)(2,1)} %pad_maximum_fusion.1), channel_id=1, source_target_pairs={{0,1},{1,0},{2,3},{3,2},{4,5},{5,4},{6,7},{7,6},{8,9},{9,8},{10,11... | collective-permute-start | bytes 1572872 | tf_op jit(solution)/shard_map/ppermute | solution.py:179
  30.4 89.4 %all-gather.8.cloned.1.call-start = ((), (), s32[]{:S(2)}) async-start(), calls=%async_computation.2 | async-start | bytes 5242880 | tf_op jit(solution)/shard_map/all_gather | solution.py:203
  31.4 14.2 %collective-permute-start.3 = (bf16[256,1024]{1,0:T(8,128)(2,1)S(1)}, bf16[256,1024]{1,0:T(8,128)(2,1)S(1)}, u32[]{:S(2)}, u32[]{:S(2)}) collective-permute-start(bf16[256,1024]{1,0:T(8,128)(2,1)S(1)} %copy-done.18), channel_id=1, source_target_pairs={{0,8},{2,10},{4,12},{6,14},{8,0},{10,2},{12,4},{14,6},{16,24},{18,... | collective-permute-start | bytes 1572872 | tf_op jit(solution)/shard_map/ppermute | solution.py:173
  33.2 24.6 %collective-permute-start.2 = (bf16[256,1024]{1,0:T(8,128)(2,1)S(1)}, bf16[256,1024]{1,0:T(8,128)(2,1)S(1)}, u32[]{:S(2)}, u32[]{:S(2)}) collective-permute-start(bf16[256,1024]{1,0:T(8,128)(2,1)S(1)} %copy-done.17), channel_id=1, source_target_pairs={{0,24},{2,26},{4,28},{6,30},{8,16},{10,18},{12,20},{14,22},{16,8},... | collective-permute-start | bytes 1572872 | tf_op jit(solution)/shard_map/ppermute | solution.py:173
  35.7 23.6 %collective-permute-start = (bf16[256,1024]{1,0:T(8,128)(2,1)S(1)}, bf16[256,1024]{1,0:T(8,128)(2,1)}, u32[]{:S(2)}, u32[]{:S(2)}) collective-permute-start(bf16[256,1024]{1,0:T(8,128)(2,1)S(1)} %copy-done.16), channel_id=1, source_target_pairs={{0,1},{1,0},{2,3},{3,2},{4,5},{5,4},{6,7},{7,6},{8,9},{9,8},{10,11... | collective-permute-start | bytes 1572872 | tf_op jit(solution)/shard_map/ppermute | solution.py:179
  45.6 17.0 %collective-permute-start.5 = (bf16[256,1024]{1,0:T(8,128)(2,1)S(1)}, bf16[256,1024]{1,0:T(8,128)(2,1)S(1)}, u32[]{:S(2)}, u32[]{:S(2)}) collective-permute-start(bf16[256,1024]{1,0:T(8,128)(2,1)S(1)} %collective-permute-done.3), channel_id=1, source_target_pairs={{0,1},{1,0},{2,3},{3,2},{4,5},{5,4},{6,7},{7,6},{8,9},{9,8},{10,11... | collective-permute-start | bytes 1572872 | tf_op jit(solution)/shard_map/ppermute | solution.py:179
  57.8 12.6 %collective-permute-start.4 = (bf16[256,1024]{1,0:T(8,128)(2,1)S(1)}, bf16[256,1024]{1,0:T(8,128)(2,1)S(1)}, u32[]{:S(2)}, u32[]{:S(2)}) collective-permute-start(bf16[256,1024]{1,0:T(8,128)(2,1)S(1)} %collective-permute-done.2), channel_id=1, source_target_pairs={{0,1},{1,0},{2,3},{3,2},{4,5},{5,4},{6,7},{7,6},{8,9},{9,8},{10,11... | collective-permute-start | bytes 1572872 | tf_op jit(solution)/shard_map/ppermute | solution.py:179
  60.7 22.7 %collective-permute-start.7 = (bf16[256,1024]{1,0:T(8,128)(2,1)S(1)}, bf16[256,1024]{1,0:T(8,128)(2,1)}, u32[]{:S(2)}, u32[]{:S(2)}) collective-permute-start(bf16[256,1024]{1,0:T(8,128)(2,1)S(1)} %get-tuple-element.80), channel_id=1, source_target_pairs={{0,16},{2,18},{4,20},{6,22},{8,24},{10,26},{12,28},{14,30},{16,0},... | collective-permute-start | bytes 1572872 | tf_op jit(solution)/shard_map/ppermute | solution.py:173
  65.1 27.4 %collective-permute-start.9 = (bf16[256,1024]{1,0:T(8,128)(2,1)}, bf16[256,1024]{1,0:T(8,128)(2,1)}, u32[]{:S(2)}, u32[]{:S(2)}) collective-permute-start(bf16[256,1024]{1,0:T(8,128)(2,1)} %convolution_convert_fusion.3), channel_id=1, source_target_pairs={{0,8},{2,10},{4,12},{6,14},{8,0},{10,2},{12,4},{14,6},{16,24},{18,... | collective-permute-start | bytes 1572872 | tf_op jit(solution)/shard_map/ppermute | solution.py:173
  70.8 48.9 %copy-start.6 = (bf16[256,2048]{1,0:T(8,128)(2,1)}, bf16[256,2048]{1,0:T(8,128)(2,1)S(1)}, u32[]{:S(2)}) copy-start(bf16[256,2048]{1,0:T(8,128)(2,1)S(1)} %maximum_select_fusion.1.high_ref) | copy-start | bytes 3145732
  72.9 29.4 %collective-permute-start.10 = (bf16[256,1024]{1,0:T(8,128)(2,1)}, bf16[256,1024]{1,0:T(8,128)(2,1)}, u32[]{:S(2)}, u32[]{:S(2)}) collective-permute-start(bf16[256,1024]{1,0:T(8,128)(2,1)} %convolution_convert_fusion.2), channel_id=1, source_target_pairs={{0,8},{2,10},{4,12},{6,14},{8,0},{10,2},{12,4},{14,6},{16,24},{18,... | collective-permute-start | bytes 1572872 | tf_op jit(solution)/shard_map/ppermute | solution.py:173
  73.6 18.1 %collective-permute-start.6 = (bf16[256,1024]{1,0:T(8,128)(2,1)S(1)}, bf16[256,1024]{1,0:T(8,128)(2,1)S(1)}, u32[]{:S(2)}, u32[]{:S(2)}) collective-permute-start(bf16[256,1024]{1,0:T(8,128)(2,1)S(1)} %get-tuple-element.86), channel_id=1, source_target_pairs={{0,1},{1,0},{2,3},{3,2},{4,5},{5,4},{6,7},{7,6},{8,9},{9,8},{10,11... | collective-permute-start | bytes 1572872 | tf_op jit(solution)/shard_map/ppermute | solution.py:179
  83.4 18.9 %collective-permute-start.8 = (bf16[256,1024]{1,0:T(8,128)(2,1)}, bf16[256,1024]{1,0:T(8,128)(2,1)}, u32[]{:S(2)}, u32[]{:S(2)}) collective-permute-start(bf16[256,1024]{1,0:T(8,128)(2,1)} %collective-permute-done.7), channel_id=1, source_target_pairs={{0,1},{1,0},{2,3},{3,2},{4,5},{5,4},{6,7},{7,6},{8,9},{9,8},{10,11... | collective-permute-start | bytes 1572872 | tf_op jit(solution)/shard_map/ppermute | solution.py:179
  88.3 53.1 %collective-permute-start.13 = (bf16[256,1024]{1,0:T(8,128)(2,1)}, bf16[256,1024]{1,0:T(8,128)(2,1)}, u32[]{:S(2)}, u32[]{:S(2)}) collective-permute-start(bf16[256,1024]{1,0:T(8,128)(2,1)} %convolution_convert_fusion), channel_id=1, source_target_pairs={{0,8},{2,10},{4,12},{6,14},{8,0},{10,2},{12,4},{14,6},{16,24},{18,... | collective-permute-start | bytes 1572872 | tf_op jit(solution)/shard_map/ppermute | solution.py:173
  91.7 49.7 %collective-permute-start.14 = (bf16[256,1024]{1,0:T(8,128)(2,1)}, bf16[256,1024]{1,0:T(8,128)(2,1)}, u32[]{:S(2)}, u32[]{:S(2)}) collective-permute-start(bf16[256,1024]{1,0:T(8,128)(2,1)} %convolution_convert_fusion.1), channel_id=1, source_target_pairs={{0,8},{2,10},{4,12},{6,14},{8,0},{10,2},{12,4},{14,6},{16,24},{18,... | collective-permute-start | bytes 1572872 | tf_op jit(solution)/shard_map/ppermute | solution.py:173
  107.9 39.0 %collective-permute-start.12 = (bf16[256,1024]{1,0:T(8,128)(2,1)}, bf16[256,1024]{1,0:T(8,128)(2,1)S(1)}, u32[]{:S(2)}, u32[]{:S(2)}) collective-permute-start(bf16[256,1024]{1,0:T(8,128)(2,1)} %add_convert_fusion.1), channel_id=1, source_target_pairs={{0,16},{2,18},{4,20},{6,22},{8,24},{10,26},{12,28},{14,30},{16,0},... | collective-permute-start | bytes 1572872 | tf_op jit(solution)/shard_map/ppermute | solution.py:173
  123.7 20.2 %copy-start.15 = (bf16[256,1024]{1,0:T(8,128)(2,1)S(1)}, bf16[256,1024]{1,0:T(8,128)(2,1)}, u32[]{:S(2)}) copy-start(bf16[256,1024]{1,0:T(8,128)(2,1)} %copy-done.14) | copy-start | bytes 1572868
  123.7 25.6 %collective-permute-start.11 = (bf16[256,1024]{1,0:T(8,128)(2,1)S(1)}, bf16[256,1024]{1,0:T(8,128)(2,1)S(1)}, u32[]{:S(2)}, u32[]{:S(2)}) collective-permute-start(bf16[256,1024]{1,0:T(8,128)(2,1)S(1)} %half_product.4), channel_id=1, source_target_pairs={{0,8},{2,10},{4,12},{6,14},{8,0},{10,2},{12,4},{14,6},{16,24},{18,... | collective-permute-start | bytes 1572872 | tf_op jit(solution)/shard_map/ppermute | solution.py:173
  144.3 18.2 %collective-permute-start.16 = (bf16[256,1024]{1,0:T(8,128)(2,1)S(1)}, bf16[256,1024]{1,0:T(8,128)(2,1)S(1)}, u32[]{:S(2)}, u32[]{:S(2)}) collective-permute-start(bf16[256,1024]{1,0:T(8,128)(2,1)S(1)} %add_convert_fusion), channel_id=1, source_target_pairs={{0,16},{2,18},{4,20},{6,22},{8,24},{10,26},{12,28},{14,30},{16,0},... | collective-permute-start | bytes 1572872 | tf_op jit(solution)/shard_map/ppermute | solution.py:173
  146.8 29.9 %copy-start = (f32[256,1024]{1,0:T(8,128)}, f32[256,1024]{1,0:T(8,128)S(1)}, u32[]{:S(2)}) copy-start(f32[256,1024]{1,0:T(8,128)S(1)} %convolution_add_fusion.1.km_ref.vm_ref) | copy-start | bytes 3145732
  146.8 29.8 %copy-start.3 = (bf16[256,1024]{1,0:T(8,128)(2,1)}, bf16[256,1024]{1,0:T(8,128)(2,1)S(1)}, u32[]{:S(2)}) copy-start(bf16[256,1024]{1,0:T(8,128)(2,1)S(1)} %collective-permute-done.12.kt_ref.vt_ref) | copy-start | bytes 1572868
  152.9 21.3 %collective-permute-start.15 = (bf16[256,1024]{1,0:T(8,128)(2,1)S(1)}, bf16[256,1024]{1,0:T(8,128)(2,1)S(1)}, u32[]{:S(2)}, u32[]{:S(2)}) collective-permute-start(bf16[256,1024]{1,0:T(8,128)(2,1)S(1)} %half_product.6), channel_id=1, source_target_pairs={{0,8},{2,10},{4,12},{6,14},{8,0},{10,2},{12,4},{14,6},{16,24},{18,... | collective-permute-start | bytes 1572872 | tf_op jit(solution)/shard_map/ppermute | solution.py:173
  153.0 23.6 %collective-permute-start.18 = (bf16[128,1024]{1,0:T(8,128)(2,1)S(1)}, bf16[128,1024]{1,0:T(8,128)(2,1)S(1)}, u32[]{:S(2)}, u32[]{:S(2)}) collective-permute-start(bf16[128,1024]{1,0:T(8,128)(2,1)S(1)} %get-tuple-element.107), channel_id=1, source_target_pairs={{0,16},{2,18},{4,20},{6,22},{8,24},{10,26},{12,28},{14,30},{16,0},... | collective-permute-start | bytes 786440 | tf_op jit(solution)/shard_map/ppermute | solution.py:173
  176.6 17.2 %collective-permute-start.17 = (bf16[128,1024]{1,0:T(8,128)(2,1)}, bf16[128,1024]{1,0:T(8,128)(2,1)}, u32[]{:S(2)}, u32[]{:S(2)}) collective-permute-start(bf16[128,1024]{1,0:T(8,128)(2,1)} %get-tuple-element.121), channel_id=1, source_target_pairs={{0,16},{2,18},{4,20},{6,22},{8,24},{10,26},{12,28},{14,30},{16,0},... | collective-permute-start | bytes 786440 | tf_op jit(solution)/shard_map/ppermute | solution.py:173
  182.4 3.1 %collective-permute-start.21 = (bf16[1,2048]{1,0:T(2,128)(2,1)S(1)}, bf16[1,2048]{1,0:T(2,128)(2,1)S(1)}, u32[]{:S(2)}, u32[]{:S(2)}) collective-permute-start(bf16[1,2048]{1,0:T(2,128)(2,1)S(1)} %pad_maximum_fusion.6.refs_0_), channel_id=1, source_target_pairs={{0,6},{2,4},{4,2},{6,0},{8,14},{10,12},{12,10},{14,8},{16,22},{18,... | collective-permute-start | bytes 12296 | tf_op jit(solution)/shard_map/ppermute | solution.py:173
  183.0 3.7 %collective-permute-start.20 = (bf16[1,2048]{1,0:T(2,128)(2,1)S(1)}, bf16[1,2048]{1,0:T(2,128)(2,1)S(1)}, u32[]{:S(2)}, u32[]{:S(2)}) collective-permute-start(bf16[1,2048]{1,0:T(2,128)(2,1)S(1)} %pad_maximum_fusion.6.refs_0_), channel_id=1, source_target_pairs={{0,4},{2,6},{4,0},{6,2},{8,12},{10,14},{12,8},{14,10},{16,20},{18,... | collective-permute-start | bytes 12296 | tf_op jit(solution)/shard_map/ppermute | solution.py:173
  183.8 2.9 %collective-permute-start.19 = (bf16[1,2048]{1,0:T(2,128)(2,1)S(1)}, bf16[1,2048]{1,0:T(2,128)(2,1)S(1)}, u32[]{:S(2)}, u32[]{:S(2)}) collective-permute-start(bf16[1,2048]{1,0:T(2,128)(2,1)S(1)} %pad_maximum_fusion.6.refs_0_), channel_id=1, source_target_pairs={{0,2},{2,0},{4,6},{6,4},{8,10},{10,8},{12,14},{14,12},{16,18},{18,... | collective-permute-start | bytes 12296 | tf_op jit(solution)/shard_map/ppermute | solution.py:173
  188.6 11.7 %collective-permute-start.24 = (bf16[4,1,2048]{2,1,0:T(2,128)(2,1)}, bf16[4,1,2048]{2,1,0:T(2,128)(2,1)S(1)}, u32[]{:S(2)}, u32[]{:S(2)}) collective-permute-start(bf16[4,1,2048]{2,1,0:T(2,128)(2,1)} %order.1), channel_id=1, source_target_pairs={{0,24},{2,26},{4,28},{6,30},{8,16},{10,18},{12,20},{14,22},{16,8},... | collective-permute-start | bytes 49160 | tf_op jit(solution)/shard_map/ppermute | solution.py:173
  190.8 9.5 %collective-permute-start.23 = (bf16[4,1,2048]{2,1,0:T(2,128)(2,1)}, bf16[4,1,2048]{2,1,0:T(2,128)(2,1)S(1)}, u32[]{:S(2)}, u32[]{:S(2)}) collective-permute-start(bf16[4,1,2048]{2,1,0:T(2,128)(2,1)} %order.1), channel_id=1, source_target_pairs={{0,16},{2,18},{4,20},{6,22},{8,24},{10,26},{12,28},{14,30},{16,0},... | collective-permute-start | bytes 49160 | tf_op jit(solution)/shard_map/ppermute | solution.py:173
  192.6 7.8 %collective-permute-start.22 = (bf16[4,1,2048]{2,1,0:T(2,128)(2,1)}, bf16[4,1,2048]{2,1,0:T(2,128)(2,1)S(1)}, u32[]{:S(2)}, u32[]{:S(2)}) collective-permute-start(bf16[4,1,2048]{2,1,0:T(2,128)(2,1)} %order.1), channel_id=1, source_target_pairs={{0,8},{2,10},{4,12},{6,14},{8,0},{10,2},{12,4},{14,6},{16,24},{18,... | collective-permute-start | bytes 49160 | tf_op jit(solution)/shard_map/ppermute | solution.py:173
  (24 other events, 166.4 us)
Sparse Core Ops, SparseCore 0:
  9.8 37.1 all-gather.3
  49.2 34.4 all-gather.5
  85.2 34.4 all-gather.7

commit v13 on v12

--- a/solution.py
+++ b/solution.py
@@ -51,6 +51,25 @@
         cost_estimate=pl.CostEstimate(flops=0, bytes_accessed=cost, transcendentals=0),
         name="half_product",
     )(low, high, weight, *([] if first else [came]))
+
+
+def beside_kernel(left_ref, right_ref, out_ref):
+    columns = left_ref.shape[1]
+    out_ref[:, :columns] = left_ref[...]
+    out_ref[:, columns:] = right_ref[...]
+
+
+def beside(left, right):
+    rows, columns = left.shape
+    return pl.pallas_call(
+        beside_kernel,
+        grid=(2,),
+        in_specs=[pl.BlockSpec((rows // 2, columns), lambda i: (i, 0))] * 2,
+        out_specs=pl.BlockSpec((rows // 2, 2 * columns), lambda i: (i, 0)),
+        out_shape=jax.ShapeDtypeStruct((rows, 2 * columns), left.dtype),
+        cost_estimate=pl.CostEstimate(flops=0, bytes_accessed=COST, transcendentals=0),
+        name="beside",
+    )(left, right)
 
 
 def order_kernel(index_ref, *refs):
@@ -204,7 +223,7 @@
 
     weights = {}
 
-    weights["kv"] = group_gather(jnp.concatenate([w_key, w_value], axis=1))
+    weights["kv"] = group_gather(beside(w_key, w_value))
 
     def gather_queries():
         source = step(w_query) if fast else w_query

time: 208 us -> 208 us (level)
  other arithmetic: 11.1 us -> 8.69 us
  Pallas kernels: 32.2 us -> 34.4 us
    concatenate x1 -> x0, other arithmetic: 2.44 us -> none  [shards(): weights['kv'] = group_gather(jnp.concatenate([w_key, w_value], axis=1))]
    pallas_call x0 -> x1, Pallas kernels: none -> 2.2 us  [beside(): pl.pallas_call(beside_kernel, grid=(2,), in_specs=[pl.BlockSpec((rows //...]
  transfers between devices with their start and end apart: 28 -> 28, of which waited for: 13 -> 13; matrix products, arithmetic and copies ran while one was open for 16% -> 16% of each run, Pallas kernels for 15% -> 16%
where the time goes in v13:
time: 208 us
  waiting for transfers between devices  90.6 us (44%)
  Pallas kernels  34.4 us (17%)
  starting transfers between devices  31.2 us (15%)
  matrix products  21.4 us (10%)
  between operations  14.9 us (7%)
  other arithmetic  8.69 us (4%)
  local copies, waits for them, and re-layouts  6.37 us (3%)
    ppermute x19, waiting for transfers between devices, over_inst(): return lax.ppermute(value, 'inst', [(i, i ^ bits) for i in range(n_inst)])  63.4 us
    pallas_call x4, Pallas kernels, attend(): pl.pallas_call(attention_kernel, grid_spec=pltpu.PrefetchScalarGridSpec(n...  23.1 us
    ppermute x19, starting transfers between devices, over_inst(): return lax.ppermute(value, 'inst', [(i, i ^ bits) for i in range(n_inst)])  21.7 us
    dot_general x8, matrix products, dot(): return jnp.dot(a, b, preferred_element_type=jnp.float32)  21.4 us
    ppermute x6, waiting for transfers between devices, over_tp(): return lax.ppermute(value, 'tp', [(0, 1), (1, 0)])  15.7 us
    all_gather x3, waiting for transfers between devices, group_gather(): lax.all_gather(value, 'inst', axis=0, tiled=True, axis_index_groups=groups)  10.8 us
    ppermute x6, starting transfers between devices, over_tp(): return lax.ppermute(value, 'tp', [(0, 1), (1, 0)])  9.38 us
    pallas_call x4, Pallas kernels, half_product(): pl.pallas_call(first_kernel if first else later_kernel, grid=(columns //...  7.74 us
  transfers between devices with their start and end apart: 28, of which 13 were waited for; matrix products, arithmetic and copies ran while one was open for 16% of the time, Pallas kernels for 16%

profile of v13, /device:TPU:0, one launch (start us, length us, event | category | flops | bytes accessed | tf_op | source)
XLA Modules:
  0.0 207.5 jit_solution(771814741874812371)
XLA Ops:
  7.2 2.2 %beside.1 = bf16[512,1024]{1,0:T(8,128)(2,1)} custom-call(bf16[512,512]{1,0:T(8,128)(2,1)} %left_ref.1, bf16[512,512]{1,0:T(8,128)(2,1)} %right_ref.1), custom_call_target="tpu_custom_call" | custom-call | bytes 1024 | tf_op jit(solution)/shard_map/beside/pallas_call | solution.py:64
  11.1 2.9 %collective-permute-start.1 = (bf16[256,1024]{1,0:T(8,128)(2,1)}, bf16[256,1024]{1,0:T(8,128)(2,1)}, u32[]{:S(2)}, u32[]{:S(2)}) collective-permute-start(bf16[256,1024]{1,0:T(8,128)(2,1)} %pad_maximum_fusion), channel_id=1, source_target_pairs={{0,1},{1,0},{2,3},{3,2},{4,5},{5,4},{6,7},{7,6},{8,9},{9,8},{10,11... | collective-permute-start | bytes 1572872 | tf_op jit(solution)/shard_map/ppermute | solution.py:198
  15.1 11.2 %collective-permute-done.1 = bf16[256,1024]{1,0:T(8,128)(2,1)} collective-permute-done((bf16[256,1024]{1,0:T(8,128)(2,1)}, bf16[256,1024]{1,0:T(8,128)(2,1)}, u32[]{:S(2)}, u32[]{:S(2)}) %collective-permute-start.1) | collective-permute-done | bytes 524320 | tf_op jit(solution)/shard_map/ppermute | solution.py:198
  26.3 2.3 %broadcast_select_fusion.1 = (bf16[256,1024]{1,0:T(8,128)(2,1)}, bf16[256,1024]{1,0:T(8,128)(2,1)}) fusion(bf16[256,1024]{1,0:T(8,128)(2,1)} %collective-permute-done.1, pred[]{:T(512)S(6)} %eq.29, bf16[128,1024]{1,0:T(8,128)(2,1)S(1)} %get-tuple-element.141, bf16[128,1024]{1,0:T(8,128)(2,1)S(1)} %get-tuple-element.142, pred[]{:T(512)S(6)} %eq.28), kind=kLoop, calls=%fused_computation.17 | loop fusion | flops 1572864 | bytes 2097154 | tf_op jit(solution)/shard_map/jit(_where)/select_n | solution.py:254
  33.0 2.5 %collective-permute-start.2 = (bf16[256,1024]{1,0:T(8,128)(2,1)S(1)}, bf16[256,1024]{1,0:T(8,128)(2,1)S(1)}, u32[]{:S(2)}, u32[]{:S(2)}) collective-permute-start(bf16[256,1024]{1,0:T(8,128)(2,1)S(1)} %copy-done.17), channel_id=1, source_target_pairs={{0,24},{2,26},{4,28},{6,30},{8,16},{10,18},{12,20},{14,22},{16,8},... | collective-permute-start | bytes 1572872 | tf_op jit(solution)/shard_map/ppermute | solution.py:192
  37.0 8.4 %collective-permute-done.3 = bf16[256,1024]{1,0:T(8,128)(2,1)S(1)} collective-permute-done((bf16[256,1024]{1,0:T(8,128)(2,1)S(1)}, bf16[256,1024]{1,0:T(8,128)(2,1)S(1)}, u32[]{:S(2)}, u32[]{:S(2)}) %collective-permute-start.3) | collective-permute-done | bytes 524320 | tf_op jit(solution)/shard_map/ppermute | solution.py:192
  46.9 10.7 %collective-permute-done.2 = bf16[256,1024]{1,0:T(8,128)(2,1)S(1)} collective-permute-done((bf16[256,1024]{1,0:T(8,128)(2,1)S(1)}, bf16[256,1024]{1,0:T(8,128)(2,1)S(1)}, u32[]{:S(2)}, u32[]{:S(2)}) %collective-permute-start.2) | collective-permute-done | bytes 524320 | tf_op jit(solution)/shard_map/ppermute | solution.py:192
  60.5 1.9 collective-permute-start.7
  62.8 2.1 %convolution_convert_fusion.3 = bf16[256,1024]{1,0:T(8,128)(2,1)} fusion(bf16[256,2048]{1,0:T(8,128)(2,1)S(1)} %maximum_select_fusion.low_ref, bf16[2048,1024]{1,0:T(8,128)(2,1)S(1)} %copy-done.23), kind=kOutput, calls=%fused_computation.5 | convolution fusion | flops 1074003968 | bytes 5767168 | tf_op jit(solution)/shard_map/dot_general | solution.py:16
  65.7 4.5 %collective-permute-done.4 = bf16[256,1024]{1,0:T(8,128)(2,1)S(1)} collective-permute-done((bf16[256,1024]{1,0:T(8,128)(2,1)S(1)}, bf16[256,1024]{1,0:T(8,128)(2,1)S(1)}, u32[]{:S(2)}, u32[]{:S(2)}) %collective-permute-start.4) | collective-permute-done | bytes 524320 | tf_op jit(solution)/shard_map/ppermute | solution.py:198
  70.6 2.1 %convolution_convert_fusion.2 = bf16[256,1024]{1,0:T(8,128)(2,1)} fusion(bf16[256,2048]{1,0:T(8,128)(2,1)S(1)} %maximum_select_fusion.1.high_ref, bf16[2048,1024]{1,0:T(8,128)(2,1)S(1)} %copy-done.23), kind=kOutput, calls=%fused_computation.4 | convolution fusion | flops 1074003968 | bytes 5767168 | tf_op jit(solution)/shard_map/dot_general | solution.py:16
  74.9 8.4 %collective-permute-done.7 = bf16[256,1024]{1,0:T(8,128)(2,1)} collective-permute-done((bf16[256,1024]{1,0:T(8,128)(2,1)S(1)}, bf16[256,1024]{1,0:T(8,128)(2,1)}, u32[]{:S(2)}, u32[]{:S(2)}) %collective-permute-start.7) | collective-permute-done | bytes 524320 | tf_op jit(solution)/shard_map/ppermute | solution.py:192
  83.7 4.4 %convolution_convert_fusion = bf16[256,1024]{1,0:T(8,128)(2,1)} fusion(bf16[256,2048]{1,0:T(8,128)(2,1)S(1)} %maximum_select_fusion.low_ref, bf16[2048,1024]{1,0:T(8,128)(2,1)} %all-gather.6.cloned.1.call-done), kind=kOutput, calls=%fused_computation.2 | convolution fusion | flops 1074003968 | bytes 5767168 | tf_op jit(solution)/shard_map/dot_general | solution.py:16
  89.3 2.1 %convolution_convert_fusion.1 = bf16[256,1024]{1,0:T(8,128)(2,1)} fusion(bf16[256,2048]{1,0:T(8,128)(2,1)S(1)} %maximum_select_fusion.1.high_ref, bf16[2048,1024]{1,0:T(8,128)(2,1)S(1)} %copy-done.26), kind=kOutput, calls=%fused_computation.3 | convolution fusion | flops 1074003968 | bytes 5767168 | tf_op jit(solution)/shard_map/dot_general | solution.py:16
  92.2 9.8 %collective-permute-done.10 = bf16[256,1024]{1,0:T(8,128)(2,1)} collective-permute-done((bf16[256,1024]{1,0:T(8,128)(2,1)}, bf16[256,1024]{1,0:T(8,128)(2,1)}, u32[]{:S(2)}, u32[]{:S(2)}) %collective-permute-start.10) | collective-permute-done | bytes 524320 | tf_op jit(solution)/shard_map/ppermute | solution.py:192
  102.1 2.0 maximum_select_fusion.3.high_ref
  104.1 3.5 %add_convert_fusion.1 = bf16[256,1024]{1,0:T(8,128)(2,1)} fusion(bf16[256,1024]{1,0:T(8,128)(2,1)} %collective-permute-done.10, bf16[256,2048]{1,0:T(8,128)(2,1)S(1)} %maximum_select_fusion.3.high_ref, bf16[2048,1024]{1,0:T(8,128)(2,1)S(1)} %copy-done.24), kind=kOutput, calls=%fused_computation.11 | convolution fusion | flops 1074528256 | bytes 6291456 | tf_op jit(solution)/shard_map/dot_general | solution.py:16
  108.8 10.8 %all-gather.8.cloned.1.call-done.w_ref = bf16[2048,1024]{1,0:T(8,128)(2,1)} async-done(((bf16[512,1024]{1,0:T(8,128)(2,1)}), bf16[2048,1024]{1,0:T(8,128)(2,1)}) %all-gather.8.cloned.1.call-update) | async-done | bytes 4194320 | tf_op jit(solution)/shard_map/all_gather | solution.py:222
  119.5 2.2 %copy-done.1 = bf16[2048,1024]{1,0:T(8,128)(2,1)S(1)} copy-done((bf16[2048,1024]{1,0:T(8,128)(2,1)S(1)}, bf16[2048,1024]{1,0:T(8,128)(2,1)}, u32[]{:S(2)}) %copy-start.1) | copy-done | bytes 4194328
  125.0 16.1 %collective-permute-done.14 = bf16[256,1024]{1,0:T(8,128)(2,1)} collective-permute-done((bf16[256,1024]{1,0:T(8,128)(2,1)}, bf16[256,1024]{1,0:T(8,128)(2,1)}, u32[]{:S(2)}, u32[]{:S(2)}) %collective-permute-start.14) | collective-permute-done | bytes 524320 | tf_op jit(solution)/shard_map/ppermute | solution.py:192
  141.2 2.4 %add_convert_fusion = bf16[256,1024]{1,0:T(8,128)(2,1)S(1)} fusion(bf16[256,1024]{1,0:T(8,128)(2,1)} %collective-permute-done.14, bf16[256,2048]{1,0:T(8,128)(2,1)S(1)} %copy-done.9, bf16[2048,1024]{1,0:T(8,128)(2,1)S(1)} %copy-done.27), kind=kOutput, calls=%fused_computation.10 | convolution fusion | flops 1074528256 | bytes 6291456 | tf_op jit(solution)/shard_map/dot_general | solution.py:16
  144.1 2.4 %convolution_add_fusion.1.km_ref.vm_ref = f32[256,1024]{1,0:T(8,128)S(1)} fusion(bf16[256,2048]{1,0:T(8,128)(2,1)S(1)} %maximum_select_fusion.2.low_ref, bf16[2048,1024]{1,0:T(8,128)(2,1)S(1)} %copy-done.25, bf16[256,1024]{1,0:T(8,128)(2,1)} %collective-permute-done.9), kind=kOutput, calls=%fused_computation.1 | convolution fusion | flops 1074266112 | bytes 6815744 | tf_op jit(solution)/shard_map/dot_general | solution.py:16
  146.6 2.4 %collective-permute-done.11.came_ref = bf16[256,1024]{1,0:T(8,128)(2,1)S(1)} collective-permute-done((bf16[256,1024]{1,0:T(8,128)(2,1)S(1)}, bf16[256,1024]{1,0:T(8,128)(2,1)S(1)}, u32[]{:S(2)}, u32[]{:S(2)}) %collective-permute-start.11) | collective-permute-done | bytes 524320 | tf_op jit(solution)/shard_map/ppermute | solution.py:192
  152.8 2.8 %collective-permute-start.18 = (bf16[128,1024]{1,0:T(8,128)(2,1)S(1)}, bf16[128,1024]{1,0:T(8,128)(2,1)S(1)}, u32[]{:S(2)}, u32[]{:S(2)}) collective-permute-start(bf16[128,1024]{1,0:T(8,128)(2,1)S(1)} %get-tuple-element.107), channel_id=1, source_target_pairs={{0,16},{2,18},{4,20},{6,22},{8,24},{10,26},{12,28},{14,30},{16,0},... | collective-permute-start | bytes 786440 | tf_op jit(solution)/shard_map/ppermute | solution.py:192
  155.7 2.3 %convolution_add_fusion.qm_ref = f32[256,1024]{1,0:T(8,128)S(1)} fusion(bf16[256,2048]{1,0:T(8,128)(2,1)S(1)} %maximum_select_fusion.2.low_ref, bf16[2048,1024]{1,0:T(8,128)(2,1)S(1)} %copy-done.27, bf16[256,1024]{1,0:T(8,128)(2,1)} %collective-permute-done.13), kind=kOutput, calls=%fused_computation | convolution fusion | flops 1074266112 | bytes 6815744 | tf_op jit(solution)/shard_map/dot_general | solution.py:16
  157.9 4.2 %collective-permute-done.16.qc_ref = bf16[256,1024]{1,0:T(8,128)(2,1)S(1)} collective-permute-done((bf16[256,1024]{1,0:T(8,128)(2,1)S(1)}, bf16[256,1024]{1,0:T(8,128)(2,1)S(1)}, u32[]{:S(2)}, u32[]{:S(2)}) %collective-permute-start.16) | collective-permute-done | bytes 524320 | tf_op jit(solution)/shard_map/ppermute | solution.py:192
  162.2 5.4 %attention.4 = (bf16[256,2048]{1,0:T(8,128)(2,1)}, bf16[1,1024]{1,0:T(2,128)(2,1)S(1)}) custom-call(s32[3]{0:T(128)S(1)} %get-tuple-element.153.place_ref, f32[256,1024]{1,0:T(8,128)S(1)} %convolution_add_fusion.qm_ref, bf16[256,1024]{1,0:T(8,128)(2,1)S(1)} %collective-permute-done.16.qc_ref, bf16[1792,512]{1,0:T(8,128)(2,1)S(1)} %copy-done.4, ...), custom_call_target="tpu_custom_call" | custom-call | bytes 1024 | tf_op jit(solution)/shard_map/attention/pallas_call | solution.py:147
  167.6 5.4 %attention.5 = (bf16[256,2048]{1,0:T(8,128)(2,1)}, bf16[1,1024]{1,0:T(2,128)(2,1)S(1)}) custom-call(s32[3]{0:T(128)S(1)} %get-tuple-element.152.place_ref, f32[256,1024]{1,0:T(8,128)S(1)} %convolution_add_fusion.qm_ref, bf16[256,1024]{1,0:T(8,128)(2,1)S(1)} %collective-permute-done.16.qc_ref, ...), custom_call_target="tpu_custom_call", output_to_operand_aliasing={{0}: (9, {})} | custom-call | bytes 1024 | tf_op jit(solution)/shard_map/attention/pallas_call | solution.py:147
  174.0 2.4 %half_product.7 = (bf16[128,1024]{1,0:T(8,128)(2,1)}, f32[128,1024]{1,0:T(8,128)S(1)}) custom-call(bf16[256,2048]{1,0:T(8,128)(2,1)S(1)} %maximum_select_fusion.2.low_ref, bf16[256,2048]{1,0:T(8,128)(2,1)S(1)} %copy-done.9, bf16[2048,1024]{1,0:T(8,128)(2,1)S(1)} %copy-done.2, bf16[256,1024]{1,0:T(8,128)(2,1)S(1)} %collective-permute-done.15.came_ref), custom_call_target="tpu_custom_call" | custom-call | bytes 1024 | tf_op jit(solution)/shard_map/half_product/pallas_call | solution.py:42
  176.4 5.7 %attention.6 = (bf16[256,2048]{1,0:T(8,128)(2,1)}, bf16[1,1024]{1,0:T(2,128)(2,1)S(1)}) custom-call(s32[3]{0:T(128)S(1)} %get-tuple-element.153.place_ref, f32[128,1024]{1,0:T(8,128)S(1)} %get-tuple-element.124.qm_ref, bf16[128,1024]{1,0:T(8,128)(2,1)S(1)} %collective-permute-done.18.qc_ref, ...), custom_call_target="tpu_custom_call", output_to_operand_aliasing={{0}: (9, {})} | custom-call | bytes 1024 | tf_op jit(solution)/shard_map/attention/pallas_call | solution.py:147
  188.4 2.2 %collective-permute-start.24 = (bf16[4,1,2048]{2,1,0:T(2,128)(2,1)}, bf16[4,1,2048]{2,1,0:T(2,128)(2,1)S(1)}, u32[]{:S(2)}, u32[]{:S(2)}) collective-permute-start(bf16[4,1,2048]{2,1,0:T(2,128)(2,1)} %order.1), channel_id=1, source_target_pairs={{0,24},{2,26},{4,28},{6,30},{8,16},{10,18},{12,20},{14,22},{16,8},... | collective-permute-start | bytes 49160 | tf_op jit(solution)/shard_map/ppermute | solution.py:192
  193.6 6.5 %attention.7 = (bf16[256,2048]{1,0:T(8,128)(2,1)}, bf16[1,1024]{1,0:T(2,128)(2,1)}) custom-call(s32[3]{0:T(128)} %copy-done.11, f32[128,1024]{1,0:T(8,128)} %copy-done.10, bf16[128,1024]{1,0:T(8,128)(2,1)} %collective-permute-done.17.qc_ref, bf16[1792,512]{1,0:T(8,128)(2,1)} %kc_ref.7, bf16[1792,512]{1,0:T(8,128)(2,1)} %vc_ref.7, ...), custom_call_target="tpu_custom_call", output_to_operand_aliasing={{0}: (9, {})} | custom-call | bytes 1024 | tf_op jit(solution)/shard_map/attention/pallas_call | solution.py:147
  (123 shorter events, 38.2 us)
Async XLA Ops:
  7.2 39.7 %all-gather.4.cloned.1.call-start = ((), (), s32[]{:S(2)}) async-start(), calls=%async_computation | async-start | bytes 5242880 | tf_op jit(solution)/shard_map/all_gather | solution.py:222
  9.4 74.2 %all-gather.6.cloned.1.call-start = ((), (), s32[]{:S(2)}) async-start(), calls=%async_computation.1 | async-start | bytes 5242880 | tf_op jit(solution)/shard_map/all_gather | solution.py:222
  11.1 15.2 %collective-permute-start.1 = (bf16[256,1024]{1,0:T(8,128)(2,1)}, bf16[256,1024]{1,0:T(8,128)(2,1)}, u32[]{:S(2)}, u32[]{:S(2)}) collective-permute-start(bf16[256,1024]{1,0:T(8,128)(2,1)} %pad_maximum_fusion), channel_id=1, source_target_pairs={{0,1},{1,0},{2,3},{3,2},{4,5},{5,4},{6,7},{7,6},{8,9},{9,8},{10,11... | collective-permute-start | bytes 1572872 | tf_op jit(solution)/shard_map/ppermute | solution.py:198
  30.1 89.4 %all-gather.8.cloned.1.call-start = ((), (), s32[]{:S(2)}) async-start(), calls=%async_computation.2 | async-start | bytes 5242880 | tf_op jit(solution)/shard_map/all_gather | solution.py:222
  31.2 14.2 %collective-permute-start.3 = (bf16[256,1024]{1,0:T(8,128)(2,1)S(1)}, bf16[256,1024]{1,0:T(8,128)(2,1)S(1)}, u32[]{:S(2)}, u32[]{:S(2)}) collective-permute-start(bf16[256,1024]{1,0:T(8,128)(2,1)S(1)} %copy-done.18), channel_id=1, source_target_pairs={{0,8},{2,10},{4,12},{6,14},{8,0},{10,2},{12,4},{14,6},{16,24},{18,... | collective-permute-start | bytes 1572872 | tf_op jit(solution)/shard_map/ppermute | solution.py:192
  33.0 24.6 %collective-permute-start.2 = (bf16[256,1024]{1,0:T(8,128)(2,1)S(1)}, bf16[256,1024]{1,0:T(8,128)(2,1)S(1)}, u32[]{:S(2)}, u32[]{:S(2)}) collective-permute-start(bf16[256,1024]{1,0:T(8,128)(2,1)S(1)} %copy-done.17), channel_id=1, source_target_pairs={{0,24},{2,26},{4,28},{6,30},{8,16},{10,18},{12,20},{14,22},{16,8},... | collective-permute-start | bytes 1572872 | tf_op jit(solution)/shard_map/ppermute | solution.py:192
  35.5 23.6 %collective-permute-start = (bf16[256,1024]{1,0:T(8,128)(2,1)S(1)}, bf16[256,1024]{1,0:T(8,128)(2,1)}, u32[]{:S(2)}, u32[]{:S(2)}) collective-permute-start(bf16[256,1024]{1,0:T(8,128)(2,1)S(1)} %copy-done.16), channel_id=1, source_target_pairs={{0,1},{1,0},{2,3},{3,2},{4,5},{5,4},{6,7},{7,6},{8,9},{9,8},{10,11... | collective-permute-start | bytes 1572872 | tf_op jit(solution)/shard_map/ppermute | solution.py:198
  45.4 17.0 %collective-permute-start.5 = (bf16[256,1024]{1,0:T(8,128)(2,1)S(1)}, bf16[256,1024]{1,0:T(8,128)(2,1)S(1)}, u32[]{:S(2)}, u32[]{:S(2)}) collective-permute-start(bf16[256,1024]{1,0:T(8,128)(2,1)S(1)} %collective-permute-done.3), channel_id=1, source_target_pairs={{0,1},{1,0},{2,3},{3,2},{4,5},{5,4},{6,7},{7,6},{8,9},{9,8},{10,11... | collective-permute-start | bytes 1572872 | tf_op jit(solution)/shard_map/ppermute | solution.py:198
  57.6 12.6 %collective-permute-start.4 = (bf16[256,1024]{1,0:T(8,128)(2,1)S(1)}, bf16[256,1024]{1,0:T(8,128)(2,1)S(1)}, u32[]{:S(2)}, u32[]{:S(2)}) collective-permute-start(bf16[256,1024]{1,0:T(8,128)(2,1)S(1)} %collective-permute-done.2), channel_id=1, source_target_pairs={{0,1},{1,0},{2,3},{3,2},{4,5},{5,4},{6,7},{7,6},{8,9},{9,8},{10,11... | collective-permute-start | bytes 1572872 | tf_op jit(solution)/shard_map/ppermute | solution.py:198
  60.5 22.7 %collective-permute-start.7 = (bf16[256,1024]{1,0:T(8,128)(2,1)S(1)}, bf16[256,1024]{1,0:T(8,128)(2,1)}, u32[]{:S(2)}, u32[]{:S(2)}) collective-permute-start(bf16[256,1024]{1,0:T(8,128)(2,1)S(1)} %get-tuple-element.80), channel_id=1, source_target_pairs={{0,16},{2,18},{4,20},{6,22},{8,24},{10,26},{12,28},{14,30},{16,0},... | collective-permute-start | bytes 1572872 | tf_op jit(solution)/shard_map/ppermute | solution.py:192
  64.8 27.4 %collective-permute-start.9 = (bf16[256,1024]{1,0:T(8,128)(2,1)}, bf16[256,1024]{1,0:T(8,128)(2,1)}, u32[]{:S(2)}, u32[]{:S(2)}) collective-permute-start(bf16[256,1024]{1,0:T(8,128)(2,1)} %convolution_convert_fusion.3), channel_id=1, source_target_pairs={{0,8},{2,10},{4,12},{6,14},{8,0},{10,2},{12,4},{14,6},{16,24},{18,... | collective-permute-start | bytes 1572872 | tf_op jit(solution)/shard_map/ppermute | solution.py:192
  70.6 48.9 %copy-start.6 = (bf16[256,2048]{1,0:T(8,128)(2,1)}, bf16[256,2048]{1,0:T(8,128)(2,1)S(1)}, u32[]{:S(2)}) copy-start(bf16[256,2048]{1,0:T(8,128)(2,1)S(1)} %maximum_select_fusion.1.high_ref) | copy-start | bytes 3145732
  72.7 29.4 %collective-permute-start.10 = (bf16[256,1024]{1,0:T(8,128)(2,1)}, bf16[256,1024]{1,0:T(8,128)(2,1)}, u32[]{:S(2)}, u32[]{:S(2)}) collective-permute-start(bf16[256,1024]{1,0:T(8,128)(2,1)} %convolution_convert_fusion.2), channel_id=1, source_target_pairs={{0,8},{2,10},{4,12},{6,14},{8,0},{10,2},{12,4},{14,6},{16,24},{18,... | collective-permute-start | bytes 1572872 | tf_op jit(solution)/shard_map/ppermute | solution.py:192
  73.4 18.1 %collective-permute-start.6 = (bf16[256,1024]{1,0:T(8,128)(2,1)S(1)}, bf16[256,1024]{1,0:T(8,128)(2,1)S(1)}, u32[]{:S(2)}, u32[]{:S(2)}) collective-permute-start(bf16[256,1024]{1,0:T(8,128)(2,1)S(1)} %get-tuple-element.86), channel_id=1, source_target_pairs={{0,1},{1,0},{2,3},{3,2},{4,5},{5,4},{6,7},{7,6},{8,9},{9,8},{10,11... | collective-permute-start | bytes 1572872 | tf_op jit(solution)/shard_map/ppermute | solution.py:198
  83.2 18.9 %collective-permute-start.8 = (bf16[256,1024]{1,0:T(8,128)(2,1)}, bf16[256,1024]{1,0:T(8,128)(2,1)}, u32[]{:S(2)}, u32[]{:S(2)}) collective-permute-start(bf16[256,1024]{1,0:T(8,128)(2,1)} %collective-permute-done.7), channel_id=1, source_target_pairs={{0,1},{1,0},{2,3},{3,2},{4,5},{5,4},{6,7},{7,6},{8,9},{9,8},{10,11... | collective-permute-start | bytes 1572872 | tf_op jit(solution)/shard_map/ppermute | solution.py:198
  88.1 53.1 %collective-permute-start.13 = (bf16[256,1024]{1,0:T(8,128)(2,1)}, bf16[256,1024]{1,0:T(8,128)(2,1)}, u32[]{:S(2)}, u32[]{:S(2)}) collective-permute-start(bf16[256,1024]{1,0:T(8,128)(2,1)} %convolution_convert_fusion), channel_id=1, source_target_pairs={{0,8},{2,10},{4,12},{6,14},{8,0},{10,2},{12,4},{14,6},{16,24},{18,... | collective-permute-start | bytes 1572872 | tf_op jit(solution)/shard_map/ppermute | solution.py:192
  91.4 49.7 %collective-permute-start.14 = (bf16[256,1024]{1,0:T(8,128)(2,1)}, bf16[256,1024]{1,0:T(8,128)(2,1)}, u32[]{:S(2)}, u32[]{:S(2)}) collective-permute-start(bf16[256,1024]{1,0:T(8,128)(2,1)} %convolution_convert_fusion.1), channel_id=1, source_target_pairs={{0,8},{2,10},{4,12},{6,14},{8,0},{10,2},{12,4},{14,6},{16,24},{18,... | collective-permute-start | bytes 1572872 | tf_op jit(solution)/shard_map/ppermute | solution.py:192
  107.6 39.0 %collective-permute-start.12 = (bf16[256,1024]{1,0:T(8,128)(2,1)}, bf16[256,1024]{1,0:T(8,128)(2,1)S(1)}, u32[]{:S(2)}, u32[]{:S(2)}) collective-permute-start(bf16[256,1024]{1,0:T(8,128)(2,1)} %add_convert_fusion.1), channel_id=1, source_target_pairs={{0,16},{2,18},{4,20},{6,22},{8,24},{10,26},{12,28},{14,30},{16,0},... | collective-permute-start | bytes 1572872 | tf_op jit(solution)/shard_map/ppermute | solution.py:192
  123.5 20.2 %copy-start.15 = (bf16[256,1024]{1,0:T(8,128)(2,1)S(1)}, bf16[256,1024]{1,0:T(8,128)(2,1)}, u32[]{:S(2)}) copy-start(bf16[256,1024]{1,0:T(8,128)(2,1)} %copy-done.14) | copy-start | bytes 1572868
  123.5 25.6 %collective-permute-start.11 = (bf16[256,1024]{1,0:T(8,128)(2,1)S(1)}, bf16[256,1024]{1,0:T(8,128)(2,1)S(1)}, u32[]{:S(2)}, u32[]{:S(2)}) collective-permute-start(bf16[256,1024]{1,0:T(8,128)(2,1)S(1)} %half_product.4), channel_id=1, source_target_pairs={{0,8},{2,10},{4,12},{6,14},{8,0},{10,2},{12,4},{14,6},{16,24},{18,... | collective-permute-start | bytes 1572872 | tf_op jit(solution)/shard_map/ppermute | solution.py:192
  144.0 18.1 %collective-permute-start.16 = (bf16[256,1024]{1,0:T(8,128)(2,1)S(1)}, bf16[256,1024]{1,0:T(8,128)(2,1)S(1)}, u32[]{:S(2)}, u32[]{:S(2)}) collective-permute-start(bf16[256,1024]{1,0:T(8,128)(2,1)S(1)} %add_convert_fusion), channel_id=1, source_target_pairs={{0,16},{2,18},{4,20},{6,22},{8,24},{10,26},{12,28},{14,30},{16,0},... | collective-permute-start | bytes 1572872 | tf_op jit(solution)/shard_map/ppermute | solution.py:192
  146.6 29.9 %copy-start = (f32[256,1024]{1,0:T(8,128)}, f32[256,1024]{1,0:T(8,128)S(1)}, u32[]{:S(2)}) copy-start(f32[256,1024]{1,0:T(8,128)S(1)} %convolution_add_fusion.1.km_ref.vm_ref) | copy-start | bytes 3145732
  146.6 29.8 %copy-start.3 = (bf16[256,1024]{1,0:T(8,128)(2,1)}, bf16[256,1024]{1,0:T(8,128)(2,1)S(1)}, u32[]{:S(2)}) copy-start(bf16[256,1024]{1,0:T(8,128)(2,1)S(1)} %collective-permute-done.12.kt_ref.vt_ref) | copy-start | bytes 1572868
  152.6 21.3 %collective-permute-start.15 = (bf16[256,1024]{1,0:T(8,128)(2,1)S(1)}, bf16[256,1024]{1,0:T(8,128)(2,1)S(1)}, u32[]{:S(2)}, u32[]{:S(2)}) collective-permute-start(bf16[256,1024]{1,0:T(8,128)(2,1)S(1)} %half_product.6), channel_id=1, source_target_pairs={{0,8},{2,10},{4,12},{6,14},{8,0},{10,2},{12,4},{14,6},{16,24},{18,... | collective-permute-start | bytes 1572872 | tf_op jit(solution)/shard_map/ppermute | solution.py:192
  152.8 23.6 %collective-permute-start.18 = (bf16[128,1024]{1,0:T(8,128)(2,1)S(1)}, bf16[128,1024]{1,0:T(8,128)(2,1)S(1)}, u32[]{:S(2)}, u32[]{:S(2)}) collective-permute-start(bf16[128,1024]{1,0:T(8,128)(2,1)S(1)} %get-tuple-element.107), channel_id=1, source_target_pairs={{0,16},{2,18},{4,20},{6,22},{8,24},{10,26},{12,28},{14,30},{16,0},... | collective-permute-start | bytes 786440 | tf_op jit(solution)/shard_map/ppermute | solution.py:192
  176.4 17.2 %collective-permute-start.17 = (bf16[128,1024]{1,0:T(8,128)(2,1)}, bf16[128,1024]{1,0:T(8,128)(2,1)}, u32[]{:S(2)}, u32[]{:S(2)}) collective-permute-start(bf16[128,1024]{1,0:T(8,128)(2,1)} %get-tuple-element.121), channel_id=1, source_target_pairs={{0,16},{2,18},{4,20},{6,22},{8,24},{10,26},{12,28},{14,30},{16,0},... | collective-permute-start | bytes 786440 | tf_op jit(solution)/shard_map/ppermute | solution.py:192
  182.1 3.1 %collective-permute-start.21 = (bf16[1,2048]{1,0:T(2,128)(2,1)S(1)}, bf16[1,2048]{1,0:T(2,128)(2,1)S(1)}, u32[]{:S(2)}, u32[]{:S(2)}) collective-permute-start(bf16[1,2048]{1,0:T(2,128)(2,1)S(1)} %pad_maximum_fusion.5.refs_0_), channel_id=1, source_target_pairs={{0,6},{2,4},{4,2},{6,0},{8,14},{10,12},{12,10},{14,8},{16,22},{18,... | collective-permute-start | bytes 12296 | tf_op jit(solution)/shard_map/ppermute | solution.py:192
  182.8 3.7 %collective-permute-start.20 = (bf16[1,2048]{1,0:T(2,128)(2,1)S(1)}, bf16[1,2048]{1,0:T(2,128)(2,1)S(1)}, u32[]{:S(2)}, u32[]{:S(2)}) collective-permute-start(bf16[1,2048]{1,0:T(2,128)(2,1)S(1)} %pad_maximum_fusion.5.refs_0_), channel_id=1, source_target_pairs={{0,4},{2,6},{4,0},{6,2},{8,12},{10,14},{12,8},{14,10},{16,20},{18,... | collective-permute-start | bytes 12296 | tf_op jit(solution)/shard_map/ppermute | solution.py:192
  183.6 2.9 %collective-permute-start.19 = (bf16[1,2048]{1,0:T(2,128)(2,1)S(1)}, bf16[1,2048]{1,0:T(2,128)(2,1)S(1)}, u32[]{:S(2)}, u32[]{:S(2)}) collective-permute-start(bf16[1,2048]{1,0:T(2,128)(2,1)S(1)} %pad_maximum_fusion.5.refs_0_), channel_id=1, source_target_pairs={{0,2},{2,0},{4,6},{6,4},{8,10},{10,8},{12,14},{14,12},{16,18},{18,... | collective-permute-start | bytes 12296 | tf_op jit(solution)/shard_map/ppermute | solution.py:192
  188.4 11.7 %collective-permute-start.24 = (bf16[4,1,2048]{2,1,0:T(2,128)(2,1)}, bf16[4,1,2048]{2,1,0:T(2,128)(2,1)S(1)}, u32[]{:S(2)}, u32[]{:S(2)}) collective-permute-start(bf16[4,1,2048]{2,1,0:T(2,128)(2,1)} %order.1), channel_id=1, source_target_pairs={{0,24},{2,26},{4,28},{6,30},{8,16},{10,18},{12,20},{14,22},{16,8},... | collective-permute-start | bytes 49160 | tf_op jit(solution)/shard_map/ppermute | solution.py:192
  190.6 9.5 %collective-permute-start.23 = (bf16[4,1,2048]{2,1,0:T(2,128)(2,1)}, bf16[4,1,2048]{2,1,0:T(2,128)(2,1)S(1)}, u32[]{:S(2)}, u32[]{:S(2)}) collective-permute-start(bf16[4,1,2048]{2,1,0:T(2,128)(2,1)} %order.1), channel_id=1, source_target_pairs={{0,16},{2,18},{4,20},{6,22},{8,24},{10,26},{12,28},{14,30},{16,0},... | collective-permute-start | bytes 49160 | tf_op jit(solution)/shard_map/ppermute | solution.py:192
  192.3 7.8 %collective-permute-start.22 = (bf16[4,1,2048]{2,1,0:T(2,128)(2,1)}, bf16[4,1,2048]{2,1,0:T(2,128)(2,1)S(1)}, u32[]{:S(2)}, u32[]{:S(2)}) collective-permute-start(bf16[4,1,2048]{2,1,0:T(2,128)(2,1)} %order.1), channel_id=1, source_target_pairs={{0,8},{2,10},{4,12},{6,14},{8,0},{10,2},{12,4},{14,6},{16,24},{18,... | collective-permute-start | bytes 49160 | tf_op jit(solution)/shard_map/ppermute | solution.py:192
  (24 other events, 166.2 us)
Sparse Core Ops, SparseCore 0:
  9.6 37.1 all-gather.3
  48.9 34.4 all-gather.5
  85.0 34.4 all-gather.7

commit v14 on v12

--- a/solution.py
+++ b/solution.py
@@ -206,11 +206,11 @@
 
     weights["kv"] = group_gather(jnp.concatenate([w_key, w_value], axis=1))
 
+    q_parts = [w_query[:, piece * chunk : (piece + 1) * chunk] for piece in range(pieces)]
+
     def gather_queries():
-        source = step(w_query) if fast else w_query
-        for piece in range(pieces):
-            part_of = source[:, piece * chunk : (piece + 1) * chunk]
-            weights[piece] = group_gather(part_of)
+        for piece, value in enumerate(q_parts):
+            weights[piece] = group_gather(value)
 
     tokens = {}
     if fast:
@@ -230,7 +230,7 @@
         swap[0] = over_tp(step(cut(source, 0, 1 - x)))
         mine = z // 2 == x
         held, came = {}, {}
-        swap[1] = step(swap[1])
+        swap[1], *q_parts = step(swap[1], *q_parts)
         own = cut(source, 1, x)
         send = {b: jnp.where(mine == (b < 2), own, swap[1]) for b in (1, 3)}
         send[1], send[3] = step(send[1], send[3])

time: 208 us -> 208 us (level)
  waiting for transfers between devices: 90.5 us -> 82.9 us
  starting transfers between devices: 31.2 us -> 34.1 us
  local copies, waits for them, and re-layouts: 6.37 us -> 8.97 us
  other arithmetic: 11.1 us -> 13.2 us
    ppermute x19, waiting for transfers between devices: 63.4 us -> 53.2 us  [over_inst(): return lax.ppermute(value, 'inst', [(i, i ^ bits) for i in range(n_inst)])]
    all_gather x3, waiting for transfers between devices: 10.8 us -> 16.2 us  [group_gather(): lax.all_gather(value, 'inst', axis=0, tiled=True, axis_index_groups=groups)]
    select_n x4, other arithmetic: 3.12 us -> 6.9 us  [swapped_if(): jnp.where(flag, jnp.concatenate([b, a], axis=axis), jnp.concatenate([a, b...]
    ppermute x6, waiting for transfers between devices: 15.7 us -> 12.9 us  [over_tp(): return lax.ppermute(value, 'tp', [(0, 1), (1, 0)])]
    unnamed x60 -> x58, local copies, waits for them, and re-layouts: 3.99 us -> 6.64 us
  transfers between devices with their start and end apart: 28 -> 28, of which waited for: 13 -> 15; matrix products, arithmetic and copies ran while one was open for 16% -> 17% of each run, Pallas kernels for 15% -> 15%
where the time goes in v14:
time: 208 us
  waiting for transfers between devices  82.9 us (40%)
  starting transfers between devices  34.1 us (16%)
  Pallas kernels  32.2 us (15%)
  matrix products  21.4 us (10%)
  between operations  14.9 us (7%)
  other arithmetic  13.2 us (6%)
  local copies, waits for them, and re-layouts  8.97 us (4%)
    ppermute x19, waiting for transfers between devices, over_inst(): return lax.ppermute(value, 'inst', [(i, i ^ bits) for i in range(n_inst)])  53.2 us
    ppermute x19, starting transfers between devices, over_inst(): return lax.ppermute(value, 'inst', [(i, i ^ bits) for i in range(n_inst)])  23.6 us
    pallas_call x4, Pallas kernels, attend(): pl.pallas_call(attention_kernel, grid_spec=pltpu.PrefetchScalarGridSpec(n...  23 us
    dot_general x8, matrix products, dot(): return jnp.dot(a, b, preferred_element_type=jnp.float32)  21.4 us
    all_gather x3, waiting for transfers between devices, group_gather(): lax.all_gather(value, 'inst', axis=0, tiled=True, axis_index_groups=groups)  16.2 us
    ppermute x6, waiting for transfers between devices, over_tp(): return lax.ppermute(value, 'tp', [(0, 1), (1, 0)])  12.9 us
    ppermute x6, starting transfers between devices, over_tp(): return lax.ppermute(value, 'tp', [(0, 1), (1, 0)])  10.4 us
    pallas_call x4, Pallas kernels, half_product(): pl.pallas_call(first_kernel if first else later_kernel, grid=(columns //...  7.76 us
  transfers between devices with their start and end apart: 28, of which 15 were waited for; matrix products, arithmetic and copies ran while one was open for 17% of the time, Pallas kernels for 15%

profile of v14, /device:TPU:0, one launch (start us, length us, event | category | flops | bytes accessed | tf_op | source)
XLA Modules:
  0.0 207.8 jit_solution(2215956639399366859)
XLA Ops:
  7.2 2.4 %pad_maximum_fusion = bf16[512,1024]{1,0:T(8,128)(2,1)} fusion(bf16[512,512]{1,0:T(8,128)(2,1)} %param.10, bf16[512,512]{1,0:T(8,128)(2,1)} %param.9), kind=kLoop, calls=%fused_computation.6 | loop fusion | flops 2097152 | bytes 2097152 | tf_op jit(solution)/shard_map/concatenate | solution.py:207
  11.4 2.9 %collective-permute-start.1 = (bf16[256,1024]{1,0:T(8,128)(2,1)}, bf16[256,1024]{1,0:T(8,128)(2,1)}, u32[]{:S(2)}, u32[]{:S(2)}) collective-permute-start(bf16[256,1024]{1,0:T(8,128)(2,1)} %pad_maximum_fusion.1), channel_id=1, source_target_pairs={{0,1},{1,0},{2,3},{3,2},{4,5},{5,4},{6,7},{7,6},{8,9},{9,8},{10,11... | collective-permute-start | bytes 1572872 | tf_op jit(solution)/shard_map/ppermute | solution.py:179
  17.4 9.2 %collective-permute-done.1 = bf16[256,1024]{1,0:T(8,128)(2,1)} collective-permute-done((bf16[256,1024]{1,0:T(8,128)(2,1)}, bf16[256,1024]{1,0:T(8,128)(2,1)}, u32[]{:S(2)}, u32[]{:S(2)}) %collective-permute-start.1) | collective-permute-done | bytes 524320 | tf_op jit(solution)/shard_map/ppermute | solution.py:179
  30.6 2.5 %collective-permute-start.2 = (bf16[256,1024]{1,0:T(8,128)(2,1)S(1)}, bf16[256,1024]{1,0:T(8,128)(2,1)S(1)}, u32[]{:S(2)}, u32[]{:S(2)}) collective-permute-start(bf16[256,1024]{1,0:T(8,128)(2,1)S(1)} %get-tuple-element.74), channel_id=1, source_target_pairs={{0,24},{2,26},{4,28},{6,30},{8,16},{10,18},{12,20},{14,22},{16,8},... | collective-permute-start | bytes 1572872 | tf_op jit(solution)/shard_map/ppermute | solution.py:173
  34.5 8.4 %collective-permute-done.3 = bf16[256,1024]{1,0:T(8,128)(2,1)S(1)} collective-permute-done((bf16[256,1024]{1,0:T(8,128)(2,1)S(1)}, bf16[256,1024]{1,0:T(8,128)(2,1)S(1)}, u32[]{:S(2)}, u32[]{:S(2)}) %collective-permute-start.3) | collective-permute-done | bytes 524320 | tf_op jit(solution)/shard_map/ppermute | solution.py:173
  44.4 2.6 %all-gather.4.cloned.1.call-done = bf16[2048,1024]{1,0:T(8,128)(2,1)} async-done(((bf16[512,1024]{1,0:T(8,128)(2,1)}), bf16[2048,1024]{1,0:T(8,128)(2,1)}) %all-gather.4.cloned.1.call-update) | async-done | bytes 4194320 | tf_op jit(solution)/shard_map/all_gather | solution.py:203
  47.0 8.1 %collective-permute-done.2 = bf16[256,1024]{1,0:T(8,128)(2,1)S(1)} collective-permute-done((bf16[256,1024]{1,0:T(8,128)(2,1)S(1)}, bf16[256,1024]{1,0:T(8,128)(2,1)S(1)}, u32[]{:S(2)}, u32[]{:S(2)}) %collective-permute-start.2) | collective-permute-done | bytes 524320 | tf_op jit(solution)/shard_map/ppermute | solution.py:173
  62.7 2.1 %convolution_convert_fusion.3 = bf16[256,1024]{1,0:T(8,128)(2,1)} fusion(bf16[256,2048]{1,0:T(8,128)(2,1)S(1)} %maximum_select_fusion.low_ref, bf16[2048,1024]{1,0:T(8,128)(2,1)S(1)} %copy-done.22), kind=kOutput, calls=%fused_computation.5 | convolution fusion | flops 1074003968 | bytes 5767168 | tf_op jit(solution)/shard_map/dot_general | solution.py:16
  65.6 3.7 %collective-permute-done.4 = bf16[256,1024]{1,0:T(8,128)(2,1)S(1)} collective-permute-done((bf16[256,1024]{1,0:T(8,128)(2,1)S(1)}, bf16[256,1024]{1,0:T(8,128)(2,1)S(1)}, u32[]{:S(2)}, u32[]{:S(2)}) %collective-permute-start.4) | collective-permute-done | bytes 524320 | tf_op jit(solution)/shard_map/ppermute | solution.py:179
  71.1 2.1 %convolution_convert_fusion.2 = bf16[256,1024]{1,0:T(8,128)(2,1)} fusion(bf16[256,2048]{1,0:T(8,128)(2,1)S(1)} %maximum_select_fusion.1.high_ref, bf16[2048,1024]{1,0:T(8,128)(2,1)S(1)} %copy-done.22), kind=kOutput, calls=%fused_computation.4 | convolution fusion | flops 1074003968 | bytes 5767168 | tf_op jit(solution)/shard_map/dot_general | solution.py:16
  76.2 4.0 %collective-permute-done.7 = bf16[256,1024]{1,0:T(8,128)(2,1)S(1)} collective-permute-done((bf16[256,1024]{1,0:T(8,128)(2,1)S(1)}, bf16[256,1024]{1,0:T(8,128)(2,1)S(1)}, u32[]{:S(2)}, u32[]{:S(2)}) %collective-permute-start.7) | collective-permute-done | bytes 524320 | tf_op jit(solution)/shard_map/ppermute | solution.py:173
  83.7 4.4 %convolution_convert_fusion = bf16[256,1024]{1,0:T(8,128)(2,1)} fusion(bf16[256,2048]{1,0:T(8,128)(2,1)S(1)} %maximum_select_fusion.low_ref, bf16[2048,1024]{1,0:T(8,128)(2,1)} %all-gather.6.cloned.1.call-done), kind=kOutput, calls=%fused_computation.2 | convolution fusion | flops 1074003968 | bytes 5767168 | tf_op jit(solution)/shard_map/dot_general | solution.py:16
  89.5 2.1 %convolution_convert_fusion.1 = bf16[256,1024]{1,0:T(8,128)(2,1)} fusion(bf16[256,2048]{1,0:T(8,128)(2,1)S(1)} %maximum_select_fusion.1.high_ref, bf16[2048,1024]{1,0:T(8,128)(2,1)S(1)} %copy-done.25), kind=kOutput, calls=%fused_computation.3 | convolution fusion | flops 1074003968 | bytes 5767168 | tf_op jit(solution)/shard_map/dot_general | solution.py:16
  92.2 8.9 %collective-permute-done.10 = bf16[256,1024]{1,0:T(8,128)(2,1)} collective-permute-done((bf16[256,1024]{1,0:T(8,128)(2,1)}, bf16[256,1024]{1,0:T(8,128)(2,1)}, u32[]{:S(2)}, u32[]{:S(2)}) %collective-permute-start.10) | collective-permute-done | bytes 524320 | tf_op jit(solution)/shard_map/ppermute | solution.py:173
  102.7 3.5 %add_convert_fusion.1 = bf16[256,1024]{1,0:T(8,128)(2,1)} fusion(bf16[256,1024]{1,0:T(8,128)(2,1)} %collective-permute-done.10, bf16[256,2048]{1,0:T(8,128)(2,1)S(1)} %maximum_select_fusion.3.high_ref, bf16[2048,1024]{1,0:T(8,128)(2,1)S(1)} %copy-done.23), kind=kOutput, calls=%fused_computation.12 | convolution fusion | flops 1074528256 | bytes 6291456 | tf_op jit(solution)/shard_map/dot_general | solution.py:16
  106.2 2.0 collective-permute-start.12
  108.1 11.6 %all-gather.8.cloned.1.call-done.w_ref = bf16[2048,1024]{1,0:T(8,128)(2,1)} async-done(((bf16[512,1024]{1,0:T(8,128)(2,1)}), bf16[2048,1024]{1,0:T(8,128)(2,1)}) %all-gather.8.cloned.1.call-update) | async-done | bytes 4194320 | tf_op jit(solution)/shard_map/all_gather | solution.py:203
  119.8 2.2 %copy-done.1 = bf16[2048,1024]{1,0:T(8,128)(2,1)S(1)} copy-done((bf16[2048,1024]{1,0:T(8,128)(2,1)S(1)}, bf16[2048,1024]{1,0:T(8,128)(2,1)}, u32[]{:S(2)}) %copy-start.1) | copy-done | bytes 4194328
  125.3 9.3 %collective-permute-done.14 = bf16[256,1024]{1,0:T(8,128)(2,1)} collective-permute-done((bf16[256,1024]{1,0:T(8,128)(2,1)}, bf16[256,1024]{1,0:T(8,128)(2,1)}, u32[]{:S(2)}, u32[]{:S(2)}) %collective-permute-start.14) | collective-permute-done | bytes 524320 | tf_op jit(solution)/shard_map/ppermute | solution.py:173
  134.6 2.5 %add_convert_fusion = bf16[256,1024]{1,0:T(8,128)(2,1)S(1)} fusion(bf16[256,1024]{1,0:T(8,128)(2,1)} %collective-permute-done.14, bf16[256,2048]{1,0:T(8,128)(2,1)S(1)} %copy-done.9, bf16[2048,1024]{1,0:T(8,128)(2,1)S(1)} %copy-done.26), kind=kOutput, calls=%fused_computation.11 | convolution fusion | flops 1074528256 | bytes 6291456 | tf_op jit(solution)/shard_map/dot_general | solution.py:16
  138.9 2.5 %convolution_add_fusion.1.km_ref.vm_ref = f32[256,1024]{1,0:T(8,128)S(1)} fusion(bf16[256,2048]{1,0:T(8,128)(2,1)S(1)} %maximum_select_fusion.2.low_ref, bf16[2048,1024]{1,0:T(8,128)(2,1)S(1)} %copy-done.24, bf16[256,1024]{1,0:T(8,128)(2,1)} %collective-permute-done.9), kind=kOutput, calls=%fused_computation.1 | convolution fusion | flops 1074266112 | bytes 6815744 | tf_op jit(solution)/shard_map/dot_general | solution.py:16
  141.4 6.2 %collective-permute-done.11.came_ref = bf16[256,1024]{1,0:T(8,128)(2,1)S(1)} collective-permute-done((bf16[256,1024]{1,0:T(8,128)(2,1)S(1)}, bf16[256,1024]{1,0:T(8,128)(2,1)S(1)}, u32[]{:S(2)}, u32[]{:S(2)}) %collective-permute-start.11) | collective-permute-done | bytes 524320 | tf_op jit(solution)/shard_map/ppermute | solution.py:173
  151.3 3.0 %collective-permute-start.18 = (bf16[128,1024]{1,0:T(8,128)(2,1)S(1)}, bf16[128,1024]{1,0:T(8,128)(2,1)S(1)}, u32[]{:S(2)}, u32[]{:S(2)}) collective-permute-start(bf16[128,1024]{1,0:T(8,128)(2,1)S(1)} %get-tuple-element.109), channel_id=1, source_target_pairs={{0,16},{2,18},{4,20},{6,22},{8,24},{10,26},{12,28},{14,30},{16,0},... | collective-permute-start | bytes 786440 | tf_op jit(solution)/shard_map/ppermute | solution.py:173
  154.4 2.3 %convolution_add_fusion.qm_ref = f32[256,1024]{1,0:T(8,128)S(1)} fusion(bf16[256,2048]{1,0:T(8,128)(2,1)S(1)} %maximum_select_fusion.2.low_ref, bf16[2048,1024]{1,0:T(8,128)(2,1)S(1)} %copy-done.26, bf16[256,1024]{1,0:T(8,128)(2,1)} %collective-permute-done.13), kind=kOutput, calls=%fused_computation | convolution fusion | flops 1074266112 | bytes 6815744 | tf_op jit(solution)/shard_map/dot_general | solution.py:16
  156.7 3.2 %collective-permute-done.16.qc_ref = bf16[256,1024]{1,0:T(8,128)(2,1)S(1)} collective-permute-done((bf16[256,1024]{1,0:T(8,128)(2,1)S(1)}, bf16[256,1024]{1,0:T(8,128)(2,1)S(1)}, u32[]{:S(2)}, u32[]{:S(2)}) %collective-permute-start.16) | collective-permute-done | bytes 524320 | tf_op jit(solution)/shard_map/ppermute | solution.py:173
  159.9 5.4 %attention.4 = (bf16[256,2048]{1,0:T(8,128)(2,1)}, bf16[1,1024]{1,0:T(2,128)(2,1)S(1)}) custom-call(s32[3]{0:T(128)S(1)} %get-tuple-element.155.place_ref, f32[256,1024]{1,0:T(8,128)S(1)} %convolution_add_fusion.qm_ref, bf16[256,1024]{1,0:T(8,128)(2,1)S(1)} %collective-permute-done.16.qc_ref, bf16[1792,512]{1,0:T(8,128)(2,1)S(1)} %copy-done.4, ...), custom_call_target="tpu_custom_call" | custom-call | bytes 1024 | tf_op jit(solution)/shard_map/attention/pallas_call | solution.py:128
  165.4 5.4 %attention.5 = (bf16[256,2048]{1,0:T(8,128)(2,1)}, bf16[1,1024]{1,0:T(2,128)(2,1)S(1)}) custom-call(s32[3]{0:T(128)S(1)} %get-tuple-element.154.place_ref, f32[256,1024]{1,0:T(8,128)S(1)} %convolution_add_fusion.qm_ref, bf16[256,1024]{1,0:T(8,128)(2,1)S(1)} %collective-permute-done.16.qc_ref, ...), custom_call_target="tpu_custom_call", output_to_operand_aliasing={{0}: (9, {})} | custom-call | bytes 1024 | tf_op jit(solution)/shard_map/attention/pallas_call | solution.py:128
  170.8 2.6 %collective-permute-done.15.came_ref = bf16[256,1024]{1,0:T(8,128)(2,1)S(1)} collective-permute-done((bf16[256,1024]{1,0:T(8,128)(2,1)S(1)}, bf16[256,1024]{1,0:T(8,128)(2,1)S(1)}, u32[]{:S(2)}, u32[]{:S(2)}) %collective-permute-start.15) | collective-permute-done | bytes 524320 | tf_op jit(solution)/shard_map/ppermute | solution.py:173
  173.4 2.4 %half_product.7 = (bf16[128,1024]{1,0:T(8,128)(2,1)}, f32[128,1024]{1,0:T(8,128)S(1)}) custom-call(bf16[256,2048]{1,0:T(8,128)(2,1)S(1)} %maximum_select_fusion.2.low_ref, bf16[256,2048]{1,0:T(8,128)(2,1)S(1)} %copy-done.9, bf16[2048,1024]{1,0:T(8,128)(2,1)S(1)} %copy-done.2, bf16[256,1024]{1,0:T(8,128)(2,1)S(1)} %collective-permute-done.15.came_ref), custom_call_target="tpu_custom_call" | custom-call | bytes 1024 | tf_op jit(solution)/shard_map/half_product/pallas_call | solution.py:42
  175.9 5.7 %attention.6 = (bf16[256,2048]{1,0:T(8,128)(2,1)}, bf16[1,1024]{1,0:T(2,128)(2,1)S(1)}) custom-call(s32[3]{0:T(128)S(1)} %get-tuple-element.155.place_ref, f32[128,1024]{1,0:T(8,128)S(1)} %get-tuple-element.126.qm_ref, bf16[128,1024]{1,0:T(8,128)(2,1)S(1)} %collective-permute-done.18.qc_ref, ...), custom_call_target="tpu_custom_call", output_to_operand_aliasing={{0}: (9, {})} | custom-call | bytes 1024 | tf_op jit(solution)/shard_map/attention/pallas_call | solution.py:128
  188.0 2.2 %collective-permute-start.24 = (bf16[4,1,2048]{2,1,0:T(2,128)(2,1)}, bf16[4,1,2048]{2,1,0:T(2,128)(2,1)S(1)}, u32[]{:S(2)}, u32[]{:S(2)}) collective-permute-start(bf16[4,1,2048]{2,1,0:T(2,128)(2,1)} %order.1), channel_id=1, source_target_pairs={{0,24},{2,26},{4,28},{6,30},{8,16},{10,18},{12,20},{14,22},{16,8},... | collective-permute-start | bytes 49160 | tf_op jit(solution)/shard_map/ppermute | solution.py:173
  193.9 6.5 %attention.7 = (bf16[256,2048]{1,0:T(8,128)(2,1)}, bf16[1,1024]{1,0:T(2,128)(2,1)}) custom-call(s32[3]{0:T(128)} %copy-done.11, f32[128,1024]{1,0:T(8,128)} %copy-done.10, bf16[128,1024]{1,0:T(8,128)(2,1)} %copy-done.17, bf16[1792,512]{1,0:T(8,128)(2,1)} %kc_ref.7, bf16[1792,512]{1,0:T(8,128)(2,1)} %vc_ref.7, ...), custom_call_target="tpu_custom_call", output_to_operand_aliasing={{0}: (9, {})} | custom-call | bytes 1024 | tf_op jit(solution)/shard_map/attention/pallas_call | solution.py:128
  (121 shorter events, 51.0 us)
Async XLA Ops:
  7.2 39.9 %all-gather.4.cloned.1.call-start = ((), (), s32[]{:S(2)}) async-start(), calls=%async_computation | async-start | bytes 5242880 | tf_op jit(solution)/shard_map/all_gather | solution.py:203
  9.7 74.0 %all-gather.6.cloned.1.call-start = ((), (), s32[]{:S(2)}) async-start(), calls=%async_computation.1 | async-start | bytes 5242880 | tf_op jit(solution)/shard_map/all_gather | solution.py:203
  11.4 15.2 %collective-permute-start.1 = (bf16[256,1024]{1,0:T(8,128)(2,1)}, bf16[256,1024]{1,0:T(8,128)(2,1)}, u32[]{:S(2)}, u32[]{:S(2)}) collective-permute-start(bf16[256,1024]{1,0:T(8,128)(2,1)} %pad_maximum_fusion.1), channel_id=1, source_target_pairs={{0,1},{1,0},{2,3},{3,2},{4,5},{5,4},{6,7},{7,6},{8,9},{9,8},{10,11... | collective-permute-start | bytes 1572872 | tf_op jit(solution)/shard_map/ppermute | solution.py:179
  26.6 93.2 %all-gather.8.cloned.1.call-start = ((), (), s32[]{:S(2)}) async-start(), calls=%async_computation.2 | async-start | bytes 5242880 | tf_op jit(solution)/shard_map/all_gather | solution.py:203
  28.7 14.3 %collective-permute-start.3 = (bf16[256,1024]{1,0:T(8,128)(2,1)S(1)}, bf16[256,1024]{1,0:T(8,128)(2,1)S(1)}, u32[]{:S(2)}, u32[]{:S(2)}) collective-permute-start(bf16[256,1024]{1,0:T(8,128)(2,1)S(1)} %get-tuple-element.75), channel_id=1, source_target_pairs={{0,8},{2,10},{4,12},{6,14},{8,0},{10,2},{12,4},{14,6},{16,24},{18,... | collective-permute-start | bytes 1572872 | tf_op jit(solution)/shard_map/ppermute | solution.py:173
  30.6 24.6 %collective-permute-start.2 = (bf16[256,1024]{1,0:T(8,128)(2,1)S(1)}, bf16[256,1024]{1,0:T(8,128)(2,1)S(1)}, u32[]{:S(2)}, u32[]{:S(2)}) collective-permute-start(bf16[256,1024]{1,0:T(8,128)(2,1)S(1)} %get-tuple-element.74), channel_id=1, source_target_pairs={{0,24},{2,26},{4,28},{6,30},{8,16},{10,18},{12,20},{14,22},{16,8},... | collective-permute-start | bytes 1572872 | tf_op jit(solution)/shard_map/ppermute | solution.py:173
  33.0 22.1 %collective-permute-start = (bf16[256,1024]{1,0:T(8,128)(2,1)S(1)}, bf16[256,1024]{1,0:T(8,128)(2,1)S(1)}, u32[]{:S(2)}, u32[]{:S(2)}) collective-permute-start(bf16[256,1024]{1,0:T(8,128)(2,1)S(1)} %pad_maximum_fusion.3), channel_id=1, source_target_pairs={{0,1},{1,0},{2,3},{3,2},{4,5},{5,4},{6,7},{7,6},{8,9},{9,8},{10,11... | collective-permute-start | bytes 1572872 | tf_op jit(solution)/shard_map/ppermute | solution.py:179
  42.9 17.8 %copy-start.15 = (bf16[256,1024]{1,0:T(8,128)(2,1)}, bf16[256,1024]{1,0:T(8,128)(2,1)S(1)}, u32[]{:S(2)}) copy-start(bf16[256,1024]{1,0:T(8,128)(2,1)S(1)} %collective-permute-done.3) | copy-start | bytes 1572868
  42.9 17.8 %collective-permute-start.5 = (bf16[256,1024]{1,0:T(8,128)(2,1)S(1)}, bf16[256,1024]{1,0:T(8,128)(2,1)}, u32[]{:S(2)}, u32[]{:S(2)}) collective-permute-start(bf16[256,1024]{1,0:T(8,128)(2,1)S(1)} %collective-permute-done.3), channel_id=1, source_target_pairs={{0,1},{1,0},{2,3},{3,2},{4,5},{5,4},{6,7},{7,6},{8,9},{9,8},{10,11... | collective-permute-start | bytes 1572872 | tf_op jit(solution)/shard_map/ppermute | solution.py:179
  57.5 22.8 %collective-permute-start.7 = (bf16[256,1024]{1,0:T(8,128)(2,1)S(1)}, bf16[256,1024]{1,0:T(8,128)(2,1)S(1)}, u32[]{:S(2)}, u32[]{:S(2)}) collective-permute-start(bf16[256,1024]{1,0:T(8,128)(2,1)S(1)} %get-tuple-element.80), channel_id=1, source_target_pairs={{0,16},{2,18},{4,20},{6,22},{8,24},{10,26},{12,28},{14,30},{16,0},... | collective-permute-start | bytes 1572872 | tf_op jit(solution)/shard_map/ppermute | solution.py:173
  59.3 10.1 %collective-permute-start.4 = (bf16[256,1024]{1,0:T(8,128)(2,1)S(1)}, bf16[256,1024]{1,0:T(8,128)(2,1)S(1)}, u32[]{:S(2)}, u32[]{:S(2)}) collective-permute-start(bf16[256,1024]{1,0:T(8,128)(2,1)S(1)} %collective-permute-done.2), channel_id=1, source_target_pairs={{0,1},{1,0},{2,3},{3,2},{4,5},{5,4},{6,7},{7,6},{8,9},{9,8},{10,11... | collective-permute-start | bytes 1572872 | tf_op jit(solution)/shard_map/ppermute | solution.py:179
  64.8 27.4 %collective-permute-start.9 = (bf16[256,1024]{1,0:T(8,128)(2,1)}, bf16[256,1024]{1,0:T(8,128)(2,1)}, u32[]{:S(2)}, u32[]{:S(2)}) collective-permute-start(bf16[256,1024]{1,0:T(8,128)(2,1)} %convolution_convert_fusion.3), channel_id=1, source_target_pairs={{0,8},{2,10},{4,12},{6,14},{8,0},{10,2},{12,4},{14,6},{16,24},{18,... | collective-permute-start | bytes 1572872 | tf_op jit(solution)/shard_map/ppermute | solution.py:173
  71.1 48.7 %copy-start.6 = (bf16[256,2048]{1,0:T(8,128)(2,1)}, bf16[256,2048]{1,0:T(8,128)(2,1)S(1)}, u32[]{:S(2)}) copy-start(bf16[256,2048]{1,0:T(8,128)(2,1)S(1)} %maximum_select_fusion.1.high_ref) | copy-start | bytes 3145732
  73.2 27.9 %collective-permute-start.10 = (bf16[256,1024]{1,0:T(8,128)(2,1)}, bf16[256,1024]{1,0:T(8,128)(2,1)}, u32[]{:S(2)}, u32[]{:S(2)}) collective-permute-start(bf16[256,1024]{1,0:T(8,128)(2,1)} %convolution_convert_fusion.2), channel_id=1, source_target_pairs={{0,8},{2,10},{4,12},{6,14},{8,0},{10,2},{12,4},{14,6},{16,24},{18,... | collective-permute-start | bytes 1572872 | tf_op jit(solution)/shard_map/ppermute | solution.py:173
  74.7 16.9 %collective-permute-start.6 = (bf16[256,1024]{1,0:T(8,128)(2,1)S(1)}, bf16[256,1024]{1,0:T(8,128)(2,1)}, u32[]{:S(2)}, u32[]{:S(2)}) collective-permute-start(bf16[256,1024]{1,0:T(8,128)(2,1)S(1)} %get-tuple-element.86), channel_id=1, source_target_pairs={{0,1},{1,0},{2,3},{3,2},{4,5},{5,4},{6,7},{7,6},{8,9},{9,8},{10,11... | collective-permute-start | bytes 1572872 | tf_op jit(solution)/shard_map/ppermute | solution.py:179
  80.2 20.8 %collective-permute-start.8 = (bf16[256,1024]{1,0:T(8,128)(2,1)S(1)}, bf16[256,1024]{1,0:T(8,128)(2,1)}, u32[]{:S(2)}, u32[]{:S(2)}) collective-permute-start(bf16[256,1024]{1,0:T(8,128)(2,1)S(1)} %collective-permute-done.7), channel_id=1, source_target_pairs={{0,1},{1,0},{2,3},{3,2},{4,5},{5,4},{6,7},{7,6},{8,9},{9,8},{10,11... | collective-permute-start | bytes 1572872 | tf_op jit(solution)/shard_map/ppermute | solution.py:179
  88.1 46.5 %collective-permute-start.13 = (bf16[256,1024]{1,0:T(8,128)(2,1)}, bf16[256,1024]{1,0:T(8,128)(2,1)}, u32[]{:S(2)}, u32[]{:S(2)}) collective-permute-start(bf16[256,1024]{1,0:T(8,128)(2,1)} %convolution_convert_fusion), channel_id=1, source_target_pairs={{0,8},{2,10},{4,12},{6,14},{8,0},{10,2},{12,4},{14,6},{16,24},{18,... | collective-permute-start | bytes 1572872 | tf_op jit(solution)/shard_map/ppermute | solution.py:173
  91.6 42.9 %collective-permute-start.14 = (bf16[256,1024]{1,0:T(8,128)(2,1)}, bf16[256,1024]{1,0:T(8,128)(2,1)}, u32[]{:S(2)}, u32[]{:S(2)}) collective-permute-start(bf16[256,1024]{1,0:T(8,128)(2,1)} %convolution_convert_fusion.1), channel_id=1, source_target_pairs={{0,8},{2,10},{4,12},{6,14},{8,0},{10,2},{12,4},{14,6},{16,24},{18,... | collective-permute-start | bytes 1572872 | tf_op jit(solution)/shard_map/ppermute | solution.py:173
  106.2 35.2 %collective-permute-start.12 = (bf16[256,1024]{1,0:T(8,128)(2,1)}, bf16[256,1024]{1,0:T(8,128)(2,1)S(1)}, u32[]{:S(2)}, u32[]{:S(2)}) collective-permute-start(bf16[256,1024]{1,0:T(8,128)(2,1)} %add_convert_fusion.1), channel_id=1, source_target_pairs={{0,16},{2,18},{4,20},{6,22},{8,24},{10,26},{12,28},{14,30},{16,0},... | collective-permute-start | bytes 1572872 | tf_op jit(solution)/shard_map/ppermute | solution.py:173
  123.7 23.9 %collective-permute-start.11 = (bf16[256,1024]{1,0:T(8,128)(2,1)S(1)}, bf16[256,1024]{1,0:T(8,128)(2,1)S(1)}, u32[]{:S(2)}, u32[]{:S(2)}) collective-permute-start(bf16[256,1024]{1,0:T(8,128)(2,1)S(1)} %half_product.4), channel_id=1, source_target_pairs={{0,8},{2,10},{4,12},{6,14},{8,0},{10,2},{12,4},{14,6},{16,24},{18,... | collective-permute-start | bytes 1572872 | tf_op jit(solution)/shard_map/ppermute | solution.py:173
  138.8 21.1 %collective-permute-start.16 = (bf16[256,1024]{1,0:T(8,128)(2,1)S(1)}, bf16[256,1024]{1,0:T(8,128)(2,1)S(1)}, u32[]{:S(2)}, u32[]{:S(2)}) collective-permute-start(bf16[256,1024]{1,0:T(8,128)(2,1)S(1)} %add_convert_fusion), channel_id=1, source_target_pairs={{0,16},{2,18},{4,20},{6,22},{8,24},{10,26},{12,28},{14,30},{16,0},... | collective-permute-start | bytes 1572872 | tf_op jit(solution)/shard_map/ppermute | solution.py:173
  141.4 34.5 %copy-start = (f32[256,1024]{1,0:T(8,128)}, f32[256,1024]{1,0:T(8,128)S(1)}, u32[]{:S(2)}) copy-start(f32[256,1024]{1,0:T(8,128)S(1)} %convolution_add_fusion.1.km_ref.vm_ref) | copy-start | bytes 3145732
  141.4 34.5 %copy-start.3 = (bf16[256,1024]{1,0:T(8,128)(2,1)}, bf16[256,1024]{1,0:T(8,128)(2,1)S(1)}, u32[]{:S(2)}) copy-start(bf16[256,1024]{1,0:T(8,128)(2,1)S(1)} %collective-permute-done.12.kt_ref.vt_ref) | copy-start | bytes 1572868
  151.2 22.2 %collective-permute-start.15 = (bf16[256,1024]{1,0:T(8,128)(2,1)S(1)}, bf16[256,1024]{1,0:T(8,128)(2,1)S(1)}, u32[]{:S(2)}, u32[]{:S(2)}) collective-permute-start(bf16[256,1024]{1,0:T(8,128)(2,1)S(1)} %half_product.6), channel_id=1, source_target_pairs={{0,8},{2,10},{4,12},{6,14},{8,0},{10,2},{12,4},{14,6},{16,24},{18,... | collective-permute-start | bytes 1572872 | tf_op jit(solution)/shard_map/ppermute | solution.py:173
  151.3 24.5 %collective-permute-start.18 = (bf16[128,1024]{1,0:T(8,128)(2,1)S(1)}, bf16[128,1024]{1,0:T(8,128)(2,1)S(1)}, u32[]{:S(2)}, u32[]{:S(2)}) collective-permute-start(bf16[128,1024]{1,0:T(8,128)(2,1)S(1)} %get-tuple-element.109), channel_id=1, source_target_pairs={{0,16},{2,18},{4,20},{6,22},{8,24},{10,26},{12,28},{14,30},{16,0},... | collective-permute-start | bytes 786440 | tf_op jit(solution)/shard_map/ppermute | solution.py:173
  175.8 17.4 %collective-permute-start.17 = (bf16[128,1024]{1,0:T(8,128)(2,1)}, bf16[128,1024]{1,0:T(8,128)(2,1)S(1)}, u32[]{:S(2)}, u32[]{:S(2)}) collective-permute-start(bf16[128,1024]{1,0:T(8,128)(2,1)} %get-tuple-element.123), channel_id=1, source_target_pairs={{0,16},{2,18},{4,20},{6,22},{8,24},{10,26},{12,28},{14,30},{16,0},... | collective-permute-start | bytes 786440 | tf_op jit(solution)/shard_map/ppermute | solution.py:173
  181.6 3.1 %collective-permute-start.21 = (bf16[1,2048]{1,0:T(2,128)(2,1)S(1)}, bf16[1,2048]{1,0:T(2,128)(2,1)S(1)}, u32[]{:S(2)}, u32[]{:S(2)}) collective-permute-start(bf16[1,2048]{1,0:T(2,128)(2,1)S(1)} %pad_maximum_fusion.6.refs_0_), channel_id=1, source_target_pairs={{0,6},{2,4},{4,2},{6,0},{8,14},{10,12},{12,10},{14,8},{16,22},{18,... | collective-permute-start | bytes 12296 | tf_op jit(solution)/shard_map/ppermute | solution.py:173
  182.3 3.7 %collective-permute-start.20 = (bf16[1,2048]{1,0:T(2,128)(2,1)S(1)}, bf16[1,2048]{1,0:T(2,128)(2,1)S(1)}, u32[]{:S(2)}, u32[]{:S(2)}) collective-permute-start(bf16[1,2048]{1,0:T(2,128)(2,1)S(1)} %pad_maximum_fusion.6.refs_0_), channel_id=1, source_target_pairs={{0,4},{2,6},{4,0},{6,2},{8,12},{10,14},{12,8},{14,10},{16,20},{18,... | collective-permute-start | bytes 12296 | tf_op jit(solution)/shard_map/ppermute | solution.py:173
  183.3 2.7 %collective-permute-start.19 = (bf16[1,2048]{1,0:T(2,128)(2,1)S(1)}, bf16[1,2048]{1,0:T(2,128)(2,1)S(1)}, u32[]{:S(2)}, u32[]{:S(2)}) collective-permute-start(bf16[1,2048]{1,0:T(2,128)(2,1)S(1)} %pad_maximum_fusion.6.refs_0_), channel_id=1, source_target_pairs={{0,2},{2,0},{4,6},{6,4},{8,10},{10,8},{12,14},{14,12},{16,18},{18,... | collective-permute-start | bytes 12296 | tf_op jit(solution)/shard_map/ppermute | solution.py:173
  188.0 12.4 %collective-permute-start.24 = (bf16[4,1,2048]{2,1,0:T(2,128)(2,1)}, bf16[4,1,2048]{2,1,0:T(2,128)(2,1)S(1)}, u32[]{:S(2)}, u32[]{:S(2)}) collective-permute-start(bf16[4,1,2048]{2,1,0:T(2,128)(2,1)} %order.1), channel_id=1, source_target_pairs={{0,24},{2,26},{4,28},{6,30},{8,16},{10,18},{12,20},{14,22},{16,8},... | collective-permute-start | bytes 49160 | tf_op jit(solution)/shard_map/ppermute | solution.py:173
  190.1 10.2 %collective-permute-start.23 = (bf16[4,1,2048]{2,1,0:T(2,128)(2,1)}, bf16[4,1,2048]{2,1,0:T(2,128)(2,1)S(1)}, u32[]{:S(2)}, u32[]{:S(2)}) collective-permute-start(bf16[4,1,2048]{2,1,0:T(2,128)(2,1)} %order.1), channel_id=1, source_target_pairs={{0,16},{2,18},{4,20},{6,22},{8,24},{10,26},{12,28},{14,30},{16,0},... | collective-permute-start | bytes 49160 | tf_op jit(solution)/shard_map/ppermute | solution.py:173
  191.9 8.5 %collective-permute-start.22 = (bf16[4,1,2048]{2,1,0:T(2,128)(2,1)}, bf16[4,1,2048]{2,1,0:T(2,128)(2,1)S(1)}, u32[]{:S(2)}, u32[]{:S(2)}) collective-permute-start(bf16[4,1,2048]{2,1,0:T(2,128)(2,1)} %order.1), channel_id=1, source_target_pairs={{0,8},{2,10},{4,12},{6,14},{8,0},{10,2},{12,4},{14,6},{16,24},{18,... | collective-permute-start | bytes 49160 | tf_op jit(solution)/shard_map/ppermute | solution.py:173
  (23 other events, 135.6 us)
Sparse Core Ops, SparseCore 0:
  9.8 37.1 all-gather.3
  49.2 34.4 all-gather.5
  85.2 34.4 all-gather.7

commit v15 on v14

--- a/solution.py
+++ b/solution.py
@@ -213,6 +213,7 @@
             weights[piece] = group_gather(value)
 
     tokens = {}
+    between = []
     if fast:
 
         def cut(source, j, p):
@@ -242,13 +243,16 @@
             came[b] = over_tp(held[b])
 
         tp_exchange(1)
+        swap[0] = step(swap[0])
         weights["kv"] = step(weights["kv"])
         tp_exchange(3)
-        swap[0] = step(swap[0])
-        own = cut(source, 0, x)
-        send = {b: jnp.where(mine == (b < 2), own, swap[0]) for b in (2, 0)}
-        send[2] = step(send[2])
-        got[2], got[0] = over_outer(send[2], 2), send[0]
+
+        def even_sends():
+            own = cut(source, 0, x)
+            got[2] = over_outer(step(jnp.where(mine, step(swap[0]), own)), 2)
+            got[0] = jnp.where(mine, own, swap[0])
+
+        between.append(even_sends)
 
         def arrived(b):
             if b not in tokens:
@@ -293,6 +297,8 @@
             for b in bits:
                 arrived(b)
                 come[b] = over_outer(step(times(tokens[b], weight).astype(jnp.bfloat16)), 1)
+                if between:
+                    between.pop()()
             return come
         if fast:
             send = half_product(tokens[1][0], tokens[3][0], h, weight)

time: 208 us -> 208 us (level)
  starting transfers between devices: 34.1 us -> 44.5 us
  waiting for transfers between devices: 82.9 us -> 76.3 us
  other arithmetic: 13.2 us -> 8.16 us
  matrix products: 21.4 us -> 24.3 us
    ppermute x19, starting transfers between devices: 23.6 us -> 35 us  [over_inst(): return lax.ppermute(value, 'inst', [(i, i ^ bits) for i in range(n_inst)])]
    select_n x4, other arithmetic: 6.9 us -> 3.1 us  [swapped_if(): jnp.where(flag, jnp.concatenate([b, a], axis=axis), jnp.concatenate([a, b...]
    ppermute x6, waiting for transfers between devices: 12.9 us -> 9.16 us  [over_tp(): return lax.ppermute(value, 'tp', [(0, 1), (1, 0)])]
    dot_general x8, matrix products: 21.4 us -> 24.3 us  [dot(): return jnp.dot(a, b, preferred_element_type=jnp.float32)]
    ppermute x19, waiting for transfers between devices: 53.2 us -> 50.5 us  [over_inst(): return lax.ppermute(value, 'inst', [(i, i ^ bits) for i in range(n_inst)])]
    unnamed x58 -> x56, local copies, waits for them, and re-layouts: 6.64 us -> 4.51 us
  transfers between devices with their start and end apart: 28 -> 28, of which waited for: 15 -> 13; matrix products, arithmetic and copies ran while one was open for 17% -> 16% of each run, Pallas kernels for 15% -> 15%
where the time goes in v15:
time: 208 us
  waiting for transfers between devices  76.3 us (37%)
  starting transfers between devices  44.5 us (21%)
  Pallas kernels  32.2 us (15%)
  matrix products  24.3 us (12%)
  between operations  14.9 us (7%)
  other arithmetic  8.16 us (4%)
  local copies, waits for them, and re-layouts  7.54 us (4%)
    ppermute x19, waiting for transfers between devices, over_inst(): return lax.ppermute(value, 'inst', [(i, i ^ bits) for i in range(n_inst)])  50.5 us
    ppermute x19, starting transfers between devices, over_inst(): return lax.ppermute(value, 'inst', [(i, i ^ bits) for i in range(n_inst)])  35 us
    dot_general x8, matrix products, dot(): return jnp.dot(a, b, preferred_element_type=jnp.float32)  24.3 us
    pallas_call x4, Pallas kernels, attend(): pl.pallas_call(attention_kernel, grid_spec=pltpu.PrefetchScalarGridSpec(n...  23.1 us
    all_gather x3, waiting for transfers between devices, group_gather(): lax.all_gather(value, 'inst', axis=0, tiled=True, axis_index_groups=groups)  16 us
    ppermute x6, starting transfers between devices, over_tp(): return lax.ppermute(value, 'tp', [(0, 1), (1, 0)])  9.4 us
    ppermute x6, waiting for transfers between devices, over_tp(): return lax.ppermute(value, 'tp', [(0, 1), (1, 0)])  9.16 us
    pallas_call x4, Pallas kernels, half_product(): pl.pallas_call(first_kernel if first else later_kernel, grid=(columns //...  7.75 us
  transfers between devices with their start and end apart: 28, of which 13 were waited for; matrix products, arithmetic and copies ran while one was open for 16% of the time, Pallas kernels for 15%

profile of v15, /device:TPU:0, one launch (start us, length us, event | category | flops | bytes accessed | tf_op | source)
XLA Modules:
  0.0 207.9 jit_solution(10458552931582290080)
XLA Ops:
  7.2 2.4 %pad_maximum_fusion = bf16[512,1024]{1,0:T(8,128)(2,1)} fusion(bf16[512,512]{1,0:T(8,128)(2,1)} %param.10, bf16[512,512]{1,0:T(8,128)(2,1)} %param.9), kind=kLoop, calls=%fused_computation.6 | loop fusion | flops 2097152 | bytes 2097152 | tf_op jit(solution)/shard_map/concatenate | solution.py:207
  11.4 2.9 %collective-permute-start.1 = (bf16[256,1024]{1,0:T(8,128)(2,1)}, bf16[256,1024]{1,0:T(8,128)(2,1)}, u32[]{:S(2)}, u32[]{:S(2)}) collective-permute-start(bf16[256,1024]{1,0:T(8,128)(2,1)} %pad_maximum_fusion.1), channel_id=1, source_target_pairs={{0,1},{1,0},{2,3},{3,2},{4,5},{5,4},{6,7},{7,6},{8,9},{9,8},{10,11... | collective-permute-start | bytes 1572872 | tf_op jit(solution)/shard_map/ppermute | solution.py:179
  17.5 9.1 %collective-permute-done.1 = bf16[256,1024]{1,0:T(8,128)(2,1)} collective-permute-done((bf16[256,1024]{1,0:T(8,128)(2,1)}, bf16[256,1024]{1,0:T(8,128)(2,1)}, u32[]{:S(2)}, u32[]{:S(2)}) %collective-permute-start.1) | collective-permute-done | bytes 524320 | tf_op jit(solution)/shard_map/ppermute | solution.py:179
  32.0 2.5 %collective-permute-start.3 = (bf16[256,1024]{1,0:T(8,128)(2,1)S(1)}, bf16[256,1024]{1,0:T(8,128)(2,1)S(1)}, u32[]{:S(2)}, u32[]{:S(2)}) collective-permute-start(bf16[256,1024]{1,0:T(8,128)(2,1)S(1)} %get-tuple-element.78), channel_id=1, source_target_pairs={{0,24},{2,26},{4,28},{6,30},{8,16},{10,18},{12,20},{14,22},{16,8},... | collective-permute-start | bytes 1572872 | tf_op jit(solution)/shard_map/ppermute | solution.py:173
  34.5 8.4 %collective-permute-done.2 = bf16[256,1024]{1,0:T(8,128)(2,1)S(1)} collective-permute-done((bf16[256,1024]{1,0:T(8,128)(2,1)S(1)}, bf16[256,1024]{1,0:T(8,128)(2,1)S(1)}, u32[]{:S(2)}, u32[]{:S(2)}) %collective-permute-start.2) | collective-permute-done | bytes 524320 | tf_op jit(solution)/shard_map/ppermute | solution.py:173
  44.4 2.6 %all-gather.4.cloned.1.call-done = bf16[2048,1024]{1,0:T(8,128)(2,1)} async-done(((bf16[512,1024]{1,0:T(8,128)(2,1)}), bf16[2048,1024]{1,0:T(8,128)(2,1)}) %all-gather.4.cloned.1.call-update) | async-done | bytes 4194320 | tf_op jit(solution)/shard_map/all_gather | solution.py:203
  47.0 8.1 %collective-permute-done.3 = bf16[256,1024]{1,0:T(8,128)(2,1)S(1)} collective-permute-done((bf16[256,1024]{1,0:T(8,128)(2,1)S(1)}, bf16[256,1024]{1,0:T(8,128)(2,1)S(1)}, u32[]{:S(2)}, u32[]{:S(2)}) %collective-permute-start.3) | collective-permute-done | bytes 524320 | tf_op jit(solution)/shard_map/ppermute | solution.py:173
  57.0 4.9 %convolution_convert_fusion.3 = bf16[256,1024]{1,0:T(8,128)(2,1)} fusion(bf16[256,2048]{1,0:T(8,128)(2,1)S(1)} %maximum_select_fusion.low_ref, bf16[2048,1024]{1,0:T(8,128)(2,1)} %all-gather.4.cloned.1.call-done), kind=kOutput, calls=%fused_computation.5 | convolution fusion | flops 1074003968 | bytes 5767168 | tf_op jit(solution)/shard_map/dot_general | solution.py:16
  61.9 2.2 %collective-permute-start.9 = (bf16[256,1024]{1,0:T(8,128)(2,1)}, bf16[256,1024]{1,0:T(8,128)(2,1)}, u32[]{:S(2)}, u32[]{:S(2)}) collective-permute-start(bf16[256,1024]{1,0:T(8,128)(2,1)} %convolution_convert_fusion.3), channel_id=1, source_target_pairs={{0,8},{2,10},{4,12},{6,14},{8,0},{10,2},{12,4},{14,6},{16,24},{18,... | collective-permute-start | bytes 1572872 | tf_op jit(solution)/shard_map/ppermute | solution.py:173
  64.3 9.5 %collective-permute-start.7 = (bf16[256,1024]{1,0:T(8,128)(2,1)S(1)}, bf16[256,1024]{1,0:T(8,128)(2,1)}, u32[]{:S(2)}, u32[]{:S(2)}) collective-permute-start(bf16[256,1024]{1,0:T(8,128)(2,1)S(1)} %get-tuple-element.85), channel_id=1, source_target_pairs={{0,16},{2,18},{4,20},{6,22},{8,24},{10,26},{12,28},{14,30},{16,0},... | collective-permute-start | bytes 1572872 | tf_op jit(solution)/shard_map/ppermute | solution.py:173
  74.3 2.1 %convolution_convert_fusion.2 = bf16[256,1024]{1,0:T(8,128)(2,1)} fusion(bf16[256,2048]{1,0:T(8,128)(2,1)S(1)} %maximum_select_fusion.1.high_ref, bf16[2048,1024]{1,0:T(8,128)(2,1)S(1)} %copy-done.21), kind=kOutput, calls=%fused_computation.4 | convolution fusion | flops 1074003968 | bytes 5767168 | tf_op jit(solution)/shard_map/dot_general | solution.py:16
  77.8 10.1 %collective-permute-done.7 = bf16[256,1024]{1,0:T(8,128)(2,1)} collective-permute-done((bf16[256,1024]{1,0:T(8,128)(2,1)S(1)}, bf16[256,1024]{1,0:T(8,128)(2,1)}, u32[]{:S(2)}, u32[]{:S(2)}) %collective-permute-start.7) | collective-permute-done | bytes 524320 | tf_op jit(solution)/shard_map/ppermute | solution.py:173
  88.4 4.4 %convolution_convert_fusion = bf16[256,1024]{1,0:T(8,128)(2,1)} fusion(bf16[256,2048]{1,0:T(8,128)(2,1)S(1)} %maximum_select_fusion.low_ref, bf16[2048,1024]{1,0:T(8,128)(2,1)} %all-gather.6.cloned.1.call-done), kind=kOutput, calls=%fused_computation.2 | convolution fusion | flops 1074003968 | bytes 5767168 | tf_op jit(solution)/shard_map/dot_general | solution.py:16
  92.8 2.4 %collective-permute-start.13 = (bf16[256,1024]{1,0:T(8,128)(2,1)}, bf16[256,1024]{1,0:T(8,128)(2,1)}, u32[]{:S(2)}, u32[]{:S(2)}) collective-permute-start(bf16[256,1024]{1,0:T(8,128)(2,1)} %convolution_convert_fusion), channel_id=1, source_target_pairs={{0,8},{2,10},{4,12},{6,14},{8,0},{10,2},{12,4},{14,6},{16,24},{18,... | collective-permute-start | bytes 1572872 | tf_op jit(solution)/shard_map/ppermute | solution.py:173
  95.2 2.1 convolution_convert_fusion.1
  99.4 3.5 %add_convert_fusion.1 = bf16[256,1024]{1,0:T(8,128)(2,1)} fusion(bf16[256,1024]{1,0:T(8,128)(2,1)} %collective-permute-done.10, bf16[256,2048]{1,0:T(8,128)(2,1)S(1)} %maximum_select_fusion.3.high_ref, bf16[2048,1024]{1,0:T(8,128)(2,1)S(1)} %copy-done.22), kind=kOutput, calls=%fused_computation.12 | convolution fusion | flops 1074528256 | bytes 6291456 | tf_op jit(solution)/shard_map/dot_general | solution.py:16
  102.9 3.4 %collective-permute-start.12 = (bf16[256,1024]{1,0:T(8,128)(2,1)}, bf16[256,1024]{1,0:T(8,128)(2,1)S(1)}, u32[]{:S(2)}, u32[]{:S(2)}) collective-permute-start(bf16[256,1024]{1,0:T(8,128)(2,1)} %add_convert_fusion.1), channel_id=1, source_target_pairs={{0,16},{2,18},{4,20},{6,22},{8,24},{10,26},{12,28},{14,30},{16,0},... | collective-permute-start | bytes 1572872 | tf_op jit(solution)/shard_map/ppermute | solution.py:173
  106.4 13.4 %all-gather.8.cloned.1.call-done.w_ref = bf16[2048,1024]{1,0:T(8,128)(2,1)} async-done(((bf16[512,1024]{1,0:T(8,128)(2,1)}), bf16[2048,1024]{1,0:T(8,128)(2,1)}) %all-gather.8.cloned.1.call-update) | async-done | bytes 4194320 | tf_op jit(solution)/shard_map/all_gather | solution.py:203
  119.8 2.2 %copy-done.1 = bf16[2048,1024]{1,0:T(8,128)(2,1)S(1)} copy-done((bf16[2048,1024]{1,0:T(8,128)(2,1)S(1)}, bf16[2048,1024]{1,0:T(8,128)(2,1)}, u32[]{:S(2)}) %copy-start.1) | copy-done | bytes 4194328
  125.3 5.6 %collective-permute-done.14 = bf16[256,1024]{1,0:T(8,128)(2,1)} collective-permute-done((bf16[256,1024]{1,0:T(8,128)(2,1)}, bf16[256,1024]{1,0:T(8,128)(2,1)}, u32[]{:S(2)}, u32[]{:S(2)}) %collective-permute-start.14) | collective-permute-done | bytes 524320 | tf_op jit(solution)/shard_map/ppermute | solution.py:173
  130.9 2.5 %add_convert_fusion = bf16[256,1024]{1,0:T(8,128)(2,1)S(1)} fusion(bf16[256,1024]{1,0:T(8,128)(2,1)} %collective-permute-done.14, bf16[256,2048]{1,0:T(8,128)(2,1)S(1)} %copy-done.9, bf16[2048,1024]{1,0:T(8,128)(2,1)S(1)} %copy-done.25), kind=kOutput, calls=%fused_computation.11 | convolution fusion | flops 1074528256 | bytes 6291456 | tf_op jit(solution)/shard_map/dot_general | solution.py:16
  133.9 2.5 %convolution_add_fusion.1.km_ref.vm_ref = f32[256,1024]{1,0:T(8,128)S(1)} fusion(bf16[256,2048]{1,0:T(8,128)(2,1)S(1)} %maximum_select_fusion.2.low_ref, bf16[2048,1024]{1,0:T(8,128)(2,1)S(1)} %copy-done.23, bf16[256,1024]{1,0:T(8,128)(2,1)} %collective-permute-done.9), kind=kOutput, calls=%fused_computation.1 | convolution fusion | flops 1074266112 | bytes 6815744 | tf_op jit(solution)/shard_map/dot_general | solution.py:16
  136.4 9.4 %collective-permute-done.11.came_ref = bf16[256,1024]{1,0:T(8,128)(2,1)S(1)} collective-permute-done((bf16[256,1024]{1,0:T(8,128)(2,1)S(1)}, bf16[256,1024]{1,0:T(8,128)(2,1)S(1)}, u32[]{:S(2)}, u32[]{:S(2)}) %collective-permute-start.11) | collective-permute-done | bytes 524320 | tf_op jit(solution)/shard_map/ppermute | solution.py:173
  149.6 5.1 %collective-permute-start.18 = (bf16[128,1024]{1,0:T(8,128)(2,1)S(1)}, bf16[128,1024]{1,0:T(8,128)(2,1)S(1)}, u32[]{:S(2)}, u32[]{:S(2)}) collective-permute-start(bf16[128,1024]{1,0:T(8,128)(2,1)S(1)} %get-tuple-element.111), channel_id=1, source_target_pairs={{0,16},{2,18},{4,20},{6,22},{8,24},{10,26},{12,28},{14,30},{16,0},... | collective-permute-start | bytes 786440 | tf_op jit(solution)/shard_map/ppermute | solution.py:173
  154.7 2.3 %convolution_add_fusion.qm_ref = f32[256,1024]{1,0:T(8,128)S(1)} fusion(bf16[256,2048]{1,0:T(8,128)(2,1)S(1)} %maximum_select_fusion.2.low_ref, bf16[2048,1024]{1,0:T(8,128)(2,1)S(1)} %copy-done.25, bf16[256,1024]{1,0:T(8,128)(2,1)} %collective-permute-done.13), kind=kOutput, calls=%fused_computation | convolution fusion | flops 1074266112 | bytes 6815744 | tf_op jit(solution)/shard_map/dot_general | solution.py:16
  157.0 3.6 %collective-permute-done.16.qc_ref = bf16[256,1024]{1,0:T(8,128)(2,1)S(1)} collective-permute-done((bf16[256,1024]{1,0:T(8,128)(2,1)S(1)}, bf16[256,1024]{1,0:T(8,128)(2,1)S(1)}, u32[]{:S(2)}, u32[]{:S(2)}) %collective-permute-start.16) | collective-permute-done | bytes 524320 | tf_op jit(solution)/shard_map/ppermute | solution.py:173
  160.6 5.4 %attention.4 = (bf16[256,2048]{1,0:T(8,128)(2,1)}, bf16[1,1024]{1,0:T(2,128)(2,1)S(1)}) custom-call(s32[3]{0:T(128)S(1)} %get-tuple-element.157.place_ref, f32[256,1024]{1,0:T(8,128)S(1)} %convolution_add_fusion.qm_ref, bf16[256,1024]{1,0:T(8,128)(2,1)S(1)} %collective-permute-done.16.qc_ref, bf16[1792,512]{1,0:T(8,128)(2,1)S(1)} %copy-done.4, ...), custom_call_target="tpu_custom_call" | custom-call | bytes 1024 | tf_op jit(solution)/shard_map/attention/pallas_call | solution.py:128
  166.1 5.4 %attention.5 = (bf16[256,2048]{1,0:T(8,128)(2,1)}, bf16[1,1024]{1,0:T(2,128)(2,1)S(1)}) custom-call(s32[3]{0:T(128)S(1)} %get-tuple-element.156.place_ref, f32[256,1024]{1,0:T(8,128)S(1)} %convolution_add_fusion.qm_ref, bf16[256,1024]{1,0:T(8,128)(2,1)S(1)} %collective-permute-done.16.qc_ref, ...), custom_call_target="tpu_custom_call", output_to_operand_aliasing={{0}: (9, {})} | custom-call | bytes 1024 | tf_op jit(solution)/shard_map/attention/pallas_call | solution.py:128
  171.5 2.7 %collective-permute-done.15.came_ref = bf16[256,1024]{1,0:T(8,128)(2,1)S(1)} collective-permute-done((bf16[256,1024]{1,0:T(8,128)(2,1)S(1)}, bf16[256,1024]{1,0:T(8,128)(2,1)S(1)}, u32[]{:S(2)}, u32[]{:S(2)}) %collective-permute-start.15) | collective-permute-done | bytes 524320 | tf_op jit(solution)/shard_map/ppermute | solution.py:173
  174.2 2.4 %half_product.7 = (bf16[128,1024]{1,0:T(8,128)(2,1)}, f32[128,1024]{1,0:T(8,128)S(1)}) custom-call(bf16[256,2048]{1,0:T(8,128)(2,1)S(1)} %maximum_select_fusion.2.low_ref, bf16[256,2048]{1,0:T(8,128)(2,1)S(1)} %copy-done.9, bf16[2048,1024]{1,0:T(8,128)(2,1)S(1)} %copy-done.2, bf16[256,1024]{1,0:T(8,128)(2,1)S(1)} %collective-permute-done.15.came_ref), custom_call_target="tpu_custom_call" | custom-call | bytes 1024 | tf_op jit(solution)/shard_map/half_product/pallas_call | solution.py:42
  176.7 5.7 %attention.6 = (bf16[256,2048]{1,0:T(8,128)(2,1)}, bf16[1,1024]{1,0:T(2,128)(2,1)S(1)}) custom-call(s32[3]{0:T(128)S(1)} %get-tuple-element.157.place_ref, f32[128,1024]{1,0:T(8,128)S(1)} %get-tuple-element.128.qm_ref, bf16[128,1024]{1,0:T(8,128)(2,1)S(1)} %collective-permute-done.18.qc_ref, ...), custom_call_target="tpu_custom_call", output_to_operand_aliasing={{0}: (9, {})} | custom-call | bytes 1024 | tf_op jit(solution)/shard_map/attention/pallas_call | solution.py:128
  194.0 6.5 %attention.7 = (bf16[256,2048]{1,0:T(8,128)(2,1)}, bf16[1,1024]{1,0:T(2,128)(2,1)}) custom-call(s32[3]{0:T(128)} %copy-done.11, f32[128,1024]{1,0:T(8,128)} %copy-done.10, bf16[128,1024]{1,0:T(8,128)(2,1)} %collective-permute-done.17.qc_ref, bf16[1792,512]{1,0:T(8,128)(2,1)} %kc_ref.7, bf16[1792,512]{1,0:T(8,128)(2,1)} %vc_ref.7, ...), custom_call_target="tpu_custom_call", output_to_operand_aliasing={{0}: (9, {})} | custom-call | bytes 1024 | tf_op jit(solution)/shard_map/attention/pallas_call | solution.py:128
  (119 shorter events, 37.6 us)
Async XLA Ops:
  7.2 39.9 %all-gather.4.cloned.1.call-start = ((), (), s32[]{:S(2)}) async-start(), calls=%async_computation | async-start | bytes 5242880 | tf_op jit(solution)/shard_map/all_gather | solution.py:203
  9.7 78.7 %all-gather.6.cloned.1.call-start = ((), (), s32[]{:S(2)}) async-start(), calls=%async_computation.1 | async-start | bytes 5242880 | tf_op jit(solution)/shard_map/all_gather | solution.py:203
  11.4 15.2 %collective-permute-start.1 = (bf16[256,1024]{1,0:T(8,128)(2,1)}, bf16[256,1024]{1,0:T(8,128)(2,1)}, u32[]{:S(2)}, u32[]{:S(2)}) collective-permute-start(bf16[256,1024]{1,0:T(8,128)(2,1)} %pad_maximum_fusion.1), channel_id=1, source_target_pairs={{0,1},{1,0},{2,3},{3,2},{4,5},{5,4},{6,7},{7,6},{8,9},{9,8},{10,11... | collective-permute-start | bytes 1572872 | tf_op jit(solution)/shard_map/ppermute | solution.py:179
  26.6 93.2 %all-gather.8.cloned.1.call-start = ((), (), s32[]{:S(2)}) async-start(), calls=%async_computation.2 | async-start | bytes 5242880 | tf_op jit(solution)/shard_map/all_gather | solution.py:203
  28.7 14.3 %collective-permute-start.2 = (bf16[256,1024]{1,0:T(8,128)(2,1)S(1)}, bf16[256,1024]{1,0:T(8,128)(2,1)S(1)}, u32[]{:S(2)}, u32[]{:S(2)}) collective-permute-start(bf16[256,1024]{1,0:T(8,128)(2,1)S(1)} %get-tuple-element.75), channel_id=1, source_target_pairs={{0,8},{2,10},{4,12},{6,14},{8,0},{10,2},{12,4},{14,6},{16,24},{18,... | collective-permute-start | bytes 1572872 | tf_op jit(solution)/shard_map/ppermute | solution.py:173
  30.6 13.9 %collective-permute-start = (bf16[256,1024]{1,0:T(8,128)(2,1)S(1)}, bf16[256,1024]{1,0:T(8,128)(2,1)S(1)}, u32[]{:S(2)}, u32[]{:S(2)}) collective-permute-start(bf16[256,1024]{1,0:T(8,128)(2,1)S(1)} %pad_maximum_fusion.3), channel_id=1, source_target_pairs={{0,1},{1,0},{2,3},{3,2},{4,5},{5,4},{6,7},{7,6},{8,9},{9,8},{10,11... | collective-permute-start | bytes 1572872 | tf_op jit(solution)/shard_map/ppermute | solution.py:179
  32.0 23.1 %collective-permute-start.3 = (bf16[256,1024]{1,0:T(8,128)(2,1)S(1)}, bf16[256,1024]{1,0:T(8,128)(2,1)S(1)}, u32[]{:S(2)}, u32[]{:S(2)}) collective-permute-start(bf16[256,1024]{1,0:T(8,128)(2,1)S(1)} %get-tuple-element.78), channel_id=1, source_target_pairs={{0,24},{2,26},{4,28},{6,30},{8,16},{10,18},{12,20},{14,22},{16,8},... | collective-permute-start | bytes 1572872 | tf_op jit(solution)/shard_map/ppermute | solution.py:173
  42.9 13.7 %collective-permute-start.5 = (bf16[256,1024]{1,0:T(8,128)(2,1)S(1)}, bf16[256,1024]{1,0:T(8,128)(2,1)S(1)}, u32[]{:S(2)}, u32[]{:S(2)}) collective-permute-start(bf16[256,1024]{1,0:T(8,128)(2,1)S(1)} %collective-permute-done.2), channel_id=1, source_target_pairs={{0,1},{1,0},{2,3},{3,2},{4,5},{5,4},{6,7},{7,6},{8,9},{9,8},{10,11... | collective-permute-start | bytes 1572872 | tf_op jit(solution)/shard_map/ppermute | solution.py:179
  55.1 18.7 %collective-permute-start.4 = (bf16[256,1024]{1,0:T(8,128)(2,1)S(1)}, bf16[256,1024]{1,0:T(8,128)(2,1)S(1)}, u32[]{:S(2)}, u32[]{:S(2)}) collective-permute-start(bf16[256,1024]{1,0:T(8,128)(2,1)S(1)} %collective-permute-done.3), channel_id=1, source_target_pairs={{0,1},{1,0},{2,3},{3,2},{4,5},{5,4},{6,7},{7,6},{8,9},{9,8},{10,11... | collective-permute-start | bytes 1572872 | tf_op jit(solution)/shard_map/ppermute | solution.py:179
  61.9 35.4 %collective-permute-start.9 = (bf16[256,1024]{1,0:T(8,128)(2,1)}, bf16[256,1024]{1,0:T(8,128)(2,1)}, u32[]{:S(2)}, u32[]{:S(2)}) collective-permute-start(bf16[256,1024]{1,0:T(8,128)(2,1)} %convolution_convert_fusion.3), channel_id=1, source_target_pairs={{0,8},{2,10},{4,12},{6,14},{8,0},{10,2},{12,4},{14,6},{16,24},{18,... | collective-permute-start | bytes 1572872 | tf_op jit(solution)/shard_map/ppermute | solution.py:173
  64.3 23.6 %collective-permute-start.7 = (bf16[256,1024]{1,0:T(8,128)(2,1)S(1)}, bf16[256,1024]{1,0:T(8,128)(2,1)}, u32[]{:S(2)}, u32[]{:S(2)}) collective-permute-start(bf16[256,1024]{1,0:T(8,128)(2,1)S(1)} %get-tuple-element.85), channel_id=1, source_target_pairs={{0,16},{2,18},{4,20},{6,22},{8,24},{10,26},{12,28},{14,30},{16,0},... | collective-permute-start | bytes 1572872 | tf_op jit(solution)/shard_map/ppermute | solution.py:173
  74.2 45.5 %copy-start.6 = (bf16[256,2048]{1,0:T(8,128)(2,1)}, bf16[256,2048]{1,0:T(8,128)(2,1)S(1)}, u32[]{:S(2)}) copy-start(bf16[256,2048]{1,0:T(8,128)(2,1)S(1)} %maximum_select_fusion.1.high_ref) | copy-start | bytes 3145732
  76.3 21.0 %collective-permute-start.10 = (bf16[256,1024]{1,0:T(8,128)(2,1)}, bf16[256,1024]{1,0:T(8,128)(2,1)}, u32[]{:S(2)}, u32[]{:S(2)}) collective-permute-start(bf16[256,1024]{1,0:T(8,128)(2,1)} %convolution_convert_fusion.2), channel_id=1, source_target_pairs={{0,8},{2,10},{4,12},{6,14},{8,0},{10,2},{12,4},{14,6},{16,24},{18,... | collective-permute-start | bytes 1572872 | tf_op jit(solution)/shard_map/ppermute | solution.py:173
  76.4 20.9 %collective-permute-start.6 = (bf16[256,1024]{1,0:T(8,128)(2,1)S(1)}, bf16[256,1024]{1,0:T(8,128)(2,1)S(1)}, u32[]{:S(2)}, u32[]{:S(2)}) collective-permute-start(bf16[256,1024]{1,0:T(8,128)(2,1)S(1)} %get-tuple-element.88), channel_id=1, source_target_pairs={{0,1},{1,0},{2,3},{3,2},{4,5},{5,4},{6,7},{7,6},{8,9},{9,8},{10,11... | collective-permute-start | bytes 1572872 | tf_op jit(solution)/shard_map/ppermute | solution.py:179
  87.9 9.5 %collective-permute-start.8 = (bf16[256,1024]{1,0:T(8,128)(2,1)}, bf16[256,1024]{1,0:T(8,128)(2,1)}, u32[]{:S(2)}, u32[]{:S(2)}) collective-permute-start(bf16[256,1024]{1,0:T(8,128)(2,1)} %collective-permute-done.7), channel_id=1, source_target_pairs={{0,1},{1,0},{2,3},{3,2},{4,5},{5,4},{6,7},{7,6},{8,9},{9,8},{10,11... | collective-permute-start | bytes 1572872 | tf_op jit(solution)/shard_map/ppermute | solution.py:179
  92.8 38.0 %collective-permute-start.13 = (bf16[256,1024]{1,0:T(8,128)(2,1)}, bf16[256,1024]{1,0:T(8,128)(2,1)}, u32[]{:S(2)}, u32[]{:S(2)}) collective-permute-start(bf16[256,1024]{1,0:T(8,128)(2,1)} %convolution_convert_fusion), channel_id=1, source_target_pairs={{0,8},{2,10},{4,12},{6,14},{8,0},{10,2},{12,4},{14,6},{16,24},{18,... | collective-permute-start | bytes 1572872 | tf_op jit(solution)/shard_map/ppermute | solution.py:173
  97.3 33.6 %collective-permute-start.14 = (bf16[256,1024]{1,0:T(8,128)(2,1)}, bf16[256,1024]{1,0:T(8,128)(2,1)}, u32[]{:S(2)}, u32[]{:S(2)}) collective-permute-start(bf16[256,1024]{1,0:T(8,128)(2,1)} %convolution_convert_fusion.1), channel_id=1, source_target_pairs={{0,8},{2,10},{4,12},{6,14},{8,0},{10,2},{12,4},{14,6},{16,24},{18,... | collective-permute-start | bytes 1572872 | tf_op jit(solution)/shard_map/ppermute | solution.py:173
  102.9 33.5 %collective-permute-start.12 = (bf16[256,1024]{1,0:T(8,128)(2,1)}, bf16[256,1024]{1,0:T(8,128)(2,1)S(1)}, u32[]{:S(2)}, u32[]{:S(2)}) collective-permute-start(bf16[256,1024]{1,0:T(8,128)(2,1)} %add_convert_fusion.1), channel_id=1, source_target_pairs={{0,16},{2,18},{4,20},{6,22},{8,24},{10,26},{12,28},{14,30},{16,0},... | collective-permute-start | bytes 1572872 | tf_op jit(solution)/shard_map/ppermute | solution.py:173
  123.7 22.1 %collective-permute-start.11 = (bf16[256,1024]{1,0:T(8,128)(2,1)S(1)}, bf16[256,1024]{1,0:T(8,128)(2,1)S(1)}, u32[]{:S(2)}, u32[]{:S(2)}) collective-permute-start(bf16[256,1024]{1,0:T(8,128)(2,1)S(1)} %half_product.4), channel_id=1, source_target_pairs={{0,8},{2,10},{4,12},{6,14},{8,0},{10,2},{12,4},{14,6},{16,24},{18,... | collective-permute-start | bytes 1572872 | tf_op jit(solution)/shard_map/ppermute | solution.py:173
  133.8 26.8 %collective-permute-start.16 = (bf16[256,1024]{1,0:T(8,128)(2,1)S(1)}, bf16[256,1024]{1,0:T(8,128)(2,1)S(1)}, u32[]{:S(2)}, u32[]{:S(2)}) collective-permute-start(bf16[256,1024]{1,0:T(8,128)(2,1)S(1)} %add_convert_fusion), channel_id=1, source_target_pairs={{0,16},{2,18},{4,20},{6,22},{8,24},{10,26},{12,28},{14,30},{16,0},... | collective-permute-start | bytes 1572872 | tf_op jit(solution)/shard_map/ppermute | solution.py:173
  136.4 40.3 %copy-start = (f32[256,1024]{1,0:T(8,128)}, f32[256,1024]{1,0:T(8,128)S(1)}, u32[]{:S(2)}) copy-start(f32[256,1024]{1,0:T(8,128)S(1)} %convolution_add_fusion.1.km_ref.vm_ref) | copy-start | bytes 3145732
  136.4 40.2 %copy-start.3 = (bf16[256,1024]{1,0:T(8,128)(2,1)}, bf16[256,1024]{1,0:T(8,128)(2,1)S(1)}, u32[]{:S(2)}) copy-start(bf16[256,1024]{1,0:T(8,128)(2,1)S(1)} %collective-permute-done.12.kt_ref.vt_ref) | copy-start | bytes 1572868
  149.4 24.7 %collective-permute-start.15 = (bf16[256,1024]{1,0:T(8,128)(2,1)S(1)}, bf16[256,1024]{1,0:T(8,128)(2,1)S(1)}, u32[]{:S(2)}, u32[]{:S(2)}) collective-permute-start(bf16[256,1024]{1,0:T(8,128)(2,1)S(1)} %half_product.6), channel_id=1, source_target_pairs={{0,8},{2,10},{4,12},{6,14},{8,0},{10,2},{12,4},{14,6},{16,24},{18,... | collective-permute-start | bytes 1572872 | tf_op jit(solution)/shard_map/ppermute | solution.py:173
  149.6 16.5 %copy-start.11 = (s32[3]{0:T(128)}, s32[3]{0:T(128)S(1)}, u32[]{:S(2)}) copy-start(s32[3]{0:T(128)S(1)} %get-tuple-element.156.place_ref) | copy-start | bytes 40
  149.6 27.0 %collective-permute-start.18 = (bf16[128,1024]{1,0:T(8,128)(2,1)S(1)}, bf16[128,1024]{1,0:T(8,128)(2,1)S(1)}, u32[]{:S(2)}, u32[]{:S(2)}) collective-permute-start(bf16[128,1024]{1,0:T(8,128)(2,1)S(1)} %get-tuple-element.111), channel_id=1, source_target_pairs={{0,16},{2,18},{4,20},{6,22},{8,24},{10,26},{12,28},{14,30},{16,0},... | collective-permute-start | bytes 786440 | tf_op jit(solution)/shard_map/ppermute | solution.py:173
  176.6 17.4 %collective-permute-start.17 = (bf16[128,1024]{1,0:T(8,128)(2,1)}, bf16[128,1024]{1,0:T(8,128)(2,1)}, u32[]{:S(2)}, u32[]{:S(2)}) collective-permute-start(bf16[128,1024]{1,0:T(8,128)(2,1)} %get-tuple-element.125), channel_id=1, source_target_pairs={{0,16},{2,18},{4,20},{6,22},{8,24},{10,26},{12,28},{14,30},{16,0},... | collective-permute-start | bytes 786440 | tf_op jit(solution)/shard_map/ppermute | solution.py:173
  182.4 3.2 %collective-permute-start.21 = (bf16[1,2048]{1,0:T(2,128)(2,1)S(1)}, bf16[1,2048]{1,0:T(2,128)(2,1)S(1)}, u32[]{:S(2)}, u32[]{:S(2)}) collective-permute-start(bf16[1,2048]{1,0:T(2,128)(2,1)S(1)} %pad_maximum_fusion.6.refs_0_), channel_id=1, source_target_pairs={{0,6},{2,4},{4,2},{6,0},{8,14},{10,12},{12,10},{14,8},{16,22},{18,... | collective-permute-start | bytes 12296 | tf_op jit(solution)/shard_map/ppermute | solution.py:173
  183.1 3.7 %collective-permute-start.20 = (bf16[1,2048]{1,0:T(2,128)(2,1)S(1)}, bf16[1,2048]{1,0:T(2,128)(2,1)S(1)}, u32[]{:S(2)}, u32[]{:S(2)}) collective-permute-start(bf16[1,2048]{1,0:T(2,128)(2,1)S(1)} %pad_maximum_fusion.6.refs_0_), channel_id=1, source_target_pairs={{0,4},{2,6},{4,0},{6,2},{8,12},{10,14},{12,8},{14,10},{16,20},{18,... | collective-permute-start | bytes 12296 | tf_op jit(solution)/shard_map/ppermute | solution.py:173
  184.0 2.8 %collective-permute-start.19 = (bf16[1,2048]{1,0:T(2,128)(2,1)S(1)}, bf16[1,2048]{1,0:T(2,128)(2,1)S(1)}, u32[]{:S(2)}, u32[]{:S(2)}) collective-permute-start(bf16[1,2048]{1,0:T(2,128)(2,1)S(1)} %pad_maximum_fusion.6.refs_0_), channel_id=1, source_target_pairs={{0,2},{2,0},{4,6},{6,4},{8,10},{10,8},{12,14},{14,12},{16,18},{18,... | collective-permute-start | bytes 12296 | tf_op jit(solution)/shard_map/ppermute | solution.py:173
  188.8 11.7 %collective-permute-start.24 = (bf16[4,1,2048]{2,1,0:T(2,128)(2,1)}, bf16[4,1,2048]{2,1,0:T(2,128)(2,1)S(1)}, u32[]{:S(2)}, u32[]{:S(2)}) collective-permute-start(bf16[4,1,2048]{2,1,0:T(2,128)(2,1)} %order.1), channel_id=1, source_target_pairs={{0,24},{2,26},{4,28},{6,30},{8,16},{10,18},{12,20},{14,22},{16,8},... | collective-permute-start | bytes 49160 | tf_op jit(solution)/shard_map/ppermute | solution.py:173
  190.4 10.1 %collective-permute-start.23 = (bf16[4,1,2048]{2,1,0:T(2,128)(2,1)}, bf16[4,1,2048]{2,1,0:T(2,128)(2,1)S(1)}, u32[]{:S(2)}, u32[]{:S(2)}) collective-permute-start(bf16[4,1,2048]{2,1,0:T(2,128)(2,1)} %order.1), channel_id=1, source_target_pairs={{0,16},{2,18},{4,20},{6,22},{8,24},{10,26},{12,28},{14,30},{16,0},... | collective-permute-start | bytes 49160 | tf_op jit(solution)/shard_map/ppermute | solution.py:173
  191.4 9.1 %collective-permute-start.22 = (bf16[4,1,2048]{2,1,0:T(2,128)(2,1)}, bf16[4,1,2048]{2,1,0:T(2,128)(2,1)S(1)}, u32[]{:S(2)}, u32[]{:S(2)}) collective-permute-start(bf16[4,1,2048]{2,1,0:T(2,128)(2,1)} %order.1), channel_id=1, source_target_pairs={{0,8},{2,10},{4,12},{6,14},{8,0},{10,2},{12,4},{14,6},{16,24},{18,... | collective-permute-start | bytes 49160 | tf_op jit(solution)/shard_map/ppermute | solution.py:173
  (22 other events, 129.6 us)
Sparse Core Ops, SparseCore 0:
  9.8 37.1 all-gather.3
  49.2 34.4 all-gather.5
  85.2 34.4 all-gather.7
